TPU v7x, 512 devices: a whole 4x8x8 slice. The times are simulated.
512 devices in a mesh: tower: 16 (over x, y_hi), rank: 32 (over y_lo, z, core).
Axes of the slice: x: 4, y: 8 (y_hi: 4, y_lo: 2; y = y_hi * 2 + y_lo), z: 8, core: 2. Of those that a mesh axis runs over, the one named last changes fastest.
Arguments:
- pooled: bfloat16 [2, 8192, 16384], P(None, ('tower', 'rank')), may hold values from -8 to 8
- feature_order: int32 [16, 4], P('tower'), may hold values from 0 to 3, as said below
- cross_weight: bfloat16 [16, 3, 512, 512], P('tower'), may hold values from -0.25 to 0.25
- cross_bias: float32 [16, 3, 512], P('tower'), may hold values from -3 to 3
- compress_weight: bfloat16 [16, 128, 512], P('tower'), may hold values from -0.25 to 0.25
- norm_gain: float32 [16, 128], P('tower'), may hold values from 0.1 to 1.9
- mlp_weight: bfloat16 [4096, 2048], P(('tower', 'rank')), may hold values from -0.125 to 0.125
- mlp_bias: bfloat16 [4096], P(('tower', 'rank')), may hold values from -3 to 3
- out_weight: bfloat16 [4096], P(('tower', 'rank')), may hold values from -0.09375 to 0.09375
Outputs:
- logits: float32 [2, 32, 512], P(None, 'rank', 'tower')
Inputs may be any that keep to these rules, and one draw needn't show every extreme that they name: `feature_order`: each row is an ordering of 0 to 3.
All inputs are finite; a program needn't handle non-finite values.
Results may differ from a plain program's by a relative error of at most 0.0076.
Values may be sent and summed in bfloat16 or wider, within the bound.
No kernel may reach another device: no remote copies, remote signals or barrier semaphores. Data moves between devices by JAX's collectives and lax.ppermute only.
A program may use at most 64 MiB of HBM per device.

v0:
```python
import math

import jax
import jax.numpy as jnp
from jax import lax
from jax.sharding import PartitionSpec as P

E = 128
CD = 128


epsilon = 1e-06


def side_by_side(arrays, axis, dim, along):
    widths = [math.prod(a.shape[along:]) for a in arrays]
    both = jnp.concatenate(
        [a.reshape(*a.shape[:along], w) for a, w in zip(arrays, widths)], axis=along
    )
    whole = lax.all_gather(both, axis, axis=dim, tiled=True)
    parts = jnp.split(whole, [sum(widths[:k]) for k in range(1, len(widths))], axis=along)
    return tuple((b.reshape(*whole.shape[:along], *a.shape[along:]) for a, b in zip(arrays, parts)))


def in_blocks(x, dim, devices):
    shape = x.shape
    parts = x.reshape(*shape[:dim], devices, shape[dim] // devices, *shape[dim + 1 :])
    return jnp.moveaxis(parts, dim, 0)


def summed_on_arrival(x, axis, dim):
    parts = in_blocks(x, dim, lax.axis_size(axis))
    arrived = lax.all_to_all(parts, axis, split_axis=0, concat_axis=0, tiled=True)
    return arrived.sum(axis=0)


def tower_block(first, weights, biases, compress, gain):
    first_f = first.astype(jnp.float32)
    current = first
    for layer in range(weights.shape[0]):
        product = (
            jnp.dot(weights[layer], current, preferred_element_type=jnp.float32)
            + biases[layer][:, None]
        )
        current = (first_f * product + current.astype(jnp.float32)).astype(jnp.bfloat16)
    squeezed = jnp.dot(compress, current, preferred_element_type=jnp.float32)
    inverse_rms = lax.rsqrt(jnp.mean(squeezed * squeezed, axis=0, keepdims=True) + epsilon)
    return (squeezed * inverse_rms * gain[:, None]).astype(jnp.bfloat16)


def interact(joined):
    samples_now = joined.shape[1]
    values_f = joined.astype(jnp.float32).reshape(-1, CD, samples_now)
    gram = jnp.einsum("tck,uck->tuk", values_f, values_f, precision=lax.Precision.HIGHEST) / CD
    mixed = values_f + jnp.einsum("tuk,uck->tck", gram, values_f, precision=lax.Precision.HIGHEST)
    return mixed.reshape(-1, samples_now).astype(jnp.bfloat16)


def logit_terms(hidden_rows, hidden_bias, hidden_out, features):
    hidden = (
        jnp.dot(hidden_rows, features, preferred_element_type=jnp.float32)
        + hidden_bias.astype(jnp.float32)[:, None]
    )
    return jnp.sum(
        jax.nn.relu(hidden) * hidden_out.astype(jnp.float32)[:, None], axis=0, keepdims=True
    )


def on_device(
    pooled,
    feature_order,
    cross_weight,
    cross_bias,
    compress_weight,
    norm_gain,
    mlp_weight,
    mlp_bias,
    out_weight,
):
    micro_count = pooled.shape[0]
    arriving = [
        lax.all_to_all(pooled[batch], "rank", split_axis=1, concat_axis=0, tiled=True)
        for batch in range(micro_count)
    ]
    hidden_rows, hidden_bias, hidden_out = side_by_side(
        (mlp_weight, mlp_bias, out_weight), "tower", 0, 1
    )
    results = []
    for batch in range(micro_count):
        arrived = arriving[batch]
        samples_here = arrived.shape[1]
        first = jnp.take(arrived.reshape(-1, E, samples_here), feature_order[0], axis=0).reshape(
            -1, samples_here
        )
        compressed = tower_block(
            first, cross_weight[0], cross_bias[0], compress_weight[0], norm_gain[0]
        )
        tower_parts = lax.all_to_all(compressed, "tower", split_axis=1, concat_axis=0, tiled=True)
        mixed = interact(tower_parts)
        partial_value = logit_terms(
            hidden_rows, hidden_bias, hidden_out, lax.all_gather(mixed, "rank", axis=1, tiled=True)
        )
        logit_row = summed_on_arrival(partial_value, "rank", 1)
        results.append(logit_row)
    return jnp.stack(results)


def solution(mesh):
    return jax.shard_map(
        on_device,
        mesh=mesh,
        in_specs=(
            P(None, ("tower", "rank"), None),
            P("tower", None),
            P("tower", None, None, None),
            P("tower", None, None),
            P("tower", None, None),
            P("tower", None),
            P(("tower", "rank"), None),
            P(("tower", "rank")),
            P(("tower", "rank")),
        ),
        out_specs=P(None, "rank", "tower"),
        check_vma=False,
    )
```

profile of v0, /device:TPU:1, one launch (start us, length us, event | category | flops | bytes accessed | tf_op | source)
XLA Modules:
  0.0 249.7 jit_solution(15419998319595481402)
XLA Ops:
  6.5 1.3 fusion.58
  7.8 0.2 copy.84
  8.0 1.1 copy.64
  9.1 13.0 %all-to-all-start = ((bf16[16,32,512]{2,0,1:T(8,128)(2,1)}), bf16[16,32,512]{2,0,1:T(8,128)(2,1)S(1)}, u32[]{:S(2)}, u32[]{:S(2)}) async-start(bf16[16,32,512]{2,0,1:T(8,128)(2,1)} %copy.64), calls=%async_computation | async-start | bytes 1048576 | tf_op jit(solution)/shard_map/all_to_all | solution.py:82
  22.1 0.2 copy.86
  22.3 1.1 copy.72
  23.4 14.4 %all-to-all-done = bf16[16,32,512]{2,0,1:T(8,128)(2,1)S(1)} async-done(((bf16[16,32,512]{2,0,1:T(8,128)(2,1)}), bf16[16,32,512]{2,0,1:T(8,128)(2,1)S(1)}, u32[]{:S(2)}, u32[]{:S(2)}) %all-to-all-start) | async-done | bytes 524320 | tf_op jit(solution)/shard_map/all_to_all | solution.py:82
  37.8 5.5 %all-to-all-start.3 = ((bf16[16,32,512]{2,0,1:T(8,128)(2,1)}), bf16[16,32,512]{2,0,1:T(8,128)(2,1)S(1)}, u32[]{:S(2)}, u32[]{:S(2)}) async-start(bf16[16,32,512]{2,0,1:T(8,128)(2,1)} %copy.72), calls=%async_computation.3 | async-start | bytes 1048576 | tf_op jit(solution)/shard_map/all_to_all | solution.py:82
  43.3 0.0 all-gather.3.cloned.1.call-start
  43.4 0.6 gather_fusion
  44.0 15.0 %all-to-all-done.3 = bf16[16,32,512]{2,0,1:T(8,128)(2,1)S(1)} async-done(((bf16[16,32,512]{2,0,1:T(8,128)(2,1)}), bf16[16,32,512]{2,0,1:T(8,128)(2,1)S(1)}, u32[]{:S(2)}, u32[]{:S(2)}) %all-to-all-start.3) | async-done | bytes 524320 | tf_op jit(solution)/shard_map/all_to_all | solution.py:82
  59.0 0.6 gather_fusion.1
  59.6 0.2 broadcast_select_fusion.1
  59.7 0.2 copy.83
  59.9 0.2 copy.82
  60.2 1.7 fusion.11
  61.9 0.5 fusion.10
  62.4 1.3 fusion.14
  63.7 0.5 fusion.12
  64.3 0.9 copy-done.7
  65.1 2.0 multiply_reduce_fusion
  67.2 0.8 multiply_reduce_fusion.1
  68.0 0.2 multiply_convert_fusion.1
  68.3 18.7 %all_to_all.68 = bf16[128,16,32]{0,2,1:T(8,128)(2,1)S(1)} all-to-all(bf16[128,16,32]{0,2,1:T(8,128)(2,1)S(1)} %bitcast.175), channel_id=1, replica_groups=mesh['tower'=16,'rank'=32] {'tower'}, dimensions={1} | all-to-all | bytes 262144 | tf_op jit(solution)/shard_map/all_to_all | solution.py:98
  87.0 0.2 fusion.27
  87.2 0.4 fusion.28
  87.6 0.7 copy.99
  88.3 0.0 all-gather.3.cloned.1.call-update
  88.3 0.0 all-gather.5.cloned.1.call-start
  88.3 12.3 %all_to_all.69 = bf16[128,16,32]{0,2,1:T(8,128)(2,1)S(1)} all-to-all(bf16[128,16,32]{0,2,1:T(8,128)(2,1)S(1)} %bitcast.174), channel_id=1, replica_groups=mesh['tower'=16,'rank'=32] {'tower'}, dimensions={1} | all-to-all | bytes 262144 | tf_op jit(solution)/shard_map/all_to_all | solution.py:98
  100.7 0.2 fusion.25
  100.9 0.4 fusion.29
  101.3 0.7 copy.98
  102.0 0.1 copy.62
  102.1 0.1 copy.63
  102.2 0.1 concatenate.3
  102.3 38.0 %all_gather.9 = bf16[128,2050]{1,0:T(8,128)(2,1)S(1)} all-gather(bf16[8,2050]{1,0:T(8,128)(2,1)S(1)} %concatenate.3), channel_id=1, replica_groups=mesh['tower'=16,'rank'=32] {'tower'}, dimensions={0}, use_global_device_ids=true | all-gather | bytes 557600 | tf_op jit(solution)/shard_map/all_gather | solution.py:20
  140.3 0.2 convert_reduce_fusion.1
  140.4 11.5 %all-gather.3.cloned.1.call-done = bf16[2048,1024]{0,1:T(8,128)(2,1)} async-done(((bf16[2048,32]{0,1:T(8,128)(2,1)}), bf16[2048,1024]{0,1:T(8,128)(2,1)}) %all-gather.3.cloned.1.call-update) | async-done | bytes 4194320 | tf_op jit(solution)/shard_map/all_gather | solution.py:101
  152.0 3.7 %fusion.23 = f32[1024]{0:T(1024)S(1)} fusion(bf16[2048,1024]{0,1:T(8,128)(2,1)} %all-gather.3.cloned.1.call-done, bf16[128,2050]{1,0:T(8,128)(2,1)S(1)} %all_gather.9, f32[128]{0:T(128)S(1)} %get-tuple-element.7, f32[128]{0:T(128)S(1)} %get-tuple-element.6), kind=kOutput, calls=%fused_computation.41 | convolution fusion | flops 537394176 | bytes 4723712 | tf_op jit(solution)/shard_map/dot_general | solution.py:61
  155.7 0.7 transpose_reshape_broadcast_in_dim.6
  156.4 6.5 %all-to-all-start.2 = ((f32[32,1,32]{2,1,0:T(1,128)}), f32[32,1,32]{2,1,0:T(1,128)S(1)}, u32[]{:S(2)}, u32[]{:S(2)}) async-start(f32[32,1,32]{2,1,0:T(1,128)} %transpose_reshape_broadcast_in_dim.6), calls=%async_computation.2 | async-start | bytes 32768 | tf_op jit(solution)/shard_map/all_to_all | solution.py:33
  162.9 60.7 %all-gather.5.cloned.1.call-done = bf16[2048,1024]{0,1:T(8,128)(2,1)} async-done(((bf16[2048,32]{0,1:T(8,128)(2,1)}), bf16[2048,1024]{0,1:T(8,128)(2,1)}) %all-gather.5.cloned.1.call-update) | async-done | bytes 4194320 | tf_op jit(solution)/shard_map/all_gather | solution.py:101
  223.5 3.7 %fusion.22 = f32[1024]{0:T(1024)S(1)} fusion(bf16[2048,1024]{0,1:T(8,128)(2,1)} %all-gather.5.cloned.1.call-done, bf16[128,2050]{1,0:T(8,128)(2,1)S(1)} %all_gather.9, f32[128]{0:T(128)S(1)} %get-tuple-element.7, f32[128]{0:T(128)S(1)} %get-tuple-element.6), kind=kOutput, calls=%fused_computation.40 | convolution fusion | flops 537394176 | bytes 4723712 | tf_op jit(solution)/shard_map/dot_general | solution.py:61
  227.3 0.7 transpose_reshape_broadcast_in_dim.7
  228.0 6.5 %all-to-all-start.5 = ((f32[32,1,32]{2,1,0:T(1,128)}), f32[32,1,32]{2,1,0:T(1,128)S(1)}, u32[]{:S(2)}, u32[]{:S(2)}) async-start(f32[32,1,32]{2,1,0:T(1,128)} %transpose_reshape_broadcast_in_dim.7), calls=%async_computation.5 | async-start | bytes 32768 | tf_op jit(solution)/shard_map/all_to_all | solution.py:33
  234.5 7.8 %all-to-all-done.5 = f32[32,1,32]{2,1,0:T(1,128)S(1)} async-done(((f32[32,1,32]{2,1,0:T(1,128)}), f32[32,1,32]{2,1,0:T(1,128)S(1)}, u32[]{:S(2)}, u32[]{:S(2)}) %all-to-all-start.5) | async-done | bytes 4128 | tf_op jit(solution)/shard_map/all_to_all | solution.py:33
  242.3 0.6 pad_maximum_fusion
  (26 shorter events, 0.1 us)
Async XLA Ops:
  6.5 57.7 %copy-start = (bf16[1,128,512]{2,1,0:T(8,128)(2,1)S(1)}, bf16[1,128,512]{2,1,0:T(8,128)(2,1)}, u32[]{:S(2)}) copy-start(bf16[1,128,512]{2,1,0:T(8,128)(2,1)} %param.15) | copy-start | bytes 393220
  9.1 28.7 %all-to-all-start = ((bf16[16,32,512]{2,0,1:T(8,128)(2,1)}), bf16[16,32,512]{2,0,1:T(8,128)(2,1)S(1)}, u32[]{:S(2)}, u32[]{:S(2)}) async-start(bf16[16,32,512]{2,0,1:T(8,128)(2,1)} %copy.64), calls=%async_computation | async-start | bytes 1048576 | tf_op jit(solution)/shard_map/all_to_all | solution.py:82
  22.1 21.2 %copy-start.8 = (s32[1,4]{1,0:T(1,128)S(1)}, s32[1,4]{1,0:T(1,128)}, u32[]{:S(2)}) copy-start(s32[1,4]{1,0:T(1,128)} %param.12) | copy-start | bytes 52
  22.1 21.3 %copy-start.2 = (f32[1,3,512]{2,0,1:T(1,128)S(1)}, f32[1,3,512]{2,0,1:T(1,128)}, u32[]{:S(2)}) copy-start(f32[1,3,512]{2,0,1:T(1,128)} %param.14) | copy-start | bytes 18436
  37.8 21.2 %all-to-all-start.3 = ((bf16[16,32,512]{2,0,1:T(8,128)(2,1)}), bf16[16,32,512]{2,0,1:T(8,128)(2,1)S(1)}, u32[]{:S(2)}, u32[]{:S(2)}) async-start(bf16[16,32,512]{2,0,1:T(8,128)(2,1)} %copy.72), calls=%async_computation.3 | async-start | bytes 1048576 | tf_op jit(solution)/shard_map/all_to_all | solution.py:82
  43.3 108.7 %all-gather.3.cloned.1.call-start = ((), (), s32[]{:S(2)}) async-start(), calls=%async_computation.6 | async-start | bytes 4325376 | tf_op jit(solution)/shard_map/all_gather | solution.py:101
  60.2 1.7 copy-start.6
  63.7 1.4 copy-start.7
  67.2 0.8 copy-start.5
  68.2 33.7 %copy-start.3 = (bf16[8]{0:T(256)(128)(2,1)S(1)}, bf16[8]{0:T(256)(128)(2,1)}, u32[]{:S(2)}) copy-start(bf16[8]{0:T(256)(128)(2,1)} %param.18) | copy-start | bytes 52
  68.2 33.8 %copy-start.4 = (bf16[8]{0:T(256)(128)(2,1)S(1)}, bf16[8]{0:T(256)(128)(2,1)}, u32[]{:S(2)}) copy-start(bf16[8]{0:T(256)(128)(2,1)} %param.19) | copy-start | bytes 52
  68.3 33.9 %copy-start.1 = (bf16[8,2048]{1,0:T(8,128)(2,1)S(1)}, bf16[8,2048]{1,0:T(8,128)(2,1)}, u32[]{:S(2)}) copy-start(bf16[8,2048]{1,0:T(8,128)(2,1)} %param.17) | copy-start | bytes 98308
  88.3 135.2 %all-gather.5.cloned.1.call-start = ((), (), s32[]{:S(2)}) async-start(), calls=%async_computation.7 | async-start | bytes 4325376 | tf_op jit(solution)/shard_map/all_gather | solution.py:101
  156.4 71.6 %all-to-all-start.2 = ((f32[32,1,32]{2,1,0:T(1,128)}), f32[32,1,32]{2,1,0:T(1,128)S(1)}, u32[]{:S(2)}, u32[]{:S(2)}) async-start(f32[32,1,32]{2,1,0:T(1,128)} %transpose_reshape_broadcast_in_dim.6), calls=%async_computation.2 | async-start | bytes 32768 | tf_op jit(solution)/shard_map/all_to_all | solution.py:33
  228.0 14.3 %all-to-all-start.5 = ((f32[32,1,32]{2,1,0:T(1,128)}), f32[32,1,32]{2,1,0:T(1,128)S(1)}, u32[]{:S(2)}, u32[]{:S(2)}) async-start(f32[32,1,32]{2,1,0:T(1,128)} %transpose_reshape_broadcast_in_dim.7), calls=%async_computation.5 | async-start | bytes 32768 | tf_op jit(solution)/shard_map/all_to_all | solution.py:33
Sparse Core Ops, SparseCore 0:
  88.4 63.5 all-gather.2
  154.1 69.3 all-gather.4
where the time goes:
time: 250 us
  waiting for transfers between devices  109 us (44%)
  blocking collectives  69 us (28%)
  starting transfers between devices  31.5 us (13%)
  matrix products  15.5 us (6%)
  between operations  13.7 us (5%)
  local copies, waits for them, and re-layouts  9.29 us (4%)
    all_gather x2, waiting for transfers between devices, on_device(): lax.all_gather(mixed, 'rank', axis=1, tiled=True)  72.2 us
    all_gather x1, blocking collectives, side_by_side(): whole = lax.all_gather(both, axis, axis=dim, tiled=True)  38 us
    all_to_all x2, blocking collectives, on_device(): lax.all_to_all(compressed, 'tower', split_axis=1, concat_axis=0, tiled=True)  31 us
    all_to_all x2, waiting for transfers between devices, on_device(): lax.all_to_all(pooled[batch], 'rank', split_axis=1, concat_axis=0, tiled=...  29.4 us
    all_to_all x2, starting transfers between devices, on_device(): lax.all_to_all(pooled[batch], 'rank', split_axis=1, concat_axis=0, tiled=...  18.4 us
    all_to_all x2, starting transfers between devices, summed_on_arrival(): lax.all_to_all(parts, axis, split_axis=0, concat_axis=0, tiled=True)  13 us
    all_to_all x2, waiting for transfers between devices, summed_on_arrival(): lax.all_to_all(parts, axis, split_axis=0, concat_axis=0, tiled=True)  7.8 us
    dot_general x2, matrix products, logit_terms(): jnp.dot(hidden_rows, features, preferred_element_type=jnp.float32)  7.43 us
  transfers between devices with their start and end apart: 6, of which 5 were waited for; matrix products, arithmetic and copies ran while one was open for 5% of the time, Pallas kernels for 0%

commit v1 on v0

v1 whole, which is shorter than its diff:
```python
import jax
import jax.numpy as jnp
from jax import lax
from jax.experimental import pallas as pl
from jax.experimental.pallas import tpu as pltpu
from jax.sharding import Mesh
from jax.sharding import PartitionSpec as P

E = 128
FT = 4
CD = 128
TD = 512
LAYERS = 3
TOWERS = 16
BLOCK = 32
GROUP = 16
WIDE = 2048 + 128
EPSILON = 1e-06

AXES = (("x", 4), ("yh", 4), ("yl", 2), ("z", 8), ("c", 2))
TOWER = ("x", "yh")
RANK = ("yl", "z", "c")


def tower_kernel(order, arrived, weights, biases, compress, gain, out):
    bias_columns = jnp.transpose(biases[...])
    gain_column = jnp.transpose(gain[...])
    for batch in range(2):
        for half in range(2):
            lanes = pl.ds(half * 256, 256)
            slots = [
                arrived[pl.ds(order[0, k] * 8, 8), batch, :, lanes].reshape(E, 256)
                for k in range(FT)
            ]
            first = jnp.concatenate(slots, axis=0)
            first_f = first.astype(jnp.float32)
            current = first
            for layer in range(LAYERS):
                product = (
                    jnp.dot(weights[layer], current, preferred_element_type=jnp.float32)
                    + bias_columns[:, layer : layer + 1]
                )
                current = (first_f * product + current.astype(jnp.float32)).astype(jnp.bfloat16)
            squeezed = jnp.dot(compress[...], current, preferred_element_type=jnp.float32)
            inverse_rms = lax.rsqrt(
                jnp.mean(squeezed * squeezed, axis=0, keepdims=True) + EPSILON
            )
            scaled = squeezed * inverse_rms * gain_column[:, :1]
            rows = jnp.transpose(scaled).astype(jnp.bfloat16)
            for block in range(8):
                t = half * 8 + block
                out[t % 4, t // 4, batch] = rows[block * BLOCK : (block + 1) * BLOCK]


def tower_block(order, arrived, weights, biases, compress, gain):
    vmem = pl.BlockSpec(memory_space=pltpu.VMEM)
    return pl.pallas_call(
        tower_kernel,
        out_shape=jax.ShapeDtypeStruct((4, 4, 2, BLOCK, CD), jnp.bfloat16),
        in_specs=[pl.BlockSpec(memory_space=pltpu.SMEM)] + [vmem] * 5,
        out_specs=vmem,
        compiler_params=pltpu.CompilerParams(vmem_limit_bytes=32 * 2**20),
        cost_estimate=pl.CostEstimate(
            flops=2 * 1024 * (3 * TD * TD + TD * CD), bytes_accessed=4 * 2**20, transcendentals=1024
        ),
    )(order, arrived, weights, biases, compress, gain)


def score_kernel(core, own, other, rows, out, mixed):
    samples = own.shape[1]
    side = TOWERS * GROUP
    same = (
        lax.broadcasted_iota(jnp.int32, (side, side), 0) % GROUP
        == lax.broadcasted_iota(jnp.int32, (side, side), 1) % GROUP
    )
    scale = jnp.where(same, jnp.float32(1.0 / CD), jnp.float32(0.0))
    for which, features in enumerate((own, other)):

        def interact(step, carry, features=features, which=which):
            at = pl.multiple_of(step * GROUP, GROUP)
            values = features[:, pl.ds(at, GROUP), :].reshape(side, CD)
            gram = (
                lax.dot_general(
                    values, values, (((1,), (1,)), ((), ())), preferred_element_type=jnp.float32
                )
                * scale
            )
            high = gram.astype(jnp.bfloat16)
            low = (gram - high.astype(jnp.float32)).astype(jnp.bfloat16)
            result = (
                values.astype(jnp.float32)
                + jnp.dot(high, values, preferred_element_type=jnp.float32)
                + jnp.dot(low, values, preferred_element_type=jnp.float32)
            ).astype(jnp.bfloat16)
            to = pl.ds(pl.multiple_of(which * samples + step * GROUP, GROUP), GROUP)
            for t in range(TOWERS):
                mixed[to, t * CD : (t + 1) * CD] = result[t * GROUP : (t + 1) * GROUP]
            return carry

        lax.fori_loop(0, samples // GROUP, interact, 0, unroll=4)

    total = jnp.zeros((1, 2 * samples), jnp.float32)
    for part in range(2):
        at = pl.ds(part * 256, 256)
        hidden = lax.dot_general(
            rows[at, : TOWERS * CD],
            mixed[...],
            (((1,), (1,)), ((), ())),
            preferred_element_type=jnp.float32,
        )
        extra = rows[at, TOWERS * CD :].astype(jnp.float32)
        terms = jnp.maximum(hidden + extra[:, 0:1], 0.0) * extra[:, 1:2]
        total = total + jnp.sum(terms, axis=0, keepdims=True)

    for which in range(2):
        mine = core[0] if which == 0 else 1 - core[0]
        for x in range(4):
            at = which * samples + x * 64
            out[mine * 4 + x, 0:1, 0:64] = total[:, at : at + 64]


def score(core, own, other, rows):
    vmem = pl.BlockSpec(memory_space=pltpu.VMEM)
    return pl.pallas_call(
        score_kernel,
        out_shape=jax.ShapeDtypeStruct((8, 8, 128), jnp.float32),
        in_specs=[pl.BlockSpec(memory_space=pltpu.SMEM)] + [vmem] * 3,
        out_specs=vmem,
        scratch_shapes=[pltpu.VMEM((512, TOWERS * CD), jnp.bfloat16)],
        compiler_params=pltpu.CompilerParams(vmem_limit_bytes=32 * 2**20),
        cost_estimate=pl.CostEstimate(
            flops=3 * 10**9, bytes_accessed=6 * 2**20, transcendentals=0
        ),
    )(core, own, other, rows)


def hidden_rows(mlp_weight, mlp_bias, out_weight):
    row = jnp.concatenate([mlp_weight, mlp_bias[:, None], out_weight[:, None]], axis=1)
    row = jnp.pad(row, ((0, 24), (0, WIDE - row.shape[1])))
    across = lax.all_gather(row, ("yh", "yl"), axis=0)
    return lax.all_gather(across[:, :8].reshape(64, WIDE), "z", axis=0, tiled=True)


def on_device(
    pooled,
    feature_order,
    cross_weight,
    cross_bias,
    compress_weight,
    norm_gain,
    mlp_weight,
    mlp_bias,
    out_weight,
):
    rows = hidden_rows(mlp_weight, mlp_bias, out_weight)
    sent = pooled.reshape(2, 16, 32, 512).transpose(2, 0, 1, 3)
    arrived = lax.all_to_all(sent, RANK, split_axis=0, concat_axis=0, tiled=True)
    towers = tower_block(
        feature_order, arrived, cross_weight[0], cross_bias[0], compress_weight[0], norm_gain
    )
    column = lax.all_to_all(towers, "yh", split_axis=0, concat_axis=0, tiled=True)
    column = column.reshape(4, 256, CD)
    features = lax.all_to_all(
        jnp.broadcast_to(column[None], (4, 4, 256, CD)), "x", split_axis=0, concat_axis=0, tiled=True
    ).reshape(TOWERS, 256, CD)
    other = lax.ppermute(features, "c", [(0, 1), (1, 0)])
    core = lax.axis_index("c").reshape(1).astype(jnp.int32)
    partial = score(core, features, other, rows)
    terms = lax.all_to_all(partial, ("c", "x"), split_axis=0, concat_axis=0, tiled=True)
    return jnp.sum(terms, axis=0)[0, :64].reshape(2, 1, BLOCK)


def solution(mesh):
    split = Mesh(
        mesh.devices.reshape([size for _, size in AXES]), tuple(name for name, _ in AXES)
    )
    every = TOWER + RANK
    return jax.shard_map(
        on_device,
        mesh=split,
        in_specs=(
            P(None, every, None),
            P(TOWER, None),
            P(TOWER, None, None, None),
            P(TOWER, None, None),
            P(TOWER, None, None),
            P(TOWER, None),
            P(every, None),
            P(every),
            P(every),
        ),
        out_specs=P(None, RANK, TOWER),
        check_vma=False,
    )
```

time: 250 us -> 131 us (0.52)
  waiting for transfers between devices: 109 us -> 32.4 us
  blocking collectives: 69 us -> 39.1 us
  matrix products: 15.5 us -> 0 us
  Pallas kernels: 0 us -> 13.9 us
  starting transfers between devices: 31.5 us -> 21.8 us
    all_gather x2, waiting for transfers between devices: 72.2 us -> 30.1 us  [the longest x1 29.2 us: hidden_rows(): across = lax.all_gather(row, ('yh', 'yl'), axis=0)]
    all_gather x1 -> x0, blocking collectives: 38 us -> none  [side_by_side(): whole = lax.all_gather(both, axis, axis=dim, tiled=True)]
    all_to_all x4 -> x1, waiting for transfers between devices: 37.2 us -> 0.01 us  [on_device(): lax.all_to_all(sent, RANK, split_axis=0, concat_axis=0, tiled=True)]
    all_to_all x4 -> x1, starting transfers between devices: 31.4 us -> 13.1 us  [on_device(): lax.all_to_all(sent, RANK, split_axis=0, concat_axis=0, tiled=True)]
    dot_general x12 -> x0, matrix products: 15.5 us -> none  [the longest x2 7.43 us: logit_terms(): jnp.dot(hidden_rows, features, preferred_element_type=jnp.float32)]
    pallas_call x0 -> x2, Pallas kernels: none -> 13.9 us  [the longest x1 8.7 us: score(): pl.pallas_call(score_kernel, out_shape=jax.ShapeDtypeStruct((8, 8, 128),...]
    ppermute x0 -> x1, starting transfers between devices: none -> 8.67 us  [on_device(): other = lax.ppermute(features, 'c', [(0, 1), (1, 0)])]
    all_to_all x2 -> x3, blocking collectives: 31 us -> 39.1 us  [the longest x1 13.6 us: on_device(): lax.all_to_all(partial, ('c', 'x'), split_axis=0, concat_axis=0, tiled=True)]
  transfers between devices with their start and end apart: 6 -> 4, of which waited for: 5 -> 3; matrix products, arithmetic and copies ran while one was open for 5% -> 3% of each run, Pallas kernels for 0% -> 4%
where the time goes in v1:
time: 131 us; the launch traced here: 130 us
  blocking collectives  39.1 us (30%)
  waiting for transfers between devices  32.4 us (25%)
  starting transfers between devices  21.8 us (17%)
  Pallas kernels  13.9 us (11%)
  between operations  13.5 us (10%)
  local copies, waits for them, and re-layouts  9.55 us (7%)
    all_gather x1, waiting for transfers between devices, hidden_rows(): across = lax.all_gather(row, ('yh', 'yl'), axis=0)  29.2 us
    all_to_all x1, blocking collectives, on_device(): lax.all_to_all(partial, ('c', 'x'), split_axis=0, concat_axis=0, tiled=True)  13.6 us
    all_to_all x1, blocking collectives, on_device(): lax.all_to_all(jnp.broadcast_to(column[None], (4, 4, 256, CD)), 'x', spli...  13.6 us
    all_to_all x1, starting transfers between devices, on_device(): lax.all_to_all(sent, RANK, split_axis=0, concat_axis=0, tiled=True)  13.1 us
    all_to_all x1, blocking collectives, on_device(): lax.all_to_all(towers, 'yh', split_axis=0, concat_axis=0, tiled=True)  11.9 us
    pallas_call x1, Pallas kernels, score(): pl.pallas_call(score_kernel, out_shape=jax.ShapeDtypeStruct((8, 8, 128),...  8.7 us
    ppermute x1, starting transfers between devices, on_device(): other = lax.ppermute(features, 'c', [(0, 1), (1, 0)])  8.67 us
    pallas_call x1, Pallas kernels, tower_block(): pl.pallas_call(tower_kernel, out_shape=jax.ShapeDtypeStruct((4, 4, 2, BLO...  5.17 us
  transfers between devices with their start and end apart: 4, of which 3 were waited for; matrix products, arithmetic and copies ran while one was open for 3% of the time, Pallas kernels for 4%

profile of v1, /device:TPU:1, one launch (start us, length us, event | category | flops | bytes accessed | tf_op | source)
XLA Modules:
  0.0 130.3 jit_solution(7216460913573340257)
XLA Ops:
  6.5 0.0 all-gather.6.cloned.1.call-start
  6.5 0.7 copy.14
  7.3 0.7 copy.15
  8.0 0.8 concatenate.3
  8.9 0.7 pad.4
  9.5 0.0 all-gather.6.cloned.1.call-update
  9.6 2.3 %copy.21 = bf16[2,2,32,8,512]{4,3,1,0,2:T(8,128)(2,1)} copy(bf16[2,2,32,8,512]{4,3,2,1,0:T(8,128)(2,1)} %bitcast.28) | data formatting | bytes 2097152 | tf_op jit(solution)/shard_map/reshape | solution.py:156
  11.9 0.0 copy-start.5
  11.9 0.0 copy-start.1
  11.9 0.0 copy-start.2
  11.9 0.0 copy-start.3
  11.9 0.0 copy-start.4
  11.9 13.1 %all-to-all-start = ((bf16[32,2,16,512]{3,2,1,0:T(8,128)(2,1)}), bf16[32,2,16,512]{3,2,1,0:T(8,128)(2,1)S(1)}, u32[]{:S(2)}, u32[]{:S(2)}) async-start(bf16[32,2,16,512]{3,2,1,0:T(8,128)(2,1)} %bitcast.26), calls=%async_computation | async-start | bytes 2097152 | tf_op jit(solution)/shard_map/all_to_all | solution.py:157
  25.1 0.0 all-gather.4.cloned.1.call-start
  25.1 29.2 %all-gather.6.cloned.1.call-done = bf16[256,2176]{1,0:T(8,128)(2,1)} async-done(((bf16[32,2176]{1,0:T(8,128)(2,1)}), bf16[256,2176]{1,0:T(8,128)(2,1)}) %all-gather.6.cloned.1.call-update) | async-done | bytes 1114128 | tf_op jit(solution)/shard_map/all_gather | solution.py:140
  54.3 1.7 %slice_bitcast_fusion = bf16[64,2176]{1,0:T(8,128)(2,1)} fusion(bf16[8,32,2176]{2,1,0:T(8,128)(2,1)} %bitcast.29), kind=kLoop, calls=%fused_computation.1 | loop fusion | bytes 557056 | tf_op jit(solution)/shard_map/reshape | solution.py:141
  56.0 0.0 all-gather.4.cloned.1.call-update
  56.0 0.0 copy-done.5
  56.1 0.0 all-to-all-done.arrived
  56.1 0.0 copy-done.1
  56.1 0.0 copy-done.2
  56.1 0.0 copy-done.3
  56.1 0.0 copy-done.4
  56.1 5.2 %shard_map.91 = bf16[4,4,2,32,128]{4,3,2,1,0:T(8,128)(2,1)S(1)} custom-call(s32[1,4]{1,0:T(1,128)S(1)} %copy-done.3, bf16[32,2,16,512]{3,2,1,0:T(8,128)(2,1)S(1)} %all-to-all-done.arrived, bf16[3,512,512]{2,1,0:T(8,128)(2,1)S(1)} %bitcast.24, f32[3,512]{1,0:T(4,128)S(1)} %bitcast.23, bf16[128,512]{1,0:T(8,128)(2,1)S(1)} %bitcast.25, f32[1,128]{1,0:T(1,128)S(1)} %copy-done.4), custom_call_target="tpu_custom_call" | custom-call | flops 1744830464 | bytes 4194304 | tf_op jit(solution)/shard_map/pallas_call | solution.py:57
  61.3 11.9 %all_to_all.20 = bf16[4,4,2,32,128]{4,3,2,1,0:T(8,128)(2,1)S(1)} all-to-all(bf16[4,4,2,32,128]{4,3,2,1,0:T(8,128)(2,1)S(1)} %shard_map.91), channel_id=1, replica_groups=mesh['x'=4,'yh'=4,'yl'=2,'z'=8,'c'=2] {'yh'}, dimensions={0} | all-to-all | bytes 524288 | tf_op jit(solution)/shard_map/all_to_all | solution.py:161
  73.2 0.2 broadcast_in_dim.14
  73.4 13.6 %all_to_all.21 = bf16[4,4,256,128]{3,2,1,0:T(8,128)(2,1)S(1)} all-to-all(bf16[4,4,256,128]{3,2,1,0:T(8,128)(2,1)S(1)} %broadcast_in_dim.14), channel_id=1, replica_groups=mesh['x'=4,'yh'=4,'yl'=2,'z'=8,'c'=2] {'x'}, dimensions={0} | all-to-all | bytes 2097152 | tf_op jit(solution)/shard_map/all_to_all | solution.py:163
  87.0 8.7 %collective-permute-start = (bf16[16,256,128]{2,1,0:T(8,128)(2,1)S(1)}, bf16[16,256,128]{2,1,0:T(8,128)(2,1)S(1)}, u32[]{:S(2)}, u32[]{:S(2)}) collective-permute-start(bf16[16,256,128]{2,1,0:T(8,128)(2,1)S(1)} %bitcast.21), channel_id=1, source_target_pairs={{0,1},{1,0},{2,3},{3,2},{4,5},{5,4},{6,7},{7,6},{8,9},{9,8},{10,11... | collective-permute-start | bytes 3145736 | tf_op jit(solution)/shard_map/ppermute | solution.py:166
  95.7 2.3 %collective-permute-done.other = bf16[16,256,128]{2,1,0:T(8,128)(2,1)S(1)} collective-permute-done((bf16[16,256,128]{2,1,0:T(8,128)(2,1)S(1)}, bf16[16,256,128]{2,1,0:T(8,128)(2,1)S(1)}, u32[]{:S(2)}, u32[]{:S(2)}) %collective-permute-start) | collective-permute-done | bytes 1048608 | tf_op jit(solution)/shard_map/ppermute | solution.py:166
  97.9 0.9 all-gather.4.cloned.1.call-done.rows
  98.8 0.0 copy-start
  98.8 1.6 %copy-done = bf16[512,2176]{1,0:T(8,128)(2,1)S(1)} copy-done((bf16[512,2176]{1,0:T(8,128)(2,1)S(1)}, bf16[512,2176]{1,0:T(8,128)(2,1)}, u32[]{:S(2)}) %copy-start) | copy-done | bytes 2228248
  100.4 8.7 %shard_map.92 = f32[8,8,128]{2,1,0:T(8,128)S(1)} custom-call(s32[1]{0:T(128)} %bitcast.core, bf16[16,256,128]{2,1,0:T(8,128)(2,1)S(1)} %bitcast.22, bf16[16,256,128]{2,1,0:T(8,128)(2,1)S(1)} %collective-permute-done.other, bf16[512,2176]{1,0:T(8,128)(2,1)S(1)} %copy-done), custom_call_target="tpu_custom_call" | custom-call | flops 3000000000 | bytes 6291456 | tf_op jit(solution)/shard_map/pallas_call | solution.py:124
  109.1 13.6 %all_to_all.22 = f32[8,8,128]{2,1,0:T(8,128)S(1)} all-to-all(f32[8,8,128]{2,1,0:T(8,128)S(1)} %shard_map.92), channel_id=1, replica_groups=mesh['x'=4,'yh'=4,'yl'=2,'z'=8,'c'=2] {'c','x'}, dimensions={0} | all-to-all | bytes 65536 | tf_op jit(solution)/shard_map/all_to_all | solution.py:169
  122.8 0.6 reshape_squeeze.3
  (3 shorter events, 0.0 us)
Async XLA Ops:
  6.5 47.8 %all-gather.6.cloned.1.call-start = ((), (), s32[]{:S(2)}) async-start(), calls=%async_computation.5 | async-start | bytes 1253376 | tf_op jit(solution)/shard_map/all_gather | solution.py:140
  11.9 44.1 %copy-start.5 = (f32[1,3,512]{2,0,1:T(1,128)S(1)}, f32[1,3,512]{2,0,1:T(1,128)}, u32[]{:S(2)}) copy-start(f32[1,3,512]{2,0,1:T(1,128)} %param.12) | copy-start | bytes 18436
  11.9 44.2 %copy-start.1 = (bf16[1,3,512,512]{3,2,1,0:T(8,128)(2,1)S(1)}, bf16[1,3,512,512]{3,2,1,0:T(8,128)(2,1)}, u32[]{:S(2)}) copy-start(bf16[1,3,512,512]{3,2,1,0:T(8,128)(2,1)} %param.11) | copy-start | bytes 4718596
  11.9 44.2 %copy-start.2 = (bf16[1,128,512]{2,1,0:T(8,128)(2,1)S(1)}, bf16[1,128,512]{2,1,0:T(8,128)(2,1)}, u32[]{:S(2)}) copy-start(bf16[1,128,512]{2,1,0:T(8,128)(2,1)} %param.13) | copy-start | bytes 393220
  11.9 44.2 %copy-start.3 = (s32[1,4]{1,0:T(1,128)S(1)}, s32[1,4]{1,0:T(1,128)}, u32[]{:S(2)}) copy-start(s32[1,4]{1,0:T(1,128)} %order.1) | copy-start | bytes 52
  11.9 44.2 %copy-start.4 = (f32[1,128]{1,0:T(1,128)S(1)}, f32[1,128]{1,0:T(1,128)}, u32[]{:S(2)}) copy-start(f32[1,128]{1,0:T(1,128)} %gain.1) | copy-start | bytes 1540
  11.9 44.1 %all-to-all-start = ((bf16[32,2,16,512]{3,2,1,0:T(8,128)(2,1)}), bf16[32,2,16,512]{3,2,1,0:T(8,128)(2,1)S(1)}, u32[]{:S(2)}, u32[]{:S(2)}) async-start(bf16[32,2,16,512]{3,2,1,0:T(8,128)(2,1)} %bitcast.26), calls=%async_computation | async-start | bytes 2097152 | tf_op jit(solution)/shard_map/all_to_all | solution.py:157
  25.1 73.7 %all-gather.4.cloned.1.call-start = ((), (), s32[]{:S(2)}) async-start(), calls=%async_computation.4 | async-start | bytes 2506752 | tf_op jit(solution)/shard_map/all_gather | solution.py:141
  87.0 10.9 %collective-permute-start = (bf16[16,256,128]{2,1,0:T(8,128)(2,1)S(1)}, bf16[16,256,128]{2,1,0:T(8,128)(2,1)S(1)}, u32[]{:S(2)}, u32[]{:S(2)}) collective-permute-start(bf16[16,256,128]{2,1,0:T(8,128)(2,1)S(1)} %bitcast.21), channel_id=1, source_target_pairs={{0,1},{1,0},{2,3},{3,2},{4,5},{5,4},{6,7},{7,6},{8,9},{9,8},{10,11... | collective-permute-start | bytes 3145736 | tf_op jit(solution)/shard_map/ppermute | solution.py:166
  98.8 1.6 %copy-start = (bf16[512,2176]{1,0:T(8,128)(2,1)S(1)}, bf16[512,2176]{1,0:T(8,128)(2,1)}, u32[]{:S(2)}) copy-start(bf16[512,2176]{1,0:T(8,128)(2,1)} %all-gather.4.cloned.1.call-done.rows) | copy-start | bytes 6684676
Sparse Core Ops, SparseCore 0:
  9.7 44.5 all-gather.5
  56.4 42.3 all-gather.3

commit v2 on v1

--- a/solution.py
+++ b/solution.py
@@ -134,11 +134,37 @@
     )(core, own, other, rows)
 
 
-def hidden_rows(mlp_weight, mlp_bias, out_weight):
-    row = jnp.concatenate([mlp_weight, mlp_bias[:, None], out_weight[:, None]], axis=1)
-    row = jnp.pad(row, ((0, 24), (0, WIDE - row.shape[1])))
-    across = lax.all_gather(row, ("yh", "yl"), axis=0)
-    return lax.all_gather(across[:, :8].reshape(64, WIDE), "z", axis=0, tiled=True)
+def prepare_kernel(pooled, weight, bias, out_weight, sent, rows):
+    eye = lax.broadcasted_iota(jnp.int32, (8, 8), 0) == lax.broadcasted_iota(jnp.int32, (8, 8), 1)
+    lane = lax.broadcasted_iota(jnp.int32, (8, 128), 1)
+
+    def column(row):
+        return jnp.sum(jnp.where(eye, row[...].astype(jnp.float32), 0.0), axis=1, keepdims=True)
+
+    extra = jnp.where(lane == 0, column(bias), jnp.where(lane == 1, column(out_weight), 0.0))
+    extra = extra.astype(jnp.bfloat16)
+    rows[:, : TOWERS * CD] = weight[...]
+    rows[:, TOWERS * CD :] = extra
+    for rank in range(32):
+        sent[rank] = pooled[:, :, rank * 512 : (rank + 1) * 512]
+
+
+def prepare(pooled, mlp_weight, mlp_bias, out_weight):
+    vmem = pl.BlockSpec(memory_space=pltpu.VMEM)
+    return pl.pallas_call(
+        prepare_kernel,
+        out_shape=(
+            jax.ShapeDtypeStruct((32, 2, 16, 512), jnp.bfloat16),
+            jax.ShapeDtypeStruct((8, WIDE), jnp.bfloat16),
+        ),
+        in_specs=[vmem] * 4,
+        out_specs=(vmem, vmem),
+        compiler_params=pltpu.CompilerParams(vmem_limit_bytes=32 * 2**20),
+    )(pooled, mlp_weight, mlp_bias[None], out_weight[None])
+
+
+def exchange(x, axes):
+    return lax.all_to_all(x, axes, split_axis=0, concat_axis=0, tiled=True)
 
 
 def on_device(
@@ -152,21 +178,20 @@
     mlp_bias,
     out_weight,
 ):
-    rows = hidden_rows(mlp_weight, mlp_bias, out_weight)
-    sent = pooled.reshape(2, 16, 32, 512).transpose(2, 0, 1, 3)
-    arrived = lax.all_to_all(sent, RANK, split_axis=0, concat_axis=0, tiled=True)
+    sent, rows = prepare(pooled, mlp_weight, mlp_bias, out_weight)
+    rows = jnp.concatenate([rows, lax.ppermute(rows, "yl", [(0, 1), (1, 0)])], axis=0)
+    rows = lax.all_gather(rows, ("yh", "z"), axis=0, tiled=True)
+    arrived = exchange(sent, RANK)
     towers = tower_block(
         feature_order, arrived, cross_weight[0], cross_bias[0], compress_weight[0], norm_gain
     )
-    column = lax.all_to_all(towers, "yh", split_axis=0, concat_axis=0, tiled=True)
-    column = column.reshape(4, 256, CD)
-    features = lax.all_to_all(
-        jnp.broadcast_to(column[None], (4, 4, 256, CD)), "x", split_axis=0, concat_axis=0, tiled=True
-    ).reshape(TOWERS, 256, CD)
+    column = exchange(towers, "yh").reshape(4, 256, CD)
+    features = exchange(jnp.broadcast_to(column[None], (4, 4, 256, CD)), "x")
+    features = features.reshape(TOWERS, 256, CD)
     other = lax.ppermute(features, "c", [(0, 1), (1, 0)])
     core = lax.axis_index("c").reshape(1).astype(jnp.int32)
     partial = score(core, features, other, rows)
-    terms = lax.all_to_all(partial, ("c", "x"), split_axis=0, concat_axis=0, tiled=True)
+    terms = exchange(partial, ("c", "x"))
     return jnp.sum(terms, axis=0)[0, :64].reshape(2, 1, BLOCK)
 
 

time: 131 us -> 147 us (1.12)
  waiting for transfers between devices: 32.4 us -> 44.9 us
  blocking collectives: 39.1 us -> 48.3 us
  local copies, waits for them, and re-layouts: 9.55 us -> 5.83 us
  starting transfers between devices: 21.8 us -> 18.1 us
    all_to_all x1, waiting for transfers between devices: 0.01 us -> 26.9 us  [exchange(): return lax.all_to_all(x, axes, split_axis=0, concat_axis=0, tiled=True)]
    all_gather x2 -> x1, waiting for transfers between devices: 30.1 us -> 15.7 us  [on_device(): rows = lax.all_gather(rows, ('yh', 'z'), axis=0, tiled=True)]
    all_to_all x3, blocking collectives: 39.1 us -> 48.3 us  [exchange(): return lax.all_to_all(x, axes, split_axis=0, concat_axis=0, tiled=True)]
    ppermute x1, starting transfers between devices: 8.67 us -> 2.59 us  [on_device(): other = lax.ppermute(features, 'c', [(0, 1), (1, 0)])]
    reshape x2 -> x0, local copies, waits for them, and re-layouts: 4.04 us -> none  [the longest x1 2.34 us: on_device(): sent = pooled.reshape(2, 16, 32, 512).transpose(2, 0, 1, 3)]
    ppermute x0 -> x1, starting transfers between devices: none -> 4.02 us  [on_device(): lax.ppermute(rows, 'yl', [(0, 1), (1, 0)])]
    unnamed x13 -> x21, local copies, waits for them, and re-layouts: 1.65 us -> 4.97 us
    all_to_all x1, starting transfers between devices: 13.1 us -> 11.4 us  [exchange(): return lax.all_to_all(x, axes, split_axis=0, concat_axis=0, tiled=True)]
  transfers between devices with their start and end apart: 4 -> 4, of which waited for: 3 -> 3; matrix products, arithmetic and copies ran while one was open for 3% -> 1% of each run, Pallas kernels for 4% -> 4%
where the time goes in v2:
time: 147 us; the launch traced here: 146 us
  blocking collectives  48.3 us (33%)
  waiting for transfers between devices  44.9 us (31%)
  starting transfers between devices  18.1 us (12%)
  Pallas kernels  15 us (10%)
  between operations  13.5 us (9%)
  local copies, waits for them, and re-layouts  5.83 us (4%)
    all_to_all x3, blocking collectives, exchange(): return lax.all_to_all(x, axes, split_axis=0, concat_axis=0, tiled=True)  48.3 us
    all_to_all x1, waiting for transfers between devices, exchange(): return lax.all_to_all(x, axes, split_axis=0, concat_axis=0, tiled=True)  26.9 us
    all_gather x1, waiting for transfers between devices, on_device(): rows = lax.all_gather(rows, ('yh', 'z'), axis=0, tiled=True)  15.7 us
    all_to_all x1, starting transfers between devices, exchange(): return lax.all_to_all(x, axes, split_axis=0, concat_axis=0, tiled=True)  11.4 us
    pallas_call x1, Pallas kernels, score(): pl.pallas_call(score_kernel, out_shape=jax.ShapeDtypeStruct((8, 8, 128),...  8.72 us
    pallas_call x1, Pallas kernels, tower_block(): pl.pallas_call(tower_kernel, out_shape=jax.ShapeDtypeStruct((4, 4, 2, BLO...  5.21 us
    unnamed x21, local copies, waits for them, and re-layouts  4.97 us
    ppermute x1, starting transfers between devices, on_device(): lax.ppermute(rows, 'yl', [(0, 1), (1, 0)])  4.02 us
  transfers between devices with their start and end apart: 4, of which 3 were waited for; matrix products, arithmetic and copies ran while one was open for 1% of the time, Pallas kernels for 4%

profile of v2, /device:TPU:1, one launch (start us, length us, event | category | flops | bytes accessed | tf_op | source)
XLA Modules:
  0.0 146.2 jit_solution(11448719658542498202)
XLA Ops:
  6.5 0.0 copy-start.8
  6.5 0.0 copy-start.7
  6.5 0.0 copy-start
  6.5 1.2 copy-done
  7.8 0.0 copy-start.1
  7.8 0.8 copy-done.1
  8.6 0.0 copy-start.2
  8.6 0.7 copy-done.2
  9.2 0.0 copy-start.3
  9.2 0.7 copy-done.3
  9.9 0.0 copy-start.9
  9.9 0.0 copy-start.5
  9.9 0.0 copy-start.6
  9.9 1.1 shard_map.91
  10.9 4.0 %collective-permute-start.1 = (bf16[8,2176]{1,0:T(8,128)(2,1)S(1)}, bf16[8,2176]{1,0:T(8,128)(2,1)S(1)}, u32[]{:S(2)}, u32[]{:S(2)}) collective-permute-start(bf16[8,2176]{1,0:T(8,128)(2,1)S(1)} %get-tuple-element.8), channel_id=1, source_target_pairs={{0,16},{16,0},{1,17},{17,1},{2,18},{18,2},{3,19},{19,3},{4,20},{20... | collective-permute-start | bytes 104456 | tf_op jit(solution)/shard_map/ppermute | solution.py:182
  15.0 11.4 %all-to-all-start = ((bf16[32,2,16,512]{3,2,1,0:T(8,128)(2,1)}), bf16[32,2,16,512]{3,2,1,0:T(8,128)(2,1)S(1)}, u32[]{:S(2)}, u32[]{:S(2)}) async-start(bf16[32,2,16,512]{3,2,1,0:T(8,128)(2,1)} %get-tuple-element.7), calls=%async_computation | async-start | bytes 2097152 | tf_op jit(solution)/shard_map/all_to_all | solution.py:167
  26.4 0.0 all-gather.2.cloned.1.call-start
  26.4 0.0 collective-permute-done.1
  26.5 0.6 pad_maximum_fusion
  27.1 0.0 all-gather.2.cloned.1.call-update
  27.1 0.0 copy-done.9
  27.2 26.9 %all-to-all-done.arrived = bf16[32,2,16,512]{3,2,1,0:T(8,128)(2,1)S(1)} async-done(((bf16[32,2,16,512]{3,2,1,0:T(8,128)(2,1)}), bf16[32,2,16,512]{3,2,1,0:T(8,128)(2,1)S(1)}, u32[]{:S(2)}, u32[]{:S(2)}) %all-to-all-start) | async-done | bytes 1048608 | tf_op jit(solution)/shard_map/all_to_all | solution.py:167
  54.0 0.0 copy-done.8
  54.0 0.0 copy-done.7
  54.0 0.0 copy-done.5
  54.0 0.0 copy-done.6
  54.0 5.2 %shard_map.92 = bf16[4,4,2,32,128]{4,3,2,1,0:T(8,128)(2,1)S(1)} custom-call(s32[1,4]{1,0:T(1,128)S(1)} %copy-done.7, bf16[32,2,16,512]{3,2,1,0:T(8,128)(2,1)S(1)} %all-to-all-done.arrived, bf16[3,512,512]{2,1,0:T(8,128)(2,1)S(1)} %bitcast.16, f32[3,512]{1,0:T(4,128)S(1)} %bitcast.13, bf16[128,512]{1,0:T(8,128)(2,1)S(1)} %bitcast.17, f32[1,128]{1,0:T(1,128)S(1)} %copy-done.8), custom_call_target="tpu_custom_call" | custom-call | flops 1744830464 | bytes 4194304 | tf_op jit(solution)/shard_map/pallas_call | solution.py:57
  59.3 18.2 %all_to_all.20 = bf16[4,4,2,32,128]{4,3,2,1,0:T(8,128)(2,1)S(1)} all-to-all(bf16[4,4,2,32,128]{4,3,2,1,0:T(8,128)(2,1)S(1)} %shard_map.92), channel_id=1, replica_groups=mesh['x'=4,'yh'=4,'yl'=2,'z'=8,'c'=2] {'yh'}, dimensions={0} | all-to-all | bytes 524288 | tf_op jit(solution)/shard_map/all_to_all | solution.py:167
  77.4 0.2 broadcast_in_dim.16
  77.6 19.2 %all_to_all.21 = bf16[4,4,256,128]{3,2,1,0:T(8,128)(2,1)S(1)} all-to-all(bf16[4,4,256,128]{3,2,1,0:T(8,128)(2,1)S(1)} %broadcast_in_dim.16), channel_id=1, replica_groups=mesh['x'=4,'yh'=4,'yl'=2,'z'=8,'c'=2] {'x'}, dimensions={0} | all-to-all | bytes 2097152 | tf_op jit(solution)/shard_map/all_to_all | solution.py:167
  96.8 2.6 %collective-permute-start = (bf16[16,256,128]{2,1,0:T(8,128)(2,1)S(1)}, bf16[16,256,128]{2,1,0:T(8,128)(2,1)S(1)}, u32[]{:S(2)}, u32[]{:S(2)}) collective-permute-start(bf16[16,256,128]{2,1,0:T(8,128)(2,1)S(1)} %bitcast.11), channel_id=1, source_target_pairs={{0,1},{1,0},{2,3},{3,2},{4,5},{5,4},{6,7},{7,6},{8,9},{9,8},{10,11... | collective-permute-start | bytes 3145736 | tf_op jit(solution)/shard_map/ppermute | solution.py:191
  99.4 2.3 %collective-permute-done.other = bf16[16,256,128]{2,1,0:T(8,128)(2,1)S(1)} collective-permute-done((bf16[16,256,128]{2,1,0:T(8,128)(2,1)S(1)}, bf16[16,256,128]{2,1,0:T(8,128)(2,1)S(1)}, u32[]{:S(2)}, u32[]{:S(2)}) %collective-permute-start) | collective-permute-done | bytes 1048608 | tf_op jit(solution)/shard_map/ppermute | solution.py:191
  101.7 15.7 %all-gather.2.cloned.1.call-done.rows = bf16[512,2176]{1,0:T(8,128)(2,1)} async-done(((bf16[16,2176]{1,0:T(8,128)(2,1)}), bf16[512,2176]{1,0:T(8,128)(2,1)}) %all-gather.2.cloned.1.call-update) | async-done | bytes 2228240 | tf_op jit(solution)/shard_map/all_gather | solution.py:183
  117.4 0.0 copy-start.4
  117.4 1.6 %copy-done.4 = bf16[512,2176]{1,0:T(8,128)(2,1)S(1)} copy-done((bf16[512,2176]{1,0:T(8,128)(2,1)S(1)}, bf16[512,2176]{1,0:T(8,128)(2,1)}, u32[]{:S(2)}) %copy-start.4) | copy-done | bytes 2228248
  119.0 8.7 %shard_map.93 = f32[8,8,128]{2,1,0:T(8,128)S(1)} custom-call(s32[1]{0:T(128)} %bitcast.core, bf16[16,256,128]{2,1,0:T(8,128)(2,1)S(1)} %bitcast.12, bf16[16,256,128]{2,1,0:T(8,128)(2,1)S(1)} %collective-permute-done.other, bf16[512,2176]{1,0:T(8,128)(2,1)S(1)} %copy-done.4), custom_call_target="tpu_custom_call" | custom-call | flops 3000000000 | bytes 6291456 | tf_op jit(solution)/shard_map/pallas_call | solution.py:124
  127.7 11.0 %all_to_all.22 = f32[8,8,128]{2,1,0:T(8,128)S(1)} all-to-all(f32[8,8,128]{2,1,0:T(8,128)S(1)} %shard_map.93), channel_id=1, replica_groups=mesh['x'=4,'yh'=4,'yl'=2,'z'=8,'c'=2] {'c','x'}, dimensions={0} | all-to-all | bytes 65536 | tf_op jit(solution)/shard_map/all_to_all | solution.py:167
  138.7 0.6 reshape_squeeze.3
  (3 shorter events, 0.0 us)
Async XLA Ops:
  6.5 47.5 %copy-start.8 = (f32[1,128]{1,0:T(1,128)S(1)}, f32[1,128]{1,0:T(1,128)}, u32[]{:S(2)}) copy-start(f32[1,128]{1,0:T(1,128)} %gain.1) | copy-start | bytes 1540
  6.5 47.5 %copy-start.7 = (s32[1,4]{1,0:T(1,128)S(1)}, s32[1,4]{1,0:T(1,128)}, u32[]{:S(2)}) copy-start(s32[1,4]{1,0:T(1,128)} %order.1) | copy-start | bytes 52
  6.5 1.3 copy-start
  7.8 0.8 copy-start.1
  8.6 0.7 copy-start.2
  9.2 0.7 copy-start.3
  9.9 17.3 %copy-start.9 = (f32[1,3,512]{2,0,1:T(1,128)S(1)}, f32[1,3,512]{2,0,1:T(1,128)}, u32[]{:S(2)}) copy-start(f32[1,3,512]{2,0,1:T(1,128)} %param.12) | copy-start | bytes 18436
  9.9 44.2 %copy-start.5 = (bf16[1,3,512,512]{3,2,1,0:T(8,128)(2,1)S(1)}, bf16[1,3,512,512]{3,2,1,0:T(8,128)(2,1)}, u32[]{:S(2)}) copy-start(bf16[1,3,512,512]{3,2,1,0:T(8,128)(2,1)} %param.11) | copy-start | bytes 4718596
  9.9 44.2 %copy-start.6 = (bf16[1,128,512]{2,1,0:T(8,128)(2,1)S(1)}, bf16[1,128,512]{2,1,0:T(8,128)(2,1)}, u32[]{:S(2)}) copy-start(bf16[1,128,512]{2,1,0:T(8,128)(2,1)} %param.13) | copy-start | bytes 393220
  10.9 15.5 %collective-permute-start.1 = (bf16[8,2176]{1,0:T(8,128)(2,1)S(1)}, bf16[8,2176]{1,0:T(8,128)(2,1)S(1)}, u32[]{:S(2)}, u32[]{:S(2)}) collective-permute-start(bf16[8,2176]{1,0:T(8,128)(2,1)S(1)} %get-tuple-element.8), channel_id=1, source_target_pairs={{0,16},{16,0},{1,17},{17,1},{2,18},{18,2},{3,19},{19,3},{4,20},{20... | collective-permute-start | bytes 104456 | tf_op jit(solution)/shard_map/ppermute | solution.py:182
  15.0 39.1 %all-to-all-start = ((bf16[32,2,16,512]{3,2,1,0:T(8,128)(2,1)}), bf16[32,2,16,512]{3,2,1,0:T(8,128)(2,1)S(1)}, u32[]{:S(2)}, u32[]{:S(2)}) async-start(bf16[32,2,16,512]{3,2,1,0:T(8,128)(2,1)} %get-tuple-element.7), calls=%async_computation | async-start | bytes 2097152 | tf_op jit(solution)/shard_map/all_to_all | solution.py:167
  26.4 91.0 %all-gather.2.cloned.1.call-start = ((), (), s32[]{:S(2)}) async-start(), calls=%async_computation.4 | async-start | bytes 2297856 | tf_op jit(solution)/shard_map/all_gather | solution.py:183
  96.8 4.9 %collective-permute-start = (bf16[16,256,128]{2,1,0:T(8,128)(2,1)S(1)}, bf16[16,256,128]{2,1,0:T(8,128)(2,1)S(1)}, u32[]{:S(2)}, u32[]{:S(2)}) collective-permute-start(bf16[16,256,128]{2,1,0:T(8,128)(2,1)S(1)} %bitcast.11), channel_id=1, source_target_pairs={{0,1},{1,0},{2,3},{3,2},{4,5},{5,4},{6,7},{7,6},{8,9},{9,8},{10,11... | collective-permute-start | bytes 3145736 | tf_op jit(solution)/shard_map/ppermute | solution.py:191
  117.4 1.6 %copy-start.4 = (bf16[512,2176]{1,0:T(8,128)(2,1)S(1)}, bf16[512,2176]{1,0:T(8,128)(2,1)}, u32[]{:S(2)}) copy-start(bf16[512,2176]{1,0:T(8,128)(2,1)} %all-gather.2.cloned.1.call-done.rows) | copy-start | bytes 6684676
Sparse Core Ops, SparseCore 0:
  30.4 86.9 all-gather.1

commit v3 on v2

--- a/solution.py
+++ b/solution.py
@@ -17,9 +17,9 @@
 WIDE = 2048 + 128
 EPSILON = 1e-06
 
-AXES = (("x", 4), ("yh", 4), ("yl", 2), ("z", 8), ("c", 2))
+AXES = (("x", 4), ("yh", 4), ("yl", 2), ("zh", 4), ("zl", 2), ("c", 2))
 TOWER = ("x", "yh")
-RANK = ("yl", "z", "c")
+RANK = ("yl", "zh", "zl", "c")
 
 
 def tower_kernel(order, arrived, weights, biases, compress, gain, out):
@@ -66,7 +66,7 @@
     )(order, arrived, weights, biases, compress, gain)
 
 
-def score_kernel(core, own, other, rows, out, mixed):
+def score_kernel(core, own, other, part0, part1, part2, part3, out, mixed):
     samples = own.shape[1]
     side = TOWERS * GROUP
     same = (
@@ -100,15 +100,14 @@
         lax.fori_loop(0, samples // GROUP, interact, 0, unroll=4)
 
     total = jnp.zeros((1, 2 * samples), jnp.float32)
-    for part in range(2):
-        at = pl.ds(part * 256, 256)
+    for rows in (part0, part1, part2, part3):
         hidden = lax.dot_general(
-            rows[at, : TOWERS * CD],
+            rows[:, : TOWERS * CD],
             mixed[...],
             (((1,), (1,)), ((), ())),
             preferred_element_type=jnp.float32,
         )
-        extra = rows[at, TOWERS * CD :].astype(jnp.float32)
+        extra = rows[:, TOWERS * CD :].astype(jnp.float32)
         terms = jnp.maximum(hidden + extra[:, 0:1], 0.0) * extra[:, 1:2]
         total = total + jnp.sum(terms, axis=0, keepdims=True)
 
@@ -119,19 +118,19 @@
             out[mine * 4 + x, 0:1, 0:64] = total[:, at : at + 64]
 
 
-def score(core, own, other, rows):
+def score(core, own, other, parts):
     vmem = pl.BlockSpec(memory_space=pltpu.VMEM)
     return pl.pallas_call(
         score_kernel,
         out_shape=jax.ShapeDtypeStruct((8, 8, 128), jnp.float32),
-        in_specs=[pl.BlockSpec(memory_space=pltpu.SMEM)] + [vmem] * 3,
+        in_specs=[pl.BlockSpec(memory_space=pltpu.SMEM)] + [vmem] * 6,
         out_specs=vmem,
         scratch_shapes=[pltpu.VMEM((512, TOWERS * CD), jnp.bfloat16)],
         compiler_params=pltpu.CompilerParams(vmem_limit_bytes=32 * 2**20),
         cost_estimate=pl.CostEstimate(
             flops=3 * 10**9, bytes_accessed=6 * 2**20, transcendentals=0
         ),
-    )(core, own, other, rows)
+    )(core, own, other, *parts)
 
 
 def prepare_kernel(pooled, weight, bias, out_weight, sent, rows):
@@ -165,6 +164,14 @@
 
 def exchange(x, axes):
     return lax.all_to_all(x, axes, split_axis=0, concat_axis=0, tiled=True)
+
+
+def from_ring(x, axis):
+    return [x] + [lax.ppermute(x, axis, [(i, (i + k) % 4) for i in range(4)]) for k in (1, 2, 3)]
+
+
+def from_square(x, axes):
+    return [x] + [lax.ppermute(x, axes, [(i, i ^ k) for i in range(4)]) for k in (1, 2, 3)]
 
 
 def on_device(
@@ -179,18 +186,21 @@
     out_weight,
 ):
     sent, rows = prepare(pooled, mlp_weight, mlp_bias, out_weight)
-    rows = jnp.concatenate([rows, lax.ppermute(rows, "yl", [(0, 1), (1, 0)])], axis=0)
-    rows = lax.all_gather(rows, ("yh", "z"), axis=0, tiled=True)
     arrived = exchange(sent, RANK)
+    rows = jnp.concatenate(from_ring(rows, "zh"), axis=0)
+    rows = jnp.concatenate(from_ring(rows, "yh"), axis=0)
+    arrived, rows = lax.optimization_barrier((arrived, rows))
+    parts = from_square(rows, ("yl", "zl"))
     towers = tower_block(
         feature_order, arrived, cross_weight[0], cross_bias[0], compress_weight[0], norm_gain
     )
     column = exchange(towers, "yh").reshape(4, 256, CD)
+    column, *parts = lax.optimization_barrier((column, *parts))
     features = exchange(jnp.broadcast_to(column[None], (4, 4, 256, CD)), "x")
     features = features.reshape(TOWERS, 256, CD)
     other = lax.ppermute(features, "c", [(0, 1), (1, 0)])
     core = lax.axis_index("c").reshape(1).astype(jnp.int32)
-    partial = score(core, features, other, rows)
+    partial = score(core, features, other, parts)
     terms = exchange(partial, ("c", "x"))
     return jnp.sum(terms, axis=0)[0, :64].reshape(2, 1, BLOCK)
 

time: 147 us -> 143 us (0.973)
  starting transfers between devices: 18.1 us -> 55.2 us
  waiting for transfers between devices: 44.9 us -> 15.3 us
  between operations: 13.5 us -> 0.28 us
  local copies, waits for them, and re-layouts: 5.83 us -> 7.46 us
  Pallas kernels: 15 us -> 16.5 us
    ppermute x1 -> x9, starting transfers between devices: 4.02 us -> 41.4 us  [the longest x6 31.6 us: from_ring(): lax.ppermute(x, axis, [(i, (i + k) % 4) for i in range(4)])]
    all_to_all x1, waiting for transfers between devices: 26.9 us -> 1.11 us  [exchange(): return lax.all_to_all(x, axes, split_axis=0, concat_axis=0, tiled=True)]
    all_gather x1 -> x0, waiting for transfers between devices: 15.7 us -> none  [on_device(): rows = lax.all_gather(rows, ('yh', 'z'), axis=0, tiled=True)]
    ppermute x1 -> x9, waiting for transfers between devices: 0.01 us -> 12 us  [the longest x6 12 us: from_ring(): lax.ppermute(x, axis, [(i, (i + k) % 4) for i in range(4)])]
    all_to_all x1, starting transfers between devices: 11.4 us -> 8.6 us  [exchange(): return lax.all_to_all(x, axes, split_axis=0, concat_axis=0, tiled=True)]
    ppermute x1, starting transfers between devices: 2.59 us -> 5.21 us  [on_device(): other = lax.ppermute(features, 'c', [(0, 1), (1, 0)])]
    unnamed x21 -> x36, local copies, waits for them, and re-layouts: 4.97 us -> 6.56 us
    pallas_call x1, Pallas kernels: 8.72 us -> 10.2 us  [score(): pl.pallas_call(score_kernel, out_shape=jax.ShapeDtypeStruct((8, 8, 128),...]
  transfers between devices with their start and end apart: 4 -> 11, of which waited for: 3 -> 4; matrix products, arithmetic and copies ran while one was open for 1% -> 0% of each run, Pallas kernels for 4% -> 4%
where the time goes in v3:
time: 143 us; the launch traced here: 142 us
  starting transfers between devices  55.2 us (39%)
  blocking collectives  47.3 us (33%)
  Pallas kernels  16.5 us (12%)
  waiting for transfers between devices  15.3 us (11%)
  local copies, waits for them, and re-layouts  7.46 us (5%)
    all_to_all x3, blocking collectives, exchange(): return lax.all_to_all(x, axes, split_axis=0, concat_axis=0, tiled=True)  47.3 us
    ppermute x6, starting transfers between devices, from_ring(): lax.ppermute(x, axis, [(i, (i + k) % 4) for i in range(4)])  31.6 us
    ppermute x6, waiting for transfers between devices, from_ring(): lax.ppermute(x, axis, [(i, (i + k) % 4) for i in range(4)])  12 us
    pallas_call x1, Pallas kernels, score(): pl.pallas_call(score_kernel, out_shape=jax.ShapeDtypeStruct((8, 8, 128),...  10.2 us
    ppermute x3, starting transfers between devices, from_square(): lax.ppermute(x, axes, [(i, i ^ k) for i in range(4)])  9.83 us
    all_to_all x1, starting transfers between devices, exchange(): return lax.all_to_all(x, axes, split_axis=0, concat_axis=0, tiled=True)  8.6 us
    unnamed x36, local copies, waits for them, and re-layouts  6.56 us
    ppermute x1, starting transfers between devices, on_device(): other = lax.ppermute(features, 'c', [(0, 1), (1, 0)])  5.21 us
  transfers between devices with their start and end apart: 11, of which 4 were waited for; matrix products, arithmetic and copies ran while one was open for 0% of the time, Pallas kernels for 4%

profile of v3, /device:TPU:1, one launch (start us, length us, event | category | flops | bytes accessed | tf_op | source)
XLA Modules:
  0.0 142.2 jit_solution(6089602637548131716)
XLA Ops:
  0.0 1.2 copy-done
  1.2 0.8 copy-done.1
  2.0 0.7 copy-done.2
  2.6 0.7 copy-done.3
  3.3 1.1 shard_map.91
  4.4 11.5 %collective-permute-start.2 = (bf16[8,2176]{1,0:T(8,128)(2,1)S(1)}, bf16[8,2176]{1,0:T(8,128)(2,1)S(1)}, u32[]{:S(2)}, u32[]{:S(2)}) collective-permute-start(bf16[8,2176]{1,0:T(8,128)(2,1)S(1)} %get-tuple-element.15), channel_id=1, source_target_pairs={{0,12},{4,0},{8,4},{12,8},{1,13},{5,1},{9,5},{13,9},{2,14},{6,2},{... | collective-permute-start | bytes 104456 | tf_op jit(solution)/shard_map/ppermute | solution.py:170
  15.9 1.9 %collective-permute-start.1 = (bf16[8,2176]{1,0:T(8,128)(2,1)S(1)}, bf16[8,2176]{1,0:T(8,128)(2,1)S(1)}, u32[]{:S(2)}, u32[]{:S(2)}) collective-permute-start(bf16[8,2176]{1,0:T(8,128)(2,1)S(1)} %get-tuple-element.15), channel_id=1, source_target_pairs={{0,8},{4,12},{8,0},{12,4},{1,9},{5,13},{9,1},{13,5},{2,10},{6,14},... | collective-permute-start | bytes 104456 | tf_op jit(solution)/shard_map/ppermute | solution.py:170
  17.8 4.2 %collective-permute-start = (bf16[8,2176]{1,0:T(8,128)(2,1)S(1)}, bf16[8,2176]{1,0:T(8,128)(2,1)S(1)}, u32[]{:S(2)}, u32[]{:S(2)}) collective-permute-start(bf16[8,2176]{1,0:T(8,128)(2,1)S(1)} %get-tuple-element.15), channel_id=1, source_target_pairs={{0,4},{4,8},{8,12},{12,0},{1,5},{5,9},{9,13},{13,1},{2,6},{6,10},{... | collective-permute-start | bytes 104456 | tf_op jit(solution)/shard_map/ppermute | solution.py:170
  22.0 0.0 copy-start.4
  22.1 0.0 copy-start.11
  22.1 0.0 copy-start.12
  22.1 0.0 copy-start.13
  22.1 8.6 %all-to-all-start = ((bf16[32,2,16,512]{3,2,1,0:T(8,128)(2,1)}), bf16[32,2,16,512]{3,2,1,0:T(8,128)(2,1)S(1)}, u32[]{:S(2)}, u32[]{:S(2)}) async-start(bf16[32,2,16,512]{3,2,1,0:T(8,128)(2,1)} %get-tuple-element.14), calls=%async_computation | async-start | bytes 2097152 | tf_op jit(solution)/shard_map/all_to_all | solution.py:166
  30.7 0.0 collective-permute-done
  30.8 0.0 collective-permute-done.1
  30.8 0.0 collective-permute-done.2
  30.8 4.2 %collective-permute-start.3 = (bf16[32,2176]{1,0:T(8,128)(2,1)S(1)}, bf16[32,2176]{1,0:T(8,128)(2,1)S(1)}, u32[]{:S(2)}, u32[]{:S(2)}) collective-permute-start(bf16[32,2176]{1,0:T(8,128)(2,1)S(1)} %get-tuple-element.23), channel_id=1, source_target_pairs={{0,32},{32,64},{64,96},{96,0},{1,33},{33,65},{65,97},{97,1},{2,34}... | collective-permute-start | bytes 417800 | tf_op jit(solution)/shard_map/ppermute | solution.py:170
  35.0 0.0 copy-done.14
  35.1 3.2 %collective-permute-start.5 = (bf16[32,2176]{1,0:T(8,128)(2,1)S(1)}, bf16[32,2176]{1,0:T(8,128)(2,1)S(1)}, u32[]{:S(2)}, u32[]{:S(2)}) collective-permute-start(bf16[32,2176]{1,0:T(8,128)(2,1)S(1)} %get-tuple-element.23), channel_id=1, source_target_pairs={{0,96},{32,0},{64,32},{96,64},{1,97},{33,1},{65,33},{97,65},{2,98}... | collective-permute-start | bytes 417800 | tf_op jit(solution)/shard_map/ppermute | solution.py:170
  38.2 6.6 %collective-permute-start.4 = (bf16[32,2176]{1,0:T(8,128)(2,1)S(1)}, bf16[32,2176]{1,0:T(8,128)(2,1)S(1)}, u32[]{:S(2)}, u32[]{:S(2)}) collective-permute-start(bf16[32,2176]{1,0:T(8,128)(2,1)S(1)} %get-tuple-element.23), channel_id=1, source_target_pairs={{0,64},{32,96},{64,0},{96,32},{1,65},{33,97},{65,1},{97,33},{2,66}... | collective-permute-start | bytes 417800 | tf_op jit(solution)/shard_map/ppermute | solution.py:170
  44.8 7.9 %collective-permute-done.3 = bf16[32,2176]{1,0:T(8,128)(2,1)S(1)} collective-permute-done((bf16[32,2176]{1,0:T(8,128)(2,1)S(1)}, bf16[32,2176]{1,0:T(8,128)(2,1)S(1)}, u32[]{:S(2)}, u32[]{:S(2)}) %collective-permute-start.3) | collective-permute-done | bytes 139296 | tf_op jit(solution)/shard_map/ppermute | solution.py:170
  52.7 4.0 %collective-permute-done.4 = bf16[32,2176]{1,0:T(8,128)(2,1)S(1)} collective-permute-done((bf16[32,2176]{1,0:T(8,128)(2,1)S(1)}, bf16[32,2176]{1,0:T(8,128)(2,1)S(1)}, u32[]{:S(2)}, u32[]{:S(2)}) %collective-permute-start.4) | collective-permute-done | bytes 139296 | tf_op jit(solution)/shard_map/ppermute | solution.py:170
  56.8 0.0 collective-permute-done.5
  56.8 1.1 all-to-all-done.arrived
  57.9 5.7 %collective-permute-start.8 = (bf16[128,2176]{1,0:T(8,128)(2,1)S(1)}, bf16[128,2176]{1,0:T(8,128)(2,1)S(1)}, u32[]{:S(2)}, u32[]{:S(2)}) collective-permute-start(bf16[128,2176]{1,0:T(8,128)(2,1)S(1)} %constant_dynamic-update-slice_fusion.4.part0), channel_id=1, source_target_pairs={{0,18},{2,16},{16,2},{18,0},{1,19},{3,17},{17,3},{19,1},{4,22},{6,... | collective-permute-start | bytes 1671176 | tf_op jit(solution)/shard_map/ppermute | solution.py:174
  63.6 1.9 %collective-permute-start.7 = (bf16[128,2176]{1,0:T(8,128)(2,1)S(1)}, bf16[128,2176]{1,0:T(8,128)(2,1)S(1)}, u32[]{:S(2)}, u32[]{:S(2)}) collective-permute-start(bf16[128,2176]{1,0:T(8,128)(2,1)S(1)} %constant_dynamic-update-slice_fusion.4.part0), channel_id=1, source_target_pairs={{0,16},{2,18},{16,0},{18,2},{1,17},{3,19},{17,1},{19,3},{4,20},{6,... | collective-permute-start | bytes 1671176 | tf_op jit(solution)/shard_map/ppermute | solution.py:174
  65.6 2.2 %collective-permute-start.6 = (bf16[128,2176]{1,0:T(8,128)(2,1)S(1)}, bf16[128,2176]{1,0:T(8,128)(2,1)S(1)}, u32[]{:S(2)}, u32[]{:S(2)}) collective-permute-start(bf16[128,2176]{1,0:T(8,128)(2,1)S(1)} %constant_dynamic-update-slice_fusion.4.part0), channel_id=1, source_target_pairs={{0,2},{2,0},{16,18},{18,16},{1,3},{3,1},{17,19},{19,17},{4,6},{6,4... | collective-permute-start | bytes 1671176 | tf_op jit(solution)/shard_map/ppermute | solution.py:174
  67.8 0.0 copy-done.4
  67.8 0.0 copy-done.11
  67.8 0.0 copy-done.12
  67.8 0.0 copy-done.13
  67.8 5.2 %shard_map.92 = bf16[4,4,2,32,128]{4,3,2,1,0:T(8,128)(2,1)S(1)} custom-call(s32[1,4]{1,0:T(1,128)S(1)} %copy-done.12, bf16[32,2,16,512]{3,2,1,0:T(8,128)(2,1)S(1)} %all-to-all-done.arrived, bf16[3,512,512]{2,1,0:T(8,128)(2,1)S(1)} %bitcast.16, f32[3,512]{1,0:T(4,128)S(1)} %bitcast.13, bf16[128,512]{1,0:T(8,128)(2,1)S(1)} %bitcast.17, f32[1,128]{1,0:T(1,128)S(1)} %copy-done.13), custom_call_target="tpu_custom_call" | custom-call | flops 1744830464 | bytes 4194304 | tf_op jit(solution)/shard_map/pallas_call | solution.py:57
  73.0 23.1 %all_to_all.20 = bf16[4,4,2,32,128]{4,3,2,1,0:T(8,128)(2,1)S(1)} all-to-all(bf16[4,4,2,32,128]{4,3,2,1,0:T(8,128)(2,1)S(1)} %shard_map.92), channel_id=1, replica_groups=mesh['x'=4,'yh'=4,'yl'=2,'zh'=4,'zl'=2,'c'=2] {'yh'}, dimensions={0} | all-to-all | bytes 524288 | tf_op jit(solution)/shard_map/all_to_all | solution.py:166
  96.1 0.0 collective-permute-done.8.part3
  96.1 0.0 collective-permute-done.7.part2
  96.1 0.0 copy-start.7
  96.1 0.0 collective-permute-done.6.part1
  96.2 0.2 broadcast_in_dim.14
  96.4 16.6 %all_to_all.21 = bf16[4,4,256,128]{3,2,1,0:T(8,128)(2,1)S(1)} all-to-all(bf16[4,4,256,128]{3,2,1,0:T(8,128)(2,1)S(1)} %broadcast_in_dim.14), channel_id=1, replica_groups=mesh['x'=4,'yh'=4,'yl'=2,'zh'=4,'zl'=2,'c'=2] {'x'}, dimensions={0} | all-to-all | bytes 2097152 | tf_op jit(solution)/shard_map/all_to_all | solution.py:166
  112.9 0.0 copy-done.9
  112.9 5.2 %collective-permute-start.9 = (bf16[16,256,128]{2,1,0:T(8,128)(2,1)S(1)}, bf16[16,256,128]{2,1,0:T(8,128)(2,1)S(1)}, u32[]{:S(2)}, u32[]{:S(2)}) collective-permute-start(bf16[16,256,128]{2,1,0:T(8,128)(2,1)S(1)} %bitcast.11), channel_id=1, source_target_pairs={{0,1},{1,0},{2,3},{3,2},{4,5},{5,4},{6,7},{7,6},{8,9},{9,8},{10,11... | collective-permute-start | bytes 3145736 | tf_op jit(solution)/shard_map/ppermute | solution.py:201
  118.2 2.3 %collective-permute-done.9.other = bf16[16,256,128]{2,1,0:T(8,128)(2,1)S(1)} collective-permute-done((bf16[16,256,128]{2,1,0:T(8,128)(2,1)S(1)}, bf16[16,256,128]{2,1,0:T(8,128)(2,1)S(1)}, u32[]{:S(2)}, u32[]{:S(2)}) %collective-permute-start.9) | collective-permute-done | bytes 1048608 | tf_op jit(solution)/shard_map/ppermute | solution.py:201
  120.4 1.1 copy-done.6
  121.5 1.1 copy-done.8
  122.5 1.1 copy-done.10
  123.6 10.2 %shard_map.93 = f32[8,8,128]{2,1,0:T(8,128)S(1)} custom-call(s32[1]{0:T(128)} %bitcast.core, bf16[16,256,128]{2,1,0:T(8,128)(2,1)S(1)} %bitcast.12, bf16[16,256,128]{2,1,0:T(8,128)(2,1)S(1)} %collective-permute-done.9.other, bf16[128,2176]{1,0:T(8,128)(2,1)S(1)} %constant_dynamic-update-slice_fusion.4.part0, bf16[128,2176]{1,0:T(8,128)(2,1)S(1)} %copy-done.10, ...), custom_call_target="tpu_custom_call" | custom-call | flops 3000000000 | bytes 6291456 | tf_op jit(solution)/shard_map/pallas_call | solution.py:123
  133.8 7.7 %all_to_all.22 = f32[8,8,128]{2,1,0:T(8,128)S(1)} all-to-all(f32[8,8,128]{2,1,0:T(8,128)S(1)} %shard_map.93), channel_id=1, replica_groups=mesh['x'=4,'yh'=4,'yl'=2,'zh'=4,'zl'=2,'c'=2] {'c','x'}, dimensions={0} | all-to-all | bytes 65536 | tf_op jit(solution)/shard_map/all_to_all | solution.py:166
  141.5 0.6 reshape_squeeze.3
  (22 shorter events, 0.2 us)
Async XLA Ops:
  0.0 1.2 copy-start
  1.2 0.8 copy-start.1
  2.0 0.7 copy-start.2
  2.6 0.7 copy-start.3
  3.3 31.7 %copy-start.14 = (f32[1,3,512]{2,0,1:T(1,128)S(1)}, f32[1,3,512]{2,0,1:T(1,128)}, u32[]{:S(2)}) copy-start(f32[1,3,512]{2,0,1:T(1,128)} %param.12) | copy-start | bytes 18436
  4.4 26.4 %collective-permute-start.2 = (bf16[8,2176]{1,0:T(8,128)(2,1)S(1)}, bf16[8,2176]{1,0:T(8,128)(2,1)S(1)}, u32[]{:S(2)}, u32[]{:S(2)}) collective-permute-start(bf16[8,2176]{1,0:T(8,128)(2,1)S(1)} %get-tuple-element.15), channel_id=1, source_target_pairs={{0,12},{4,0},{8,4},{12,8},{1,13},{5,1},{9,5},{13,9},{2,14},{6,2},{... | collective-permute-start | bytes 104456 | tf_op jit(solution)/shard_map/ppermute | solution.py:170
  15.9 14.9 %collective-permute-start.1 = (bf16[8,2176]{1,0:T(8,128)(2,1)S(1)}, bf16[8,2176]{1,0:T(8,128)(2,1)S(1)}, u32[]{:S(2)}, u32[]{:S(2)}) collective-permute-start(bf16[8,2176]{1,0:T(8,128)(2,1)S(1)} %get-tuple-element.15), channel_id=1, source_target_pairs={{0,8},{4,12},{8,0},{12,4},{1,9},{5,13},{9,1},{13,5},{2,10},{6,14},... | collective-permute-start | bytes 104456 | tf_op jit(solution)/shard_map/ppermute | solution.py:170
  17.8 12.9 %collective-permute-start = (bf16[8,2176]{1,0:T(8,128)(2,1)S(1)}, bf16[8,2176]{1,0:T(8,128)(2,1)S(1)}, u32[]{:S(2)}, u32[]{:S(2)}) collective-permute-start(bf16[8,2176]{1,0:T(8,128)(2,1)S(1)} %get-tuple-element.15), channel_id=1, source_target_pairs={{0,4},{4,8},{8,12},{12,0},{1,5},{5,9},{9,13},{13,1},{2,6},{6,10},{... | collective-permute-start | bytes 104456 | tf_op jit(solution)/shard_map/ppermute | solution.py:170
  22.0 45.7 %copy-start.4 = (bf16[1,3,512,512]{3,2,1,0:T(8,128)(2,1)S(1)}, bf16[1,3,512,512]{3,2,1,0:T(8,128)(2,1)}, u32[]{:S(2)}) copy-start(bf16[1,3,512,512]{3,2,1,0:T(8,128)(2,1)} %param.11) | copy-start | bytes 4718596
  22.1 45.7 %copy-start.11 = (bf16[1,128,512]{2,1,0:T(8,128)(2,1)S(1)}, bf16[1,128,512]{2,1,0:T(8,128)(2,1)}, u32[]{:S(2)}) copy-start(bf16[1,128,512]{2,1,0:T(8,128)(2,1)} %param.13) | copy-start | bytes 393220
  22.1 45.7 %copy-start.12 = (s32[1,4]{1,0:T(1,128)S(1)}, s32[1,4]{1,0:T(1,128)}, u32[]{:S(2)}) copy-start(s32[1,4]{1,0:T(1,128)} %order.1) | copy-start | bytes 52
  22.1 45.7 %copy-start.13 = (f32[1,128]{1,0:T(1,128)S(1)}, f32[1,128]{1,0:T(1,128)}, u32[]{:S(2)}) copy-start(f32[1,128]{1,0:T(1,128)} %gain.1) | copy-start | bytes 1540
  22.1 35.8 %all-to-all-start = ((bf16[32,2,16,512]{3,2,1,0:T(8,128)(2,1)}), bf16[32,2,16,512]{3,2,1,0:T(8,128)(2,1)S(1)}, u32[]{:S(2)}, u32[]{:S(2)}) async-start(bf16[32,2,16,512]{3,2,1,0:T(8,128)(2,1)} %get-tuple-element.14), calls=%async_computation | async-start | bytes 2097152 | tf_op jit(solution)/shard_map/all_to_all | solution.py:166
  30.8 21.9 %collective-permute-start.3 = (bf16[32,2176]{1,0:T(8,128)(2,1)S(1)}, bf16[32,2176]{1,0:T(8,128)(2,1)S(1)}, u32[]{:S(2)}, u32[]{:S(2)}) collective-permute-start(bf16[32,2176]{1,0:T(8,128)(2,1)S(1)} %get-tuple-element.23), channel_id=1, source_target_pairs={{0,32},{32,64},{64,96},{96,0},{1,33},{33,65},{65,97},{97,1},{2,34}... | collective-permute-start | bytes 417800 | tf_op jit(solution)/shard_map/ppermute | solution.py:170
  35.1 21.7 %collective-permute-start.5 = (bf16[32,2176]{1,0:T(8,128)(2,1)S(1)}, bf16[32,2176]{1,0:T(8,128)(2,1)S(1)}, u32[]{:S(2)}, u32[]{:S(2)}) collective-permute-start(bf16[32,2176]{1,0:T(8,128)(2,1)S(1)} %get-tuple-element.23), channel_id=1, source_target_pairs={{0,96},{32,0},{64,32},{96,64},{1,97},{33,1},{65,33},{97,65},{2,98}... | collective-permute-start | bytes 417800 | tf_op jit(solution)/shard_map/ppermute | solution.py:170
  38.2 18.5 %collective-permute-start.4 = (bf16[32,2176]{1,0:T(8,128)(2,1)S(1)}, bf16[32,2176]{1,0:T(8,128)(2,1)S(1)}, u32[]{:S(2)}, u32[]{:S(2)}) collective-permute-start(bf16[32,2176]{1,0:T(8,128)(2,1)S(1)} %get-tuple-element.23), channel_id=1, source_target_pairs={{0,64},{32,96},{64,0},{96,32},{1,65},{33,97},{65,1},{97,33},{2,66}... | collective-permute-start | bytes 417800 | tf_op jit(solution)/shard_map/ppermute | solution.py:170
  57.9 38.2 %collective-permute-start.8 = (bf16[128,2176]{1,0:T(8,128)(2,1)S(1)}, bf16[128,2176]{1,0:T(8,128)(2,1)S(1)}, u32[]{:S(2)}, u32[]{:S(2)}) collective-permute-start(bf16[128,2176]{1,0:T(8,128)(2,1)S(1)} %constant_dynamic-update-slice_fusion.4.part0), channel_id=1, source_target_pairs={{0,18},{2,16},{16,2},{18,0},{1,19},{3,17},{17,3},{19,1},{4,22},{6,... | collective-permute-start | bytes 1671176 | tf_op jit(solution)/shard_map/ppermute | solution.py:174
  63.6 32.5 %collective-permute-start.7 = (bf16[128,2176]{1,0:T(8,128)(2,1)S(1)}, bf16[128,2176]{1,0:T(8,128)(2,1)S(1)}, u32[]{:S(2)}, u32[]{:S(2)}) collective-permute-start(bf16[128,2176]{1,0:T(8,128)(2,1)S(1)} %constant_dynamic-update-slice_fusion.4.part0), channel_id=1, source_target_pairs={{0,16},{2,18},{16,0},{18,2},{1,17},{3,19},{17,1},{19,3},{4,20},{6,... | collective-permute-start | bytes 1671176 | tf_op jit(solution)/shard_map/ppermute | solution.py:174
  65.6 30.6 %collective-permute-start.6 = (bf16[128,2176]{1,0:T(8,128)(2,1)S(1)}, bf16[128,2176]{1,0:T(8,128)(2,1)S(1)}, u32[]{:S(2)}, u32[]{:S(2)}) collective-permute-start(bf16[128,2176]{1,0:T(8,128)(2,1)S(1)} %constant_dynamic-update-slice_fusion.4.part0), channel_id=1, source_target_pairs={{0,2},{2,0},{16,18},{18,16},{1,3},{3,1},{17,19},{19,17},{4,6},{6,4... | collective-permute-start | bytes 1671176 | tf_op jit(solution)/shard_map/ppermute | solution.py:174
  96.1 16.8 %copy-start.5 = (bf16[128,2176]{1,0:T(8,128)(2,1)}, bf16[128,2176]{1,0:T(8,128)(2,1)S(1)}, u32[]{:S(2)}) copy-start(bf16[128,2176]{1,0:T(8,128)(2,1)S(1)} %collective-permute-done.8.part3) | copy-start | bytes 1671172
  96.1 16.8 %copy-start.7 = (bf16[128,2176]{1,0:T(8,128)(2,1)}, bf16[128,2176]{1,0:T(8,128)(2,1)S(1)}, u32[]{:S(2)}) copy-start(bf16[128,2176]{1,0:T(8,128)(2,1)S(1)} %collective-permute-done.7.part2) | copy-start | bytes 1671172
  96.2 16.8 %copy-start.9 = (bf16[128,2176]{1,0:T(8,128)(2,1)}, bf16[128,2176]{1,0:T(8,128)(2,1)S(1)}, u32[]{:S(2)}) copy-start(bf16[128,2176]{1,0:T(8,128)(2,1)S(1)} %collective-permute-done.6.part1) | copy-start | bytes 1671172
  112.9 7.5 %collective-permute-start.9 = (bf16[16,256,128]{2,1,0:T(8,128)(2,1)S(1)}, bf16[16,256,128]{2,1,0:T(8,128)(2,1)S(1)}, u32[]{:S(2)}, u32[]{:S(2)}) collective-permute-start(bf16[16,256,128]{2,1,0:T(8,128)(2,1)S(1)} %bitcast.11), channel_id=1, source_target_pairs={{0,1},{1,0},{2,3},{3,2},{4,5},{5,4},{6,7},{7,6},{8,9},{9,8},{10,11... | collective-permute-start | bytes 3145736 | tf_op jit(solution)/shard_map/ppermute | solution.py:201
  120.4 1.1 copy-start.6
  121.5 1.1 copy-start.8
  122.5 1.1 copy-start.10

commit v4 on v3

v4 whole, which is shorter than its diff:
```python
import jax
import jax.numpy as jnp
from jax import lax
from jax.experimental import pallas as pl
from jax.experimental.pallas import tpu as pltpu
from jax.sharding import Mesh
from jax.sharding import PartitionSpec as P

E = 128
FT = 4
CD = 128
TD = 512
LAYERS = 3
TOWERS = 16
BLOCK = 32
GROUP = 16
WIDE = 2048 + 128
EPSILON = 1e-06

AXES = (("x", 4), ("yh", 4), ("yl", 2), ("z2", 2), ("z1", 2), ("z0", 2), ("c", 2))
TOWER = ("x", "yh")
RANK = ("yl", "z2", "z1", "z0", "c")
SWAP = [(0, 1), (1, 0)]


def tower_kernel(order, arrived, weights, biases, compress, gain, out):
    bias_columns = jnp.transpose(biases[...])
    gain_column = jnp.transpose(gain[...])
    places = [(batch, half) for batch in range(2) for half in range(2)]
    firsts = []
    for batch, half in places:
        slots = [
            arrived[pl.ds(order[0, k] * 8, 8), batch, :, pl.ds(half * 256, 256)].reshape(E, 256)
            for k in range(FT)
        ]
        firsts.append(jnp.concatenate(slots, axis=0))
    states = list(firsts)
    for layer in range(LAYERS):
        for k, first in enumerate(firsts):
            product = (
                jnp.dot(weights[layer], states[k], preferred_element_type=jnp.float32)
                + bias_columns[:, layer : layer + 1]
            )
            states[k] = (
                first.astype(jnp.float32) * product + states[k].astype(jnp.float32)
            ).astype(jnp.bfloat16)
    for (batch, half), current in zip(places, states):
        squeezed = jnp.dot(compress[...], current, preferred_element_type=jnp.float32)
        inverse_rms = lax.rsqrt(jnp.mean(squeezed * squeezed, axis=0, keepdims=True) + EPSILON)
        scaled = squeezed * inverse_rms * gain_column[:, :1]
        rows = jnp.transpose(scaled).astype(jnp.bfloat16)
        for block in range(8):
            t = half * 8 + block
            out[t % 4, t // 4, batch] = rows[block * BLOCK : (block + 1) * BLOCK]


def tower_block(order, arrived, weights, biases, compress, gain):
    vmem = pl.BlockSpec(memory_space=pltpu.VMEM)
    return pl.pallas_call(
        tower_kernel,
        out_shape=jax.ShapeDtypeStruct((4, 4, 2, BLOCK, CD), jnp.bfloat16),
        in_specs=[pl.BlockSpec(memory_space=pltpu.SMEM)] + [vmem] * 5,
        out_specs=vmem,
        compiler_params=pltpu.CompilerParams(vmem_limit_bytes=32 * 2**20),
        cost_estimate=pl.CostEstimate(
            flops=2 * 1024 * (3 * TD * TD + TD * CD), bytes_accessed=4 * 2**20, transcendentals=1024
        ),
    )(order, arrived, weights, biases, compress, gain)


def interact(features, mixed, first_row):
    side = TOWERS * GROUP
    row = lax.broadcasted_iota(jnp.int32, (side, side), 0)
    col = lax.broadcasted_iota(jnp.int32, (side, side), 1)
    scale = jnp.where(row % GROUP == col % GROUP, jnp.float32(1.0 / CD), jnp.float32(0.0))
    eye = jnp.where(row == col, jnp.float32(1.0), jnp.float32(0.0))

    def group(step, carry):
        at = pl.multiple_of(step * GROUP, GROUP)
        values = features[:, pl.ds(at, GROUP), :].reshape(side, CD)
        gram = lax.dot_general(
            values, values, (((1,), (1,)), ((), ())), preferred_element_type=jnp.float32
        )
        factor = (gram * scale + eye).astype(jnp.bfloat16)
        result = jnp.dot(factor, values, preferred_element_type=jnp.float32).astype(jnp.bfloat16)
        to = pl.ds(pl.multiple_of(first_row + step * GROUP, GROUP), GROUP)
        for t in range(TOWERS):
            mixed[to, t * CD : (t + 1) * CD] = result[t * GROUP : (t + 1) * GROUP]
        return carry

    lax.fori_loop(0, features.shape[1] // GROUP, group, 0, unroll=4)


def interact_kernel(features, mixed):
    interact(features, mixed, 0)


def interact_own(features):
    vmem = pl.BlockSpec(memory_space=pltpu.VMEM)
    return pl.pallas_call(
        interact_kernel,
        out_shape=jax.ShapeDtypeStruct((features.shape[1], TOWERS * CD), jnp.bfloat16),
        in_specs=[vmem],
        out_specs=vmem,
        compiler_params=pltpu.CompilerParams(vmem_limit_bytes=32 * 2**20),
        cost_estimate=pl.CostEstimate(flops=10**9, bytes_accessed=2 * 2**20, transcendentals=0),
    )(features)


def score_kernel(core, own, other, part0, part1, out, mixed, rows, sem):
    copies = [
        pltpu.make_async_copy(part, rows.at[k], sem.at[k]) for k, part in enumerate((part0, part1))
    ]
    for copy in copies:
        copy.start()
    interact(other, mixed, 0)
    totals = [jnp.zeros((1, 256), jnp.float32), jnp.zeros((1, 256), jnp.float32)]
    for k, copy in enumerate(copies):
        copy.wait()
        extra = rows[k, :, TOWERS * CD :].astype(jnp.float32)
        for which, features in enumerate((own, mixed)):
            hidden = lax.dot_general(
                rows[k, :, : TOWERS * CD],
                features[...],
                (((1,), (1,)), ((), ())),
                preferred_element_type=jnp.float32,
            )
            terms = jnp.maximum(hidden + extra[:, 0:1], 0.0) * extra[:, 1:2]
            totals[which] = totals[which] + jnp.sum(terms, axis=0, keepdims=True)
    for which in range(2):
        mine = core[0] if which == 0 else 1 - core[0]
        for x in range(4):
            out[mine * 4 + x, 0:1, 0:64] = totals[which][:, x * 64 : (x + 1) * 64]


def score(core, own, other, parts):
    vmem = pl.BlockSpec(memory_space=pltpu.VMEM)
    anywhere = pl.BlockSpec(memory_space=pl.ANY)
    return pl.pallas_call(
        score_kernel,
        out_shape=jax.ShapeDtypeStruct((8, 8, 128), jnp.float32),
        in_specs=[pl.BlockSpec(memory_space=pltpu.SMEM), vmem, vmem, anywhere, anywhere],
        out_specs=vmem,
        scratch_shapes=[
            pltpu.VMEM((256, TOWERS * CD), jnp.bfloat16),
            pltpu.VMEM((2, 256, WIDE), jnp.bfloat16),
            pltpu.SemaphoreType.DMA((2,)),
        ],
        compiler_params=pltpu.CompilerParams(vmem_limit_bytes=32 * 2**20),
        cost_estimate=pl.CostEstimate(
            flops=2 * 10**9, bytes_accessed=6 * 2**20, transcendentals=0
        ),
    )(core, own, other, *parts)


def lay_out_kernel(pooled, sent, sem):
    copies = [
        pltpu.make_async_copy(
            pooled.at[:, :, pl.ds(rank * 512, 512)], sent.at[rank], sem.at[rank]
        )
        for rank in range(32)
    ]
    for copy in copies:
        copy.start()
    for copy in copies:
        copy.wait()


def lay_out(pooled):
    anywhere = pl.BlockSpec(memory_space=pl.ANY)
    return pl.pallas_call(
        lay_out_kernel,
        out_shape=jax.ShapeDtypeStruct((32, 2, 16, 512), jnp.bfloat16),
        in_specs=[anywhere],
        out_specs=anywhere,
        scratch_shapes=[pltpu.SemaphoreType.DMA((32,))],
    )(pooled)


def join_kernel(weight, bias, out_weight, rows):
    eye = lax.broadcasted_iota(jnp.int32, (8, 8), 0) == lax.broadcasted_iota(jnp.int32, (8, 8), 1)
    lane = lax.broadcasted_iota(jnp.int32, (8, 128), 1)

    def column(row):
        return jnp.sum(jnp.where(eye, row[...].astype(jnp.float32), 0.0), axis=1, keepdims=True)

    extra = jnp.where(lane == 0, column(bias), jnp.where(lane == 1, column(out_weight), 0.0))
    rows[:, : TOWERS * CD] = weight[...]
    rows[:, TOWERS * CD :] = extra.astype(jnp.bfloat16)


def join(mlp_weight, mlp_bias, out_weight):
    vmem = pl.BlockSpec(memory_space=pltpu.VMEM)
    return pl.pallas_call(
        join_kernel,
        out_shape=jax.ShapeDtypeStruct((8, WIDE), jnp.bfloat16),
        in_specs=[vmem] * 3,
        out_specs=vmem,
    )(mlp_weight, mlp_bias[None], out_weight[None])


def exchange(x, axes):
    return lax.all_to_all(x, axes, split_axis=0, concat_axis=0, tiled=True)


def from_ring(x, axis):
    return [x] + [lax.ppermute(x, axis, [(i, (i + k) % 4) for i in range(4)]) for k in (1, 2, 3)]


def from_square(x, axes):
    return [x] + [lax.ppermute(x, axes, [(i, i ^ k) for i in range(4)]) for k in (1, 2, 3)]


def on_device(
    pooled,
    feature_order,
    cross_weight,
    cross_bias,
    compress_weight,
    norm_gain,
    mlp_weight,
    mlp_bias,
    out_weight,
):
    rows = join(mlp_weight, mlp_bias, out_weight)
    arrived = exchange(lay_out(pooled), RANK)
    rows = jnp.concatenate(from_ring(rows, "yh"), axis=0)
    rows = jnp.concatenate(from_square(rows, ("yl", "z2")), axis=0)
    towers = tower_block(
        feature_order, arrived, cross_weight[0], cross_bias[0], compress_weight[0], norm_gain
    )
    towers, rows = lax.optimization_barrier((towers, rows))
    rows = jnp.concatenate([rows, lax.ppermute(rows, "z1", SWAP)], axis=0)
    column = exchange(towers, "yh").reshape(4, 256, CD)
    column, rows = lax.optimization_barrier((column, rows))
    more = lax.ppermute(rows, "z0", SWAP)
    features = exchange(jnp.broadcast_to(column[None], (4, 4, 256, CD)), "x")
    features = features.reshape(TOWERS, 256, CD)
    features, rows, more = lax.optimization_barrier((features, rows, more))
    other = lax.ppermute(features, "c", SWAP)
    own = interact_own(features)
    core = lax.axis_index("c").reshape(1).astype(jnp.int32)
    partial = score(core, own, other, (rows, more))
    terms = exchange(partial, ("c", "x"))
    return jnp.sum(terms, axis=0)[0, :64].reshape(2, 1, BLOCK)


def solution(mesh):
    split = Mesh(
        mesh.devices.reshape([size for _, size in AXES]), tuple(name for name, _ in AXES)
    )
    every = TOWER + RANK
    return jax.shard_map(
        on_device,
        mesh=split,
        in_specs=(
            P(None, every, None),
            P(TOWER, None),
            P(TOWER, None, None, None),
            P(TOWER, None, None),
            P(TOWER, None, None),
            P(TOWER, None),
            P(every, None),
            P(every),
            P(every),
        ),
        out_specs=P(None, RANK, TOWER),
        check_vma=False,
    )
```

time: 143 us -> 186 us (1.30)
  waiting for transfers between devices: 15.3 us -> 59 us
  Pallas kernels: 16.5 us -> 46.7 us
  blocking collectives: 47.3 us -> 27 us
  local copies, waits for them, and re-layouts: 7.46 us -> 1 us
  starting transfers between devices: 55.2 us -> 51.2 us
    pallas_call x1 -> x3, Pallas kernels: 1.09 us -> 37.3 us  [the longest x1 33.2 us: lay_out(): pl.pallas_call(lay_out_kernel, out_shape=jax.ShapeDtypeStruct((32, 2, 16,...]
    ppermute x3, waiting for transfers between devices: 0.01 us -> 28.5 us  [from_square(): lax.ppermute(x, axes, [(i, i ^ k) for i in range(4)])]
    ppermute x1 -> x3, waiting for transfers between devices: 2.26 us -> 30.5 us  [the longest x1 23 us: on_device(): rows = jnp.concatenate([rows, lax.ppermute(rows, 'z1', SWAP)], axis=0)]
    all_to_all x3 -> x2, blocking collectives: 47.3 us -> 27 us  [exchange(): return lax.all_to_all(x, axes, split_axis=0, concat_axis=0, tiled=True)]
    ppermute x6 -> x3, starting transfers between devices: 31.6 us -> 15.7 us  [from_ring(): lax.ppermute(x, axis, [(i, (i + k) % 4) for i in range(4)])]
    ppermute x6 -> x3, waiting for transfers between devices: 12 us -> 0.01 us  [from_ring(): lax.ppermute(x, axis, [(i, (i + k) % 4) for i in range(4)])]
    all_to_all x1 -> x2, starting transfers between devices: 8.6 us -> 15.7 us  [exchange(): return lax.all_to_all(x, axes, split_axis=0, concat_axis=0, tiled=True)]
    unnamed x36 -> x19, local copies, waits for them, and re-layouts: 6.56 us -> 0.11 us
  transfers between devices with their start and end apart: 11 -> 11, of which waited for: 4 -> 3; matrix products, arithmetic and copies ran while one was open for 0% -> 0% of each run, Pallas kernels for 4% -> 19%
where the time goes in v4:
time: 186 us; the launch traced here: 185 us
  waiting for transfers between devices  59 us (32%)
  starting transfers between devices  51.2 us (28%)
  Pallas kernels  46.7 us (25%)
  blocking collectives  27 us (15%)
    pallas_call x1, Pallas kernels, lay_out(): pl.pallas_call(lay_out_kernel, out_shape=jax.ShapeDtypeStruct((32, 2, 16,...  33.2 us
    ppermute x3, waiting for transfers between devices, from_square(): lax.ppermute(x, axes, [(i, i ^ k) for i in range(4)])  28.5 us
    all_to_all x2, blocking collectives, exchange(): return lax.all_to_all(x, axes, split_axis=0, concat_axis=0, tiled=True)  27 us
    ppermute x1, waiting for transfers between devices, on_device(): rows = jnp.concatenate([rows, lax.ppermute(rows, 'z1', SWAP)], axis=0)  23 us
    ppermute x3, starting transfers between devices, from_ring(): lax.ppermute(x, axis, [(i, (i + k) % 4) for i in range(4)])  15.7 us
    all_to_all x2, starting transfers between devices, exchange(): return lax.all_to_all(x, axes, split_axis=0, concat_axis=0, tiled=True)  15.7 us
    ppermute x3, starting transfers between devices, from_square(): lax.ppermute(x, axes, [(i, i ^ k) for i in range(4)])  12.3 us
    ppermute x1, waiting for transfers between devices, on_device(): more = lax.ppermute(rows, 'z0', SWAP)  7.48 us
  transfers between devices with their start and end apart: 11, of which 3 were waited for; matrix products, arithmetic and copies ran while one was open for 0% of the time, Pallas kernels for 19%

profile of v4, /device:TPU:1, one launch (start us, length us, event | category | flops | bytes accessed | tf_op | source)
XLA Modules:
  0.0 185.4 jit_solution(8470594888560762015)
XLA Ops:
  0.0 1.5 shard_map.93
  1.5 5.0 %collective-permute-start = (bf16[8,2176]{1,0:T(8,128)(2,1)}, bf16[8,2176]{1,0:T(8,128)(2,1)S(1)}, u32[]{:S(2)}, u32[]{:S(2)}) collective-permute-start(bf16[8,2176]{1,0:T(8,128)(2,1)} %shard_map.93), channel_id=1, source_target_pairs={{0,32},{32,64},{64,96},{96,0},{1,33},{33,65},{65,97},{97,1},{2,34}... | collective-permute-start | bytes 104456 | tf_op jit(solution)/shard_map/ppermute | solution.py:207
  6.5 5.7 %collective-permute-start.1 = (bf16[8,2176]{1,0:T(8,128)(2,1)}, bf16[8,2176]{1,0:T(8,128)(2,1)S(1)}, u32[]{:S(2)}, u32[]{:S(2)}) collective-permute-start(bf16[8,2176]{1,0:T(8,128)(2,1)} %shard_map.93), channel_id=1, source_target_pairs={{0,64},{32,96},{64,0},{96,32},{1,65},{33,97},{65,1},{97,33},{2,66}... | collective-permute-start | bytes 104456 | tf_op jit(solution)/shard_map/ppermute | solution.py:207
  12.2 5.0 %collective-permute-start.2 = (bf16[8,2176]{1,0:T(8,128)(2,1)}, bf16[8,2176]{1,0:T(8,128)(2,1)S(1)}, u32[]{:S(2)}, u32[]{:S(2)}) collective-permute-start(bf16[8,2176]{1,0:T(8,128)(2,1)} %shard_map.93), channel_id=1, source_target_pairs={{0,96},{32,0},{64,32},{96,64},{1,97},{33,1},{65,33},{97,65},{2,98}... | collective-permute-start | bytes 104456 | tf_op jit(solution)/shard_map/ppermute | solution.py:207
  17.2 33.2 %shard_map.91 = bf16[32,2,16,512]{3,2,1,0:T(8,128)(2,1)} custom-call(bf16[2,16,16384]{2,1,0:T(8,128)(2,1)} %pooled.1), custom_call_target="tpu_custom_call" | custom-call | tf_op jit(solution)/shard_map/pallas_call | solution.py:171
  50.3 0.0 copy-start.4
  50.3 0.0 copy-start.5
  50.3 0.0 copy-start
  50.3 12.2 %all-to-all-start = ((bf16[32,2,16,512]{3,2,1,0:T(8,128)(2,1)}), bf16[32,2,16,512]{3,2,1,0:T(8,128)(2,1)S(1)}, u32[]{:S(2)}, u32[]{:S(2)}) async-start(bf16[32,2,16,512]{3,2,1,0:T(8,128)(2,1)} %shard_map.91), calls=%async_computation | async-start | bytes 2097152 | tf_op jit(solution)/shard_map/all_to_all | solution.py:203
  62.6 0.0 copy-done.4
  62.6 0.0 copy-start.1
  62.6 0.0 copy-start.2
  62.6 0.0 copy-start.3
  62.7 0.0 copy-done.5
  62.7 0.0 collective-permute-done
  62.7 0.0 collective-permute-done.1
  62.7 0.0 collective-permute-done.2
  62.7 7.2 %collective-permute-start.3 = (bf16[32,2176]{1,0:T(8,128)(2,1)S(1)}, bf16[32,2176]{1,0:T(8,128)(2,1)S(1)}, u32[]{:S(2)}, u32[]{:S(2)}) collective-permute-start(bf16[32,2176]{1,0:T(8,128)(2,1)S(1)} %pad_maximum_fusion.1), channel_id=1, source_target_pairs={{0,8},{8,0},{16,24},{24,16},{1,9},{9,1},{17,25},{25,17},{2,10},{10... | collective-permute-start | bytes 417800 | tf_op jit(solution)/shard_map/ppermute | solution.py:211
  69.9 3.1 %collective-permute-start.4 = (bf16[32,2176]{1,0:T(8,128)(2,1)S(1)}, bf16[32,2176]{1,0:T(8,128)(2,1)S(1)}, u32[]{:S(2)}, u32[]{:S(2)}) collective-permute-start(bf16[32,2176]{1,0:T(8,128)(2,1)S(1)} %pad_maximum_fusion.1), channel_id=1, source_target_pairs={{0,16},{8,24},{16,0},{24,8},{1,17},{9,25},{17,1},{25,9},{2,18},{10... | collective-permute-start | bytes 417800 | tf_op jit(solution)/shard_map/ppermute | solution.py:211
  73.1 1.9 %collective-permute-start.5 = (bf16[32,2176]{1,0:T(8,128)(2,1)S(1)}, bf16[32,2176]{1,0:T(8,128)(2,1)S(1)}, u32[]{:S(2)}, u32[]{:S(2)}) collective-permute-start(bf16[32,2176]{1,0:T(8,128)(2,1)S(1)} %pad_maximum_fusion.1), channel_id=1, source_target_pairs={{0,24},{8,16},{16,8},{24,0},{1,25},{9,17},{17,9},{25,1},{2,26},{10... | collective-permute-start | bytes 417800 | tf_op jit(solution)/shard_map/ppermute | solution.py:211
  75.1 28.5 %collective-permute-done.3 = bf16[32,2176]{1,0:T(8,128)(2,1)S(1)} collective-permute-done((bf16[32,2176]{1,0:T(8,128)(2,1)S(1)}, bf16[32,2176]{1,0:T(8,128)(2,1)S(1)}, u32[]{:S(2)}, u32[]{:S(2)}) %collective-permute-start.3) | collective-permute-done | bytes 139296 | tf_op jit(solution)/shard_map/ppermute | solution.py:211
  103.6 0.0 collective-permute-done.4
  103.6 0.0 collective-permute-done.5
  103.7 0.0 all-to-all-done.arrived
  103.7 0.0 copy-done
  103.7 0.0 copy-done.1
  103.7 0.0 copy-done.2
  103.7 0.0 copy-done.3
  103.7 3.5 %shard_map.92 = bf16[4,4,2,32,128]{4,3,2,1,0:T(8,128)(2,1)} custom-call(s32[1,4]{1,0:T(1,128)S(1)} %copy-done.2, bf16[32,2,16,512]{3,2,1,0:T(8,128)(2,1)S(1)} %all-to-all-done.arrived, bf16[3,512,512]{2,1,0:T(8,128)(2,1)S(1)} %bitcast.14, f32[3,512]{1,0:T(4,128)S(1)} %bitcast.13, bf16[128,512]{1,0:T(8,128)(2,1)S(1)} %bitcast.15, f32[1,128]{1,0:T(1,128)S(1)} %copy-done.3), custom_call_target="tpu_custom_call" | custom-call | flops 1744830464 | bytes 4194304 | tf_op jit(solution)/shard_map/pallas_call | solution.py:59
  107.3 2.4 %collective-permute-start.6 = (bf16[128,2176]{1,0:T(8,128)(2,1)S(1)}, bf16[128,2176]{1,0:T(8,128)(2,1)S(1)}, u32[]{:S(2)}, u32[]{:S(2)}) collective-permute-start(bf16[128,2176]{1,0:T(8,128)(2,1)S(1)} %constant_dynamic-update-slice_fusion), channel_id=1, source_target_pairs={{0,4},{4,0},{1,5},{5,1},{2,6},{6,2},{3,7},{7,3},{8,12},{12,8},{9,1... | collective-permute-start | bytes 1671176 | tf_op jit(solution)/shard_map/ppermute | solution.py:233
  109.7 3.4 %all-to-all-start.1 = ((bf16[4,4,2,32,128]{4,3,2,1,0:T(8,128)(2,1)}), bf16[4,4,2,32,128]{4,3,2,1,0:T(8,128)(2,1)S(1)}, u32[]{:S(2)}, u32[]{:S(2)}) async-start(bf16[4,4,2,32,128]{4,3,2,1,0:T(8,128)(2,1)} %shard_map.92), calls=%async_computation.1 | async-start | bytes 524288 | tf_op jit(solution)/shard_map/all_to_all | solution.py:203
  113.1 23.0 %collective-permute-done.6 = bf16[128,2176]{1,0:T(8,128)(2,1)S(1)} collective-permute-done((bf16[128,2176]{1,0:T(8,128)(2,1)S(1)}, bf16[128,2176]{1,0:T(8,128)(2,1)S(1)}, u32[]{:S(2)}, u32[]{:S(2)}) %collective-permute-start.6) | collective-permute-done | bytes 557088 | tf_op jit(solution)/shard_map/ppermute | solution.py:233
  136.1 0.1 pad_maximum_fusion.part0
  136.2 0.0 all-to-all-done.1
  136.2 1.9 %collective-permute-start.7 = (bf16[256,2176]{1,0:T(8,128)(2,1)S(1)}, bf16[256,2176]{1,0:T(8,128)(2,1)S(1)}, u32[]{:S(2)}, u32[]{:S(2)}) collective-permute-start(bf16[256,2176]{1,0:T(8,128)(2,1)S(1)} %pad_maximum_fusion.part0), channel_id=1, source_target_pairs={{0,2},{2,0},{1,3},{3,1},{4,6},{6,4},{5,7},{7,5},{8,10},{10,8},{9,1... | collective-permute-start | bytes 3342344 | tf_op jit(solution)/shard_map/ppermute | solution.py:236
  138.1 0.2 broadcast_in_dim.14
  138.3 17.9 %all_to_all.20 = bf16[4,4,256,128]{3,2,1,0:T(8,128)(2,1)S(1)} all-to-all(bf16[4,4,256,128]{3,2,1,0:T(8,128)(2,1)S(1)} %broadcast_in_dim.14), channel_id=1, replica_groups=mesh['x'=4,'yh'=4,'yl'=2,'z2'=2,'z1'=2,'z0'=2,'c'=2] {'x'}, dimensions={0} | all-to-all | bytes 2097152 | tf_op jit(solution)/shard_map/all_to_all | solution.py:203
  156.2 7.5 %collective-permute-done.7.part1 = bf16[256,2176]{1,0:T(8,128)(2,1)S(1)} collective-permute-done((bf16[256,2176]{1,0:T(8,128)(2,1)S(1)}, bf16[256,2176]{1,0:T(8,128)(2,1)S(1)}, u32[]{:S(2)}, u32[]{:S(2)}) %collective-permute-start.7) | collective-permute-done | bytes 1114144 | tf_op jit(solution)/shard_map/ppermute | solution.py:236
  163.7 3.2 %collective-permute-start.8 = (bf16[16,256,128]{2,1,0:T(8,128)(2,1)S(1)}, bf16[16,256,128]{2,1,0:T(8,128)(2,1)}, u32[]{:S(2)}, u32[]{:S(2)}) collective-permute-start(bf16[16,256,128]{2,1,0:T(8,128)(2,1)S(1)} %bitcast.11), channel_id=1, source_target_pairs={{0,1},{1,0},{2,3},{3,2},{4,5},{5,4},{6,7},{7,6},{8,9},{9,8},{10,11... | collective-permute-start | bytes 3145736 | tf_op jit(solution)/shard_map/ppermute | solution.py:240
  167.0 2.7 %shard_map.94.own = bf16[256,2048]{1,0:T(8,128)(2,1)S(1)} custom-call(bf16[16,256,128]{2,1,0:T(8,128)(2,1)S(1)} %bitcast.12), custom_call_target="tpu_custom_call" | custom-call | flops 1000000000 | bytes 2097152 | tf_op jit(solution)/shard_map/pallas_call | solution.py:100
  169.7 0.0 collective-permute-done.8.other
  169.7 5.8 %shard_map.95 = f32[8,8,128]{2,1,0:T(8,128)S(1)} custom-call(s32[1]{0:T(128)} %bitcast.core, bf16[256,2048]{1,0:T(8,128)(2,1)S(1)} %shard_map.94.own, bf16[16,256,128]{2,1,0:T(8,128)(2,1)} %collective-permute-done.8.other, bf16[256,2176]{1,0:T(8,128)(2,1)S(1)} %pad_maximum_fusion.part0, bf16[256,2176]{1,0:T(8,128)(2,1)S(1)} %collective-permute-done.7.part1), custom_call_target="tpu_custom_call" | custom-call | flops 2000000000 | bytes 6291456 | tf_op jit(solution)/shard_map/pallas_call | solution.py:139
  175.6 9.1 %all_to_all.21 = f32[8,8,128]{2,1,0:T(8,128)S(1)} all-to-all(f32[8,8,128]{2,1,0:T(8,128)S(1)} %shard_map.95), channel_id=1, replica_groups=mesh['x'=4,'yh'=4,'yl'=2,'z2'=2,'z1'=2,'z0'=2,'c'=2] {'c','x'}, dimensions={0} | all-to-all | bytes 65536 | tf_op jit(solution)/shard_map/all_to_all | solution.py:203
  184.7 0.6 reshape_squeeze.3
  (11 shorter events, 0.1 us)
Async XLA Ops:
  1.5 61.2 %collective-permute-start = (bf16[8,2176]{1,0:T(8,128)(2,1)}, bf16[8,2176]{1,0:T(8,128)(2,1)S(1)}, u32[]{:S(2)}, u32[]{:S(2)}) collective-permute-start(bf16[8,2176]{1,0:T(8,128)(2,1)} %shard_map.93), channel_id=1, source_target_pairs={{0,32},{32,64},{64,96},{96,0},{1,33},{33,65},{65,97},{97,1},{2,34}... | collective-permute-start | bytes 104456 | tf_op jit(solution)/shard_map/ppermute | solution.py:207
  6.5 56.2 %collective-permute-start.1 = (bf16[8,2176]{1,0:T(8,128)(2,1)}, bf16[8,2176]{1,0:T(8,128)(2,1)S(1)}, u32[]{:S(2)}, u32[]{:S(2)}) collective-permute-start(bf16[8,2176]{1,0:T(8,128)(2,1)} %shard_map.93), channel_id=1, source_target_pairs={{0,64},{32,96},{64,0},{96,32},{1,65},{33,97},{65,1},{97,33},{2,66}... | collective-permute-start | bytes 104456 | tf_op jit(solution)/shard_map/ppermute | solution.py:207
  12.2 50.5 %collective-permute-start.2 = (bf16[8,2176]{1,0:T(8,128)(2,1)}, bf16[8,2176]{1,0:T(8,128)(2,1)S(1)}, u32[]{:S(2)}, u32[]{:S(2)}) collective-permute-start(bf16[8,2176]{1,0:T(8,128)(2,1)} %shard_map.93), channel_id=1, source_target_pairs={{0,96},{32,0},{64,32},{96,64},{1,97},{33,1},{65,33},{97,65},{2,98}... | collective-permute-start | bytes 104456 | tf_op jit(solution)/shard_map/ppermute | solution.py:207
  50.3 12.3 %copy-start.4 = (bf16[8,2176]{1,0:T(8,128)(2,1)S(1)}, bf16[8,2176]{1,0:T(8,128)(2,1)}, u32[]{:S(2)}) copy-start(bf16[8,2176]{1,0:T(8,128)(2,1)} %shard_map.93) | copy-start | bytes 104452
  50.3 12.3 %copy-start.5 = (f32[1,3,512]{2,0,1:T(1,128)S(1)}, f32[1,3,512]{2,0,1:T(1,128)}, u32[]{:S(2)}) copy-start(f32[1,3,512]{2,0,1:T(1,128)} %param.12) | copy-start | bytes 18436
  50.3 53.3 %copy-start = (bf16[1,3,512,512]{3,2,1,0:T(8,128)(2,1)S(1)}, bf16[1,3,512,512]{3,2,1,0:T(8,128)(2,1)}, u32[]{:S(2)}) copy-start(bf16[1,3,512,512]{3,2,1,0:T(8,128)(2,1)} %param.11) | copy-start | bytes 4718596
  50.3 53.3 %all-to-all-start = ((bf16[32,2,16,512]{3,2,1,0:T(8,128)(2,1)}), bf16[32,2,16,512]{3,2,1,0:T(8,128)(2,1)S(1)}, u32[]{:S(2)}, u32[]{:S(2)}) async-start(bf16[32,2,16,512]{3,2,1,0:T(8,128)(2,1)} %shard_map.91), calls=%async_computation | async-start | bytes 2097152 | tf_op jit(solution)/shard_map/all_to_all | solution.py:203
  62.6 41.1 %copy-start.1 = (bf16[1,128,512]{2,1,0:T(8,128)(2,1)S(1)}, bf16[1,128,512]{2,1,0:T(8,128)(2,1)}, u32[]{:S(2)}) copy-start(bf16[1,128,512]{2,1,0:T(8,128)(2,1)} %param.13) | copy-start | bytes 393220
  62.6 41.1 %copy-start.2 = (s32[1,4]{1,0:T(1,128)S(1)}, s32[1,4]{1,0:T(1,128)}, u32[]{:S(2)}) copy-start(s32[1,4]{1,0:T(1,128)} %order.1) | copy-start | bytes 52
  62.6 41.1 %copy-start.3 = (f32[1,128]{1,0:T(1,128)S(1)}, f32[1,128]{1,0:T(1,128)}, u32[]{:S(2)}) copy-start(f32[1,128]{1,0:T(1,128)} %gain.1) | copy-start | bytes 1540
  62.7 40.9 %collective-permute-start.3 = (bf16[32,2176]{1,0:T(8,128)(2,1)S(1)}, bf16[32,2176]{1,0:T(8,128)(2,1)S(1)}, u32[]{:S(2)}, u32[]{:S(2)}) collective-permute-start(bf16[32,2176]{1,0:T(8,128)(2,1)S(1)} %pad_maximum_fusion.1), channel_id=1, source_target_pairs={{0,8},{8,0},{16,24},{24,16},{1,9},{9,1},{17,25},{25,17},{2,10},{10... | collective-permute-start | bytes 417800 | tf_op jit(solution)/shard_map/ppermute | solution.py:211
  69.9 33.7 %collective-permute-start.4 = (bf16[32,2176]{1,0:T(8,128)(2,1)S(1)}, bf16[32,2176]{1,0:T(8,128)(2,1)S(1)}, u32[]{:S(2)}, u32[]{:S(2)}) collective-permute-start(bf16[32,2176]{1,0:T(8,128)(2,1)S(1)} %pad_maximum_fusion.1), channel_id=1, source_target_pairs={{0,16},{8,24},{16,0},{24,8},{1,17},{9,25},{17,1},{25,9},{2,18},{10... | collective-permute-start | bytes 417800 | tf_op jit(solution)/shard_map/ppermute | solution.py:211
  73.1 30.6 %collective-permute-start.5 = (bf16[32,2176]{1,0:T(8,128)(2,1)S(1)}, bf16[32,2176]{1,0:T(8,128)(2,1)S(1)}, u32[]{:S(2)}, u32[]{:S(2)}) collective-permute-start(bf16[32,2176]{1,0:T(8,128)(2,1)S(1)} %pad_maximum_fusion.1), channel_id=1, source_target_pairs={{0,24},{8,16},{16,8},{24,0},{1,25},{9,17},{17,9},{25,1},{2,26},{10... | collective-permute-start | bytes 417800 | tf_op jit(solution)/shard_map/ppermute | solution.py:211
  107.3 28.8 %collective-permute-start.6 = (bf16[128,2176]{1,0:T(8,128)(2,1)S(1)}, bf16[128,2176]{1,0:T(8,128)(2,1)S(1)}, u32[]{:S(2)}, u32[]{:S(2)}) collective-permute-start(bf16[128,2176]{1,0:T(8,128)(2,1)S(1)} %constant_dynamic-update-slice_fusion), channel_id=1, source_target_pairs={{0,4},{4,0},{1,5},{5,1},{2,6},{6,2},{3,7},{7,3},{8,12},{12,8},{9,1... | collective-permute-start | bytes 1671176 | tf_op jit(solution)/shard_map/ppermute | solution.py:233
  109.7 26.5 %all-to-all-start.1 = ((bf16[4,4,2,32,128]{4,3,2,1,0:T(8,128)(2,1)}), bf16[4,4,2,32,128]{4,3,2,1,0:T(8,128)(2,1)S(1)}, u32[]{:S(2)}, u32[]{:S(2)}) async-start(bf16[4,4,2,32,128]{4,3,2,1,0:T(8,128)(2,1)} %shard_map.92), calls=%async_computation.1 | async-start | bytes 524288 | tf_op jit(solution)/shard_map/all_to_all | solution.py:203
  136.2 27.5 %collective-permute-start.7 = (bf16[256,2176]{1,0:T(8,128)(2,1)S(1)}, bf16[256,2176]{1,0:T(8,128)(2,1)S(1)}, u32[]{:S(2)}, u32[]{:S(2)}) collective-permute-start(bf16[256,2176]{1,0:T(8,128)(2,1)S(1)} %pad_maximum_fusion.part0), channel_id=1, source_target_pairs={{0,2},{2,0},{1,3},{3,1},{4,6},{6,4},{5,7},{7,5},{8,10},{10,8},{9,1... | collective-permute-start | bytes 3342344 | tf_op jit(solution)/shard_map/ppermute | solution.py:236
  163.7 6.0 %collective-permute-start.8 = (bf16[16,256,128]{2,1,0:T(8,128)(2,1)S(1)}, bf16[16,256,128]{2,1,0:T(8,128)(2,1)}, u32[]{:S(2)}, u32[]{:S(2)}) collective-permute-start(bf16[16,256,128]{2,1,0:T(8,128)(2,1)S(1)} %bitcast.11), channel_id=1, source_target_pairs={{0,1},{1,0},{2,3},{3,2},{4,5},{5,4},{6,7},{7,6},{8,9},{9,8},{10,11... | collective-permute-start | bytes 3145736 | tf_op jit(solution)/shard_map/ppermute | solution.py:240

commit v5 on v4

--- a/solution.py
+++ b/solution.py
@@ -17,10 +17,10 @@
 WIDE = 2048 + 128
 EPSILON = 1e-06
 
-AXES = (("x", 4), ("yh", 4), ("yl", 2), ("z2", 2), ("z1", 2), ("z0", 2), ("c", 2))
+AXES = (("x", 4), ("yh", 4), ("yl", 2), ("z", 8), ("c", 2))
 TOWER = ("x", "yh")
-RANK = ("yl", "z2", "z1", "z0", "c")
-SWAP = [(0, 1), (1, 0)]
+RANK = ("yl", "z", "c")
+CHUNKS = 8
 
 
 def tower_kernel(order, arrived, weights, biases, compress, gain, out):
@@ -91,89 +91,78 @@
     lax.fori_loop(0, features.shape[1] // GROUP, group, 0, unroll=4)
 
 
-def interact_kernel(features, mixed):
-    interact(features, mixed, 0)
-
-
-def interact_own(features):
-    vmem = pl.BlockSpec(memory_space=pltpu.VMEM)
-    return pl.pallas_call(
-        interact_kernel,
-        out_shape=jax.ShapeDtypeStruct((features.shape[1], TOWERS * CD), jnp.bfloat16),
-        in_specs=[vmem],
-        out_specs=vmem,
-        compiler_params=pltpu.CompilerParams(vmem_limit_bytes=32 * 2**20),
-        cost_estimate=pl.CostEstimate(flops=10**9, bytes_accessed=2 * 2**20, transcendentals=0),
-    )(features)
-
-
-def score_kernel(core, own, other, part0, part1, out, mixed, rows, sem):
+def score_kernel(features, part0, part1, out, mixed, rows, sem):
     copies = [
         pltpu.make_async_copy(part, rows.at[k], sem.at[k]) for k, part in enumerate((part0, part1))
     ]
     for copy in copies:
         copy.start()
-    interact(other, mixed, 0)
-    totals = [jnp.zeros((1, 256), jnp.float32), jnp.zeros((1, 256), jnp.float32)]
+    interact(features, mixed, 0)
+    total = jnp.zeros((1, 256), jnp.float32)
     for k, copy in enumerate(copies):
         copy.wait()
-        extra = rows[k, :, TOWERS * CD :].astype(jnp.float32)
-        for which, features in enumerate((own, mixed)):
+        for half in range(2):
+            at = pl.ds(half * 256, 256)
             hidden = lax.dot_general(
-                rows[k, :, : TOWERS * CD],
-                features[...],
+                rows[k, at, : TOWERS * CD],
+                mixed[...],
                 (((1,), (1,)), ((), ())),
                 preferred_element_type=jnp.float32,
             )
+            extra = rows[k, at, TOWERS * CD :].astype(jnp.float32)
             terms = jnp.maximum(hidden + extra[:, 0:1], 0.0) * extra[:, 1:2]
-            totals[which] = totals[which] + jnp.sum(terms, axis=0, keepdims=True)
-    for which in range(2):
-        mine = core[0] if which == 0 else 1 - core[0]
-        for x in range(4):
-            out[mine * 4 + x, 0:1, 0:64] = totals[which][:, x * 64 : (x + 1) * 64]
-
-
-def score(core, own, other, parts):
+            total = total + jnp.sum(terms, axis=0, keepdims=True)
+    for x in range(4):
+        out[x, 0:1, 0:64] = total[:, x * 64 : (x + 1) * 64]
+
+
+def score(features, parts):
     vmem = pl.BlockSpec(memory_space=pltpu.VMEM)
     anywhere = pl.BlockSpec(memory_space=pl.ANY)
     return pl.pallas_call(
         score_kernel,
-        out_shape=jax.ShapeDtypeStruct((8, 8, 128), jnp.float32),
-        in_specs=[pl.BlockSpec(memory_space=pltpu.SMEM), vmem, vmem, anywhere, anywhere],
+        out_shape=jax.ShapeDtypeStruct((4, 8, 128), jnp.float32),
+        in_specs=[vmem, anywhere, anywhere],
         out_specs=vmem,
         scratch_shapes=[
             pltpu.VMEM((256, TOWERS * CD), jnp.bfloat16),
-            pltpu.VMEM((2, 256, WIDE), jnp.bfloat16),
+            pltpu.VMEM((2, 512, WIDE), jnp.bfloat16),
             pltpu.SemaphoreType.DMA((2,)),
         ],
         compiler_params=pltpu.CompilerParams(vmem_limit_bytes=32 * 2**20),
         cost_estimate=pl.CostEstimate(
             flops=2 * 10**9, bytes_accessed=6 * 2**20, transcendentals=0
         ),
-    )(core, own, other, *parts)
-
-
-def lay_out_kernel(pooled, sent, sem):
+    )(features, *parts)
+
+
+def lay_out_kernel(pooled, sent, held, sem):
+    width = held.shape[2] // CHUNKS
     copies = [
         pltpu.make_async_copy(
-            pooled.at[:, :, pl.ds(rank * 512, 512)], sent.at[rank], sem.at[rank]
+            pooled.at[:, :, pl.ds(k * width, width)], held.at[:, :, pl.ds(k * width, width)], sem.at[k]
         )
-        for rank in range(32)
+        for k in range(CHUNKS)
     ]
     for copy in copies:
         copy.start()
-    for copy in copies:
+    for k, copy in enumerate(copies):
         copy.wait()
+        for rank in range(k * width // 512, (k + 1) * width // 512):
+            sent[rank] = held[:, :, rank * 512 : (rank + 1) * 512]
 
 
 def lay_out(pooled):
-    anywhere = pl.BlockSpec(memory_space=pl.ANY)
     return pl.pallas_call(
         lay_out_kernel,
         out_shape=jax.ShapeDtypeStruct((32, 2, 16, 512), jnp.bfloat16),
-        in_specs=[anywhere],
-        out_specs=anywhere,
-        scratch_shapes=[pltpu.SemaphoreType.DMA((32,))],
+        in_specs=[pl.BlockSpec(memory_space=pl.ANY)],
+        out_specs=pl.BlockSpec(memory_space=pltpu.VMEM),
+        scratch_shapes=[
+            pltpu.VMEM(pooled.shape, pooled.dtype),
+            pltpu.SemaphoreType.DMA((CHUNKS,)),
+        ],
+        cost_estimate=pl.CostEstimate(flops=0, bytes_accessed=4 * 2**20, transcendentals=0),
     )(pooled)
 
 
@@ -185,15 +174,16 @@
         return jnp.sum(jnp.where(eye, row[...].astype(jnp.float32), 0.0), axis=1, keepdims=True)
 
     extra = jnp.where(lane == 0, column(bias), jnp.where(lane == 1, column(out_weight), 0.0))
-    rows[:, : TOWERS * CD] = weight[...]
-    rows[:, TOWERS * CD :] = extra.astype(jnp.bfloat16)
+    for peer in range(8):
+        rows[peer, :, : TOWERS * CD] = weight[...]
+        rows[peer, :, TOWERS * CD :] = extra.astype(jnp.bfloat16)
 
 
 def join(mlp_weight, mlp_bias, out_weight):
     vmem = pl.BlockSpec(memory_space=pltpu.VMEM)
     return pl.pallas_call(
         join_kernel,
-        out_shape=jax.ShapeDtypeStruct((8, WIDE), jnp.bfloat16),
+        out_shape=jax.ShapeDtypeStruct((8, 8, WIDE), jnp.bfloat16),
         in_specs=[vmem] * 3,
         out_specs=vmem,
     )(mlp_weight, mlp_bias[None], out_weight[None])
@@ -201,14 +191,6 @@
 
 def exchange(x, axes):
     return lax.all_to_all(x, axes, split_axis=0, concat_axis=0, tiled=True)
-
-
-def from_ring(x, axis):
-    return [x] + [lax.ppermute(x, axis, [(i, (i + k) % 4) for i in range(4)]) for k in (1, 2, 3)]
-
-
-def from_square(x, axes):
-    return [x] + [lax.ppermute(x, axes, [(i, i ^ k) for i in range(4)]) for k in (1, 2, 3)]
 
 
 def on_device(
@@ -222,26 +204,20 @@
     mlp_bias,
     out_weight,
 ):
-    rows = join(mlp_weight, mlp_bias, out_weight)
-    arrived = exchange(lay_out(pooled), RANK)
-    rows = jnp.concatenate(from_ring(rows, "yh"), axis=0)
-    rows = jnp.concatenate(from_square(rows, ("yl", "z2")), axis=0)
+    rows = exchange(join(mlp_weight, mlp_bias, out_weight), "z").reshape(64, WIDE)
+    sent, rows = lax.optimization_barrier((lay_out(pooled), rows))
+    rows = lax.all_gather(rows, ("yh", "yl"), axis=0, tiled=True)
+    arrived = exchange(sent, RANK)
     towers = tower_block(
         feature_order, arrived, cross_weight[0], cross_bias[0], compress_weight[0], norm_gain
     )
-    towers, rows = lax.optimization_barrier((towers, rows))
-    rows = jnp.concatenate([rows, lax.ppermute(rows, "z1", SWAP)], axis=0)
     column = exchange(towers, "yh").reshape(4, 256, CD)
     column, rows = lax.optimization_barrier((column, rows))
-    more = lax.ppermute(rows, "z0", SWAP)
+    more = lax.ppermute(rows, "c", [(0, 1), (1, 0)])
     features = exchange(jnp.broadcast_to(column[None], (4, 4, 256, CD)), "x")
     features = features.reshape(TOWERS, 256, CD)
     features, rows, more = lax.optimization_barrier((features, rows, more))
-    other = lax.ppermute(features, "c", SWAP)
-    own = interact_own(features)
-    core = lax.axis_index("c").reshape(1).astype(jnp.int32)
-    partial = score(core, own, other, (rows, more))
-    terms = exchange(partial, ("c", "x"))
+    terms = exchange(score(features, (rows, more)), "x")
     return jnp.sum(terms, axis=0)[0, :64].reshape(2, 1, BLOCK)
 
 

time: 186 us -> 126 us (0.68)
  the two profiles are of different devices: /device:TPU:1 before, /device:TPU:72 now
where the time goes in v5:
time: 126 us
  blocking collectives  45.8 us (36%)
  waiting for transfers between devices  35.7 us (28%)
  starting transfers between devices  17.1 us (14%)
  between operations  13.5 us (11%)
  Pallas kernels  11.8 us (9%)
  local copies, waits for them, and re-layouts  1.62 us (1%)
    all_to_all x3, blocking collectives, exchange(): return lax.all_to_all(x, axes, split_axis=0, concat_axis=0, tiled=True)  45.8 us
    all_to_all x2, waiting for transfers between devices, exchange(): return lax.all_to_all(x, axes, split_axis=0, concat_axis=0, tiled=True)  35.7 us
    all_to_all x2, starting transfers between devices, exchange(): return lax.all_to_all(x, axes, split_axis=0, concat_axis=0, tiled=True)  15 us
    pallas_call x1, Pallas kernels, score(): pl.pallas_call(score_kernel, out_shape=jax.ShapeDtypeStruct((4, 8, 128),...  4.99 us
    pallas_call x1, Pallas kernels, tower_block(): pl.pallas_call(tower_kernel, out_shape=jax.ShapeDtypeStruct((4, 4, 2, BLO...  2.83 us
  transfers between devices with their start and end apart: 4, of which 2 were waited for; matrix products, arithmetic and copies ran while one was open for 0% of the time, Pallas kernels for 4%

profile of v5, /device:TPU:72, one launch (start us, length us, event | category | flops | bytes accessed | tf_op | source)
XLA Modules:
  0.0 125.6 jit_solution(8751954428733617527)
XLA Ops:
  6.5 1.6 %shard_map.92 = bf16[8,8,2176]{2,1,0:T(8,128)(2,1)} custom-call(bf16[8,2048]{1,0:T(8,128)(2,1)} %weight.1, bf16[1,8]{1,0:T(2,128)(2,1)} %bitcast.17, bf16[1,8]{1,0:T(2,128)(2,1)} %bitcast.18), custom_call_target="tpu_custom_call" | custom-call | tf_op jit(solution)/shard_map/pallas_call | solution.py:184
  8.1 10.0 %all-to-all-start = ((bf16[8,8,2176]{2,1,0:T(8,128)(2,1)}), bf16[8,8,2176]{2,1,0:T(8,128)(2,1)S(1)}, u32[]{:S(2)}, u32[]{:S(2)}) async-start(bf16[8,8,2176]{2,1,0:T(8,128)(2,1)} %shard_map.92), calls=%async_computation | async-start | bytes 557056 | tf_op jit(solution)/shard_map/all_to_all | solution.py:193
  18.1 0.0 copy-start.6
  18.1 0.0 copy-start.1
  18.1 0.0 copy-start.2
  18.1 0.0 copy-start.3
  18.1 0.0 copy-start.4
  18.1 0.0 all-gather.2.cloned.1.call-start
  18.2 2.4 %shard_map.91 = bf16[32,2,16,512]{3,2,1,0:T(8,128)(2,1)} custom-call(bf16[2,16,16384]{2,1,0:T(8,128)(2,1)} %pooled.1), custom_call_target="tpu_custom_call" | custom-call | bytes 4194304 | tf_op jit(solution)/shard_map/pallas_call | solution.py:156
  20.6 8.2 %all-to-all-done = bf16[8,8,2176]{2,1,0:T(8,128)(2,1)S(1)} async-done(((bf16[8,8,2176]{2,1,0:T(8,128)(2,1)}), bf16[8,8,2176]{2,1,0:T(8,128)(2,1)S(1)}, u32[]{:S(2)}, u32[]{:S(2)}) %all-to-all-start) | async-done | bytes 278560 | tf_op jit(solution)/shard_map/all_to_all | solution.py:193
  28.8 0.0 copy-start.5
  28.9 0.7 copy-done.5
  29.6 0.0 all-gather.2.cloned.1.call-update
  29.6 5.1 %all-to-all-start.1 = ((bf16[32,2,16,512]{3,2,1,0:T(8,128)(2,1)}), bf16[32,2,16,512]{3,2,1,0:T(8,128)(2,1)S(1)}, u32[]{:S(2)}, u32[]{:S(2)}) async-start(bf16[32,2,16,512]{3,2,1,0:T(8,128)(2,1)} %shard_map.91), calls=%async_computation.1 | async-start | bytes 2097152 | tf_op jit(solution)/shard_map/all_to_all | solution.py:193
  34.7 0.0 copy-done.6
  34.7 27.5 %all-to-all-done.1.arrived = bf16[32,2,16,512]{3,2,1,0:T(8,128)(2,1)S(1)} async-done(((bf16[32,2,16,512]{3,2,1,0:T(8,128)(2,1)}), bf16[32,2,16,512]{3,2,1,0:T(8,128)(2,1)S(1)}, u32[]{:S(2)}, u32[]{:S(2)}) %all-to-all-start.1) | async-done | bytes 1048608 | tf_op jit(solution)/shard_map/all_to_all | solution.py:193
  62.1 0.0 copy-done.1
  62.1 0.0 copy-done.2
  62.1 0.0 copy-done.3
  62.2 0.0 copy-done.4
  62.2 2.8 %shard_map.93 = bf16[4,4,2,32,128]{4,3,2,1,0:T(8,128)(2,1)S(1)} custom-call(s32[1,4]{1,0:T(1,128)S(1)} %copy-done.3, bf16[32,2,16,512]{3,2,1,0:T(8,128)(2,1)S(1)} %all-to-all-done.1.arrived, bf16[3,512,512]{2,1,0:T(8,128)(2,1)S(1)} %bitcast.13, f32[3,512]{1,0:T(4,128)S(1)} %bitcast.12, bf16[128,512]{1,0:T(8,128)(2,1)S(1)} %bitcast.14, f32[1,128]{1,0:T(1,128)S(1)} %copy-done.4), custom_call_target="tpu_custom_call" | custom-call | flops 1744830464 | bytes 4194304 | tf_op jit(solution)/shard_map/pallas_call | solution.py:59
  65.0 18.2 %all_to_all.25 = bf16[4,4,2,32,128]{4,3,2,1,0:T(8,128)(2,1)S(1)} all-to-all(bf16[4,4,2,32,128]{4,3,2,1,0:T(8,128)(2,1)S(1)} %shard_map.93), channel_id=1, replica_groups=mesh['x'=4,'yh'=4,'yl'=2,'z'=8,'c'=2] {'yh'}, dimensions={0} | all-to-all | bytes 524288 | tf_op jit(solution)/shard_map/all_to_all | solution.py:193
  83.2 0.0 all-gather.2.cloned.1.call-done.part0
  83.2 0.0 copy-start
  83.2 2.0 %collective-permute-start = (bf16[512,2176]{1,0:T(8,128)(2,1)}, bf16[512,2176]{1,0:T(8,128)(2,1)S(1)}, u32[]{:S(2)}, u32[]{:S(2)}) collective-permute-start(bf16[512,2176]{1,0:T(8,128)(2,1)} %all-gather.2.cloned.1.call-done.part0), channel_id=1, source_target_pairs={{0,1},{1,0},{2,3},{3,2},{4,5},{5,4},{6,7},{7,6},{8,9},{9,8},{10,11... | collective-permute-start | bytes 6684680 | tf_op jit(solution)/shard_map/ppermute | solution.py:216
  85.3 0.2 broadcast_in_dim.14
  85.5 19.9 %all_to_all.26 = bf16[4,4,256,128]{3,2,1,0:T(8,128)(2,1)S(1)} all-to-all(bf16[4,4,256,128]{3,2,1,0:T(8,128)(2,1)S(1)} %broadcast_in_dim.14), channel_id=1, replica_groups=mesh['x'=4,'yh'=4,'yl'=2,'z'=8,'c'=2] {'x'}, dimensions={0} | all-to-all | bytes 2097152 | tf_op jit(solution)/shard_map/all_to_all | solution.py:193
  105.3 0.0 collective-permute-done.part1
  105.3 0.0 copy-done
  105.3 5.0 %shard_map.94 = f32[4,8,128]{2,1,0:T(8,128)S(1)} custom-call(bf16[16,256,128]{2,1,0:T(8,128)(2,1)S(1)} %bitcast.11, bf16[512,2176]{1,0:T(8,128)(2,1)S(1)} %copy-done, bf16[512,2176]{1,0:T(8,128)(2,1)S(1)} %collective-permute-done.part1), custom_call_target="tpu_custom_call" | custom-call | flops 2000000000 | bytes 6291456 | tf_op jit(solution)/shard_map/pallas_call | solution.py:122
  110.3 7.7 %all_to_all.27 = f32[4,8,128]{2,1,0:T(8,128)S(1)} all-to-all(f32[4,8,128]{2,1,0:T(8,128)S(1)} %shard_map.94), channel_id=1, replica_groups=mesh['x'=4,'yh'=4,'yl'=2,'z'=8,'c'=2] {'x'}, dimensions={0} | all-to-all | bytes 32768 | tf_op jit(solution)/shard_map/all_to_all | solution.py:193
  118.1 0.6 reshape_squeeze.3
  (3 shorter events, 0.0 us)
Async XLA Ops:
  8.1 20.7 %all-to-all-start = ((bf16[8,8,2176]{2,1,0:T(8,128)(2,1)}), bf16[8,8,2176]{2,1,0:T(8,128)(2,1)S(1)}, u32[]{:S(2)}, u32[]{:S(2)}) async-start(bf16[8,8,2176]{2,1,0:T(8,128)(2,1)} %shard_map.92), calls=%async_computation | async-start | bytes 557056 | tf_op jit(solution)/shard_map/all_to_all | solution.py:193
  18.1 16.6 %copy-start.6 = (f32[1,3,512]{2,0,1:T(1,128)S(1)}, f32[1,3,512]{2,0,1:T(1,128)}, u32[]{:S(2)}) copy-start(f32[1,3,512]{2,0,1:T(1,128)} %param.12) | copy-start | bytes 18436
  18.1 44.1 %copy-start.1 = (bf16[1,3,512,512]{3,2,1,0:T(8,128)(2,1)S(1)}, bf16[1,3,512,512]{3,2,1,0:T(8,128)(2,1)}, u32[]{:S(2)}) copy-start(bf16[1,3,512,512]{3,2,1,0:T(8,128)(2,1)} %param.11) | copy-start | bytes 4718596
  18.1 44.1 %copy-start.2 = (bf16[1,128,512]{2,1,0:T(8,128)(2,1)S(1)}, bf16[1,128,512]{2,1,0:T(8,128)(2,1)}, u32[]{:S(2)}) copy-start(bf16[1,128,512]{2,1,0:T(8,128)(2,1)} %param.13) | copy-start | bytes 393220
  18.1 44.1 %copy-start.3 = (s32[1,4]{1,0:T(1,128)S(1)}, s32[1,4]{1,0:T(1,128)}, u32[]{:S(2)}) copy-start(s32[1,4]{1,0:T(1,128)} %order.1) | copy-start | bytes 52
  18.1 44.1 %copy-start.4 = (f32[1,128]{1,0:T(1,128)S(1)}, f32[1,128]{1,0:T(1,128)}, u32[]{:S(2)}) copy-start(f32[1,128]{1,0:T(1,128)} %gain.1) | copy-start | bytes 1540
  18.1 65.1 %all-gather.2.cloned.1.call-start = ((), (), s32[]{:S(2)}) async-start(), calls=%async_computation.5 | async-start | bytes 2506752 | tf_op jit(solution)/shard_map/all_gather | solution.py:209
  28.8 0.7 copy-start.5
  29.6 32.5 %all-to-all-start.1 = ((bf16[32,2,16,512]{3,2,1,0:T(8,128)(2,1)}), bf16[32,2,16,512]{3,2,1,0:T(8,128)(2,1)S(1)}, u32[]{:S(2)}, u32[]{:S(2)}) async-start(bf16[32,2,16,512]{3,2,1,0:T(8,128)(2,1)} %shard_map.91), calls=%async_computation.1 | async-start | bytes 2097152 | tf_op jit(solution)/shard_map/all_to_all | solution.py:193
  83.2 22.1 %copy-start = (bf16[512,2176]{1,0:T(8,128)(2,1)S(1)}, bf16[512,2176]{1,0:T(8,128)(2,1)}, u32[]{:S(2)}) copy-start(bf16[512,2176]{1,0:T(8,128)(2,1)} %all-gather.2.cloned.1.call-done.part0) | copy-start | bytes 6684676
  83.2 22.1 %collective-permute-start = (bf16[512,2176]{1,0:T(8,128)(2,1)}, bf16[512,2176]{1,0:T(8,128)(2,1)S(1)}, u32[]{:S(2)}, u32[]{:S(2)}) collective-permute-start(bf16[512,2176]{1,0:T(8,128)(2,1)} %all-gather.2.cloned.1.call-done.part0), channel_id=1, source_target_pairs={{0,1},{1,0},{2,3},{3,2},{4,5},{5,4},{6,7},{7,6},{8,9},{9,8},{10,11... | collective-permute-start | bytes 6684680 | tf_op jit(solution)/shard_map/ppermute | solution.py:216
Sparse Core Ops, SparseCore 0:
  29.7 46.4 all-gather.1

commit v6 on v4

--- a/solution.py
+++ b/solution.py
@@ -17,10 +17,10 @@
 WIDE = 2048 + 128
 EPSILON = 1e-06
 
-AXES = (("x", 4), ("yh", 4), ("yl", 2), ("z2", 2), ("z1", 2), ("z0", 2), ("c", 2))
+AXES = (("x", 4), ("yh", 4), ("yl", 2), ("z", 8), ("c", 2))
 TOWER = ("x", "yh")
-RANK = ("yl", "z2", "z1", "z0", "c")
-SWAP = [(0, 1), (1, 0)]
+RANK = ("yl", "z", "c")
+CHUNKS = 8
 
 
 def tower_kernel(order, arrived, weights, biases, compress, gain, out):
@@ -107,9 +107,10 @@
     )(features)
 
 
-def score_kernel(core, own, other, part0, part1, out, mixed, rows, sem):
+def score_kernel(core, own, other, gathered, out, mixed, rows, sem):
     copies = [
-        pltpu.make_async_copy(part, rows.at[k], sem.at[k]) for k, part in enumerate((part0, part1))
+        pltpu.make_async_copy(gathered.at[pl.ds(k * 256, 256)], rows.at[k], sem.at[k])
+        for k in range(2)
     ]
     for copy in copies:
         copy.start()
@@ -133,13 +134,13 @@
             out[mine * 4 + x, 0:1, 0:64] = totals[which][:, x * 64 : (x + 1) * 64]
 
 
-def score(core, own, other, parts):
+def score(core, own, other, rows):
     vmem = pl.BlockSpec(memory_space=pltpu.VMEM)
     anywhere = pl.BlockSpec(memory_space=pl.ANY)
     return pl.pallas_call(
         score_kernel,
         out_shape=jax.ShapeDtypeStruct((8, 8, 128), jnp.float32),
-        in_specs=[pl.BlockSpec(memory_space=pltpu.SMEM), vmem, vmem, anywhere, anywhere],
+        in_specs=[pl.BlockSpec(memory_space=pltpu.SMEM), vmem, vmem, anywhere],
         out_specs=vmem,
         scratch_shapes=[
             pltpu.VMEM((256, TOWERS * CD), jnp.bfloat16),
@@ -150,30 +151,36 @@
         cost_estimate=pl.CostEstimate(
             flops=2 * 10**9, bytes_accessed=6 * 2**20, transcendentals=0
         ),
-    )(core, own, other, *parts)
-
-
-def lay_out_kernel(pooled, sent, sem):
+    )(core, own, other, rows)
+
+
+def lay_out_kernel(pooled, sent, held, sem):
+    width = held.shape[2] // CHUNKS
     copies = [
         pltpu.make_async_copy(
-            pooled.at[:, :, pl.ds(rank * 512, 512)], sent.at[rank], sem.at[rank]
+            pooled.at[:, :, pl.ds(k * width, width)], held.at[:, :, pl.ds(k * width, width)], sem.at[k]
         )
-        for rank in range(32)
+        for k in range(CHUNKS)
     ]
     for copy in copies:
         copy.start()
-    for copy in copies:
+    for k, copy in enumerate(copies):
         copy.wait()
+        for rank in range(k * width // 512, (k + 1) * width // 512):
+            sent[rank] = held[:, :, rank * 512 : (rank + 1) * 512]
 
 
 def lay_out(pooled):
-    anywhere = pl.BlockSpec(memory_space=pl.ANY)
     return pl.pallas_call(
         lay_out_kernel,
         out_shape=jax.ShapeDtypeStruct((32, 2, 16, 512), jnp.bfloat16),
-        in_specs=[anywhere],
-        out_specs=anywhere,
-        scratch_shapes=[pltpu.SemaphoreType.DMA((32,))],
+        in_specs=[pl.BlockSpec(memory_space=pl.ANY)],
+        out_specs=pl.BlockSpec(memory_space=pltpu.VMEM),
+        scratch_shapes=[
+            pltpu.VMEM(pooled.shape, pooled.dtype),
+            pltpu.SemaphoreType.DMA((CHUNKS,)),
+        ],
+        cost_estimate=pl.CostEstimate(flops=0, bytes_accessed=4 * 2**20, transcendentals=0),
     )(pooled)
 
 
@@ -201,14 +208,6 @@
 
 def exchange(x, axes):
     return lax.all_to_all(x, axes, split_axis=0, concat_axis=0, tiled=True)
-
-
-def from_ring(x, axis):
-    return [x] + [lax.ppermute(x, axis, [(i, (i + k) % 4) for i in range(4)]) for k in (1, 2, 3)]
-
-
-def from_square(x, axes):
-    return [x] + [lax.ppermute(x, axes, [(i, i ^ k) for i in range(4)]) for k in (1, 2, 3)]
 
 
 def on_device(
@@ -222,26 +221,23 @@
     mlp_bias,
     out_weight,
 ):
+    arrived = exchange(lay_out(pooled), RANK)
     rows = join(mlp_weight, mlp_bias, out_weight)
-    arrived = exchange(lay_out(pooled), RANK)
-    rows = jnp.concatenate(from_ring(rows, "yh"), axis=0)
-    rows = jnp.concatenate(from_square(rows, ("yl", "z2")), axis=0)
+    rows = jnp.concatenate([rows, lax.ppermute(rows, "yl", [(0, 1), (1, 0)])], axis=0)
+    rows = [rows] + [
+        lax.ppermute(rows, "yh", [(i, (i + k) % 4) for i in range(4)]) for k in range(1, 4)
+    ]
+    rows = lax.all_gather(jnp.concatenate(rows, axis=0), "z", axis=0, tiled=True)
     towers = tower_block(
         feature_order, arrived, cross_weight[0], cross_bias[0], compress_weight[0], norm_gain
     )
-    towers, rows = lax.optimization_barrier((towers, rows))
-    rows = jnp.concatenate([rows, lax.ppermute(rows, "z1", SWAP)], axis=0)
     column = exchange(towers, "yh").reshape(4, 256, CD)
-    column, rows = lax.optimization_barrier((column, rows))
-    more = lax.ppermute(rows, "z0", SWAP)
     features = exchange(jnp.broadcast_to(column[None], (4, 4, 256, CD)), "x")
     features = features.reshape(TOWERS, 256, CD)
-    features, rows, more = lax.optimization_barrier((features, rows, more))
-    other = lax.ppermute(features, "c", SWAP)
+    other = lax.ppermute(features, "c", [(0, 1), (1, 0)])
     own = interact_own(features)
     core = lax.axis_index("c").reshape(1).astype(jnp.int32)
-    partial = score(core, own, other, (rows, more))
-    terms = exchange(partial, ("c", "x"))
+    terms = exchange(score(core, own, other, rows), ("c", "x"))
     return jnp.sum(terms, axis=0)[0, :64].reshape(2, 1, BLOCK)
 
 

time: 186 us -> 125 us (0.67)
  waiting for transfers between devices: 59 us -> 12.6 us
  Pallas kernels: 46.7 us -> 14.1 us
  blocking collectives: 27 us -> 43.6 us
  starting transfers between devices: 51.2 us -> 35.5 us
  between operations: 0.33 us -> 13.6 us
  local copies, waits for them, and re-layouts: 1 us -> 4.04 us
    ppermute x9 -> x5, waiting for transfers between devices: 59 us -> 12.6 us  [the longest x1 9.03 us: on_device(): lax.ppermute(rows, 'yl', [(0, 1), (1, 0)])]
    pallas_call x1, Pallas kernels: 33.2 us -> 2.45 us  [lay_out(): pl.pallas_call(lay_out_kernel, out_shape=jax.ShapeDtypeStruct((32, 2, 16,...]
    all_to_all x2 -> x3, blocking collectives: 27 us -> 43.6 us  [exchange(): return lax.all_to_all(x, axes, split_axis=0, concat_axis=0, tiled=True)]
    ppermute x9 -> x5, starting transfers between devices: 35.5 us -> 22.4 us  [the longest x3 13.9 us: on_device(): lax.ppermute(rows, 'yh', [(i, (i + k) % 4) for i in range(4)])]
    unnamed x19, local copies, waits for them, and re-layouts: 0.11 us -> 3.16 us
    all_to_all x2 -> x1, starting transfers between devices: 15.7 us -> 13 us  [exchange(): return lax.all_to_all(x, axes, split_axis=0, concat_axis=0, tiled=True)]
  transfers between devices with their start and end apart: 11 -> 7, of which waited for: 3 -> 2; matrix products, arithmetic and copies ran while one was open for 0% -> 1% of each run, Pallas kernels for 19% -> 6%
where the time goes in v6:
time: 125 us; the launch traced here: 124 us
  blocking collectives  43.6 us (35%)
  starting transfers between devices  35.5 us (28%)
  Pallas kernels  14.1 us (11%)
  between operations  13.6 us (11%)
  waiting for transfers between devices  12.6 us (10%)
  local copies, waits for them, and re-layouts  4.04 us (3%)
    all_to_all x3, blocking collectives, exchange(): return lax.all_to_all(x, axes, split_axis=0, concat_axis=0, tiled=True)  43.6 us
    ppermute x3, starting transfers between devices, on_device(): lax.ppermute(rows, 'yh', [(i, (i + k) % 4) for i in range(4)])  13.9 us
    all_to_all x1, starting transfers between devices, exchange(): return lax.all_to_all(x, axes, split_axis=0, concat_axis=0, tiled=True)  13 us
    ppermute x1, waiting for transfers between devices, on_device(): lax.ppermute(rows, 'yl', [(0, 1), (1, 0)])  9.03 us
    ppermute x1, starting transfers between devices, on_device(): other = lax.ppermute(features, 'c', [(0, 1), (1, 0)])  5.19 us
    pallas_call x1, Pallas kernels, score(): pl.pallas_call(score_kernel, out_shape=jax.ShapeDtypeStruct((8, 8, 128),...  4.62 us
    ppermute x3, waiting for transfers between devices, on_device(): lax.ppermute(rows, 'yh', [(i, (i + k) % 4) for i in range(4)])  3.55 us
    ppermute x1, starting transfers between devices, on_device(): lax.ppermute(rows, 'yl', [(0, 1), (1, 0)])  3.29 us
  transfers between devices with their start and end apart: 7, of which 2 were waited for; matrix products, arithmetic and copies ran while one was open for 1% of the time, Pallas kernels for 6%

profile of v6, /device:TPU:1, one launch (start us, length us, event | category | flops | bytes accessed | tf_op | source)
XLA Modules:
  0.0 124.1 jit_solution(8442015665194392244)
XLA Ops:
  6.5 0.0 copy-start.6
  6.5 0.0 copy-start.3
  6.5 0.0 copy-start.1
  6.5 0.0 copy-start.2
  6.5 0.0 copy-start.4
  6.5 2.4 %shard_map.91 = bf16[32,2,16,512]{3,2,1,0:T(8,128)(2,1)} custom-call(bf16[2,16,16384]{2,1,0:T(8,128)(2,1)} %pooled.1), custom_call_target="tpu_custom_call" | custom-call | bytes 4194304 | tf_op jit(solution)/shard_map/pallas_call | solution.py:174
  9.0 13.0 %all-to-all-start = ((bf16[32,2,16,512]{3,2,1,0:T(8,128)(2,1)}), bf16[32,2,16,512]{3,2,1,0:T(8,128)(2,1)S(1)}, u32[]{:S(2)}, u32[]{:S(2)}) async-start(bf16[32,2,16,512]{3,2,1,0:T(8,128)(2,1)} %shard_map.91), calls=%async_computation | async-start | bytes 2097152 | tf_op jit(solution)/shard_map/all_to_all | solution.py:210
  22.0 0.0 all-gather.2.cloned.1.call-start
  22.1 1.5 %shard_map.94 = bf16[8,2176]{1,0:T(8,128)(2,1)} custom-call(bf16[8,2048]{1,0:T(8,128)(2,1)} %weight.1, bf16[1,8]{1,0:T(2,128)(2,1)} %bitcast.17, bf16[1,8]{1,0:T(2,128)(2,1)} %bitcast.18), custom_call_target="tpu_custom_call" | custom-call | tf_op jit(solution)/shard_map/pallas_call | solution.py:201
  23.5 3.3 %collective-permute-start.1 = (bf16[8,2176]{1,0:T(8,128)(2,1)}, bf16[8,2176]{1,0:T(8,128)(2,1)S(1)}, u32[]{:S(2)}, u32[]{:S(2)}) collective-permute-start(bf16[8,2176]{1,0:T(8,128)(2,1)} %shard_map.94), channel_id=1, source_target_pairs={{0,16},{16,0},{1,17},{17,1},{2,18},{18,2},{3,19},{19,3},{4,20},{20... | collective-permute-start | bytes 104456 | tf_op jit(solution)/shard_map/ppermute | solution.py:226
  26.8 0.8 constant_dynamic-update-slice_fusion.4
  27.6 9.0 %collective-permute-done.1 = bf16[8,2176]{1,0:T(8,128)(2,1)S(1)} collective-permute-done((bf16[8,2176]{1,0:T(8,128)(2,1)}, bf16[8,2176]{1,0:T(8,128)(2,1)S(1)}, u32[]{:S(2)}, u32[]{:S(2)}) %collective-permute-start.1) | collective-permute-done | bytes 34848 | tf_op jit(solution)/shard_map/ppermute | solution.py:226
  36.6 0.8 pad_maximum_fusion
  37.4 4.2 %collective-permute-start.2 = (bf16[16,2176]{1,0:T(8,128)(2,1)S(1)}, bf16[16,2176]{1,0:T(8,128)(2,1)S(1)}, u32[]{:S(2)}, u32[]{:S(2)}) collective-permute-start(bf16[16,2176]{1,0:T(8,128)(2,1)S(1)} %pad_maximum_fusion), channel_id=1, source_target_pairs={{0,32},{32,64},{64,96},{96,0},{1,33},{33,65},{65,97},{97,1},{2,34}... | collective-permute-start | bytes 208904 | tf_op jit(solution)/shard_map/ppermute | solution.py:228
  41.6 4.8 %collective-permute-start.3 = (bf16[16,2176]{1,0:T(8,128)(2,1)S(1)}, bf16[16,2176]{1,0:T(8,128)(2,1)S(1)}, u32[]{:S(2)}, u32[]{:S(2)}) collective-permute-start(bf16[16,2176]{1,0:T(8,128)(2,1)S(1)} %pad_maximum_fusion), channel_id=1, source_target_pairs={{0,64},{32,96},{64,0},{96,32},{1,65},{33,97},{65,1},{97,33},{2,66}... | collective-permute-start | bytes 208904 | tf_op jit(solution)/shard_map/ppermute | solution.py:228
  46.4 5.0 %collective-permute-start.4 = (bf16[16,2176]{1,0:T(8,128)(2,1)S(1)}, bf16[16,2176]{1,0:T(8,128)(2,1)S(1)}, u32[]{:S(2)}, u32[]{:S(2)}) collective-permute-start(bf16[16,2176]{1,0:T(8,128)(2,1)S(1)} %pad_maximum_fusion), channel_id=1, source_target_pairs={{0,96},{32,0},{64,32},{96,64},{1,97},{33,1},{65,33},{97,65},{2,98}... | collective-permute-start | bytes 208904 | tf_op jit(solution)/shard_map/ppermute | solution.py:228
  51.4 0.0 collective-permute-done.2
  51.4 0.0 collective-permute-done.3
  51.4 3.5 %collective-permute-done.4 = bf16[16,2176]{1,0:T(8,128)(2,1)S(1)} collective-permute-done((bf16[16,2176]{1,0:T(8,128)(2,1)S(1)}, bf16[16,2176]{1,0:T(8,128)(2,1)S(1)}, u32[]{:S(2)}, u32[]{:S(2)}) %collective-permute-start.4) | collective-permute-done | bytes 69664 | tf_op jit(solution)/shard_map/ppermute | solution.py:228
  55.0 0.0 copy-start.5
  55.0 0.7 copy-done.5
  55.7 0.0 all-gather.2.cloned.1.call-update
  55.7 0.0 copy-done.6
  55.7 0.0 all-to-all-done.arrived
  55.7 0.0 copy-done.3
  55.7 0.0 copy-done.1
  55.8 0.0 copy-done.2
  55.8 0.0 copy-done.4
  55.8 2.8 %shard_map.92 = bf16[4,4,2,32,128]{4,3,2,1,0:T(8,128)(2,1)S(1)} custom-call(s32[1,4]{1,0:T(1,128)S(1)} %copy-done.3, bf16[32,2,16,512]{3,2,1,0:T(8,128)(2,1)S(1)} %all-to-all-done.arrived, bf16[3,512,512]{2,1,0:T(8,128)(2,1)S(1)} %bitcast.14, f32[3,512]{1,0:T(4,128)S(1)} %bitcast.13, bf16[128,512]{1,0:T(8,128)(2,1)S(1)} %bitcast.15, f32[1,128]{1,0:T(1,128)S(1)} %copy-done.4), custom_call_target="tpu_custom_call" | custom-call | flops 1744830464 | bytes 4194304 | tf_op jit(solution)/shard_map/pallas_call | solution.py:59
  58.6 14.8 %all_to_all.20 = bf16[4,4,2,32,128]{4,3,2,1,0:T(8,128)(2,1)S(1)} all-to-all(bf16[4,4,2,32,128]{4,3,2,1,0:T(8,128)(2,1)S(1)} %shard_map.92), channel_id=1, replica_groups=mesh['x'=4,'yh'=4,'yl'=2,'z'=8,'c'=2] {'yh'}, dimensions={0} | all-to-all | bytes 524288 | tf_op jit(solution)/shard_map/all_to_all | solution.py:210
  73.4 0.2 broadcast_in_dim.14
  73.6 16.6 %all_to_all.21 = bf16[4,4,256,128]{3,2,1,0:T(8,128)(2,1)S(1)} all-to-all(bf16[4,4,256,128]{3,2,1,0:T(8,128)(2,1)S(1)} %broadcast_in_dim.14), channel_id=1, replica_groups=mesh['x'=4,'yh'=4,'yl'=2,'z'=8,'c'=2] {'x'}, dimensions={0} | all-to-all | bytes 2097152 | tf_op jit(solution)/shard_map/all_to_all | solution.py:210
  90.2 5.2 %collective-permute-start = (bf16[16,256,128]{2,1,0:T(8,128)(2,1)S(1)}, bf16[16,256,128]{2,1,0:T(8,128)(2,1)S(1)}, u32[]{:S(2)}, u32[]{:S(2)}) collective-permute-start(bf16[16,256,128]{2,1,0:T(8,128)(2,1)S(1)} %bitcast.11), channel_id=1, source_target_pairs={{0,1},{1,0},{2,3},{3,2},{4,5},{5,4},{6,7},{7,6},{8,9},{9,8},{10,11... | collective-permute-start | bytes 3145736 | tf_op jit(solution)/shard_map/ppermute | solution.py:237
  95.4 2.7 %shard_map.93.own = bf16[256,2048]{1,0:T(8,128)(2,1)S(1)} custom-call(bf16[16,256,128]{2,1,0:T(8,128)(2,1)S(1)} %bitcast.12), custom_call_target="tpu_custom_call" | custom-call | flops 1000000000 | bytes 2097152 | tf_op jit(solution)/shard_map/pallas_call | solution.py:100
  98.1 0.0 all-gather.2.cloned.1.call-done.gathered
  98.1 0.0 collective-permute-done.other
  98.1 0.0 copy-start
  98.1 1.6 %copy-done = bf16[512,2176]{1,0:T(8,128)(2,1)S(1)} copy-done((bf16[512,2176]{1,0:T(8,128)(2,1)S(1)}, bf16[512,2176]{1,0:T(8,128)(2,1)}, u32[]{:S(2)}) %copy-start) | copy-done | bytes 2228248
  99.8 4.6 %shard_map.95 = f32[8,8,128]{2,1,0:T(8,128)S(1)} custom-call(s32[1]{0:T(128)} %bitcast.core, bf16[256,2048]{1,0:T(8,128)(2,1)S(1)} %shard_map.93.own, bf16[16,256,128]{2,1,0:T(8,128)(2,1)S(1)} %collective-permute-done.other, bf16[512,2176]{1,0:T(8,128)(2,1)S(1)} %copy-done), custom_call_target="tpu_custom_call" | custom-call | flops 2000000000 | bytes 6291456 | tf_op jit(solution)/shard_map/pallas_call | solution.py:140
  104.4 12.2 %all_to_all.22 = f32[8,8,128]{2,1,0:T(8,128)S(1)} all-to-all(f32[8,8,128]{2,1,0:T(8,128)S(1)} %shard_map.95), channel_id=1, replica_groups=mesh['x'=4,'yh'=4,'yl'=2,'z'=8,'c'=2] {'c','x'}, dimensions={0} | all-to-all | bytes 65536 | tf_op jit(solution)/shard_map/all_to_all | solution.py:210
  116.6 0.6 reshape_squeeze.3
  (7 shorter events, 0.1 us)
Async XLA Ops:
  6.5 49.2 %copy-start.6 = (f32[1,3,512]{2,0,1:T(1,128)S(1)}, f32[1,3,512]{2,0,1:T(1,128)}, u32[]{:S(2)}) copy-start(f32[1,3,512]{2,0,1:T(1,128)} %param.12) | copy-start | bytes 18436
  6.5 49.2 %copy-start.3 = (s32[1,4]{1,0:T(1,128)S(1)}, s32[1,4]{1,0:T(1,128)}, u32[]{:S(2)}) copy-start(s32[1,4]{1,0:T(1,128)} %order.1) | copy-start | bytes 52
  6.5 49.2 %copy-start.1 = (bf16[1,3,512,512]{3,2,1,0:T(8,128)(2,1)S(1)}, bf16[1,3,512,512]{3,2,1,0:T(8,128)(2,1)}, u32[]{:S(2)}) copy-start(bf16[1,3,512,512]{3,2,1,0:T(8,128)(2,1)} %param.11) | copy-start | bytes 4718596
  6.5 49.2 %copy-start.2 = (bf16[1,128,512]{2,1,0:T(8,128)(2,1)S(1)}, bf16[1,128,512]{2,1,0:T(8,128)(2,1)}, u32[]{:S(2)}) copy-start(bf16[1,128,512]{2,1,0:T(8,128)(2,1)} %param.13) | copy-start | bytes 393220
  6.5 49.2 %copy-start.4 = (f32[1,128]{1,0:T(1,128)S(1)}, f32[1,128]{1,0:T(1,128)}, u32[]{:S(2)}) copy-start(f32[1,128]{1,0:T(1,128)} %gain.1) | copy-start | bytes 1540
  9.0 46.7 %all-to-all-start = ((bf16[32,2,16,512]{3,2,1,0:T(8,128)(2,1)}), bf16[32,2,16,512]{3,2,1,0:T(8,128)(2,1)S(1)}, u32[]{:S(2)}, u32[]{:S(2)}) async-start(bf16[32,2,16,512]{3,2,1,0:T(8,128)(2,1)} %shard_map.91), calls=%async_computation | async-start | bytes 2097152 | tf_op jit(solution)/shard_map/all_to_all | solution.py:210
  22.0 76.1 %all-gather.2.cloned.1.call-start = ((), (), s32[]{:S(2)}) async-start(), calls=%async_computation.4 | async-start | bytes 2506752 | tf_op jit(solution)/shard_map/all_gather | solution.py:230
  23.5 13.1 %collective-permute-start.1 = (bf16[8,2176]{1,0:T(8,128)(2,1)}, bf16[8,2176]{1,0:T(8,128)(2,1)S(1)}, u32[]{:S(2)}, u32[]{:S(2)}) collective-permute-start(bf16[8,2176]{1,0:T(8,128)(2,1)} %shard_map.94), channel_id=1, source_target_pairs={{0,16},{16,0},{1,17},{17,1},{2,18},{18,2},{3,19},{19,3},{4,20},{20... | collective-permute-start | bytes 104456 | tf_op jit(solution)/shard_map/ppermute | solution.py:226
  37.4 14.0 %collective-permute-start.2 = (bf16[16,2176]{1,0:T(8,128)(2,1)S(1)}, bf16[16,2176]{1,0:T(8,128)(2,1)S(1)}, u32[]{:S(2)}, u32[]{:S(2)}) collective-permute-start(bf16[16,2176]{1,0:T(8,128)(2,1)S(1)} %pad_maximum_fusion), channel_id=1, source_target_pairs={{0,32},{32,64},{64,96},{96,0},{1,33},{33,65},{65,97},{97,1},{2,34}... | collective-permute-start | bytes 208904 | tf_op jit(solution)/shard_map/ppermute | solution.py:228
  41.6 9.8 %collective-permute-start.3 = (bf16[16,2176]{1,0:T(8,128)(2,1)S(1)}, bf16[16,2176]{1,0:T(8,128)(2,1)S(1)}, u32[]{:S(2)}, u32[]{:S(2)}) collective-permute-start(bf16[16,2176]{1,0:T(8,128)(2,1)S(1)} %pad_maximum_fusion), channel_id=1, source_target_pairs={{0,64},{32,96},{64,0},{96,32},{1,65},{33,97},{65,1},{97,33},{2,66}... | collective-permute-start | bytes 208904 | tf_op jit(solution)/shard_map/ppermute | solution.py:228
  46.4 8.6 %collective-permute-start.4 = (bf16[16,2176]{1,0:T(8,128)(2,1)S(1)}, bf16[16,2176]{1,0:T(8,128)(2,1)S(1)}, u32[]{:S(2)}, u32[]{:S(2)}) collective-permute-start(bf16[16,2176]{1,0:T(8,128)(2,1)S(1)} %pad_maximum_fusion), channel_id=1, source_target_pairs={{0,96},{32,0},{64,32},{96,64},{1,97},{33,1},{65,33},{97,65},{2,98}... | collective-permute-start | bytes 208904 | tf_op jit(solution)/shard_map/ppermute | solution.py:228
  55.0 0.7 copy-start.5
  90.2 7.9 %collective-permute-start = (bf16[16,256,128]{2,1,0:T(8,128)(2,1)S(1)}, bf16[16,256,128]{2,1,0:T(8,128)(2,1)S(1)}, u32[]{:S(2)}, u32[]{:S(2)}) collective-permute-start(bf16[16,256,128]{2,1,0:T(8,128)(2,1)S(1)} %bitcast.11), channel_id=1, source_target_pairs={{0,1},{1,0},{2,3},{3,2},{4,5},{5,4},{6,7},{7,6},{8,9},{9,8},{10,11... | collective-permute-start | bytes 3145736 | tf_op jit(solution)/shard_map/ppermute | solution.py:237
  98.1 1.6 %copy-start = (bf16[512,2176]{1,0:T(8,128)(2,1)S(1)}, bf16[512,2176]{1,0:T(8,128)(2,1)}, u32[]{:S(2)}) copy-start(bf16[512,2176]{1,0:T(8,128)(2,1)} %all-gather.2.cloned.1.call-done.gathered) | copy-start | bytes 6684676
Sparse Core Ops, SparseCore 0:
  55.8 41.0 all-gather.1

commit v7 on v6

--- a/solution.py
+++ b/solution.py
@@ -20,7 +20,6 @@
 AXES = (("x", 4), ("yh", 4), ("yl", 2), ("z", 8), ("c", 2))
 TOWER = ("x", "yh")
 RANK = ("yl", "z", "c")
-CHUNKS = 8
 
 
 def tower_kernel(order, arrived, weights, biases, compress, gain, out):
@@ -154,20 +153,17 @@
     )(core, own, other, rows)
 
 
-def lay_out_kernel(pooled, sent, held, sem):
-    width = held.shape[2] // CHUNKS
+def lay_out_kernel(pooled, sent, sem):
     copies = [
         pltpu.make_async_copy(
-            pooled.at[:, :, pl.ds(k * width, width)], held.at[:, :, pl.ds(k * width, width)], sem.at[k]
+            pooled.at[:, :, pl.ds(rank * 512, 512)], sent.at[rank], sem.at[rank]
         )
-        for k in range(CHUNKS)
+        for rank in range(32)
     ]
     for copy in copies:
         copy.start()
-    for k, copy in enumerate(copies):
+    for copy in copies:
         copy.wait()
-        for rank in range(k * width // 512, (k + 1) * width // 512):
-            sent[rank] = held[:, :, rank * 512 : (rank + 1) * 512]
 
 
 def lay_out(pooled):
@@ -176,10 +172,7 @@
         out_shape=jax.ShapeDtypeStruct((32, 2, 16, 512), jnp.bfloat16),
         in_specs=[pl.BlockSpec(memory_space=pl.ANY)],
         out_specs=pl.BlockSpec(memory_space=pltpu.VMEM),
-        scratch_shapes=[
-            pltpu.VMEM(pooled.shape, pooled.dtype),
-            pltpu.SemaphoreType.DMA((CHUNKS,)),
-        ],
+        scratch_shapes=[pltpu.SemaphoreType.DMA((32,))],
         cost_estimate=pl.CostEstimate(flops=0, bytes_accessed=4 * 2**20, transcendentals=0),
     )(pooled)
 
@@ -221,9 +214,10 @@
     mlp_bias,
     out_weight,
 ):
-    arrived = exchange(lay_out(pooled), RANK)
     rows = join(mlp_weight, mlp_bias, out_weight)
     rows = jnp.concatenate([rows, lax.ppermute(rows, "yl", [(0, 1), (1, 0)])], axis=0)
+    sent, rows = lax.optimization_barrier((lay_out(pooled), rows))
+    arrived = exchange(sent, RANK)
     rows = [rows] + [
         lax.ppermute(rows, "yh", [(i, (i + k) % 4) for i in range(4)]) for k in range(1, 4)
     ]
@@ -233,7 +227,7 @@
     )
     column = exchange(towers, "yh").reshape(4, 256, CD)
     features = exchange(jnp.broadcast_to(column[None], (4, 4, 256, CD)), "x")
-    features = features.reshape(TOWERS, 256, CD)
+    features, rows = lax.optimization_barrier((features.reshape(TOWERS, 256, CD), rows))
     other = lax.ppermute(features, "c", [(0, 1), (1, 0)])
     own = interact_own(features)
     core = lax.axis_index("c").reshape(1).astype(jnp.int32)

time: 125 us -> 142 us (1.14)
  waiting for transfers between devices: 12.6 us -> 32.8 us
  local copies, waits for them, and re-layouts: 4.04 us -> 0.89 us
  blocking collectives: 43.6 us -> 41.3 us
    all_to_all x1, waiting for transfers between devices: 0.01 us -> 31.5 us  [exchange(): return lax.all_to_all(x, axes, split_axis=0, concat_axis=0, tiled=True)]
    ppermute x1, waiting for transfers between devices: 9.03 us -> 0.01 us  [on_device(): lax.ppermute(rows, 'yl', [(0, 1), (1, 0)])]
    ppermute x1, starting transfers between devices: 5.19 us -> 2.04 us  [on_device(): other = lax.ppermute(features, 'c', [(0, 1), (1, 0)])]
    unnamed x19 -> x13, local copies, waits for them, and re-layouts: 3.16 us -> 0.03 us
    all_to_all x3, blocking collectives: 43.6 us -> 41.3 us  [exchange(): return lax.all_to_all(x, axes, split_axis=0, concat_axis=0, tiled=True)]
    ppermute x3, waiting for transfers between devices: 3.55 us -> 1.33 us  [on_device(): lax.ppermute(rows, 'yh', [(i, (i + k) % 4) for i in range(4)])]
    all_to_all x1, starting transfers between devices: 13 us -> 14.5 us  [exchange(): return lax.all_to_all(x, axes, split_axis=0, concat_axis=0, tiled=True)]
  transfers between devices with their start and end apart: 7 -> 7, of which waited for: 2 -> 2; matrix products, arithmetic and copies ran while one was open for 1% -> 0% of each run, Pallas kernels for 6% -> 6%
where the time goes in v7:
time: 142 us; the launch traced here: 140 us
  blocking collectives  41.3 us (29%)
  starting transfers between devices  34.7 us (24%)
  waiting for transfers between devices  32.8 us (23%)
  Pallas kernels  15.3 us (11%)
  between operations  13.6 us (10%)
  other arithmetic  1.52 us (1%)
    all_to_all x3, blocking collectives, exchange(): return lax.all_to_all(x, axes, split_axis=0, concat_axis=0, tiled=True)  41.3 us
    all_to_all x1, waiting for transfers between devices, exchange(): return lax.all_to_all(x, axes, split_axis=0, concat_axis=0, tiled=True)  31.5 us
    all_to_all x1, starting transfers between devices, exchange(): return lax.all_to_all(x, axes, split_axis=0, concat_axis=0, tiled=True)  14.5 us
    ppermute x3, starting transfers between devices, on_device(): lax.ppermute(rows, 'yh', [(i, (i + k) % 4) for i in range(4)])  14 us
    pallas_call x1, Pallas kernels, score(): pl.pallas_call(score_kernel, out_shape=jax.ShapeDtypeStruct((8, 8, 128),...  5.84 us
    ppermute x1, starting transfers between devices, on_device(): lax.ppermute(rows, 'yl', [(0, 1), (1, 0)])  4.17 us
  transfers between devices with their start and end apart: 7, of which 2 were waited for; matrix products, arithmetic and copies ran while one was open for 0% of the time, Pallas kernels for 6%

profile of v7, /device:TPU:1, one launch (start us, length us, event | category | flops | bytes accessed | tf_op | source)
XLA Modules:
  0.0 140.2 jit_solution(11731830702261583414)
XLA Ops:
  6.5 0.0 all-gather.2.cloned.1.call-start
  6.5 1.5 %shard_map.92 = bf16[8,2176]{1,0:T(8,128)(2,1)} custom-call(bf16[8,2048]{1,0:T(8,128)(2,1)} %weight.1, bf16[1,8]{1,0:T(2,128)(2,1)} %bitcast.17, bf16[1,8]{1,0:T(2,128)(2,1)} %bitcast.18), custom_call_target="tpu_custom_call" | custom-call | tf_op jit(solution)/shard_map/pallas_call | solution.py:194
  8.0 0.0 copy-start.5
  8.0 0.0 copy-start.1
  8.0 0.0 copy-start.2
  8.0 0.0 copy-start.3
  8.0 0.0 copy-start.4
  8.0 4.2 %collective-permute-start = (bf16[8,2176]{1,0:T(8,128)(2,1)}, bf16[8,2176]{1,0:T(8,128)(2,1)S(1)}, u32[]{:S(2)}, u32[]{:S(2)}) collective-permute-start(bf16[8,2176]{1,0:T(8,128)(2,1)} %shard_map.92), channel_id=1, source_target_pairs={{0,16},{16,0},{1,17},{17,1},{2,18},{18,2},{3,19},{19,3},{4,20},{20... | collective-permute-start | bytes 104456 | tf_op jit(solution)/shard_map/ppermute | solution.py:218
  12.2 2.5 %shard_map.91 = bf16[32,2,16,512]{3,2,1,0:T(8,128)(2,1)} custom-call(bf16[2,16,16384]{2,1,0:T(8,128)(2,1)} %pooled.1), custom_call_target="tpu_custom_call" | custom-call | bytes 4194304 | tf_op jit(solution)/shard_map/pallas_call | solution.py:170
  14.7 0.0 collective-permute-done
  14.7 0.8 pad_maximum_fusion.1
  15.5 4.2 %collective-permute-start.1 = (bf16[16,2176]{1,0:T(8,128)(2,1)S(1)}, bf16[16,2176]{1,0:T(8,128)(2,1)S(1)}, u32[]{:S(2)}, u32[]{:S(2)}) collective-permute-start(bf16[16,2176]{1,0:T(8,128)(2,1)S(1)} %pad_maximum_fusion.1), channel_id=1, source_target_pairs={{0,32},{32,64},{64,96},{96,0},{1,33},{33,65},{65,97},{97,1},{2,34}... | collective-permute-start | bytes 208904 | tf_op jit(solution)/shard_map/ppermute | solution.py:222
  19.7 4.8 %collective-permute-start.2 = (bf16[16,2176]{1,0:T(8,128)(2,1)S(1)}, bf16[16,2176]{1,0:T(8,128)(2,1)S(1)}, u32[]{:S(2)}, u32[]{:S(2)}) collective-permute-start(bf16[16,2176]{1,0:T(8,128)(2,1)S(1)} %pad_maximum_fusion.1), channel_id=1, source_target_pairs={{0,64},{32,96},{64,0},{96,32},{1,65},{33,97},{65,1},{97,33},{2,66}... | collective-permute-start | bytes 208904 | tf_op jit(solution)/shard_map/ppermute | solution.py:222
  24.5 5.0 %collective-permute-start.3 = (bf16[16,2176]{1,0:T(8,128)(2,1)S(1)}, bf16[16,2176]{1,0:T(8,128)(2,1)S(1)}, u32[]{:S(2)}, u32[]{:S(2)}) collective-permute-start(bf16[16,2176]{1,0:T(8,128)(2,1)S(1)} %pad_maximum_fusion.1), channel_id=1, source_target_pairs={{0,96},{32,0},{64,32},{96,64},{1,97},{33,1},{65,33},{97,65},{2,98}... | collective-permute-start | bytes 208904 | tf_op jit(solution)/shard_map/ppermute | solution.py:222
  29.5 0.0 collective-permute-done.1
  29.5 0.0 collective-permute-done.2
  29.5 1.3 collective-permute-done.3
  30.9 0.7 pad_maximum_fusion
  31.6 0.0 all-gather.2.cloned.1.call-update
  31.6 14.5 %all-to-all-start = ((bf16[32,2,16,512]{3,2,1,0:T(8,128)(2,1)}), bf16[32,2,16,512]{3,2,1,0:T(8,128)(2,1)S(1)}, u32[]{:S(2)}, u32[]{:S(2)}) async-start(bf16[32,2,16,512]{3,2,1,0:T(8,128)(2,1)} %shard_map.91), calls=%async_computation | async-start | bytes 2097152 | tf_op jit(solution)/shard_map/all_to_all | solution.py:203
  46.1 0.0 copy-done.5
  46.2 31.5 %all-to-all-done.arrived = bf16[32,2,16,512]{3,2,1,0:T(8,128)(2,1)S(1)} async-done(((bf16[32,2,16,512]{3,2,1,0:T(8,128)(2,1)}), bf16[32,2,16,512]{3,2,1,0:T(8,128)(2,1)S(1)}, u32[]{:S(2)}, u32[]{:S(2)}) %all-to-all-start) | async-done | bytes 1048608 | tf_op jit(solution)/shard_map/all_to_all | solution.py:203
  77.6 0.0 copy-done.1
  77.6 0.0 copy-done.2
  77.6 0.0 copy-done.3
  77.6 0.0 copy-done.4
  77.6 2.8 %shard_map.93 = bf16[4,4,2,32,128]{4,3,2,1,0:T(8,128)(2,1)S(1)} custom-call(s32[1,4]{1,0:T(1,128)S(1)} %copy-done.3, bf16[32,2,16,512]{3,2,1,0:T(8,128)(2,1)S(1)} %all-to-all-done.arrived, bf16[3,512,512]{2,1,0:T(8,128)(2,1)S(1)} %bitcast.14, f32[3,512]{1,0:T(4,128)S(1)} %bitcast.13, bf16[128,512]{1,0:T(8,128)(2,1)S(1)} %bitcast.15, f32[1,128]{1,0:T(1,128)S(1)} %copy-done.4), custom_call_target="tpu_custom_call" | custom-call | flops 1744830464 | bytes 4194304 | tf_op jit(solution)/shard_map/pallas_call | solution.py:58
  80.5 16.3 %all_to_all.20 = bf16[4,4,2,32,128]{4,3,2,1,0:T(8,128)(2,1)S(1)} all-to-all(bf16[4,4,2,32,128]{4,3,2,1,0:T(8,128)(2,1)S(1)} %shard_map.93), channel_id=1, replica_groups=mesh['x'=4,'yh'=4,'yl'=2,'z'=8,'c'=2] {'yh'}, dimensions={0} | all-to-all | bytes 524288 | tf_op jit(solution)/shard_map/all_to_all | solution.py:203
  96.7 0.2 broadcast_in_dim.16
  96.9 17.3 %all_to_all.21 = bf16[4,4,256,128]{3,2,1,0:T(8,128)(2,1)S(1)} all-to-all(bf16[4,4,256,128]{3,2,1,0:T(8,128)(2,1)S(1)} %broadcast_in_dim.16), channel_id=1, replica_groups=mesh['x'=4,'yh'=4,'yl'=2,'z'=8,'c'=2] {'x'}, dimensions={0} | all-to-all | bytes 2097152 | tf_op jit(solution)/shard_map/all_to_all | solution.py:203
  114.2 0.0 all-gather.2.cloned.1.call-done.gathered
  114.2 0.0 copy-start
  114.2 2.0 %collective-permute-start.4 = (bf16[16,256,128]{2,1,0:T(8,128)(2,1)S(1)}, bf16[16,256,128]{2,1,0:T(8,128)(2,1)}, u32[]{:S(2)}, u32[]{:S(2)}) collective-permute-start(bf16[16,256,128]{2,1,0:T(8,128)(2,1)S(1)} %bitcast.11), channel_id=1, source_target_pairs={{0,1},{1,0},{2,3},{3,2},{4,5},{5,4},{6,7},{7,6},{8,9},{9,8},{10,11... | collective-permute-start | bytes 3145736 | tf_op jit(solution)/shard_map/ppermute | solution.py:231
  116.3 2.7 %shard_map.94.own = bf16[256,2048]{1,0:T(8,128)(2,1)S(1)} custom-call(bf16[16,256,128]{2,1,0:T(8,128)(2,1)S(1)} %bitcast.12), custom_call_target="tpu_custom_call" | custom-call | flops 1000000000 | bytes 2097152 | tf_op jit(solution)/shard_map/pallas_call | solution.py:99
  119.0 0.0 collective-permute-done.4.other
  119.0 0.0 copy-done
  119.0 5.8 %shard_map.95 = f32[8,8,128]{2,1,0:T(8,128)S(1)} custom-call(s32[1]{0:T(128)} %bitcast.core, bf16[256,2048]{1,0:T(8,128)(2,1)S(1)} %shard_map.94.own, bf16[16,256,128]{2,1,0:T(8,128)(2,1)} %collective-permute-done.4.other, bf16[512,2176]{1,0:T(8,128)(2,1)S(1)} %copy-done), custom_call_target="tpu_custom_call" | custom-call | flops 2000000000 | bytes 6291456 | tf_op jit(solution)/shard_map/pallas_call | solution.py:139
  124.9 7.8 %all_to_all.22 = f32[8,8,128]{2,1,0:T(8,128)S(1)} all-to-all(f32[8,8,128]{2,1,0:T(8,128)S(1)} %shard_map.95), channel_id=1, replica_groups=mesh['x'=4,'yh'=4,'yl'=2,'z'=8,'c'=2] {'c','x'}, dimensions={0} | all-to-all | bytes 65536 | tf_op jit(solution)/shard_map/all_to_all | solution.py:203
  132.7 0.6 reshape_squeeze.3
  (3 shorter events, 0.0 us)
Async XLA Ops:
  6.5 107.7 %all-gather.2.cloned.1.call-start = ((), (), s32[]{:S(2)}) async-start(), calls=%async_computation.4 | async-start | bytes 2506752 | tf_op jit(solution)/shard_map/all_gather | solution.py:224
  8.0 38.1 %copy-start.5 = (f32[1,3,512]{2,0,1:T(1,128)S(1)}, f32[1,3,512]{2,0,1:T(1,128)}, u32[]{:S(2)}) copy-start(f32[1,3,512]{2,0,1:T(1,128)} %param.12) | copy-start | bytes 18436
  8.0 69.6 %copy-start.1 = (bf16[1,3,512,512]{3,2,1,0:T(8,128)(2,1)S(1)}, bf16[1,3,512,512]{3,2,1,0:T(8,128)(2,1)}, u32[]{:S(2)}) copy-start(bf16[1,3,512,512]{3,2,1,0:T(8,128)(2,1)} %param.11) | copy-start | bytes 4718596
  8.0 69.6 %copy-start.2 = (bf16[1,128,512]{2,1,0:T(8,128)(2,1)S(1)}, bf16[1,128,512]{2,1,0:T(8,128)(2,1)}, u32[]{:S(2)}) copy-start(bf16[1,128,512]{2,1,0:T(8,128)(2,1)} %param.13) | copy-start | bytes 393220
  8.0 69.6 %copy-start.3 = (s32[1,4]{1,0:T(1,128)S(1)}, s32[1,4]{1,0:T(1,128)}, u32[]{:S(2)}) copy-start(s32[1,4]{1,0:T(1,128)} %order.1) | copy-start | bytes 52
  8.0 69.6 %copy-start.4 = (f32[1,128]{1,0:T(1,128)S(1)}, f32[1,128]{1,0:T(1,128)}, u32[]{:S(2)}) copy-start(f32[1,128]{1,0:T(1,128)} %gain.1) | copy-start | bytes 1540
  8.0 6.7 %collective-permute-start = (bf16[8,2176]{1,0:T(8,128)(2,1)}, bf16[8,2176]{1,0:T(8,128)(2,1)S(1)}, u32[]{:S(2)}, u32[]{:S(2)}) collective-permute-start(bf16[8,2176]{1,0:T(8,128)(2,1)} %shard_map.92), channel_id=1, source_target_pairs={{0,16},{16,0},{1,17},{17,1},{2,18},{18,2},{3,19},{19,3},{4,20},{20... | collective-permute-start | bytes 104456 | tf_op jit(solution)/shard_map/ppermute | solution.py:218
  15.5 14.1 %collective-permute-start.1 = (bf16[16,2176]{1,0:T(8,128)(2,1)S(1)}, bf16[16,2176]{1,0:T(8,128)(2,1)S(1)}, u32[]{:S(2)}, u32[]{:S(2)}) collective-permute-start(bf16[16,2176]{1,0:T(8,128)(2,1)S(1)} %pad_maximum_fusion.1), channel_id=1, source_target_pairs={{0,32},{32,64},{64,96},{96,0},{1,33},{33,65},{65,97},{97,1},{2,34}... | collective-permute-start | bytes 208904 | tf_op jit(solution)/shard_map/ppermute | solution.py:222
  19.7 9.8 %collective-permute-start.2 = (bf16[16,2176]{1,0:T(8,128)(2,1)S(1)}, bf16[16,2176]{1,0:T(8,128)(2,1)S(1)}, u32[]{:S(2)}, u32[]{:S(2)}) collective-permute-start(bf16[16,2176]{1,0:T(8,128)(2,1)S(1)} %pad_maximum_fusion.1), channel_id=1, source_target_pairs={{0,64},{32,96},{64,0},{96,32},{1,65},{33,97},{65,1},{97,33},{2,66}... | collective-permute-start | bytes 208904 | tf_op jit(solution)/shard_map/ppermute | solution.py:222
  24.5 6.3 %collective-permute-start.3 = (bf16[16,2176]{1,0:T(8,128)(2,1)S(1)}, bf16[16,2176]{1,0:T(8,128)(2,1)S(1)}, u32[]{:S(2)}, u32[]{:S(2)}) collective-permute-start(bf16[16,2176]{1,0:T(8,128)(2,1)S(1)} %pad_maximum_fusion.1), channel_id=1, source_target_pairs={{0,96},{32,0},{64,32},{96,64},{1,97},{33,1},{65,33},{97,65},{2,98}... | collective-permute-start | bytes 208904 | tf_op jit(solution)/shard_map/ppermute | solution.py:222
  31.6 46.0 %all-to-all-start = ((bf16[32,2,16,512]{3,2,1,0:T(8,128)(2,1)}), bf16[32,2,16,512]{3,2,1,0:T(8,128)(2,1)S(1)}, u32[]{:S(2)}, u32[]{:S(2)}) async-start(bf16[32,2,16,512]{3,2,1,0:T(8,128)(2,1)} %shard_map.91), calls=%async_computation | async-start | bytes 2097152 | tf_op jit(solution)/shard_map/all_to_all | solution.py:203
  114.2 4.8 %copy-start = (bf16[512,2176]{1,0:T(8,128)(2,1)S(1)}, bf16[512,2176]{1,0:T(8,128)(2,1)}, u32[]{:S(2)}) copy-start(bf16[512,2176]{1,0:T(8,128)(2,1)} %all-gather.2.cloned.1.call-done.gathered) | copy-start | bytes 6684676
  114.2 4.8 %collective-permute-start.4 = (bf16[16,256,128]{2,1,0:T(8,128)(2,1)S(1)}, bf16[16,256,128]{2,1,0:T(8,128)(2,1)}, u32[]{:S(2)}, u32[]{:S(2)}) collective-permute-start(bf16[16,256,128]{2,1,0:T(8,128)(2,1)S(1)} %bitcast.11), channel_id=1, source_target_pairs={{0,1},{1,0},{2,3},{3,2},{4,5},{5,4},{6,7},{7,6},{8,9},{9,8},{10,11... | collective-permute-start | bytes 3145736 | tf_op jit(solution)/shard_map/ppermute | solution.py:231
Sparse Core Ops, SparseCore 0:
  31.8 63.9 all-gather.1

commit v8 on v7

--- a/solution.py
+++ b/solution.py
@@ -146,7 +146,7 @@
             pltpu.VMEM((2, 256, WIDE), jnp.bfloat16),
             pltpu.SemaphoreType.DMA((2,)),
         ],
-        compiler_params=pltpu.CompilerParams(vmem_limit_bytes=32 * 2**20),
+        compiler_params=pltpu.CompilerParams(vmem_limit_bytes=50 * 2**20),
         cost_estimate=pl.CostEstimate(
             flops=2 * 10**9, bytes_accessed=6 * 2**20, transcendentals=0
         ),
@@ -227,7 +227,7 @@
     )
     column = exchange(towers, "yh").reshape(4, 256, CD)
     features = exchange(jnp.broadcast_to(column[None], (4, 4, 256, CD)), "x")
-    features, rows = lax.optimization_barrier((features.reshape(TOWERS, 256, CD), rows))
+    features = features.reshape(TOWERS, 256, CD)
     other = lax.ppermute(features, "c", [(0, 1), (1, 0)])
     own = interact_own(features)
     core = lax.axis_index("c").reshape(1).astype(jnp.int32)

time: 142 us -> 120 us (0.85)
  waiting for transfers between devices: 32.8 us -> 13.9 us
  starting transfers between devices: 34.7 us -> 33.1 us
  Pallas kernels: 15.3 us -> 13.8 us
    all_to_all x1, waiting for transfers between devices: 31.5 us -> 4.73 us  [exchange(): return lax.all_to_all(x, axes, split_axis=0, concat_axis=0, tiled=True)]
    ppermute x3, waiting for transfers between devices: 1.33 us -> 9.16 us  [on_device(): lax.ppermute(rows, 'yh', [(i, (i + k) % 4) for i in range(4)])]
    all_to_all x1, starting transfers between devices: 14.5 us -> 12.5 us  [exchange(): return lax.all_to_all(x, axes, split_axis=0, concat_axis=0, tiled=True)]
    ppermute x1, starting transfers between devices: 2.04 us -> 3.61 us  [on_device(): other = lax.ppermute(features, 'c', [(0, 1), (1, 0)])]
    pallas_call x1, Pallas kernels: 5.84 us -> 4.32 us  [score(): pl.pallas_call(score_kernel, out_shape=jax.ShapeDtypeStruct((8, 8, 128),...]
  transfers between devices with their start and end apart: 7 -> 7, of which waited for: 2 -> 3; matrix products, arithmetic and copies ran while one was open for 0% -> 1% of each run, Pallas kernels for 6% -> 7%
where the time goes in v8:
time: 120 us; the launch traced here: 119 us
  blocking collectives  42.4 us (35%)
  starting transfers between devices  33.1 us (28%)
  waiting for transfers between devices  13.9 us (12%)
  Pallas kernels  13.8 us (12%)
  between operations  13.6 us (11%)
  other arithmetic  1.52 us (1%)
    all_to_all x3, blocking collectives, exchange(): return lax.all_to_all(x, axes, split_axis=0, concat_axis=0, tiled=True)  42.4 us
    ppermute x3, starting transfers between devices, on_device(): lax.ppermute(rows, 'yh', [(i, (i + k) % 4) for i in range(4)])  12.7 us
    all_to_all x1, starting transfers between devices, exchange(): return lax.all_to_all(x, axes, split_axis=0, concat_axis=0, tiled=True)  12.5 us
    ppermute x3, waiting for transfers between devices, on_device(): lax.ppermute(rows, 'yh', [(i, (i + k) % 4) for i in range(4)])  9.16 us
    all_to_all x1, waiting for transfers between devices, exchange(): return lax.all_to_all(x, axes, split_axis=0, concat_axis=0, tiled=True)  4.73 us
    pallas_call x1, Pallas kernels, score(): pl.pallas_call(score_kernel, out_shape=jax.ShapeDtypeStruct((8, 8, 128),...  4.32 us
    ppermute x1, starting transfers between devices, on_device(): lax.ppermute(rows, 'yl', [(0, 1), (1, 0)])  4.17 us
    ppermute x1, starting transfers between devices, on_device(): other = lax.ppermute(features, 'c', [(0, 1), (1, 0)])  3.61 us
  transfers between devices with their start and end apart: 7, of which 3 were waited for; matrix products, arithmetic and copies ran while one was open for 1% of the time, Pallas kernels for 7%

profile of v8, /device:TPU:1, one launch (start us, length us, event | category | flops | bytes accessed | tf_op | source)
XLA Modules:
  0.0 119.1 jit_solution(16585069449785303591)
XLA Ops:
  6.5 1.5 %shard_map.92 = bf16[8,2176]{1,0:T(8,128)(2,1)} custom-call(bf16[8,2048]{1,0:T(8,128)(2,1)} %weight.1, bf16[1,8]{1,0:T(2,128)(2,1)} %bitcast.17, bf16[1,8]{1,0:T(2,128)(2,1)} %bitcast.18), custom_call_target="tpu_custom_call" | custom-call | tf_op jit(solution)/shard_map/pallas_call | solution.py:194
  8.0 0.0 copy-start.4
  8.0 0.0 copy-start
  8.0 0.0 copy-start.1
  8.0 0.0 copy-start.2
  8.0 0.0 copy-start.3
  8.0 4.2 %collective-permute-start = (bf16[8,2176]{1,0:T(8,128)(2,1)}, bf16[8,2176]{1,0:T(8,128)(2,1)S(1)}, u32[]{:S(2)}, u32[]{:S(2)}) collective-permute-start(bf16[8,2176]{1,0:T(8,128)(2,1)} %shard_map.92), channel_id=1, source_target_pairs={{0,16},{16,0},{1,17},{17,1},{2,18},{18,2},{3,19},{19,3},{4,20},{20... | collective-permute-start | bytes 104456 | tf_op jit(solution)/shard_map/ppermute | solution.py:218
  12.2 2.5 %shard_map.91 = bf16[32,2,16,512]{3,2,1,0:T(8,128)(2,1)} custom-call(bf16[2,16,16384]{2,1,0:T(8,128)(2,1)} %pooled.1), custom_call_target="tpu_custom_call" | custom-call | bytes 4194304 | tf_op jit(solution)/shard_map/pallas_call | solution.py:170
  14.7 0.0 collective-permute-done
  14.7 0.8 pad_maximum_fusion.1
  15.4 12.5 %all-to-all-start = ((bf16[32,2,16,512]{3,2,1,0:T(8,128)(2,1)}), bf16[32,2,16,512]{3,2,1,0:T(8,128)(2,1)S(1)}, u32[]{:S(2)}, u32[]{:S(2)}) async-start(bf16[32,2,16,512]{3,2,1,0:T(8,128)(2,1)} %shard_map.91), calls=%async_computation | async-start | bytes 2097152 | tf_op jit(solution)/shard_map/all_to_all | solution.py:203
  28.0 0.0 all-gather.2.cloned.1.call-start
  28.0 5.0 %collective-permute-start.4 = (bf16[16,2176]{1,0:T(8,128)(2,1)S(1)}, bf16[16,2176]{1,0:T(8,128)(2,1)S(1)}, u32[]{:S(2)}, u32[]{:S(2)}) collective-permute-start(bf16[16,2176]{1,0:T(8,128)(2,1)S(1)} %pad_maximum_fusion.1), channel_id=1, source_target_pairs={{0,96},{32,0},{64,32},{96,64},{1,97},{33,1},{65,33},{97,65},{2,98}... | collective-permute-start | bytes 208904 | tf_op jit(solution)/shard_map/ppermute | solution.py:222
  33.0 4.4 %collective-permute-start.3 = (bf16[16,2176]{1,0:T(8,128)(2,1)S(1)}, bf16[16,2176]{1,0:T(8,128)(2,1)S(1)}, u32[]{:S(2)}, u32[]{:S(2)}) collective-permute-start(bf16[16,2176]{1,0:T(8,128)(2,1)S(1)} %pad_maximum_fusion.1), channel_id=1, source_target_pairs={{0,64},{32,96},{64,0},{96,32},{1,65},{33,97},{65,1},{97,33},{2,66}... | collective-permute-start | bytes 208904 | tf_op jit(solution)/shard_map/ppermute | solution.py:222
  37.4 3.3 %collective-permute-start.2 = (bf16[16,2176]{1,0:T(8,128)(2,1)S(1)}, bf16[16,2176]{1,0:T(8,128)(2,1)S(1)}, u32[]{:S(2)}, u32[]{:S(2)}) collective-permute-start(bf16[16,2176]{1,0:T(8,128)(2,1)S(1)} %pad_maximum_fusion.1), channel_id=1, source_target_pairs={{0,32},{32,64},{64,96},{96,0},{1,33},{33,65},{65,97},{97,1},{2,34}... | collective-permute-start | bytes 208904 | tf_op jit(solution)/shard_map/ppermute | solution.py:222
  40.8 0.0 collective-permute-done.4
  40.8 6.3 %collective-permute-done.3 = bf16[16,2176]{1,0:T(8,128)(2,1)S(1)} collective-permute-done((bf16[16,2176]{1,0:T(8,128)(2,1)S(1)}, bf16[16,2176]{1,0:T(8,128)(2,1)S(1)}, u32[]{:S(2)}, u32[]{:S(2)}) %collective-permute-start.3) | collective-permute-done | bytes 69664 | tf_op jit(solution)/shard_map/ppermute | solution.py:222
  47.1 2.8 %collective-permute-done.2 = bf16[16,2176]{1,0:T(8,128)(2,1)S(1)} collective-permute-done((bf16[16,2176]{1,0:T(8,128)(2,1)S(1)}, bf16[16,2176]{1,0:T(8,128)(2,1)S(1)}, u32[]{:S(2)}, u32[]{:S(2)}) %collective-permute-start.2) | collective-permute-done | bytes 69664 | tf_op jit(solution)/shard_map/ppermute | solution.py:222
  49.9 0.7 pad_maximum_fusion
  50.7 0.0 all-gather.2.cloned.1.call-update
  50.7 0.0 copy-done.4
  50.7 4.7 %all-to-all-done.arrived = bf16[32,2,16,512]{3,2,1,0:T(8,128)(2,1)S(1)} async-done(((bf16[32,2,16,512]{3,2,1,0:T(8,128)(2,1)}), bf16[32,2,16,512]{3,2,1,0:T(8,128)(2,1)S(1)}, u32[]{:S(2)}, u32[]{:S(2)}) %all-to-all-start) | async-done | bytes 1048608 | tf_op jit(solution)/shard_map/all_to_all | solution.py:203
  55.5 0.0 copy-done
  55.5 0.0 copy-done.1
  55.5 0.0 copy-done.2
  55.5 0.0 copy-done.3
  55.5 2.8 %shard_map.93 = bf16[4,4,2,32,128]{4,3,2,1,0:T(8,128)(2,1)S(1)} custom-call(s32[1,4]{1,0:T(1,128)S(1)} %copy-done.2, bf16[32,2,16,512]{3,2,1,0:T(8,128)(2,1)S(1)} %all-to-all-done.arrived, bf16[3,512,512]{2,1,0:T(8,128)(2,1)S(1)} %bitcast.14, f32[3,512]{1,0:T(4,128)S(1)} %bitcast.13, bf16[128,512]{1,0:T(8,128)(2,1)S(1)} %bitcast.15, f32[1,128]{1,0:T(1,128)S(1)} %copy-done.3), custom_call_target="tpu_custom_call" | custom-call | flops 1744830464 | bytes 4194304 | tf_op jit(solution)/shard_map/pallas_call | solution.py:58
  58.3 17.6 %all_to_all.20 = bf16[4,4,2,32,128]{4,3,2,1,0:T(8,128)(2,1)S(1)} all-to-all(bf16[4,4,2,32,128]{4,3,2,1,0:T(8,128)(2,1)S(1)} %shard_map.93), channel_id=1, replica_groups=mesh['x'=4,'yh'=4,'yl'=2,'z'=8,'c'=2] {'yh'}, dimensions={0} | all-to-all | bytes 524288 | tf_op jit(solution)/shard_map/all_to_all | solution.py:203
  75.9 0.2 broadcast_in_dim.16
  76.1 17.5 %all_to_all.21 = bf16[4,4,256,128]{3,2,1,0:T(8,128)(2,1)S(1)} all-to-all(bf16[4,4,256,128]{3,2,1,0:T(8,128)(2,1)S(1)} %broadcast_in_dim.16), channel_id=1, replica_groups=mesh['x'=4,'yh'=4,'yl'=2,'z'=8,'c'=2] {'x'}, dimensions={0} | all-to-all | bytes 2097152 | tf_op jit(solution)/shard_map/all_to_all | solution.py:203
  93.6 3.6 %collective-permute-start.1 = (bf16[16,256,128]{2,1,0:T(8,128)(2,1)S(1)}, bf16[16,256,128]{2,1,0:T(8,128)(2,1)S(1)}, u32[]{:S(2)}, u32[]{:S(2)}) collective-permute-start(bf16[16,256,128]{2,1,0:T(8,128)(2,1)S(1)} %bitcast.11), channel_id=1, source_target_pairs={{0,1},{1,0},{2,3},{3,2},{4,5},{5,4},{6,7},{7,6},{8,9},{9,8},{10,11... | collective-permute-start | bytes 3145736 | tf_op jit(solution)/shard_map/ppermute | solution.py:231
  97.2 2.7 %shard_map.94.own = bf16[256,2048]{1,0:T(8,128)(2,1)S(1)} custom-call(bf16[16,256,128]{2,1,0:T(8,128)(2,1)S(1)} %bitcast.12), custom_call_target="tpu_custom_call" | custom-call | flops 1000000000 | bytes 2097152 | tf_op jit(solution)/shard_map/pallas_call | solution.py:99
  99.9 0.0 all-gather.2.cloned.1.call-done.gathered
  100.0 0.0 collective-permute-done.1.other
  100.0 4.3 %shard_map.95 = f32[8,8,128]{2,1,0:T(8,128)S(1)} custom-call(s32[1]{0:T(128)} %bitcast.core, bf16[256,2048]{1,0:T(8,128)(2,1)S(1)} %shard_map.94.own, bf16[16,256,128]{2,1,0:T(8,128)(2,1)S(1)} %collective-permute-done.1.other, bf16[512,2176]{1,0:T(8,128)(2,1)} %all-gather.2.cloned.1.call-done.gathered), custom_call_target="tpu_custom_call" | custom-call | flops 2000000000 | bytes 6291456 | tf_op jit(solution)/shard_map/pallas_call | solution.py:139
  104.3 7.3 %all_to_all.22 = f32[8,8,128]{2,1,0:T(8,128)S(1)} all-to-all(f32[8,8,128]{2,1,0:T(8,128)S(1)} %shard_map.95), channel_id=1, replica_groups=mesh['x'=4,'yh'=4,'yl'=2,'z'=8,'c'=2] {'c','x'}, dimensions={0} | all-to-all | bytes 65536 | tf_op jit(solution)/shard_map/all_to_all | solution.py:203
  111.6 0.6 reshape_squeeze.3
  (3 shorter events, 0.0 us)
Async XLA Ops:
  8.0 42.7 %copy-start.4 = (f32[1,3,512]{2,0,1:T(1,128)S(1)}, f32[1,3,512]{2,0,1:T(1,128)}, u32[]{:S(2)}) copy-start(f32[1,3,512]{2,0,1:T(1,128)} %param.12) | copy-start | bytes 18436
  8.0 47.5 %copy-start = (bf16[1,3,512,512]{3,2,1,0:T(8,128)(2,1)S(1)}, bf16[1,3,512,512]{3,2,1,0:T(8,128)(2,1)}, u32[]{:S(2)}) copy-start(bf16[1,3,512,512]{3,2,1,0:T(8,128)(2,1)} %param.11) | copy-start | bytes 4718596
  8.0 47.5 %copy-start.1 = (bf16[1,128,512]{2,1,0:T(8,128)(2,1)S(1)}, bf16[1,128,512]{2,1,0:T(8,128)(2,1)}, u32[]{:S(2)}) copy-start(bf16[1,128,512]{2,1,0:T(8,128)(2,1)} %param.13) | copy-start | bytes 393220
  8.0 47.5 %copy-start.2 = (s32[1,4]{1,0:T(1,128)S(1)}, s32[1,4]{1,0:T(1,128)}, u32[]{:S(2)}) copy-start(s32[1,4]{1,0:T(1,128)} %order.1) | copy-start | bytes 52
  8.0 47.5 %copy-start.3 = (f32[1,128]{1,0:T(1,128)S(1)}, f32[1,128]{1,0:T(1,128)}, u32[]{:S(2)}) copy-start(f32[1,128]{1,0:T(1,128)} %gain.1) | copy-start | bytes 1540
  8.0 6.6 %collective-permute-start = (bf16[8,2176]{1,0:T(8,128)(2,1)}, bf16[8,2176]{1,0:T(8,128)(2,1)S(1)}, u32[]{:S(2)}, u32[]{:S(2)}) collective-permute-start(bf16[8,2176]{1,0:T(8,128)(2,1)} %shard_map.92), channel_id=1, source_target_pairs={{0,16},{16,0},{1,17},{17,1},{2,18},{18,2},{3,19},{19,3},{4,20},{20... | collective-permute-start | bytes 104456 | tf_op jit(solution)/shard_map/ppermute | solution.py:218
  15.4 40.0 %all-to-all-start = ((bf16[32,2,16,512]{3,2,1,0:T(8,128)(2,1)}), bf16[32,2,16,512]{3,2,1,0:T(8,128)(2,1)S(1)}, u32[]{:S(2)}, u32[]{:S(2)}) async-start(bf16[32,2,16,512]{3,2,1,0:T(8,128)(2,1)} %shard_map.91), calls=%async_computation | async-start | bytes 2097152 | tf_op jit(solution)/shard_map/all_to_all | solution.py:203
  28.0 72.0 %all-gather.2.cloned.1.call-start = ((), (), s32[]{:S(2)}) async-start(), calls=%async_computation.4 | async-start | bytes 2506752 | tf_op jit(solution)/shard_map/all_gather | solution.py:224
  28.0 12.8 %collective-permute-start.4 = (bf16[16,2176]{1,0:T(8,128)(2,1)S(1)}, bf16[16,2176]{1,0:T(8,128)(2,1)S(1)}, u32[]{:S(2)}, u32[]{:S(2)}) collective-permute-start(bf16[16,2176]{1,0:T(8,128)(2,1)S(1)} %pad_maximum_fusion.1), channel_id=1, source_target_pairs={{0,96},{32,0},{64,32},{96,64},{1,97},{33,1},{65,33},{97,65},{2,98}... | collective-permute-start | bytes 208904 | tf_op jit(solution)/shard_map/ppermute | solution.py:222
  33.0 14.1 %collective-permute-start.3 = (bf16[16,2176]{1,0:T(8,128)(2,1)S(1)}, bf16[16,2176]{1,0:T(8,128)(2,1)S(1)}, u32[]{:S(2)}, u32[]{:S(2)}) collective-permute-start(bf16[16,2176]{1,0:T(8,128)(2,1)S(1)} %pad_maximum_fusion.1), channel_id=1, source_target_pairs={{0,64},{32,96},{64,0},{96,32},{1,65},{33,97},{65,1},{97,33},{2,66}... | collective-permute-start | bytes 208904 | tf_op jit(solution)/shard_map/ppermute | solution.py:222
  37.4 12.5 %collective-permute-start.2 = (bf16[16,2176]{1,0:T(8,128)(2,1)S(1)}, bf16[16,2176]{1,0:T(8,128)(2,1)S(1)}, u32[]{:S(2)}, u32[]{:S(2)}) collective-permute-start(bf16[16,2176]{1,0:T(8,128)(2,1)S(1)} %pad_maximum_fusion.1), channel_id=1, source_target_pairs={{0,32},{32,64},{64,96},{96,0},{1,33},{33,65},{65,97},{97,1},{2,34}... | collective-permute-start | bytes 208904 | tf_op jit(solution)/shard_map/ppermute | solution.py:222
  93.6 6.4 %collective-permute-start.1 = (bf16[16,256,128]{2,1,0:T(8,128)(2,1)S(1)}, bf16[16,256,128]{2,1,0:T(8,128)(2,1)S(1)}, u32[]{:S(2)}, u32[]{:S(2)}) collective-permute-start(bf16[16,256,128]{2,1,0:T(8,128)(2,1)S(1)} %bitcast.11), channel_id=1, source_target_pairs={{0,1},{1,0},{2,3},{3,2},{4,5},{5,4},{6,7},{7,6},{8,9},{9,8},{10,11... | collective-permute-start | bytes 3145736 | tf_op jit(solution)/shard_map/ppermute | solution.py:231
Sparse Core Ops, SparseCore 0:
  50.8 39.0 all-gather.1

commit v9 on v6

--- a/solution.py
+++ b/solution.py
@@ -68,31 +68,32 @@
     )(order, arrived, weights, biases, compress, gain)
 
 
-def interact(features, mixed, first_row):
+def interact(features, mixed):
     side = TOWERS * GROUP
     row = lax.broadcasted_iota(jnp.int32, (side, side), 0)
     col = lax.broadcasted_iota(jnp.int32, (side, side), 1)
     scale = jnp.where(row % GROUP == col % GROUP, jnp.float32(1.0 / CD), jnp.float32(0.0))
     eye = jnp.where(row == col, jnp.float32(1.0), jnp.float32(0.0))
 
-    def group(step, carry):
-        at = pl.multiple_of(step * GROUP, GROUP)
-        values = features[:, pl.ds(at, GROUP), :].reshape(side, CD)
-        gram = lax.dot_general(
-            values, values, (((1,), (1,)), ((), ())), preferred_element_type=jnp.float32
-        )
-        factor = (gram * scale + eye).astype(jnp.bfloat16)
-        result = jnp.dot(factor, values, preferred_element_type=jnp.float32).astype(jnp.bfloat16)
-        to = pl.ds(pl.multiple_of(first_row + step * GROUP, GROUP), GROUP)
-        for t in range(TOWERS):
-            mixed[to, t * CD : (t + 1) * CD] = result[t * GROUP : (t + 1) * GROUP]
-        return carry
-
-    lax.fori_loop(0, features.shape[1] // GROUP, group, 0, unroll=4)
+    for start in range(0, features.shape[1], 4 * GROUP):
+        places = [start + k * GROUP for k in range(4)]
+        values = [features[:, at : at + GROUP, :].reshape(side, CD) for at in places]
+        grams = [
+            lax.dot_general(v, v, (((1,), (1,)), ((), ())), preferred_element_type=jnp.float32)
+            for v in values
+        ]
+        factors = [(gram * scale + eye).astype(jnp.bfloat16) for gram in grams]
+        results = [
+            jnp.dot(factor, v, preferred_element_type=jnp.float32).astype(jnp.bfloat16)
+            for factor, v in zip(factors, values)
+        ]
+        for at, result in zip(places, results):
+            for t in range(TOWERS):
+                mixed[at : at + GROUP, t * CD : (t + 1) * CD] = result[t * GROUP : (t + 1) * GROUP]
 
 
 def interact_kernel(features, mixed):
-    interact(features, mixed, 0)
+    interact(features, mixed)
 
 
 def interact_own(features):
@@ -114,7 +115,7 @@
     ]
     for copy in copies:
         copy.start()
-    interact(other, mixed, 0)
+    interact(other, mixed)
     totals = [jnp.zeros((1, 256), jnp.float32), jnp.zeros((1, 256), jnp.float32)]
     for k, copy in enumerate(copies):
         copy.wait()
@@ -147,38 +148,51 @@
             pltpu.VMEM((2, 256, WIDE), jnp.bfloat16),
             pltpu.SemaphoreType.DMA((2,)),
         ],
-        compiler_params=pltpu.CompilerParams(vmem_limit_bytes=32 * 2**20),
+        compiler_params=pltpu.CompilerParams(vmem_limit_bytes=50 * 2**20),
         cost_estimate=pl.CostEstimate(
             flops=2 * 10**9, bytes_accessed=6 * 2**20, transcendentals=0
         ),
     )(core, own, other, rows)
 
 
-def lay_out_kernel(pooled, sent, held, sem):
+def lay_out_kernel(pooled, sent, held, sem_in, sem_out):
     width = held.shape[2] // CHUNKS
-    copies = [
+    into = [
         pltpu.make_async_copy(
-            pooled.at[:, :, pl.ds(k * width, width)], held.at[:, :, pl.ds(k * width, width)], sem.at[k]
+            pooled.at[:, :, pl.ds(k * width, width)],
+            held.at[:, :, pl.ds(k * width, width)],
+            sem_in.at[k],
         )
         for k in range(CHUNKS)
     ]
-    for copy in copies:
+    out_of = [
+        pltpu.make_async_copy(
+            held.at[:, :, pl.ds(rank * 512, 512)], sent.at[rank], sem_out.at[rank]
+        )
+        for rank in range(32)
+    ]
+    for copy in into:
         copy.start()
-    for k, copy in enumerate(copies):
+    each = 32 // CHUNKS
+    for k, copy in enumerate(into):
         copy.wait()
-        for rank in range(k * width // 512, (k + 1) * width // 512):
-            sent[rank] = held[:, :, rank * 512 : (rank + 1) * 512]
+        for leaving in out_of[k * each : (k + 1) * each]:
+            leaving.start()
+    for copy in out_of:
+        copy.wait()
 
 
 def lay_out(pooled):
+    anywhere = pl.BlockSpec(memory_space=pl.ANY)
     return pl.pallas_call(
         lay_out_kernel,
         out_shape=jax.ShapeDtypeStruct((32, 2, 16, 512), jnp.bfloat16),
-        in_specs=[pl.BlockSpec(memory_space=pl.ANY)],
-        out_specs=pl.BlockSpec(memory_space=pltpu.VMEM),
+        in_specs=[anywhere],
+        out_specs=anywhere,
         scratch_shapes=[
             pltpu.VMEM(pooled.shape, pooled.dtype),
             pltpu.SemaphoreType.DMA((CHUNKS,)),
+            pltpu.SemaphoreType.DMA((32,)),
         ],
         cost_estimate=pl.CostEstimate(flops=0, bytes_accessed=4 * 2**20, transcendentals=0),
     )(pooled)
@@ -204,6 +218,23 @@
         in_specs=[vmem] * 3,
         out_specs=vmem,
     )(mlp_weight, mlp_bias[None], out_weight[None])
+
+
+def stack_kernel(*refs):
+    for k, part in enumerate(refs[:-1]):
+        refs[-1][k] = part[...]
+
+
+def stack(*parts):
+    vmem = pl.BlockSpec(memory_space=pltpu.VMEM)
+    depth, width = parts[0].shape
+    return pl.pallas_call(
+        stack_kernel,
+        out_shape=jax.ShapeDtypeStruct((len(parts), depth, width), parts[0].dtype),
+        in_specs=[vmem] * len(parts),
+        out_specs=vmem,
+        cost_estimate=pl.CostEstimate(flops=0, bytes_accessed=0, transcendentals=0),
+    )(*parts).reshape(len(parts) * depth, width)
 
 
 def exchange(x, axes):
@@ -223,11 +254,11 @@
 ):
     arrived = exchange(lay_out(pooled), RANK)
     rows = join(mlp_weight, mlp_bias, out_weight)
-    rows = jnp.concatenate([rows, lax.ppermute(rows, "yl", [(0, 1), (1, 0)])], axis=0)
-    rows = [rows] + [
-        lax.ppermute(rows, "yh", [(i, (i + k) % 4) for i in range(4)]) for k in range(1, 4)
-    ]
-    rows = lax.all_gather(jnp.concatenate(rows, axis=0), "z", axis=0, tiled=True)
+    rows = stack(
+        rows, *[lax.ppermute(rows, "yh", [(i, (i + k) % 4) for i in range(4)]) for k in (1, 2, 3)]
+    )
+    rows = stack(rows, lax.ppermute(rows, "yl", [(0, 1), (1, 0)]))
+    rows = lax.all_gather(rows, "z", axis=0, tiled=True)
     towers = tower_block(
         feature_order, arrived, cross_weight[0], cross_bias[0], compress_weight[0], norm_gain
     )

time: 125 us -> 118 us (0.944)
  blocking collectives: 43.6 us -> 38.9 us
  waiting for transfers between devices: 12.6 us -> 10.3 us
  local copies, waits for them, and re-layouts: 4.04 us -> 2.74 us
    ppermute x1, waiting for transfers between devices: 9.03 us -> 4.09 us  [on_device(): rows = stack(rows, lax.ppermute(rows, 'yl', [(0, 1), (1, 0)]))]
    all_to_all x3, blocking collectives: 43.6 us -> 38.9 us  [exchange(): return lax.all_to_all(x, axes, split_axis=0, concat_axis=0, tiled=True)]
    pallas_call x0 -> x2, Pallas kernels: none -> 3.16 us  [stack(): pl.pallas_call(stack_kernel, out_shape=jax.ShapeDtypeStruct((len(parts),...]
    all_gather x1, waiting for transfers between devices: 0.02 us -> 2.21 us  [on_device(): rows = lax.all_gather(rows, 'z', axis=0, tiled=True)]
    ppermute x1, starting transfers between devices: 5.19 us -> 7.35 us  [on_device(): other = lax.ppermute(features, 'c', [(0, 1), (1, 0)])]
    pallas_call x1, Pallas kernels: 2.71 us -> 1.26 us  [interact_own(): pl.pallas_call(interact_kernel, out_shape=jax.ShapeDtypeStruct((features....]
    unnamed x19, local copies, waits for them, and re-layouts: 3.16 us -> 1.87 us
  transfers between devices with their start and end apart: 7 -> 7, of which waited for: 2 -> 4; matrix products, arithmetic and copies ran while one was open for 1% -> 0% of each run, Pallas kernels for 6% -> 7%
where the time goes in v9:
time: 118 us; the launch traced here: 117 us
  blocking collectives  38.9 us (33%)
  starting transfers between devices  36.7 us (31%)
  Pallas kernels  15 us (13%)
  between operations  13.6 us (12%)
  waiting for transfers between devices  10.3 us (9%)
  local copies, waits for them, and re-layouts  2.74 us (2%)
    all_to_all x3, blocking collectives, exchange(): return lax.all_to_all(x, axes, split_axis=0, concat_axis=0, tiled=True)  38.9 us
    ppermute x3, starting transfers between devices, on_device(): lax.ppermute(rows, 'yh', [(i, (i + k) % 4) for i in range(4)])  13.9 us
    all_to_all x1, starting transfers between devices, exchange(): return lax.all_to_all(x, axes, split_axis=0, concat_axis=0, tiled=True)  13 us
    ppermute x1, starting transfers between devices, on_device(): other = lax.ppermute(features, 'c', [(0, 1), (1, 0)])  7.35 us
    ppermute x1, waiting for transfers between devices, on_device(): rows = stack(rows, lax.ppermute(rows, 'yl', [(0, 1), (1, 0)]))  4.09 us
    ppermute x3, waiting for transfers between devices, on_device(): lax.ppermute(rows, 'yh', [(i, (i + k) % 4) for i in range(4)])  3.96 us
    pallas_call x1, Pallas kernels, score(): pl.pallas_call(score_kernel, out_shape=jax.ShapeDtypeStruct((8, 8, 128),...  3.88 us
    pallas_call x2, Pallas kernels, stack(): pl.pallas_call(stack_kernel, out_shape=jax.ShapeDtypeStruct((len(parts),...  3.16 us
  transfers between devices with their start and end apart: 7, of which 4 were waited for; matrix products, arithmetic and copies ran while one was open for 0% of the time, Pallas kernels for 7%

profile of v9, /device:TPU:1, one launch (start us, length us, event | category | flops | bytes accessed | tf_op | source)
XLA Modules:
  0.0 117.3 jit_solution(8982619110199592128)
XLA Ops:
  6.5 0.0 copy-start.8
  6.5 0.0 copy-start.2
  6.5 0.0 copy-start
  6.5 0.0 copy-start.1
  6.5 0.0 copy-start.3
  6.5 2.4 %shard_map.91 = bf16[32,2,16,512]{3,2,1,0:T(8,128)(2,1)} custom-call(bf16[2,16,16384]{2,1,0:T(8,128)(2,1)} %pooled.1), custom_call_target="tpu_custom_call" | custom-call | bytes 4194304 | tf_op jit(solution)/shard_map/pallas_call | solution.py:187
  9.0 13.0 %all-to-all-start = ((bf16[32,2,16,512]{3,2,1,0:T(8,128)(2,1)}), bf16[32,2,16,512]{3,2,1,0:T(8,128)(2,1)S(1)}, u32[]{:S(2)}, u32[]{:S(2)}) async-start(bf16[32,2,16,512]{3,2,1,0:T(8,128)(2,1)} %shard_map.91), calls=%async_computation | async-start | bytes 2097152 | tf_op jit(solution)/shard_map/all_to_all | solution.py:241
  22.0 0.0 all-gather.2.cloned.1.call-start
  22.0 1.5 %shard_map.94.refs_0_ = bf16[8,2176]{1,0:T(8,128)(2,1)} custom-call(bf16[8,2048]{1,0:T(8,128)(2,1)} %weight.1, bf16[1,8]{1,0:T(2,128)(2,1)} %bitcast.22, bf16[1,8]{1,0:T(2,128)(2,1)} %bitcast.23), custom_call_target="tpu_custom_call" | custom-call | tf_op jit(solution)/shard_map/pallas_call | solution.py:215
  23.5 4.2 %collective-permute-start.1 = (bf16[8,2176]{1,0:T(8,128)(2,1)}, bf16[8,2176]{1,0:T(8,128)(2,1)S(1)}, u32[]{:S(2)}, u32[]{:S(2)}) collective-permute-start(bf16[8,2176]{1,0:T(8,128)(2,1)} %shard_map.94.refs_0_), channel_id=1, source_target_pairs={{0,32},{32,64},{64,96},{96,0},{1,33},{33,65},{65,97},{97,1},{2,34}... | collective-permute-start | bytes 104456 | tf_op jit(solution)/shard_map/ppermute | solution.py:258
  27.7 4.8 %collective-permute-start.2 = (bf16[8,2176]{1,0:T(8,128)(2,1)}, bf16[8,2176]{1,0:T(8,128)(2,1)S(1)}, u32[]{:S(2)}, u32[]{:S(2)}) collective-permute-start(bf16[8,2176]{1,0:T(8,128)(2,1)} %shard_map.94.refs_0_), channel_id=1, source_target_pairs={{0,64},{32,96},{64,0},{96,32},{1,65},{33,97},{65,1},{97,33},{2,66}... | collective-permute-start | bytes 104456 | tf_op jit(solution)/shard_map/ppermute | solution.py:258
  32.5 5.0 %collective-permute-start.3 = (bf16[8,2176]{1,0:T(8,128)(2,1)}, bf16[8,2176]{1,0:T(8,128)(2,1)S(1)}, u32[]{:S(2)}, u32[]{:S(2)}) collective-permute-start(bf16[8,2176]{1,0:T(8,128)(2,1)} %shard_map.94.refs_0_), channel_id=1, source_target_pairs={{0,96},{32,0},{64,32},{96,64},{1,97},{33,1},{65,33},{97,65},{2,98}... | collective-permute-start | bytes 104456 | tf_op jit(solution)/shard_map/ppermute | solution.py:258
  37.5 1.4 %collective-permute-done.1.refs_1_ = bf16[8,2176]{1,0:T(8,128)(2,1)S(1)} collective-permute-done((bf16[8,2176]{1,0:T(8,128)(2,1)}, bf16[8,2176]{1,0:T(8,128)(2,1)S(1)}, u32[]{:S(2)}, u32[]{:S(2)}) %collective-permute-start.1) | collective-permute-done | bytes 34848 | tf_op jit(solution)/shard_map/ppermute | solution.py:258
  38.9 0.0 copy-start.5
  38.9 2.6 %collective-permute-done.2.refs_2_ = bf16[8,2176]{1,0:T(8,128)(2,1)S(1)} collective-permute-done((bf16[8,2176]{1,0:T(8,128)(2,1)}, bf16[8,2176]{1,0:T(8,128)(2,1)S(1)}, u32[]{:S(2)}, u32[]{:S(2)}) %collective-permute-start.2) | collective-permute-done | bytes 34848 | tf_op jit(solution)/shard_map/ppermute | solution.py:258
  41.4 0.0 copy-start.6
  41.4 0.0 collective-permute-done.3.refs_3_
  41.4 0.0 copy-done.5
  41.4 0.6 copy-done.6
  42.0 0.0 copy-start.7
  42.0 0.6 copy-done.7
  42.6 1.5 %shard_map.95 = bf16[4,8,2176]{2,1,0:T(8,128)(2,1)} custom-call(bf16[8,2176]{1,0:T(8,128)(2,1)} %shard_map.94.refs_0_, bf16[8,2176]{1,0:T(8,128)(2,1)} %copy-done.5, bf16[8,2176]{1,0:T(8,128)(2,1)} %copy-done.6, bf16[8,2176]{1,0:T(8,128)(2,1)} %copy-done.7), custom_call_target="tpu_custom_call" | custom-call | tf_op jit(solution)/shard_map/pallas_call | solution.py:231
  44.1 2.4 %collective-permute-start.4 = (bf16[32,2176]{1,0:T(8,128)(2,1)}, bf16[32,2176]{1,0:T(8,128)(2,1)S(1)}, u32[]{:S(2)}, u32[]{:S(2)}) collective-permute-start(bf16[32,2176]{1,0:T(8,128)(2,1)} %bitcast.20), channel_id=1, source_target_pairs={{0,16},{16,0},{1,17},{17,1},{2,18},{18,2},{3,19},{19,3},{4,20},{20... | collective-permute-start | bytes 417800 | tf_op jit(solution)/shard_map/ppermute | solution.py:260
  46.5 4.1 %collective-permute-done.4.refs_1_ = bf16[32,2176]{1,0:T(8,128)(2,1)S(1)} collective-permute-done((bf16[32,2176]{1,0:T(8,128)(2,1)}, bf16[32,2176]{1,0:T(8,128)(2,1)S(1)}, u32[]{:S(2)}, u32[]{:S(2)}) %collective-permute-start.4) | collective-permute-done | bytes 139296 | tf_op jit(solution)/shard_map/ppermute | solution.py:260
  50.6 0.0 copy-start.4
  50.6 0.6 copy-done.4
  51.3 1.7 %shard_map.96 = bf16[2,32,2176]{2,1,0:T(8,128)(2,1)} custom-call(bf16[32,2176]{1,0:T(8,128)(2,1)} %bitcast.21, bf16[32,2176]{1,0:T(8,128)(2,1)} %copy-done.4), custom_call_target="tpu_custom_call" | custom-call | tf_op jit(solution)/shard_map/pallas_call | solution.py:231
  52.9 0.0 all-gather.2.cloned.1.call-update
  53.0 0.0 copy-done.8
  53.0 0.0 all-to-all-done.arrived
  53.0 0.0 copy-done.2
  53.0 0.0 copy-done
  53.0 0.0 copy-done.1
  53.0 0.0 copy-done.3
  53.0 2.8 %shard_map.92 = bf16[4,4,2,32,128]{4,3,2,1,0:T(8,128)(2,1)S(1)} custom-call(s32[1,4]{1,0:T(1,128)S(1)} %copy-done.2, bf16[32,2,16,512]{3,2,1,0:T(8,128)(2,1)S(1)} %all-to-all-done.arrived, bf16[3,512,512]{2,1,0:T(8,128)(2,1)S(1)} %bitcast.16, f32[3,512]{1,0:T(4,128)S(1)} %bitcast.15, bf16[128,512]{1,0:T(8,128)(2,1)S(1)} %bitcast.17, f32[1,128]{1,0:T(1,128)S(1)} %copy-done.3), custom_call_target="tpu_custom_call" | custom-call | flops 1744830464 | bytes 4194304 | tf_op jit(solution)/shard_map/pallas_call | solution.py:59
  55.9 10.9 %all_to_all.20 = bf16[4,4,2,32,128]{4,3,2,1,0:T(8,128)(2,1)S(1)} all-to-all(bf16[4,4,2,32,128]{4,3,2,1,0:T(8,128)(2,1)S(1)} %shard_map.92), channel_id=1, replica_groups=mesh['x'=4,'yh'=4,'yl'=2,'z'=8,'c'=2] {'yh'}, dimensions={0} | all-to-all | bytes 524288 | tf_op jit(solution)/shard_map/all_to_all | solution.py:241
  66.8 0.2 broadcast_in_dim.14
  67.0 14.4 %all_to_all.21 = bf16[4,4,256,128]{3,2,1,0:T(8,128)(2,1)S(1)} all-to-all(bf16[4,4,256,128]{3,2,1,0:T(8,128)(2,1)S(1)} %broadcast_in_dim.14), channel_id=1, replica_groups=mesh['x'=4,'yh'=4,'yl'=2,'z'=8,'c'=2] {'x'}, dimensions={0} | all-to-all | bytes 2097152 | tf_op jit(solution)/shard_map/all_to_all | solution.py:241
  81.4 7.3 %collective-permute-start = (bf16[16,256,128]{2,1,0:T(8,128)(2,1)S(1)}, bf16[16,256,128]{2,1,0:T(8,128)(2,1)S(1)}, u32[]{:S(2)}, u32[]{:S(2)}) collective-permute-start(bf16[16,256,128]{2,1,0:T(8,128)(2,1)S(1)} %bitcast.13), channel_id=1, source_target_pairs={{0,1},{1,0},{2,3},{3,2},{4,5},{5,4},{6,7},{7,6},{8,9},{9,8},{10,11... | collective-permute-start | bytes 3145736 | tf_op jit(solution)/shard_map/ppermute | solution.py:268
  88.8 1.3 %shard_map.93.own = bf16[256,2048]{1,0:T(8,128)(2,1)S(1)} custom-call(bf16[16,256,128]{2,1,0:T(8,128)(2,1)S(1)} %bitcast.14), custom_call_target="tpu_custom_call" | custom-call | flops 1000000000 | bytes 2097152 | tf_op jit(solution)/shard_map/pallas_call | solution.py:101
  90.1 2.2 %all-gather.2.cloned.1.call-done.gathered = bf16[512,2176]{1,0:T(8,128)(2,1)} async-done(((bf16[64,2176]{1,0:T(8,128)(2,1)}), bf16[512,2176]{1,0:T(8,128)(2,1)}) %all-gather.2.cloned.1.call-update) | async-done | bytes 2228240 | tf_op jit(solution)/shard_map/all_gather | solution.py:261
  92.3 0.0 collective-permute-done.other
  92.3 3.9 %shard_map.97 = f32[8,8,128]{2,1,0:T(8,128)S(1)} custom-call(s32[1]{0:T(128)} %bitcast.core, bf16[256,2048]{1,0:T(8,128)(2,1)S(1)} %shard_map.93.own, bf16[16,256,128]{2,1,0:T(8,128)(2,1)S(1)} %collective-permute-done.other, bf16[512,2176]{1,0:T(8,128)(2,1)} %all-gather.2.cloned.1.call-done.gathered), custom_call_target="tpu_custom_call" | custom-call | flops 2000000000 | bytes 6291456 | tf_op jit(solution)/shard_map/pallas_call | solution.py:141
  96.2 13.6 %all_to_all.22 = f32[8,8,128]{2,1,0:T(8,128)S(1)} all-to-all(f32[8,8,128]{2,1,0:T(8,128)S(1)} %shard_map.97), channel_id=1, replica_groups=mesh['x'=4,'yh'=4,'yl'=2,'z'=8,'c'=2] {'c','x'}, dimensions={0} | all-to-all | bytes 65536 | tf_op jit(solution)/shard_map/all_to_all | solution.py:241
  109.8 0.6 reshape_squeeze.3
  (3 shorter events, 0.0 us)
Async XLA Ops:
  6.5 46.4 %copy-start.8 = (f32[1,3,512]{2,0,1:T(1,128)S(1)}, f32[1,3,512]{2,0,1:T(1,128)}, u32[]{:S(2)}) copy-start(f32[1,3,512]{2,0,1:T(1,128)} %param.12) | copy-start | bytes 18436
  6.5 46.5 %copy-start.2 = (s32[1,4]{1,0:T(1,128)S(1)}, s32[1,4]{1,0:T(1,128)}, u32[]{:S(2)}) copy-start(s32[1,4]{1,0:T(1,128)} %order.1) | copy-start | bytes 52
  6.5 46.5 %copy-start = (bf16[1,3,512,512]{3,2,1,0:T(8,128)(2,1)S(1)}, bf16[1,3,512,512]{3,2,1,0:T(8,128)(2,1)}, u32[]{:S(2)}) copy-start(bf16[1,3,512,512]{3,2,1,0:T(8,128)(2,1)} %param.11) | copy-start | bytes 4718596
  6.5 46.5 %copy-start.1 = (bf16[1,128,512]{2,1,0:T(8,128)(2,1)S(1)}, bf16[1,128,512]{2,1,0:T(8,128)(2,1)}, u32[]{:S(2)}) copy-start(bf16[1,128,512]{2,1,0:T(8,128)(2,1)} %param.13) | copy-start | bytes 393220
  6.5 46.5 %copy-start.3 = (f32[1,128]{1,0:T(1,128)S(1)}, f32[1,128]{1,0:T(1,128)}, u32[]{:S(2)}) copy-start(f32[1,128]{1,0:T(1,128)} %gain.1) | copy-start | bytes 1540
  9.0 44.0 %all-to-all-start = ((bf16[32,2,16,512]{3,2,1,0:T(8,128)(2,1)}), bf16[32,2,16,512]{3,2,1,0:T(8,128)(2,1)S(1)}, u32[]{:S(2)}, u32[]{:S(2)}) async-start(bf16[32,2,16,512]{3,2,1,0:T(8,128)(2,1)} %shard_map.91), calls=%async_computation | async-start | bytes 2097152 | tf_op jit(solution)/shard_map/all_to_all | solution.py:241
  22.0 70.3 %all-gather.2.cloned.1.call-start = ((), (), s32[]{:S(2)}) async-start(), calls=%async_computation.4 | async-start | bytes 2506752 | tf_op jit(solution)/shard_map/all_gather | solution.py:261
  23.5 15.4 %collective-permute-start.1 = (bf16[8,2176]{1,0:T(8,128)(2,1)}, bf16[8,2176]{1,0:T(8,128)(2,1)S(1)}, u32[]{:S(2)}, u32[]{:S(2)}) collective-permute-start(bf16[8,2176]{1,0:T(8,128)(2,1)} %shard_map.94.refs_0_), channel_id=1, source_target_pairs={{0,32},{32,64},{64,96},{96,0},{1,33},{33,65},{65,97},{97,1},{2,34}... | collective-permute-start | bytes 104456 | tf_op jit(solution)/shard_map/ppermute | solution.py:258
  27.7 13.7 %collective-permute-start.2 = (bf16[8,2176]{1,0:T(8,128)(2,1)}, bf16[8,2176]{1,0:T(8,128)(2,1)S(1)}, u32[]{:S(2)}, u32[]{:S(2)}) collective-permute-start(bf16[8,2176]{1,0:T(8,128)(2,1)} %shard_map.94.refs_0_), channel_id=1, source_target_pairs={{0,64},{32,96},{64,0},{96,32},{1,65},{33,97},{65,1},{97,33},{2,66}... | collective-permute-start | bytes 104456 | tf_op jit(solution)/shard_map/ppermute | solution.py:258
  32.5 8.9 %collective-permute-start.3 = (bf16[8,2176]{1,0:T(8,128)(2,1)}, bf16[8,2176]{1,0:T(8,128)(2,1)S(1)}, u32[]{:S(2)}, u32[]{:S(2)}) collective-permute-start(bf16[8,2176]{1,0:T(8,128)(2,1)} %shard_map.94.refs_0_), channel_id=1, source_target_pairs={{0,96},{32,0},{64,32},{96,64},{1,97},{33,1},{65,33},{97,65},{2,98}... | collective-permute-start | bytes 104456 | tf_op jit(solution)/shard_map/ppermute | solution.py:258
  38.9 2.6 %copy-start.5 = (bf16[8,2176]{1,0:T(8,128)(2,1)}, bf16[8,2176]{1,0:T(8,128)(2,1)S(1)}, u32[]{:S(2)}) copy-start(bf16[8,2176]{1,0:T(8,128)(2,1)S(1)} %collective-permute-done.1.refs_1_) | copy-start | bytes 104452
  41.4 0.6 copy-start.6
  42.0 0.6 copy-start.7
  44.1 6.5 %collective-permute-start.4 = (bf16[32,2176]{1,0:T(8,128)(2,1)}, bf16[32,2176]{1,0:T(8,128)(2,1)S(1)}, u32[]{:S(2)}, u32[]{:S(2)}) collective-permute-start(bf16[32,2176]{1,0:T(8,128)(2,1)} %bitcast.20), channel_id=1, source_target_pairs={{0,16},{16,0},{1,17},{17,1},{2,18},{18,2},{3,19},{19,3},{4,20},{20... | collective-permute-start | bytes 417800 | tf_op jit(solution)/shard_map/ppermute | solution.py:260
  50.6 0.6 copy-start.4
  81.4 10.8 %collective-permute-start = (bf16[16,256,128]{2,1,0:T(8,128)(2,1)S(1)}, bf16[16,256,128]{2,1,0:T(8,128)(2,1)S(1)}, u32[]{:S(2)}, u32[]{:S(2)}) collective-permute-start(bf16[16,256,128]{2,1,0:T(8,128)(2,1)S(1)} %bitcast.13), channel_id=1, source_target_pairs={{0,1},{1,0},{2,3},{3,2},{4,5},{5,4},{6,7},{7,6},{8,9},{9,8},{10,11... | collective-permute-start | bytes 3145736 | tf_op jit(solution)/shard_map/ppermute | solution.py:268
Sparse Core Ops, SparseCore 0:
  53.1 39.1 all-gather.1

commit v10 on v9

--- a/solution.py
+++ b/solution.py
@@ -155,7 +155,7 @@
     )(core, own, other, rows)
 
 
-def lay_out_kernel(pooled, sent, held, sem_in, sem_out):
+def prepare_kernel(pooled, weight, bias, out_weight, sent, rows, held, sem_in, sem_out):
     width = held.shape[2] // CHUNKS
     into = [
         pltpu.make_async_copy(
@@ -173,6 +173,15 @@
     ]
     for copy in into:
         copy.start()
+    eye = lax.broadcasted_iota(jnp.int32, (8, 8), 0) == lax.broadcasted_iota(jnp.int32, (8, 8), 1)
+    lane = lax.broadcasted_iota(jnp.int32, (8, 128), 1)
+
+    def column(row):
+        return jnp.sum(jnp.where(eye, row[...].astype(jnp.float32), 0.0), axis=1, keepdims=True)
+
+    extra = jnp.where(lane == 0, column(bias), jnp.where(lane == 1, column(out_weight), 0.0))
+    rows[:, : TOWERS * CD] = weight[...]
+    rows[:, TOWERS * CD :] = extra.astype(jnp.bfloat16)
     each = 32 // CHUNKS
     for k, copy in enumerate(into):
         copy.wait()
@@ -182,42 +191,24 @@
         copy.wait()
 
 
-def lay_out(pooled):
+def prepare(pooled, mlp_weight, mlp_bias, out_weight):
+    vmem = pl.BlockSpec(memory_space=pltpu.VMEM)
     anywhere = pl.BlockSpec(memory_space=pl.ANY)
     return pl.pallas_call(
-        lay_out_kernel,
-        out_shape=jax.ShapeDtypeStruct((32, 2, 16, 512), jnp.bfloat16),
-        in_specs=[anywhere],
-        out_specs=anywhere,
+        prepare_kernel,
+        out_shape=(
+            jax.ShapeDtypeStruct((32, 2, 16, 512), jnp.bfloat16),
+            jax.ShapeDtypeStruct((8, WIDE), jnp.bfloat16),
+        ),
+        in_specs=[anywhere] + [vmem] * 3,
+        out_specs=(anywhere, vmem),
         scratch_shapes=[
             pltpu.VMEM(pooled.shape, pooled.dtype),
             pltpu.SemaphoreType.DMA((CHUNKS,)),
             pltpu.SemaphoreType.DMA((32,)),
         ],
         cost_estimate=pl.CostEstimate(flops=0, bytes_accessed=4 * 2**20, transcendentals=0),
-    )(pooled)
-
-
-def join_kernel(weight, bias, out_weight, rows):
-    eye = lax.broadcasted_iota(jnp.int32, (8, 8), 0) == lax.broadcasted_iota(jnp.int32, (8, 8), 1)
-    lane = lax.broadcasted_iota(jnp.int32, (8, 128), 1)
-
-    def column(row):
-        return jnp.sum(jnp.where(eye, row[...].astype(jnp.float32), 0.0), axis=1, keepdims=True)
-
-    extra = jnp.where(lane == 0, column(bias), jnp.where(lane == 1, column(out_weight), 0.0))
-    rows[:, : TOWERS * CD] = weight[...]
-    rows[:, TOWERS * CD :] = extra.astype(jnp.bfloat16)
-
-
-def join(mlp_weight, mlp_bias, out_weight):
-    vmem = pl.BlockSpec(memory_space=pltpu.VMEM)
-    return pl.pallas_call(
-        join_kernel,
-        out_shape=jax.ShapeDtypeStruct((8, WIDE), jnp.bfloat16),
-        in_specs=[vmem] * 3,
-        out_specs=vmem,
-    )(mlp_weight, mlp_bias[None], out_weight[None])
+    )(pooled, mlp_weight, mlp_bias[None], out_weight[None])
 
 
 def stack_kernel(*refs):
@@ -252,12 +243,12 @@
     mlp_bias,
     out_weight,
 ):
-    arrived = exchange(lay_out(pooled), RANK)
-    rows = join(mlp_weight, mlp_bias, out_weight)
+    sent, rows = prepare(pooled, mlp_weight, mlp_bias, out_weight)
+    arrived = exchange(sent, RANK)
     rows = stack(
         rows, *[lax.ppermute(rows, "yh", [(i, (i + k) % 4) for i in range(4)]) for k in (1, 2, 3)]
     )
-    rows = stack(rows, lax.ppermute(rows, "yl", [(0, 1), (1, 0)]))
+    rows = jnp.concatenate([rows, lax.ppermute(rows, "yl", [(0, 1), (1, 0)])], axis=0)
     rows = lax.all_gather(rows, "z", axis=0, tiled=True)
     towers = tower_block(
         feature_order, arrived, cross_weight[0], cross_bias[0], compress_weight[0], norm_gain

time: 118 us -> 119 us (level)
  blocking collectives: 38.9 us -> 41.3 us
  Pallas kernels: 15 us -> 13.3 us
  other arithmetic: 0.01 us -> 1.63 us
    all_to_all x3, blocking collectives: 38.9 us -> 41.3 us  [exchange(): return lax.all_to_all(x, axes, split_axis=0, concat_axis=0, tiled=True)]
    pallas_call x2 -> x1, Pallas kernels: 3.16 us -> 1.47 us  [stack(): pl.pallas_call(stack_kernel, out_shape=jax.ShapeDtypeStruct((len(parts),...]
    concatenate x0 -> x1, other arithmetic: none -> 1.62 us  [on_device(): jnp.concatenate([rows, lax.ppermute(rows, 'yl', [(0, 1), (1, 0)])], axis=0)]
    ppermute x1, waiting for transfers between devices: 4.09 us -> 2.84 us  [on_device(): lax.ppermute(rows, 'yl', [(0, 1), (1, 0)])]
    ppermute x3, waiting for transfers between devices: 3.96 us -> 5.17 us  [on_device(): lax.ppermute(rows, 'yh', [(i, (i + k) % 4) for i in range(4)])]
    pallas_call x2 -> x1, Pallas kernels: 3.9 us -> 3.83 us  [prepare(): pl.pallas_call(prepare_kernel, out_shape=(jax.ShapeDtypeStruct((32, 2, 16...]
  transfers between devices with their start and end apart: 7 -> 7, of which waited for: 4 -> 4; matrix products, arithmetic and copies ran while one was open for 0% -> 2% of each run, Pallas kernels for 7% -> 5%
where the time goes in v10:
time: 119 us; the launch traced here: 118 us
  blocking collectives  41.3 us (35%)
  starting transfers between devices  36.6 us (31%)
  between operations  13.6 us (11%)
  Pallas kernels  13.3 us (11%)
  waiting for transfers between devices  9.55 us (8%)
  local copies, waits for them, and re-layouts  2.09 us (2%)
  other arithmetic  1.63 us (1%)
    all_to_all x3, blocking collectives, exchange(): return lax.all_to_all(x, axes, split_axis=0, concat_axis=0, tiled=True)  41.3 us
    ppermute x3, starting transfers between devices, on_device(): lax.ppermute(rows, 'yh', [(i, (i + k) % 4) for i in range(4)])  13.9 us
    all_to_all x1, starting transfers between devices, exchange(): return lax.all_to_all(x, axes, split_axis=0, concat_axis=0, tiled=True)  13 us
    ppermute x1, starting transfers between devices, on_device(): other = lax.ppermute(features, 'c', [(0, 1), (1, 0)])  6.51 us
    ppermute x3, waiting for transfers between devices, on_device(): lax.ppermute(rows, 'yh', [(i, (i + k) % 4) for i in range(4)])  5.17 us
    pallas_call x1, Pallas kernels, score(): pl.pallas_call(score_kernel, out_shape=jax.ShapeDtypeStruct((8, 8, 128),...  3.88 us
    pallas_call x1, Pallas kernels, prepare(): pl.pallas_call(prepare_kernel, out_shape=(jax.ShapeDtypeStruct((32, 2, 16...  3.83 us
    ppermute x1, starting transfers between devices, on_device(): lax.ppermute(rows, 'yl', [(0, 1), (1, 0)])  3.15 us
  transfers between devices with their start and end apart: 7, of which 4 were waited for; matrix products, arithmetic and copies ran while one was open for 2% of the time, Pallas kernels for 5%

profile of v10, /device:TPU:1, one launch (start us, length us, event | category | flops | bytes accessed | tf_op | source)
XLA Modules:
  0.0 118.0 jit_solution(3498133533241289524)
XLA Ops:
  6.5 0.0 copy-start.7
  6.5 0.0 copy-start.2
  6.5 0.0 copy-start
  6.5 0.0 copy-start.1
  6.5 0.0 copy-start.3
  6.5 3.8 %shard_map.91 = (bf16[32,2,16,512]{3,2,1,0:T(8,128)(2,1)}, bf16[8,2176]{1,0:T(8,128)(2,1)}) custom-call(bf16[2,16,16384]{2,1,0:T(8,128)(2,1)} %pooled.1, bf16[8,2048]{1,0:T(8,128)(2,1)} %weight.1, bf16[1,8]{1,0:T(2,128)(2,1)} %bitcast.20, bf16[1,8]{1,0:T(2,128)(2,1)} %bitcast.21), custom_call_target="tpu_custom_call" | custom-call | bytes 4194304 | tf_op jit(solution)/shard_map/pallas_call | solution.py:197
  10.4 13.0 %all-to-all-start = ((bf16[32,2,16,512]{3,2,1,0:T(8,128)(2,1)}), bf16[32,2,16,512]{3,2,1,0:T(8,128)(2,1)S(1)}, u32[]{:S(2)}, u32[]{:S(2)}) async-start(bf16[32,2,16,512]{3,2,1,0:T(8,128)(2,1)} %get-tuple-element.7), calls=%async_computation | async-start | bytes 2097152 | tf_op jit(solution)/shard_map/all_to_all | solution.py:232
  23.4 0.0 all-gather.2.cloned.1.call-start
  23.4 4.2 %collective-permute-start.1 = (bf16[8,2176]{1,0:T(8,128)(2,1)}, bf16[8,2176]{1,0:T(8,128)(2,1)S(1)}, u32[]{:S(2)}, u32[]{:S(2)}) collective-permute-start(bf16[8,2176]{1,0:T(8,128)(2,1)} %get-tuple-element.8.refs_0_), channel_id=1, source_target_pairs={{0,32},{32,64},{64,96},{96,0},{1,33},{33,65},{65,97},{97,1},{2,34}... | collective-permute-start | bytes 104456 | tf_op jit(solution)/shard_map/ppermute | solution.py:249
  27.7 4.8 %collective-permute-start.2 = (bf16[8,2176]{1,0:T(8,128)(2,1)}, bf16[8,2176]{1,0:T(8,128)(2,1)S(1)}, u32[]{:S(2)}, u32[]{:S(2)}) collective-permute-start(bf16[8,2176]{1,0:T(8,128)(2,1)} %get-tuple-element.8.refs_0_), channel_id=1, source_target_pairs={{0,64},{32,96},{64,0},{96,32},{1,65},{33,97},{65,1},{97,33},{2,66}... | collective-permute-start | bytes 104456 | tf_op jit(solution)/shard_map/ppermute | solution.py:249
  32.4 5.0 %collective-permute-start.3 = (bf16[8,2176]{1,0:T(8,128)(2,1)}, bf16[8,2176]{1,0:T(8,128)(2,1)S(1)}, u32[]{:S(2)}, u32[]{:S(2)}) collective-permute-start(bf16[8,2176]{1,0:T(8,128)(2,1)} %get-tuple-element.8.refs_0_), channel_id=1, source_target_pairs={{0,96},{32,0},{64,32},{96,64},{1,97},{33,1},{65,33},{97,65},{2,98}... | collective-permute-start | bytes 104456 | tf_op jit(solution)/shard_map/ppermute | solution.py:249
  37.4 3.0 %collective-permute-done.1.refs_1_ = bf16[8,2176]{1,0:T(8,128)(2,1)S(1)} collective-permute-done((bf16[8,2176]{1,0:T(8,128)(2,1)}, bf16[8,2176]{1,0:T(8,128)(2,1)S(1)}, u32[]{:S(2)}, u32[]{:S(2)}) %collective-permute-start.1) | collective-permute-done | bytes 34848 | tf_op jit(solution)/shard_map/ppermute | solution.py:249
  40.4 0.0 copy-start.4
  40.4 2.2 %collective-permute-done.2.refs_2_ = bf16[8,2176]{1,0:T(8,128)(2,1)S(1)} collective-permute-done((bf16[8,2176]{1,0:T(8,128)(2,1)}, bf16[8,2176]{1,0:T(8,128)(2,1)S(1)}, u32[]{:S(2)}, u32[]{:S(2)}) %collective-permute-start.2) | collective-permute-done | bytes 34848 | tf_op jit(solution)/shard_map/ppermute | solution.py:249
  42.6 0.0 copy-start.5
  42.6 0.0 collective-permute-done.3.refs_3_
  42.6 0.0 copy-done.4
  42.6 0.6 copy-done.5
  43.2 0.0 copy-start.6
  43.2 0.6 copy-done.6
  43.8 1.5 %shard_map.94 = bf16[4,8,2176]{2,1,0:T(8,128)(2,1)} custom-call(bf16[8,2176]{1,0:T(8,128)(2,1)} %get-tuple-element.8.refs_0_, bf16[8,2176]{1,0:T(8,128)(2,1)} %copy-done.4, bf16[8,2176]{1,0:T(8,128)(2,1)} %copy-done.5, bf16[8,2176]{1,0:T(8,128)(2,1)} %copy-done.6), custom_call_target="tpu_custom_call" | custom-call | tf_op jit(solution)/shard_map/pallas_call | solution.py:222
  45.3 3.1 %collective-permute-start.4 = (bf16[32,2176]{1,0:T(8,128)(2,1)}, bf16[32,2176]{1,0:T(8,128)(2,1)S(1)}, u32[]{:S(2)}, u32[]{:S(2)}) collective-permute-start(bf16[32,2176]{1,0:T(8,128)(2,1)} %bitcast.18), channel_id=1, source_target_pairs={{0,16},{16,0},{1,17},{17,1},{2,18},{18,2},{3,19},{19,3},{4,20},{20... | collective-permute-start | bytes 417800 | tf_op jit(solution)/shard_map/ppermute | solution.py:251
  48.4 2.8 %collective-permute-done.4 = bf16[32,2176]{1,0:T(8,128)(2,1)S(1)} collective-permute-done((bf16[32,2176]{1,0:T(8,128)(2,1)}, bf16[32,2176]{1,0:T(8,128)(2,1)S(1)}, u32[]{:S(2)}, u32[]{:S(2)}) %collective-permute-start.4) | collective-permute-done | bytes 139296 | tf_op jit(solution)/shard_map/ppermute | solution.py:251
  51.3 1.6 %pad_maximum_fusion = bf16[64,2176]{1,0:T(8,128)(2,1)} fusion(bf16[32,2176]{1,0:T(8,128)(2,1)S(1)} %collective-permute-done.4, bf16[32,2176]{1,0:T(8,128)(2,1)} %bitcast.19), kind=kLoop, calls=%fused_computation | loop fusion | flops 557056 | bytes 557056 | tf_op jit(solution)/shard_map/concatenate | solution.py:251
  52.9 0.0 all-gather.2.cloned.1.call-update
  52.9 0.0 copy-done.7
  52.9 0.0 all-to-all-done.arrived
  52.9 0.0 copy-done.2
  52.9 0.0 copy-done
  53.0 0.0 copy-done.1
  53.0 0.0 copy-done.3
  53.0 2.8 %shard_map.92 = bf16[4,4,2,32,128]{4,3,2,1,0:T(8,128)(2,1)S(1)} custom-call(s32[1,4]{1,0:T(1,128)S(1)} %copy-done.2, bf16[32,2,16,512]{3,2,1,0:T(8,128)(2,1)S(1)} %all-to-all-done.arrived, bf16[3,512,512]{2,1,0:T(8,128)(2,1)S(1)} %bitcast.15, f32[3,512]{1,0:T(4,128)S(1)} %bitcast.14, bf16[128,512]{1,0:T(8,128)(2,1)S(1)} %bitcast.16, f32[1,128]{1,0:T(1,128)S(1)} %copy-done.3), custom_call_target="tpu_custom_call" | custom-call | flops 1744830464 | bytes 4194304 | tf_op jit(solution)/shard_map/pallas_call | solution.py:59
  55.8 12.6 %all_to_all.20 = bf16[4,4,2,32,128]{4,3,2,1,0:T(8,128)(2,1)S(1)} all-to-all(bf16[4,4,2,32,128]{4,3,2,1,0:T(8,128)(2,1)S(1)} %shard_map.92), channel_id=1, replica_groups=mesh['x'=4,'yh'=4,'yl'=2,'z'=8,'c'=2] {'yh'}, dimensions={0} | all-to-all | bytes 524288 | tf_op jit(solution)/shard_map/all_to_all | solution.py:232
  68.4 0.2 broadcast_in_dim.16
  68.6 15.2 %all_to_all.21 = bf16[4,4,256,128]{3,2,1,0:T(8,128)(2,1)S(1)} all-to-all(bf16[4,4,256,128]{3,2,1,0:T(8,128)(2,1)S(1)} %broadcast_in_dim.16), channel_id=1, replica_groups=mesh['x'=4,'yh'=4,'yl'=2,'z'=8,'c'=2] {'x'}, dimensions={0} | all-to-all | bytes 2097152 | tf_op jit(solution)/shard_map/all_to_all | solution.py:232
  83.8 6.5 %collective-permute-start = (bf16[16,256,128]{2,1,0:T(8,128)(2,1)S(1)}, bf16[16,256,128]{2,1,0:T(8,128)(2,1)S(1)}, u32[]{:S(2)}, u32[]{:S(2)}) collective-permute-start(bf16[16,256,128]{2,1,0:T(8,128)(2,1)S(1)} %bitcast.12), channel_id=1, source_target_pairs={{0,1},{1,0},{2,3},{3,2},{4,5},{5,4},{6,7},{7,6},{8,9},{9,8},{10,11... | collective-permute-start | bytes 3145736 | tf_op jit(solution)/shard_map/ppermute | solution.py:259
  90.4 1.3 %shard_map.93.own = bf16[256,2048]{1,0:T(8,128)(2,1)S(1)} custom-call(bf16[16,256,128]{2,1,0:T(8,128)(2,1)S(1)} %bitcast.13), custom_call_target="tpu_custom_call" | custom-call | flops 1000000000 | bytes 2097152 | tf_op jit(solution)/shard_map/pallas_call | solution.py:101
  91.6 1.5 %all-gather.2.cloned.1.call-done.gathered = bf16[512,2176]{1,0:T(8,128)(2,1)} async-done(((bf16[64,2176]{1,0:T(8,128)(2,1)}), bf16[512,2176]{1,0:T(8,128)(2,1)}) %all-gather.2.cloned.1.call-update) | async-done | bytes 2228240 | tf_op jit(solution)/shard_map/all_gather | solution.py:252
  93.1 0.0 collective-permute-done.other
  93.1 3.9 %shard_map.95 = f32[8,8,128]{2,1,0:T(8,128)S(1)} custom-call(s32[1]{0:T(128)} %bitcast.core, bf16[256,2048]{1,0:T(8,128)(2,1)S(1)} %shard_map.93.own, bf16[16,256,128]{2,1,0:T(8,128)(2,1)S(1)} %collective-permute-done.other, bf16[512,2176]{1,0:T(8,128)(2,1)} %all-gather.2.cloned.1.call-done.gathered), custom_call_target="tpu_custom_call" | custom-call | flops 2000000000 | bytes 6291456 | tf_op jit(solution)/shard_map/pallas_call | solution.py:141
  97.0 13.5 %all_to_all.22 = f32[8,8,128]{2,1,0:T(8,128)S(1)} all-to-all(f32[8,8,128]{2,1,0:T(8,128)S(1)} %shard_map.95), channel_id=1, replica_groups=mesh['x'=4,'yh'=4,'yl'=2,'z'=8,'c'=2] {'c','x'}, dimensions={0} | all-to-all | bytes 65536 | tf_op jit(solution)/shard_map/all_to_all | solution.py:232
  110.5 0.6 reshape_squeeze.3
  (3 shorter events, 0.0 us)
Async XLA Ops:
  6.5 46.4 %copy-start.7 = (f32[1,3,512]{2,0,1:T(1,128)S(1)}, f32[1,3,512]{2,0,1:T(1,128)}, u32[]{:S(2)}) copy-start(f32[1,3,512]{2,0,1:T(1,128)} %param.12) | copy-start | bytes 18436
  6.5 46.4 %copy-start.2 = (s32[1,4]{1,0:T(1,128)S(1)}, s32[1,4]{1,0:T(1,128)}, u32[]{:S(2)}) copy-start(s32[1,4]{1,0:T(1,128)} %order.1) | copy-start | bytes 52
  6.5 46.4 %copy-start = (bf16[1,3,512,512]{3,2,1,0:T(8,128)(2,1)S(1)}, bf16[1,3,512,512]{3,2,1,0:T(8,128)(2,1)}, u32[]{:S(2)}) copy-start(bf16[1,3,512,512]{3,2,1,0:T(8,128)(2,1)} %param.11) | copy-start | bytes 4718596
  6.5 46.4 %copy-start.1 = (bf16[1,128,512]{2,1,0:T(8,128)(2,1)S(1)}, bf16[1,128,512]{2,1,0:T(8,128)(2,1)}, u32[]{:S(2)}) copy-start(bf16[1,128,512]{2,1,0:T(8,128)(2,1)} %param.13) | copy-start | bytes 393220
  6.5 46.4 %copy-start.3 = (f32[1,128]{1,0:T(1,128)S(1)}, f32[1,128]{1,0:T(1,128)}, u32[]{:S(2)}) copy-start(f32[1,128]{1,0:T(1,128)} %gain.1) | copy-start | bytes 1540
  10.4 42.5 %all-to-all-start = ((bf16[32,2,16,512]{3,2,1,0:T(8,128)(2,1)}), bf16[32,2,16,512]{3,2,1,0:T(8,128)(2,1)S(1)}, u32[]{:S(2)}, u32[]{:S(2)}) async-start(bf16[32,2,16,512]{3,2,1,0:T(8,128)(2,1)} %get-tuple-element.7), calls=%async_computation | async-start | bytes 2097152 | tf_op jit(solution)/shard_map/all_to_all | solution.py:232
  23.4 69.8 %all-gather.2.cloned.1.call-start = ((), (), s32[]{:S(2)}) async-start(), calls=%async_computation.4 | async-start | bytes 2506752 | tf_op jit(solution)/shard_map/all_gather | solution.py:252
  23.4 16.9 %collective-permute-start.1 = (bf16[8,2176]{1,0:T(8,128)(2,1)}, bf16[8,2176]{1,0:T(8,128)(2,1)S(1)}, u32[]{:S(2)}, u32[]{:S(2)}) collective-permute-start(bf16[8,2176]{1,0:T(8,128)(2,1)} %get-tuple-element.8.refs_0_), channel_id=1, source_target_pairs={{0,32},{32,64},{64,96},{96,0},{1,33},{33,65},{65,97},{97,1},{2,34}... | collective-permute-start | bytes 104456 | tf_op jit(solution)/shard_map/ppermute | solution.py:249
  27.7 14.9 %collective-permute-start.2 = (bf16[8,2176]{1,0:T(8,128)(2,1)}, bf16[8,2176]{1,0:T(8,128)(2,1)S(1)}, u32[]{:S(2)}, u32[]{:S(2)}) collective-permute-start(bf16[8,2176]{1,0:T(8,128)(2,1)} %get-tuple-element.8.refs_0_), channel_id=1, source_target_pairs={{0,64},{32,96},{64,0},{96,32},{1,65},{33,97},{65,1},{97,33},{2,66}... | collective-permute-start | bytes 104456 | tf_op jit(solution)/shard_map/ppermute | solution.py:249
  32.4 10.2 %collective-permute-start.3 = (bf16[8,2176]{1,0:T(8,128)(2,1)}, bf16[8,2176]{1,0:T(8,128)(2,1)S(1)}, u32[]{:S(2)}, u32[]{:S(2)}) collective-permute-start(bf16[8,2176]{1,0:T(8,128)(2,1)} %get-tuple-element.8.refs_0_), channel_id=1, source_target_pairs={{0,96},{32,0},{64,32},{96,64},{1,97},{33,1},{65,33},{97,65},{2,98}... | collective-permute-start | bytes 104456 | tf_op jit(solution)/shard_map/ppermute | solution.py:249
  40.4 2.2 %copy-start.4 = (bf16[8,2176]{1,0:T(8,128)(2,1)}, bf16[8,2176]{1,0:T(8,128)(2,1)S(1)}, u32[]{:S(2)}) copy-start(bf16[8,2176]{1,0:T(8,128)(2,1)S(1)} %collective-permute-done.1.refs_1_) | copy-start | bytes 104452
  42.6 0.6 copy-start.5
  43.2 0.6 copy-start.6
  45.3 6.0 %collective-permute-start.4 = (bf16[32,2176]{1,0:T(8,128)(2,1)}, bf16[32,2176]{1,0:T(8,128)(2,1)S(1)}, u32[]{:S(2)}, u32[]{:S(2)}) collective-permute-start(bf16[32,2176]{1,0:T(8,128)(2,1)} %bitcast.18), channel_id=1, source_target_pairs={{0,16},{16,0},{1,17},{17,1},{2,18},{18,2},{3,19},{19,3},{4,20},{20... | collective-permute-start | bytes 417800 | tf_op jit(solution)/shard_map/ppermute | solution.py:251
  83.8 9.3 %collective-permute-start = (bf16[16,256,128]{2,1,0:T(8,128)(2,1)S(1)}, bf16[16,256,128]{2,1,0:T(8,128)(2,1)S(1)}, u32[]{:S(2)}, u32[]{:S(2)}) collective-permute-start(bf16[16,256,128]{2,1,0:T(8,128)(2,1)S(1)} %bitcast.12), channel_id=1, source_target_pairs={{0,1},{1,0},{2,3},{3,2},{4,5},{5,4},{6,7},{7,6},{8,9},{9,8},{10,11... | collective-permute-start | bytes 3145736 | tf_op jit(solution)/shard_map/ppermute | solution.py:259
Sparse Core Ops, SparseCore 0:
  53.0 40.0 all-gather.1

commit v11 on v8

--- a/solution.py
+++ b/solution.py
@@ -20,6 +20,7 @@
 AXES = (("x", 4), ("yh", 4), ("yl", 2), ("z", 8), ("c", 2))
 TOWER = ("x", "yh")
 RANK = ("yl", "z", "c")
+CHUNKS = 4
 
 
 def tower_kernel(order, arrived, weights, biases, compress, gain, out):
@@ -67,34 +68,35 @@
     )(order, arrived, weights, biases, compress, gain)
 
 
-def interact(features, mixed, first_row):
+def interact(features, mixed):
     side = TOWERS * GROUP
     row = lax.broadcasted_iota(jnp.int32, (side, side), 0)
     col = lax.broadcasted_iota(jnp.int32, (side, side), 1)
     scale = jnp.where(row % GROUP == col % GROUP, jnp.float32(1.0 / CD), jnp.float32(0.0))
     eye = jnp.where(row == col, jnp.float32(1.0), jnp.float32(0.0))
 
-    def group(step, carry):
-        at = pl.multiple_of(step * GROUP, GROUP)
-        values = features[:, pl.ds(at, GROUP), :].reshape(side, CD)
-        gram = lax.dot_general(
-            values, values, (((1,), (1,)), ((), ())), preferred_element_type=jnp.float32
-        )
-        factor = (gram * scale + eye).astype(jnp.bfloat16)
-        result = jnp.dot(factor, values, preferred_element_type=jnp.float32).astype(jnp.bfloat16)
-        to = pl.ds(pl.multiple_of(first_row + step * GROUP, GROUP), GROUP)
-        for t in range(TOWERS):
-            mixed[to, t * CD : (t + 1) * CD] = result[t * GROUP : (t + 1) * GROUP]
-        return carry
-
-    lax.fori_loop(0, features.shape[1] // GROUP, group, 0, unroll=4)
+    for start in range(0, features.shape[1], 4 * GROUP):
+        places = [start + k * GROUP for k in range(4)]
+        values = [features[:, at : at + GROUP, :].reshape(side, CD) for at in places]
+        grams = [
+            lax.dot_general(v, v, (((1,), (1,)), ((), ())), preferred_element_type=jnp.float32)
+            for v in values
+        ]
+        factors = [(gram * scale + eye).astype(jnp.bfloat16) for gram in grams]
+        results = [
+            jnp.dot(factor, v, preferred_element_type=jnp.float32).astype(jnp.bfloat16)
+            for factor, v in zip(factors, values)
+        ]
+        for at, result in zip(places, results):
+            for t in range(TOWERS):
+                mixed[at : at + GROUP, t * CD : (t + 1) * CD] = result[t * GROUP : (t + 1) * GROUP]
 
 
 def interact_kernel(features, mixed):
-    interact(features, mixed, 0)
-
-
-def interact_own(features):
+    interact(features, mixed)
+
+
+def interact_all(features):
     vmem = pl.BlockSpec(memory_space=pltpu.VMEM)
     return pl.pallas_call(
         interact_kernel,
@@ -106,19 +108,19 @@
     )(features)
 
 
-def score_kernel(core, own, other, gathered, out, mixed, rows, sem):
+def score_kernel(core, own, other, gathered, out, rows, sem):
+    size = gathered.shape[0] // CHUNKS
     copies = [
-        pltpu.make_async_copy(gathered.at[pl.ds(k * 256, 256)], rows.at[k], sem.at[k])
-        for k in range(2)
+        pltpu.make_async_copy(gathered.at[pl.ds(k * size, size)], rows.at[k], sem.at[k])
+        for k in range(CHUNKS)
     ]
     for copy in copies:
         copy.start()
-    interact(other, mixed, 0)
     totals = [jnp.zeros((1, 256), jnp.float32), jnp.zeros((1, 256), jnp.float32)]
     for k, copy in enumerate(copies):
         copy.wait()
         extra = rows[k, :, TOWERS * CD :].astype(jnp.float32)
-        for which, features in enumerate((own, mixed)):
+        for which, features in enumerate((own, other)):
             hidden = lax.dot_general(
                 rows[k, :, : TOWERS * CD],
                 features[...],
@@ -135,16 +137,20 @@
 
 def score(core, own, other, rows):
     vmem = pl.BlockSpec(memory_space=pltpu.VMEM)
-    anywhere = pl.BlockSpec(memory_space=pl.ANY)
+    size = rows.shape[0] // CHUNKS
     return pl.pallas_call(
         score_kernel,
         out_shape=jax.ShapeDtypeStruct((8, 8, 128), jnp.float32),
-        in_specs=[pl.BlockSpec(memory_space=pltpu.SMEM), vmem, vmem, anywhere],
+        in_specs=[
+            pl.BlockSpec(memory_space=pltpu.SMEM),
+            vmem,
+            vmem,
+            pl.BlockSpec(memory_space=pl.ANY),
+        ],
         out_specs=vmem,
         scratch_shapes=[
-            pltpu.VMEM((256, TOWERS * CD), jnp.bfloat16),
-            pltpu.VMEM((2, 256, WIDE), jnp.bfloat16),
-            pltpu.SemaphoreType.DMA((2,)),
+            pltpu.VMEM((CHUNKS, size, WIDE), jnp.bfloat16),
+            pltpu.SemaphoreType.DMA((CHUNKS,)),
         ],
         compiler_params=pltpu.CompilerParams(vmem_limit_bytes=50 * 2**20),
         cost_estimate=pl.CostEstimate(
@@ -219,17 +225,18 @@
     sent, rows = lax.optimization_barrier((lay_out(pooled), rows))
     arrived = exchange(sent, RANK)
     rows = [rows] + [
-        lax.ppermute(rows, "yh", [(i, (i + k) % 4) for i in range(4)]) for k in range(1, 4)
+        lax.ppermute(rows, "yh", [(i, (i + k) % 4) for i in range(4)]) for k in (1, 2, 3)
     ]
-    rows = lax.all_gather(jnp.concatenate(rows, axis=0), "z", axis=0, tiled=True)
+    rows = jnp.concatenate(rows, axis=0)
+    rows = lax.all_gather(rows, "z", axis=0, tiled=True)
     towers = tower_block(
         feature_order, arrived, cross_weight[0], cross_bias[0], compress_weight[0], norm_gain
     )
     column = exchange(towers, "yh").reshape(4, 256, CD)
     features = exchange(jnp.broadcast_to(column[None], (4, 4, 256, CD)), "x")
     features = features.reshape(TOWERS, 256, CD)
-    other = lax.ppermute(features, "c", [(0, 1), (1, 0)])
-    own = interact_own(features)
+    other = interact_all(lax.ppermute(features, "c", [(0, 1), (1, 0)]))
+    own = interact_all(features)
     core = lax.axis_index("c").reshape(1).astype(jnp.int32)
     terms = exchange(score(core, own, other, rows), ("c", "x"))
     return jnp.sum(terms, axis=0)[0, :64].reshape(2, 1, BLOCK)

time: 120 us -> 121 us (level)
    pallas_call x1 -> x2, Pallas kernels: 2.71 us -> 2.52 us  [interact_all(): pl.pallas_call(interact_kernel, out_shape=jax.ShapeDtypeStruct((features....]
  transfers between devices with their start and end apart: 7 -> 7, of which waited for: 3 -> 4; matrix products, arithmetic and copies ran while one was open for 1% -> 1% of each run, Pallas kernels for 7% -> 6%
where the time goes in v11:
time: 121 us; the launch traced here: 120 us
  blocking collectives  42.7 us (35%)
  starting transfers between devices  33.1 us (27%)
  waiting for transfers between devices  14.9 us (12%)
  Pallas kernels  13.8 us (11%)
  between operations  13.6 us (11%)
  other arithmetic  1.52 us (1%)
    all_to_all x3, blocking collectives, exchange(): return lax.all_to_all(x, axes, split_axis=0, concat_axis=0, tiled=True)  42.7 us
    ppermute x3, starting transfers between devices, on_device(): lax.ppermute(rows, 'yh', [(i, (i + k) % 4) for i in range(4)])  12.7 us
    all_to_all x1, starting transfers between devices, exchange(): return lax.all_to_all(x, axes, split_axis=0, concat_axis=0, tiled=True)  12.5 us
    ppermute x3, waiting for transfers between devices, on_device(): lax.ppermute(rows, 'yh', [(i, (i + k) % 4) for i in range(4)])  9.16 us
    all_to_all x1, waiting for transfers between devices, exchange(): return lax.all_to_all(x, axes, split_axis=0, concat_axis=0, tiled=True)  4.73 us
    pallas_call x1, Pallas kernels, score(): pl.pallas_call(score_kernel, out_shape=jax.ShapeDtypeStruct((8, 8, 128),...  4.48 us
    ppermute x1, starting transfers between devices, on_device(): lax.ppermute(rows, 'yl', [(0, 1), (1, 0)])  4.17 us
    ppermute x1, starting transfers between devices, on_device(): other = interact_all(lax.ppermute(features, 'c', [(0, 1), (1, 0)]))  3.61 us
  transfers between devices with their start and end apart: 7, of which 4 were waited for; matrix products, arithmetic and copies ran while one was open for 1% of the time, Pallas kernels for 6%

profile of v11, /device:TPU:1, one launch (start us, length us, event | category | flops | bytes accessed | tf_op | source)
XLA Modules:
  0.0 120.5 jit_solution(1654205621175485453)
XLA Ops:
  6.5 1.5 %shard_map.92 = bf16[8,2176]{1,0:T(8,128)(2,1)} custom-call(bf16[8,2048]{1,0:T(8,128)(2,1)} %weight.1, bf16[1,8]{1,0:T(2,128)(2,1)} %bitcast.17, bf16[1,8]{1,0:T(2,128)(2,1)} %bitcast.18), custom_call_target="tpu_custom_call" | custom-call | tf_op jit(solution)/shard_map/pallas_call | solution.py:200
  8.0 0.0 copy-start.4
  8.0 0.0 copy-start
  8.0 0.0 copy-start.1
  8.0 0.0 copy-start.2
  8.0 0.0 copy-start.3
  8.0 4.2 %collective-permute-start = (bf16[8,2176]{1,0:T(8,128)(2,1)}, bf16[8,2176]{1,0:T(8,128)(2,1)S(1)}, u32[]{:S(2)}, u32[]{:S(2)}) collective-permute-start(bf16[8,2176]{1,0:T(8,128)(2,1)} %shard_map.92), channel_id=1, source_target_pairs={{0,16},{16,0},{1,17},{17,1},{2,18},{18,2},{3,19},{19,3},{4,20},{20... | collective-permute-start | bytes 104456 | tf_op jit(solution)/shard_map/ppermute | solution.py:224
  12.2 2.5 %shard_map.91 = bf16[32,2,16,512]{3,2,1,0:T(8,128)(2,1)} custom-call(bf16[2,16,16384]{2,1,0:T(8,128)(2,1)} %pooled.1), custom_call_target="tpu_custom_call" | custom-call | bytes 4194304 | tf_op jit(solution)/shard_map/pallas_call | solution.py:176
  14.7 0.0 collective-permute-done
  14.7 0.8 pad_maximum_fusion.1
  15.4 12.5 %all-to-all-start = ((bf16[32,2,16,512]{3,2,1,0:T(8,128)(2,1)}), bf16[32,2,16,512]{3,2,1,0:T(8,128)(2,1)S(1)}, u32[]{:S(2)}, u32[]{:S(2)}) async-start(bf16[32,2,16,512]{3,2,1,0:T(8,128)(2,1)} %shard_map.91), calls=%async_computation | async-start | bytes 2097152 | tf_op jit(solution)/shard_map/all_to_all | solution.py:209
  28.0 0.0 all-gather.2.cloned.1.call-start
  28.0 5.0 %collective-permute-start.4 = (bf16[16,2176]{1,0:T(8,128)(2,1)S(1)}, bf16[16,2176]{1,0:T(8,128)(2,1)S(1)}, u32[]{:S(2)}, u32[]{:S(2)}) collective-permute-start(bf16[16,2176]{1,0:T(8,128)(2,1)S(1)} %pad_maximum_fusion.1), channel_id=1, source_target_pairs={{0,96},{32,0},{64,32},{96,64},{1,97},{33,1},{65,33},{97,65},{2,98}... | collective-permute-start | bytes 208904 | tf_op jit(solution)/shard_map/ppermute | solution.py:228
  33.0 4.4 %collective-permute-start.3 = (bf16[16,2176]{1,0:T(8,128)(2,1)S(1)}, bf16[16,2176]{1,0:T(8,128)(2,1)S(1)}, u32[]{:S(2)}, u32[]{:S(2)}) collective-permute-start(bf16[16,2176]{1,0:T(8,128)(2,1)S(1)} %pad_maximum_fusion.1), channel_id=1, source_target_pairs={{0,64},{32,96},{64,0},{96,32},{1,65},{33,97},{65,1},{97,33},{2,66}... | collective-permute-start | bytes 208904 | tf_op jit(solution)/shard_map/ppermute | solution.py:228
  37.4 3.3 %collective-permute-start.2 = (bf16[16,2176]{1,0:T(8,128)(2,1)S(1)}, bf16[16,2176]{1,0:T(8,128)(2,1)S(1)}, u32[]{:S(2)}, u32[]{:S(2)}) collective-permute-start(bf16[16,2176]{1,0:T(8,128)(2,1)S(1)} %pad_maximum_fusion.1), channel_id=1, source_target_pairs={{0,32},{32,64},{64,96},{96,0},{1,33},{33,65},{65,97},{97,1},{2,34}... | collective-permute-start | bytes 208904 | tf_op jit(solution)/shard_map/ppermute | solution.py:228
  40.8 0.0 collective-permute-done.4
  40.8 6.3 %collective-permute-done.3 = bf16[16,2176]{1,0:T(8,128)(2,1)S(1)} collective-permute-done((bf16[16,2176]{1,0:T(8,128)(2,1)S(1)}, bf16[16,2176]{1,0:T(8,128)(2,1)S(1)}, u32[]{:S(2)}, u32[]{:S(2)}) %collective-permute-start.3) | collective-permute-done | bytes 69664 | tf_op jit(solution)/shard_map/ppermute | solution.py:228
  47.1 2.8 %collective-permute-done.2 = bf16[16,2176]{1,0:T(8,128)(2,1)S(1)} collective-permute-done((bf16[16,2176]{1,0:T(8,128)(2,1)S(1)}, bf16[16,2176]{1,0:T(8,128)(2,1)S(1)}, u32[]{:S(2)}, u32[]{:S(2)}) %collective-permute-start.2) | collective-permute-done | bytes 69664 | tf_op jit(solution)/shard_map/ppermute | solution.py:228
  49.9 0.7 pad_maximum_fusion
  50.7 0.0 all-gather.2.cloned.1.call-update
  50.7 0.0 copy-done.4
  50.7 4.7 %all-to-all-done.arrived = bf16[32,2,16,512]{3,2,1,0:T(8,128)(2,1)S(1)} async-done(((bf16[32,2,16,512]{3,2,1,0:T(8,128)(2,1)}), bf16[32,2,16,512]{3,2,1,0:T(8,128)(2,1)S(1)}, u32[]{:S(2)}, u32[]{:S(2)}) %all-to-all-start) | async-done | bytes 1048608 | tf_op jit(solution)/shard_map/all_to_all | solution.py:209
  55.5 0.0 copy-done
  55.5 0.0 copy-done.1
  55.5 0.0 copy-done.2
  55.5 0.0 copy-done.3
  55.5 2.8 %shard_map.93 = bf16[4,4,2,32,128]{4,3,2,1,0:T(8,128)(2,1)S(1)} custom-call(s32[1,4]{1,0:T(1,128)S(1)} %copy-done.2, bf16[32,2,16,512]{3,2,1,0:T(8,128)(2,1)S(1)} %all-to-all-done.arrived, bf16[3,512,512]{2,1,0:T(8,128)(2,1)S(1)} %bitcast.14, f32[3,512]{1,0:T(4,128)S(1)} %bitcast.13, bf16[128,512]{1,0:T(8,128)(2,1)S(1)} %bitcast.15, f32[1,128]{1,0:T(1,128)S(1)} %copy-done.3), custom_call_target="tpu_custom_call" | custom-call | flops 1744830464 | bytes 4194304 | tf_op jit(solution)/shard_map/pallas_call | solution.py:59
  58.3 17.6 %all_to_all.20 = bf16[4,4,2,32,128]{4,3,2,1,0:T(8,128)(2,1)S(1)} all-to-all(bf16[4,4,2,32,128]{4,3,2,1,0:T(8,128)(2,1)S(1)} %shard_map.93), channel_id=1, replica_groups=mesh['x'=4,'yh'=4,'yl'=2,'z'=8,'c'=2] {'yh'}, dimensions={0} | all-to-all | bytes 524288 | tf_op jit(solution)/shard_map/all_to_all | solution.py:209
  75.9 0.2 broadcast_in_dim.16
  76.1 17.5 %all_to_all.21 = bf16[4,4,256,128]{3,2,1,0:T(8,128)(2,1)S(1)} all-to-all(bf16[4,4,256,128]{3,2,1,0:T(8,128)(2,1)S(1)} %broadcast_in_dim.16), channel_id=1, replica_groups=mesh['x'=4,'yh'=4,'yl'=2,'z'=8,'c'=2] {'x'}, dimensions={0} | all-to-all | bytes 2097152 | tf_op jit(solution)/shard_map/all_to_all | solution.py:209
  93.6 3.6 %collective-permute-start.1 = (bf16[16,256,128]{2,1,0:T(8,128)(2,1)S(1)}, bf16[16,256,128]{2,1,0:T(8,128)(2,1)S(1)}, u32[]{:S(2)}, u32[]{:S(2)}) collective-permute-start(bf16[16,256,128]{2,1,0:T(8,128)(2,1)S(1)} %bitcast.11), channel_id=1, source_target_pairs={{0,1},{1,0},{2,3},{3,2},{4,5},{5,4},{6,7},{7,6},{8,9},{9,8},{10,11... | collective-permute-start | bytes 3145736 | tf_op jit(solution)/shard_map/ppermute | solution.py:238
  97.2 1.3 %shard_map.94.own = bf16[256,2048]{1,0:T(8,128)(2,1)S(1)} custom-call(bf16[16,256,128]{2,1,0:T(8,128)(2,1)S(1)} %bitcast.12), custom_call_target="tpu_custom_call" | custom-call | flops 1000000000 | bytes 2097152 | tf_op jit(solution)/shard_map/pallas_call | solution.py:101
  98.5 1.0 collective-permute-done.1.features
  99.5 1.3 %shard_map.95.other = bf16[256,2048]{1,0:T(8,128)(2,1)S(1)} custom-call(bf16[16,256,128]{2,1,0:T(8,128)(2,1)S(1)} %collective-permute-done.1.features), custom_call_target="tpu_custom_call" | custom-call | flops 1000000000 | bytes 2097152 | tf_op jit(solution)/shard_map/pallas_call | solution.py:101
  100.8 0.0 all-gather.2.cloned.1.call-done.gathered
  100.8 4.5 %shard_map.96 = f32[8,8,128]{2,1,0:T(8,128)S(1)} custom-call(s32[1]{0:T(128)} %bitcast.core, bf16[256,2048]{1,0:T(8,128)(2,1)S(1)} %shard_map.94.own, bf16[256,2048]{1,0:T(8,128)(2,1)S(1)} %shard_map.95.other, bf16[512,2176]{1,0:T(8,128)(2,1)} %all-gather.2.cloned.1.call-done.gathered), custom_call_target="tpu_custom_call" | custom-call | flops 2000000000 | bytes 6291456 | tf_op jit(solution)/shard_map/pallas_call | solution.py:141
  105.3 7.7 %all_to_all.22 = f32[8,8,128]{2,1,0:T(8,128)S(1)} all-to-all(f32[8,8,128]{2,1,0:T(8,128)S(1)} %shard_map.96), channel_id=1, replica_groups=mesh['x'=4,'yh'=4,'yl'=2,'z'=8,'c'=2] {'c','x'}, dimensions={0} | all-to-all | bytes 65536 | tf_op jit(solution)/shard_map/all_to_all | solution.py:209
  113.0 0.6 reshape_squeeze.3
  (3 shorter events, 0.0 us)
Async XLA Ops:
  8.0 42.7 %copy-start.4 = (f32[1,3,512]{2,0,1:T(1,128)S(1)}, f32[1,3,512]{2,0,1:T(1,128)}, u32[]{:S(2)}) copy-start(f32[1,3,512]{2,0,1:T(1,128)} %param.12) | copy-start | bytes 18436
  8.0 47.5 %copy-start = (bf16[1,3,512,512]{3,2,1,0:T(8,128)(2,1)S(1)}, bf16[1,3,512,512]{3,2,1,0:T(8,128)(2,1)}, u32[]{:S(2)}) copy-start(bf16[1,3,512,512]{3,2,1,0:T(8,128)(2,1)} %param.11) | copy-start | bytes 4718596
  8.0 47.5 %copy-start.1 = (bf16[1,128,512]{2,1,0:T(8,128)(2,1)S(1)}, bf16[1,128,512]{2,1,0:T(8,128)(2,1)}, u32[]{:S(2)}) copy-start(bf16[1,128,512]{2,1,0:T(8,128)(2,1)} %param.13) | copy-start | bytes 393220
  8.0 47.5 %copy-start.2 = (s32[1,4]{1,0:T(1,128)S(1)}, s32[1,4]{1,0:T(1,128)}, u32[]{:S(2)}) copy-start(s32[1,4]{1,0:T(1,128)} %order.1) | copy-start | bytes 52
  8.0 47.5 %copy-start.3 = (f32[1,128]{1,0:T(1,128)S(1)}, f32[1,128]{1,0:T(1,128)}, u32[]{:S(2)}) copy-start(f32[1,128]{1,0:T(1,128)} %gain.1) | copy-start | bytes 1540
  8.0 6.6 %collective-permute-start = (bf16[8,2176]{1,0:T(8,128)(2,1)}, bf16[8,2176]{1,0:T(8,128)(2,1)S(1)}, u32[]{:S(2)}, u32[]{:S(2)}) collective-permute-start(bf16[8,2176]{1,0:T(8,128)(2,1)} %shard_map.92), channel_id=1, source_target_pairs={{0,16},{16,0},{1,17},{17,1},{2,18},{18,2},{3,19},{19,3},{4,20},{20... | collective-permute-start | bytes 104456 | tf_op jit(solution)/shard_map/ppermute | solution.py:224
  15.4 40.0 %all-to-all-start = ((bf16[32,2,16,512]{3,2,1,0:T(8,128)(2,1)}), bf16[32,2,16,512]{3,2,1,0:T(8,128)(2,1)S(1)}, u32[]{:S(2)}, u32[]{:S(2)}) async-start(bf16[32,2,16,512]{3,2,1,0:T(8,128)(2,1)} %shard_map.91), calls=%async_computation | async-start | bytes 2097152 | tf_op jit(solution)/shard_map/all_to_all | solution.py:209
  28.0 72.8 %all-gather.2.cloned.1.call-start = ((), (), s32[]{:S(2)}) async-start(), calls=%async_computation.4 | async-start | bytes 2506752 | tf_op jit(solution)/shard_map/all_gather | solution.py:231
  28.0 12.8 %collective-permute-start.4 = (bf16[16,2176]{1,0:T(8,128)(2,1)S(1)}, bf16[16,2176]{1,0:T(8,128)(2,1)S(1)}, u32[]{:S(2)}, u32[]{:S(2)}) collective-permute-start(bf16[16,2176]{1,0:T(8,128)(2,1)S(1)} %pad_maximum_fusion.1), channel_id=1, source_target_pairs={{0,96},{32,0},{64,32},{96,64},{1,97},{33,1},{65,33},{97,65},{2,98}... | collective-permute-start | bytes 208904 | tf_op jit(solution)/shard_map/ppermute | solution.py:228
  33.0 14.1 %collective-permute-start.3 = (bf16[16,2176]{1,0:T(8,128)(2,1)S(1)}, bf16[16,2176]{1,0:T(8,128)(2,1)S(1)}, u32[]{:S(2)}, u32[]{:S(2)}) collective-permute-start(bf16[16,2176]{1,0:T(8,128)(2,1)S(1)} %pad_maximum_fusion.1), channel_id=1, source_target_pairs={{0,64},{32,96},{64,0},{96,32},{1,65},{33,97},{65,1},{97,33},{2,66}... | collective-permute-start | bytes 208904 | tf_op jit(solution)/shard_map/ppermute | solution.py:228
  37.4 12.5 %collective-permute-start.2 = (bf16[16,2176]{1,0:T(8,128)(2,1)S(1)}, bf16[16,2176]{1,0:T(8,128)(2,1)S(1)}, u32[]{:S(2)}, u32[]{:S(2)}) collective-permute-start(bf16[16,2176]{1,0:T(8,128)(2,1)S(1)} %pad_maximum_fusion.1), channel_id=1, source_target_pairs={{0,32},{32,64},{64,96},{96,0},{1,33},{33,65},{65,97},{97,1},{2,34}... | collective-permute-start | bytes 208904 | tf_op jit(solution)/shard_map/ppermute | solution.py:228
  93.6 5.9 %collective-permute-start.1 = (bf16[16,256,128]{2,1,0:T(8,128)(2,1)S(1)}, bf16[16,256,128]{2,1,0:T(8,128)(2,1)S(1)}, u32[]{:S(2)}, u32[]{:S(2)}) collective-permute-start(bf16[16,256,128]{2,1,0:T(8,128)(2,1)S(1)} %bitcast.11), channel_id=1, source_target_pairs={{0,1},{1,0},{2,3},{3,2},{4,5},{5,4},{6,7},{7,6},{8,9},{9,8},{10,11... | collective-permute-start | bytes 3145736 | tf_op jit(solution)/shard_map/ppermute | solution.py:238
Sparse Core Ops, SparseCore 0:
  50.8 39.0 all-gather.1

commit v12 on v9

--- a/solution.py
+++ b/solution.py
@@ -21,6 +21,7 @@
 TOWER = ("x", "yh")
 RANK = ("yl", "z", "c")
 CHUNKS = 8
+PIECES = 2
 
 
 def tower_kernel(order, arrived, weights, biases, compress, gain, out):
@@ -96,7 +97,7 @@
     interact(features, mixed)
 
 
-def interact_own(features):
+def interact_all(features):
     vmem = pl.BlockSpec(memory_space=pltpu.VMEM)
     return pl.pallas_call(
         interact_kernel,
@@ -108,19 +109,19 @@
     )(features)
 
 
-def score_kernel(core, own, other, gathered, out, mixed, rows, sem):
+def score_kernel(core, own, other, gathered, out, rows, sem):
+    size = gathered.shape[0] // PIECES
     copies = [
-        pltpu.make_async_copy(gathered.at[pl.ds(k * 256, 256)], rows.at[k], sem.at[k])
-        for k in range(2)
+        pltpu.make_async_copy(gathered.at[pl.ds(k * size, size)], rows.at[k], sem.at[k])
+        for k in range(PIECES)
     ]
     for copy in copies:
         copy.start()
-    interact(other, mixed)
     totals = [jnp.zeros((1, 256), jnp.float32), jnp.zeros((1, 256), jnp.float32)]
     for k, copy in enumerate(copies):
         copy.wait()
         extra = rows[k, :, TOWERS * CD :].astype(jnp.float32)
-        for which, features in enumerate((own, mixed)):
+        for which, features in enumerate((own, other)):
             hidden = lax.dot_general(
                 rows[k, :, : TOWERS * CD],
                 features[...],
@@ -137,16 +138,20 @@
 
 def score(core, own, other, rows):
     vmem = pl.BlockSpec(memory_space=pltpu.VMEM)
-    anywhere = pl.BlockSpec(memory_space=pl.ANY)
+    size = rows.shape[0] // PIECES
     return pl.pallas_call(
         score_kernel,
         out_shape=jax.ShapeDtypeStruct((8, 8, 128), jnp.float32),
-        in_specs=[pl.BlockSpec(memory_space=pltpu.SMEM), vmem, vmem, anywhere],
+        in_specs=[
+            pl.BlockSpec(memory_space=pltpu.SMEM),
+            vmem,
+            vmem,
+            pl.BlockSpec(memory_space=pl.ANY),
+        ],
         out_specs=vmem,
         scratch_shapes=[
-            pltpu.VMEM((256, TOWERS * CD), jnp.bfloat16),
-            pltpu.VMEM((2, 256, WIDE), jnp.bfloat16),
-            pltpu.SemaphoreType.DMA((2,)),
+            pltpu.VMEM((PIECES, size, WIDE), jnp.bfloat16),
+            pltpu.SemaphoreType.DMA((PIECES,)),
         ],
         compiler_params=pltpu.CompilerParams(vmem_limit_bytes=50 * 2**20),
         cost_estimate=pl.CostEstimate(
@@ -254,10 +259,9 @@
 ):
     arrived = exchange(lay_out(pooled), RANK)
     rows = join(mlp_weight, mlp_bias, out_weight)
-    rows = stack(
-        rows, *[lax.ppermute(rows, "yh", [(i, (i + k) % 4) for i in range(4)]) for k in (1, 2, 3)]
-    )
-    rows = stack(rows, lax.ppermute(rows, "yl", [(0, 1), (1, 0)]))
+    rows = stack(rows, lax.ppermute(rows, "yh", [(i, i ^ 1) for i in range(4)]))
+    rows = stack(rows, lax.ppermute(rows, "yh", [(i, i ^ 2) for i in range(4)]))
+    rows = jnp.concatenate([rows, lax.ppermute(rows, "yl", [(0, 1), (1, 0)])], axis=0)
     rows = lax.all_gather(rows, "z", axis=0, tiled=True)
     towers = tower_block(
         feature_order, arrived, cross_weight[0], cross_bias[0], compress_weight[0], norm_gain
@@ -265,8 +269,8 @@
     column = exchange(towers, "yh").reshape(4, 256, CD)
     features = exchange(jnp.broadcast_to(column[None], (4, 4, 256, CD)), "x")
     features = features.reshape(TOWERS, 256, CD)
-    other = lax.ppermute(features, "c", [(0, 1), (1, 0)])
-    own = interact_own(features)
+    other = interact_all(lax.ppermute(features, "c", [(0, 1), (1, 0)]))
+    own = interact_all(features)
     core = lax.axis_index("c").reshape(1).astype(jnp.int32)
     terms = exchange(score(core, own, other, rows), ("c", "x"))
     return jnp.sum(terms, axis=0)[0, :64].reshape(2, 1, BLOCK)

time: 118 us -> 126 us (1.068)
  waiting for transfers between devices: 10.3 us -> 14.1 us
  blocking collectives: 38.9 us -> 40.6 us
  other arithmetic: 0.01 us -> 1.65 us
  starting transfers between devices: 36.7 us -> 38.1 us
    ppermute x5 -> x4, waiting for transfers between devices: 8.05 us -> 14.1 us  [the longest x1 7.31 us: on_device(): rows = stack(rows, lax.ppermute(rows, 'yh', [(i, i ^ 1) for i in range(4)]))]
    all_gather x1, waiting for transfers between devices: 2.21 us -> 0.02 us  [on_device(): rows = lax.all_gather(rows, 'z', axis=0, tiled=True)]
    concatenate x0 -> x1, other arithmetic: none -> 1.64 us  [on_device(): jnp.concatenate([rows, lax.ppermute(rows, 'yl', [(0, 1), (1, 0)])], axis=0)]
    all_to_all x3, blocking collectives: 38.9 us -> 40.6 us  [exchange(): return lax.all_to_all(x, axes, split_axis=0, concat_axis=0, tiled=True)]
    pallas_call x1 -> x2, Pallas kernels: 1.26 us -> 2.52 us  [interact_all(): pl.pallas_call(interact_kernel, out_shape=jax.ShapeDtypeStruct((features....]
    ppermute x5 -> x4, starting transfers between devices: 23.7 us -> 24.9 us  [the longest x1 7.22 us: on_device(): other = interact_all(lax.ppermute(features, 'c', [(0, 1), (1, 0)]))]
  transfers between devices with their start and end apart: 7 -> 6, of which waited for: 4 -> 4; matrix products, arithmetic and copies ran while one was open for 0% -> 1% of each run, Pallas kernels for 7% -> 8%
where the time goes in v12:
time: 126 us; the launch traced here: 125 us
  blocking collectives  40.6 us (32%)
  starting transfers between devices  38.1 us (30%)
  Pallas kernels  15 us (12%)
  waiting for transfers between devices  14.1 us (11%)
  between operations  13.6 us (11%)
  local copies, waits for them, and re-layouts  2.13 us (2%)
  other arithmetic  1.65 us (1%)
    all_to_all x3, blocking collectives, exchange(): return lax.all_to_all(x, axes, split_axis=0, concat_axis=0, tiled=True)  40.6 us
    all_to_all x1, starting transfers between devices, exchange(): return lax.all_to_all(x, axes, split_axis=0, concat_axis=0, tiled=True)  13.1 us
    ppermute x1, waiting for transfers between devices, on_device(): rows = stack(rows, lax.ppermute(rows, 'yh', [(i, i ^ 1) for i in range(4)]))  7.31 us
    ppermute x1, starting transfers between devices, on_device(): other = interact_all(lax.ppermute(features, 'c', [(0, 1), (1, 0)]))  7.22 us
    ppermute x1, starting transfers between devices, on_device(): lax.ppermute(rows, 'yl', [(0, 1), (1, 0)])  6.93 us
    ppermute x1, starting transfers between devices, on_device(): rows = stack(rows, lax.ppermute(rows, 'yh', [(i, i ^ 2) for i in range(4)]))  6.54 us
    ppermute x1, starting transfers between devices, on_device(): rows = stack(rows, lax.ppermute(rows, 'yh', [(i, i ^ 1) for i in range(4)]))  4.2 us
    ppermute x1, waiting for transfers between devices, on_device(): lax.ppermute(rows, 'yl', [(0, 1), (1, 0)])  3.19 us
  transfers between devices with their start and end apart: 6, of which 4 were waited for; matrix products, arithmetic and copies ran while one was open for 1% of the time, Pallas kernels for 8%

profile of v12, /device:TPU:1, one launch (start us, length us, event | category | flops | bytes accessed | tf_op | source)
XLA Modules:
  0.0 125.1 jit_solution(8557471382904016530)
XLA Ops:
  6.5 2.3 %shard_map.91 = bf16[32,2,16,512]{3,2,1,0:T(8,128)(2,1)} custom-call(bf16[2,16,16384]{2,1,0:T(8,128)(2,1)} %pooled.1), custom_call_target="tpu_custom_call" | custom-call | bytes 4194304 | tf_op jit(solution)/shard_map/pallas_call | solution.py:192
  8.9 0.0 copy-start.6
  8.9 0.0 copy-start
  8.9 0.0 copy-start.1
  8.9 0.0 copy-start.2
  8.9 0.0 copy-start.3
  8.9 13.1 %all-to-all-start = ((bf16[32,2,16,512]{3,2,1,0:T(8,128)(2,1)}), bf16[32,2,16,512]{3,2,1,0:T(8,128)(2,1)S(1)}, u32[]{:S(2)}, u32[]{:S(2)}) async-start(bf16[32,2,16,512]{3,2,1,0:T(8,128)(2,1)} %shard_map.91), calls=%async_computation | async-start | bytes 2097152 | tf_op jit(solution)/shard_map/all_to_all | solution.py:246
  22.1 0.0 all-gather.2.cloned.1.call-start
  22.1 1.5 %shard_map.95.refs_0_ = bf16[8,2176]{1,0:T(8,128)(2,1)} custom-call(bf16[8,2048]{1,0:T(8,128)(2,1)} %weight.1, bf16[1,8]{1,0:T(2,128)(2,1)} %bitcast.23, bf16[1,8]{1,0:T(2,128)(2,1)} %bitcast.24), custom_call_target="tpu_custom_call" | custom-call | tf_op jit(solution)/shard_map/pallas_call | solution.py:220
  23.6 4.2 %collective-permute-start.1 = (bf16[8,2176]{1,0:T(8,128)(2,1)}, bf16[8,2176]{1,0:T(8,128)(2,1)S(1)}, u32[]{:S(2)}, u32[]{:S(2)}) collective-permute-start(bf16[8,2176]{1,0:T(8,128)(2,1)} %shard_map.95.refs_0_), channel_id=1, source_target_pairs={{0,32},{32,0},{64,96},{96,64},{1,33},{33,1},{65,97},{97,65},{2,34}... | collective-permute-start | bytes 104456 | tf_op jit(solution)/shard_map/ppermute | solution.py:262
  27.8 7.3 %collective-permute-done.1.refs_1_ = bf16[8,2176]{1,0:T(8,128)(2,1)S(1)} collective-permute-done((bf16[8,2176]{1,0:T(8,128)(2,1)}, bf16[8,2176]{1,0:T(8,128)(2,1)S(1)}, u32[]{:S(2)}, u32[]{:S(2)}) %collective-permute-start.1) | collective-permute-done | bytes 34848 | tf_op jit(solution)/shard_map/ppermute | solution.py:262
  35.1 0.0 copy-start.5
  35.1 0.6 copy-done.5
  35.7 1.4 %shard_map.96 = bf16[2,8,2176]{2,1,0:T(8,128)(2,1)} custom-call(bf16[8,2176]{1,0:T(8,128)(2,1)} %shard_map.95.refs_0_, bf16[8,2176]{1,0:T(8,128)(2,1)} %copy-done.5), custom_call_target="tpu_custom_call" | custom-call | tf_op jit(solution)/shard_map/pallas_call | solution.py:236
  37.1 6.5 %collective-permute-start.2 = (bf16[16,2176]{1,0:T(8,128)(2,1)}, bf16[16,2176]{1,0:T(8,128)(2,1)S(1)}, u32[]{:S(2)}, u32[]{:S(2)}) collective-permute-start(bf16[16,2176]{1,0:T(8,128)(2,1)} %bitcast.21), channel_id=1, source_target_pairs={{0,64},{32,96},{64,0},{96,32},{1,65},{33,97},{65,1},{97,33},{2,66}... | collective-permute-start | bytes 208904 | tf_op jit(solution)/shard_map/ppermute | solution.py:263
  43.7 2.6 %collective-permute-done.2.refs_1_ = bf16[16,2176]{1,0:T(8,128)(2,1)S(1)} collective-permute-done((bf16[16,2176]{1,0:T(8,128)(2,1)}, bf16[16,2176]{1,0:T(8,128)(2,1)S(1)}, u32[]{:S(2)}, u32[]{:S(2)}) %collective-permute-start.2) | collective-permute-done | bytes 69664 | tf_op jit(solution)/shard_map/ppermute | solution.py:263
  46.3 0.0 copy-start.4
  46.3 0.6 copy-done.4
  46.9 1.6 %shard_map.97 = bf16[2,16,2176]{2,1,0:T(8,128)(2,1)} custom-call(bf16[16,2176]{1,0:T(8,128)(2,1)} %bitcast.22, bf16[16,2176]{1,0:T(8,128)(2,1)} %copy-done.4), custom_call_target="tpu_custom_call" | custom-call | tf_op jit(solution)/shard_map/pallas_call | solution.py:236
  48.5 6.9 %collective-permute-start.3 = (bf16[32,2176]{1,0:T(8,128)(2,1)}, bf16[32,2176]{1,0:T(8,128)(2,1)S(1)}, u32[]{:S(2)}, u32[]{:S(2)}) collective-permute-start(bf16[32,2176]{1,0:T(8,128)(2,1)} %bitcast.19), channel_id=1, source_target_pairs={{0,16},{16,0},{1,17},{17,1},{2,18},{18,2},{3,19},{19,3},{4,20},{20... | collective-permute-start | bytes 417800 | tf_op jit(solution)/shard_map/ppermute | solution.py:264
  55.4 3.2 %collective-permute-done.3 = bf16[32,2176]{1,0:T(8,128)(2,1)S(1)} collective-permute-done((bf16[32,2176]{1,0:T(8,128)(2,1)}, bf16[32,2176]{1,0:T(8,128)(2,1)S(1)}, u32[]{:S(2)}, u32[]{:S(2)}) %collective-permute-start.3) | collective-permute-done | bytes 139296 | tf_op jit(solution)/shard_map/ppermute | solution.py:264
  58.6 1.6 %pad_maximum_fusion = bf16[64,2176]{1,0:T(8,128)(2,1)} fusion(bf16[32,2176]{1,0:T(8,128)(2,1)S(1)} %collective-permute-done.3, bf16[32,2176]{1,0:T(8,128)(2,1)} %bitcast.20), kind=kLoop, calls=%fused_computation | loop fusion | flops 557056 | bytes 557056 | tf_op jit(solution)/shard_map/concatenate | solution.py:264
  60.3 0.0 all-gather.2.cloned.1.call-update
  60.3 0.0 copy-done.6
  60.3 0.0 all-to-all-done.arrived
  60.3 0.0 copy-done
  60.3 0.0 copy-done.1
  60.3 0.0 copy-done.2
  60.3 0.0 copy-done.3
  60.3 2.8 %shard_map.92 = bf16[4,4,2,32,128]{4,3,2,1,0:T(8,128)(2,1)S(1)} custom-call(s32[1,4]{1,0:T(1,128)S(1)} %copy-done.2, bf16[32,2,16,512]{3,2,1,0:T(8,128)(2,1)S(1)} %all-to-all-done.arrived, bf16[3,512,512]{2,1,0:T(8,128)(2,1)S(1)} %bitcast.16, f32[3,512]{1,0:T(4,128)S(1)} %bitcast.15, bf16[128,512]{1,0:T(8,128)(2,1)S(1)} %bitcast.17, f32[1,128]{1,0:T(1,128)S(1)} %copy-done.3), custom_call_target="tpu_custom_call" | custom-call | flops 1744830464 | bytes 4194304 | tf_op jit(solution)/shard_map/pallas_call | solution.py:60
  63.2 12.6 %all_to_all.20 = bf16[4,4,2,32,128]{4,3,2,1,0:T(8,128)(2,1)S(1)} all-to-all(bf16[4,4,2,32,128]{4,3,2,1,0:T(8,128)(2,1)S(1)} %shard_map.92), channel_id=1, replica_groups=mesh['x'=4,'yh'=4,'yl'=2,'z'=8,'c'=2] {'yh'}, dimensions={0} | all-to-all | bytes 524288 | tf_op jit(solution)/shard_map/all_to_all | solution.py:246
  75.8 0.2 broadcast_in_dim.14
  76.0 14.5 %all_to_all.21 = bf16[4,4,256,128]{3,2,1,0:T(8,128)(2,1)S(1)} all-to-all(bf16[4,4,256,128]{3,2,1,0:T(8,128)(2,1)S(1)} %broadcast_in_dim.14), channel_id=1, replica_groups=mesh['x'=4,'yh'=4,'yl'=2,'z'=8,'c'=2] {'x'}, dimensions={0} | all-to-all | bytes 2097152 | tf_op jit(solution)/shard_map/all_to_all | solution.py:246
  90.5 7.2 %collective-permute-start = (bf16[16,256,128]{2,1,0:T(8,128)(2,1)S(1)}, bf16[16,256,128]{2,1,0:T(8,128)(2,1)S(1)}, u32[]{:S(2)}, u32[]{:S(2)}) collective-permute-start(bf16[16,256,128]{2,1,0:T(8,128)(2,1)S(1)} %bitcast.13), channel_id=1, source_target_pairs={{0,1},{1,0},{2,3},{3,2},{4,5},{5,4},{6,7},{7,6},{8,9},{9,8},{10,11... | collective-permute-start | bytes 3145736 | tf_op jit(solution)/shard_map/ppermute | solution.py:272
  97.8 1.3 %shard_map.93.own = bf16[256,2048]{1,0:T(8,128)(2,1)S(1)} custom-call(bf16[16,256,128]{2,1,0:T(8,128)(2,1)S(1)} %bitcast.14), custom_call_target="tpu_custom_call" | custom-call | flops 1000000000 | bytes 2097152 | tf_op jit(solution)/shard_map/pallas_call | solution.py:102
  99.0 1.0 collective-permute-done.features
  100.0 1.3 %shard_map.94.other = bf16[256,2048]{1,0:T(8,128)(2,1)S(1)} custom-call(bf16[16,256,128]{2,1,0:T(8,128)(2,1)S(1)} %collective-permute-done.features), custom_call_target="tpu_custom_call" | custom-call | flops 1000000000 | bytes 2097152 | tf_op jit(solution)/shard_map/pallas_call | solution.py:102
  101.3 0.0 all-gather.2.cloned.1.call-done.gathered
  101.3 2.8 %shard_map.98 = f32[8,8,128]{2,1,0:T(8,128)S(1)} custom-call(s32[1]{0:T(128)} %bitcast.core, bf16[256,2048]{1,0:T(8,128)(2,1)S(1)} %shard_map.93.own, bf16[256,2048]{1,0:T(8,128)(2,1)S(1)} %shard_map.94.other, bf16[512,2176]{1,0:T(8,128)(2,1)} %all-gather.2.cloned.1.call-done.gathered), custom_call_target="tpu_custom_call" | custom-call | flops 2000000000 | bytes 6291456 | tf_op jit(solution)/shard_map/pallas_call | solution.py:142
  104.2 13.4 %all_to_all.22 = f32[8,8,128]{2,1,0:T(8,128)S(1)} all-to-all(f32[8,8,128]{2,1,0:T(8,128)S(1)} %shard_map.98), channel_id=1, replica_groups=mesh['x'=4,'yh'=4,'yl'=2,'z'=8,'c'=2] {'c','x'}, dimensions={0} | all-to-all | bytes 65536 | tf_op jit(solution)/shard_map/all_to_all | solution.py:246
  117.6 0.6 reshape_squeeze.3
  (3 shorter events, 0.0 us)
Async XLA Ops:
  8.9 51.4 %copy-start.6 = (f32[1,3,512]{2,0,1:T(1,128)S(1)}, f32[1,3,512]{2,0,1:T(1,128)}, u32[]{:S(2)}) copy-start(f32[1,3,512]{2,0,1:T(1,128)} %param.12) | copy-start | bytes 18436
  8.9 51.4 %copy-start = (bf16[1,3,512,512]{3,2,1,0:T(8,128)(2,1)S(1)}, bf16[1,3,512,512]{3,2,1,0:T(8,128)(2,1)}, u32[]{:S(2)}) copy-start(bf16[1,3,512,512]{3,2,1,0:T(8,128)(2,1)} %param.11) | copy-start | bytes 4718596
  8.9 51.4 %copy-start.1 = (bf16[1,128,512]{2,1,0:T(8,128)(2,1)S(1)}, bf16[1,128,512]{2,1,0:T(8,128)(2,1)}, u32[]{:S(2)}) copy-start(bf16[1,128,512]{2,1,0:T(8,128)(2,1)} %param.13) | copy-start | bytes 393220
  8.9 51.4 %copy-start.2 = (s32[1,4]{1,0:T(1,128)S(1)}, s32[1,4]{1,0:T(1,128)}, u32[]{:S(2)}) copy-start(s32[1,4]{1,0:T(1,128)} %order.1) | copy-start | bytes 52
  8.9 51.4 %copy-start.3 = (f32[1,128]{1,0:T(1,128)S(1)}, f32[1,128]{1,0:T(1,128)}, u32[]{:S(2)}) copy-start(f32[1,128]{1,0:T(1,128)} %gain.1) | copy-start | bytes 1540
  8.9 51.4 %all-to-all-start = ((bf16[32,2,16,512]{3,2,1,0:T(8,128)(2,1)}), bf16[32,2,16,512]{3,2,1,0:T(8,128)(2,1)S(1)}, u32[]{:S(2)}, u32[]{:S(2)}) async-start(bf16[32,2,16,512]{3,2,1,0:T(8,128)(2,1)} %shard_map.91), calls=%async_computation | async-start | bytes 2097152 | tf_op jit(solution)/shard_map/all_to_all | solution.py:246
  22.1 79.2 %all-gather.2.cloned.1.call-start = ((), (), s32[]{:S(2)}) async-start(), calls=%async_computation.4 | async-start | bytes 2506752 | tf_op jit(solution)/shard_map/all_gather | solution.py:265
  23.6 11.5 %collective-permute-start.1 = (bf16[8,2176]{1,0:T(8,128)(2,1)}, bf16[8,2176]{1,0:T(8,128)(2,1)S(1)}, u32[]{:S(2)}, u32[]{:S(2)}) collective-permute-start(bf16[8,2176]{1,0:T(8,128)(2,1)} %shard_map.95.refs_0_), channel_id=1, source_target_pairs={{0,32},{32,0},{64,96},{96,64},{1,33},{33,1},{65,97},{97,65},{2,34}... | collective-permute-start | bytes 104456 | tf_op jit(solution)/shard_map/ppermute | solution.py:262
  35.1 0.6 copy-start.5
  37.1 9.2 %collective-permute-start.2 = (bf16[16,2176]{1,0:T(8,128)(2,1)}, bf16[16,2176]{1,0:T(8,128)(2,1)S(1)}, u32[]{:S(2)}, u32[]{:S(2)}) collective-permute-start(bf16[16,2176]{1,0:T(8,128)(2,1)} %bitcast.21), channel_id=1, source_target_pairs={{0,64},{32,96},{64,0},{96,32},{1,65},{33,97},{65,1},{97,33},{2,66}... | collective-permute-start | bytes 208904 | tf_op jit(solution)/shard_map/ppermute | solution.py:263
  46.3 0.6 copy-start.4
  48.5 10.1 %collective-permute-start.3 = (bf16[32,2176]{1,0:T(8,128)(2,1)}, bf16[32,2176]{1,0:T(8,128)(2,1)S(1)}, u32[]{:S(2)}, u32[]{:S(2)}) collective-permute-start(bf16[32,2176]{1,0:T(8,128)(2,1)} %bitcast.19), channel_id=1, source_target_pairs={{0,16},{16,0},{1,17},{17,1},{2,18},{18,2},{3,19},{19,3},{4,20},{20... | collective-permute-start | bytes 417800 | tf_op jit(solution)/shard_map/ppermute | solution.py:264
  90.5 9.5 %collective-permute-start = (bf16[16,256,128]{2,1,0:T(8,128)(2,1)S(1)}, bf16[16,256,128]{2,1,0:T(8,128)(2,1)S(1)}, u32[]{:S(2)}, u32[]{:S(2)}) collective-permute-start(bf16[16,256,128]{2,1,0:T(8,128)(2,1)S(1)} %bitcast.13), channel_id=1, source_target_pairs={{0,1},{1,0},{2,3},{3,2},{4,5},{5,4},{6,7},{7,6},{8,9},{9,8},{10,11... | collective-permute-start | bytes 3145736 | tf_op jit(solution)/shard_map/ppermute | solution.py:272
Sparse Core Ops, SparseCore 0:
  60.4 40.8 all-gather.1

commit v13 on v12

--- a/solution.py
+++ b/solution.py
@@ -225,23 +225,6 @@
     )(mlp_weight, mlp_bias[None], out_weight[None])
 
 
-def stack_kernel(*refs):
-    for k, part in enumerate(refs[:-1]):
-        refs[-1][k] = part[...]
-
-
-def stack(*parts):
-    vmem = pl.BlockSpec(memory_space=pltpu.VMEM)
-    depth, width = parts[0].shape
-    return pl.pallas_call(
-        stack_kernel,
-        out_shape=jax.ShapeDtypeStruct((len(parts), depth, width), parts[0].dtype),
-        in_specs=[vmem] * len(parts),
-        out_specs=vmem,
-        cost_estimate=pl.CostEstimate(flops=0, bytes_accessed=0, transcendentals=0),
-    )(*parts).reshape(len(parts) * depth, width)
-
-
 def exchange(x, axes):
     return lax.all_to_all(x, axes, split_axis=0, concat_axis=0, tiled=True)
 
@@ -259,8 +242,11 @@
 ):
     arrived = exchange(lay_out(pooled), RANK)
     rows = join(mlp_weight, mlp_bias, out_weight)
-    rows = stack(rows, lax.ppermute(rows, "yh", [(i, i ^ 1) for i in range(4)]))
-    rows = stack(rows, lax.ppermute(rows, "yh", [(i, i ^ 2) for i in range(4)]))
+    rows = jnp.concatenate(
+        [rows] + [lax.ppermute(rows, "yh", [(i, (i + k) % 4) for i in range(4)]) for k in (1, 2, 3)],
+        axis=0,
+    )
+    rows = lax.optimization_barrier(rows)
     rows = jnp.concatenate([rows, lax.ppermute(rows, "yl", [(0, 1), (1, 0)])], axis=0)
     rows = lax.all_gather(rows, "z", axis=0, tiled=True)
     towers = tower_block(

time: 126 us -> 126 us (level)
  waiting for transfers between devices: 14.1 us -> 23.9 us
  starting transfers between devices: 38.1 us -> 33.8 us
  Pallas kernels: 15 us -> 12 us
    ppermute x1, waiting for transfers between devices: 3.19 us -> 13.4 us  [on_device(): lax.ppermute(rows, 'yl', [(0, 1), (1, 0)])]
    ppermute x2 -> x3, waiting for transfers between devices: 9.92 us -> 0.01 us  [on_device(): lax.ppermute(rows, 'yh', [(i, (i + k) % 4) for i in range(4)])]
    all_to_all x1, waiting for transfers between devices: 0.01 us -> 9.42 us  [exchange(): return lax.all_to_all(x, axes, split_axis=0, concat_axis=0, tiled=True)]
    ppermute x2 -> x3, starting transfers between devices: 10.7 us -> 14.6 us  [on_device(): lax.ppermute(rows, 'yh', [(i, (i + k) % 4) for i in range(4)])]
    ppermute x1, starting transfers between devices: 6.93 us -> 3.3 us  [on_device(): lax.ppermute(rows, 'yl', [(0, 1), (1, 0)])]
    ppermute x1, starting transfers between devices: 7.22 us -> 3.8 us  [on_device(): other = interact_all(lax.ppermute(features, 'c', [(0, 1), (1, 0)]))]
    pallas_call x2 -> x0, Pallas kernels: 2.98 us -> none  [stack(): pl.pallas_call(stack_kernel, out_shape=jax.ShapeDtypeStruct((len(parts),...]
  transfers between devices with their start and end apart: 6 -> 7, of which waited for: 4 -> 3; matrix products, arithmetic and copies ran while one was open for 1% -> 1% of each run, Pallas kernels for 8% -> 6%
where the time goes in v13:
time: 126 us
  blocking collectives  40.6 us (32%)
  starting transfers between devices  33.8 us (27%)
  waiting for transfers between devices  23.9 us (19%)
  between operations  13.6 us (11%)
  Pallas kernels  12 us (10%)
    all_to_all x3, blocking collectives, exchange(): return lax.all_to_all(x, axes, split_axis=0, concat_axis=0, tiled=True)  40.6 us
    ppermute x3, starting transfers between devices, on_device(): lax.ppermute(rows, 'yh', [(i, (i + k) % 4) for i in range(4)])  14.6 us
    ppermute x1, waiting for transfers between devices, on_device(): lax.ppermute(rows, 'yl', [(0, 1), (1, 0)])  13.4 us
    all_to_all x1, starting transfers between devices, exchange(): return lax.all_to_all(x, axes, split_axis=0, concat_axis=0, tiled=True)  12.1 us
    all_to_all x1, waiting for transfers between devices, exchange(): return lax.all_to_all(x, axes, split_axis=0, concat_axis=0, tiled=True)  9.42 us
    ppermute x1, starting transfers between devices, on_device(): other = interact_all(lax.ppermute(features, 'c', [(0, 1), (1, 0)]))  3.8 us
    ppermute x1, starting transfers between devices, on_device(): lax.ppermute(rows, 'yl', [(0, 1), (1, 0)])  3.3 us
    pallas_call x1, Pallas kernels, score(): pl.pallas_call(score_kernel, out_shape=jax.ShapeDtypeStruct((8, 8, 128),...  2.84 us
  transfers between devices with their start and end apart: 7, of which 3 were waited for; matrix products, arithmetic and copies ran while one was open for 1% of the time, Pallas kernels for 6%

profile of v13, /device:TPU:1, one launch (start us, length us, event | category | flops | bytes accessed | tf_op | source)
XLA Modules:
  0.0 125.5 jit_solution(3221577583402208865)
XLA Ops:
  6.5 1.5 %shard_map.95 = bf16[8,2176]{1,0:T(8,128)(2,1)} custom-call(bf16[8,2048]{1,0:T(8,128)(2,1)} %weight.1, bf16[1,8]{1,0:T(2,128)(2,1)} %bitcast.17, bf16[1,8]{1,0:T(2,128)(2,1)} %bitcast.18), custom_call_target="tpu_custom_call" | custom-call | tf_op jit(solution)/shard_map/pallas_call | solution.py:220
  8.0 0.0 copy-start.4
  8.0 0.0 copy-start.5
  8.0 0.0 copy-start
  8.0 0.0 copy-start.1
  8.0 0.0 copy-start.2
  8.0 0.0 copy-start.3
  8.0 6.8 %collective-permute-start.3 = (bf16[8,2176]{1,0:T(8,128)(2,1)}, bf16[8,2176]{1,0:T(8,128)(2,1)S(1)}, u32[]{:S(2)}, u32[]{:S(2)}) collective-permute-start(bf16[8,2176]{1,0:T(8,128)(2,1)} %shard_map.95), channel_id=1, source_target_pairs={{0,96},{32,0},{64,32},{96,64},{1,97},{33,1},{65,33},{97,65},{2,98}... | collective-permute-start | bytes 104456 | tf_op jit(solution)/shard_map/ppermute | solution.py:246
  14.9 3.5 %collective-permute-start.2 = (bf16[8,2176]{1,0:T(8,128)(2,1)}, bf16[8,2176]{1,0:T(8,128)(2,1)S(1)}, u32[]{:S(2)}, u32[]{:S(2)}) collective-permute-start(bf16[8,2176]{1,0:T(8,128)(2,1)} %shard_map.95), channel_id=1, source_target_pairs={{0,64},{32,96},{64,0},{96,32},{1,65},{33,97},{65,1},{97,33},{2,66}... | collective-permute-start | bytes 104456 | tf_op jit(solution)/shard_map/ppermute | solution.py:246
  18.4 4.2 %collective-permute-start.1 = (bf16[8,2176]{1,0:T(8,128)(2,1)}, bf16[8,2176]{1,0:T(8,128)(2,1)S(1)}, u32[]{:S(2)}, u32[]{:S(2)}) collective-permute-start(bf16[8,2176]{1,0:T(8,128)(2,1)} %shard_map.95), channel_id=1, source_target_pairs={{0,32},{32,64},{64,96},{96,0},{1,33},{33,65},{65,97},{97,1},{2,34}... | collective-permute-start | bytes 104456 | tf_op jit(solution)/shard_map/ppermute | solution.py:246
  22.7 2.3 %shard_map.91 = bf16[32,2,16,512]{3,2,1,0:T(8,128)(2,1)} custom-call(bf16[2,16,16384]{2,1,0:T(8,128)(2,1)} %pooled.1), custom_call_target="tpu_custom_call" | custom-call | bytes 4194304 | tf_op jit(solution)/shard_map/pallas_call | solution.py:192
  25.0 12.1 %all-to-all-start = ((bf16[32,2,16,512]{3,2,1,0:T(8,128)(2,1)}), bf16[32,2,16,512]{3,2,1,0:T(8,128)(2,1)S(1)}, u32[]{:S(2)}, u32[]{:S(2)}) async-start(bf16[32,2,16,512]{3,2,1,0:T(8,128)(2,1)} %shard_map.91), calls=%async_computation | async-start | bytes 2097152 | tf_op jit(solution)/shard_map/all_to_all | solution.py:229
  37.1 0.0 all-gather.2.cloned.1.call-start
  37.2 0.0 collective-permute-done.3
  37.2 0.0 collective-permute-done.2
  37.2 0.0 collective-permute-done.1
  37.2 0.0 copy-done.4
  37.2 3.3 %collective-permute-start.4 = (bf16[32,2176]{1,0:T(8,128)(2,1)S(1)}, bf16[32,2176]{1,0:T(8,128)(2,1)S(1)}, u32[]{:S(2)}, u32[]{:S(2)}) collective-permute-start(bf16[32,2176]{1,0:T(8,128)(2,1)S(1)} %pad_maximum_fusion.1), channel_id=1, source_target_pairs={{0,16},{16,0},{1,17},{17,1},{2,18},{18,2},{3,19},{19,3},{4,20},{20... | collective-permute-start | bytes 417800 | tf_op jit(solution)/shard_map/ppermute | solution.py:250
  40.5 13.4 %collective-permute-done.4 = bf16[32,2176]{1,0:T(8,128)(2,1)S(1)} collective-permute-done((bf16[32,2176]{1,0:T(8,128)(2,1)S(1)}, bf16[32,2176]{1,0:T(8,128)(2,1)S(1)}, u32[]{:S(2)}, u32[]{:S(2)}) %collective-permute-start.4) | collective-permute-done | bytes 139296 | tf_op jit(solution)/shard_map/ppermute | solution.py:250
  54.0 0.7 pad_maximum_fusion
  54.7 0.0 all-gather.2.cloned.1.call-update
  54.7 0.0 copy-done.5
  54.8 9.4 %all-to-all-done.arrived = bf16[32,2,16,512]{3,2,1,0:T(8,128)(2,1)S(1)} async-done(((bf16[32,2,16,512]{3,2,1,0:T(8,128)(2,1)}), bf16[32,2,16,512]{3,2,1,0:T(8,128)(2,1)S(1)}, u32[]{:S(2)}, u32[]{:S(2)}) %all-to-all-start) | async-done | bytes 1048608 | tf_op jit(solution)/shard_map/all_to_all | solution.py:229
  64.2 0.0 copy-done
  64.2 0.0 copy-done.1
  64.2 0.0 copy-done.2
  64.2 0.0 copy-done.3
  64.2 2.8 %shard_map.92 = bf16[4,4,2,32,128]{4,3,2,1,0:T(8,128)(2,1)S(1)} custom-call(s32[1,4]{1,0:T(1,128)S(1)} %copy-done.2, bf16[32,2,16,512]{3,2,1,0:T(8,128)(2,1)S(1)} %all-to-all-done.arrived, bf16[3,512,512]{2,1,0:T(8,128)(2,1)S(1)} %bitcast.14, f32[3,512]{1,0:T(4,128)S(1)} %bitcast.13, bf16[128,512]{1,0:T(8,128)(2,1)S(1)} %bitcast.15, f32[1,128]{1,0:T(1,128)S(1)} %copy-done.3), custom_call_target="tpu_custom_call" | custom-call | flops 1744830464 | bytes 4194304 | tf_op jit(solution)/shard_map/pallas_call | solution.py:60
  67.0 14.9 %all_to_all.20 = bf16[4,4,2,32,128]{4,3,2,1,0:T(8,128)(2,1)S(1)} all-to-all(bf16[4,4,2,32,128]{4,3,2,1,0:T(8,128)(2,1)S(1)} %shard_map.92), channel_id=1, replica_groups=mesh['x'=4,'yh'=4,'yl'=2,'z'=8,'c'=2] {'yh'}, dimensions={0} | all-to-all | bytes 524288 | tf_op jit(solution)/shard_map/all_to_all | solution.py:229
  82.0 0.2 broadcast_in_dim.14
  82.2 18.0 %all_to_all.21 = bf16[4,4,256,128]{3,2,1,0:T(8,128)(2,1)S(1)} all-to-all(bf16[4,4,256,128]{3,2,1,0:T(8,128)(2,1)S(1)} %broadcast_in_dim.14), channel_id=1, replica_groups=mesh['x'=4,'yh'=4,'yl'=2,'z'=8,'c'=2] {'x'}, dimensions={0} | all-to-all | bytes 2097152 | tf_op jit(solution)/shard_map/all_to_all | solution.py:229
  100.1 3.8 %collective-permute-start = (bf16[16,256,128]{2,1,0:T(8,128)(2,1)S(1)}, bf16[16,256,128]{2,1,0:T(8,128)(2,1)S(1)}, u32[]{:S(2)}, u32[]{:S(2)}) collective-permute-start(bf16[16,256,128]{2,1,0:T(8,128)(2,1)S(1)} %bitcast.11), channel_id=1, source_target_pairs={{0,1},{1,0},{2,3},{3,2},{4,5},{5,4},{6,7},{7,6},{8,9},{9,8},{10,11... | collective-permute-start | bytes 3145736 | tf_op jit(solution)/shard_map/ppermute | solution.py:258
  104.0 1.3 %shard_map.93.own = bf16[256,2048]{1,0:T(8,128)(2,1)S(1)} custom-call(bf16[16,256,128]{2,1,0:T(8,128)(2,1)S(1)} %bitcast.12), custom_call_target="tpu_custom_call" | custom-call | flops 1000000000 | bytes 2097152 | tf_op jit(solution)/shard_map/pallas_call | solution.py:102
  105.2 1.0 collective-permute-done.features
  106.2 1.3 %shard_map.94.other = bf16[256,2048]{1,0:T(8,128)(2,1)S(1)} custom-call(bf16[16,256,128]{2,1,0:T(8,128)(2,1)S(1)} %collective-permute-done.features), custom_call_target="tpu_custom_call" | custom-call | flops 1000000000 | bytes 2097152 | tf_op jit(solution)/shard_map/pallas_call | solution.py:102
  107.5 0.0 all-gather.2.cloned.1.call-done.gathered
  107.5 2.8 %shard_map.96 = f32[8,8,128]{2,1,0:T(8,128)S(1)} custom-call(s32[1]{0:T(128)} %bitcast.core, bf16[256,2048]{1,0:T(8,128)(2,1)S(1)} %shard_map.93.own, bf16[256,2048]{1,0:T(8,128)(2,1)S(1)} %shard_map.94.other, bf16[512,2176]{1,0:T(8,128)(2,1)} %all-gather.2.cloned.1.call-done.gathered), custom_call_target="tpu_custom_call" | custom-call | flops 2000000000 | bytes 6291456 | tf_op jit(solution)/shard_map/pallas_call | solution.py:142
  110.3 7.7 %all_to_all.22 = f32[8,8,128]{2,1,0:T(8,128)S(1)} all-to-all(f32[8,8,128]{2,1,0:T(8,128)S(1)} %shard_map.96), channel_id=1, replica_groups=mesh['x'=4,'yh'=4,'yl'=2,'z'=8,'c'=2] {'c','x'}, dimensions={0} | all-to-all | bytes 65536 | tf_op jit(solution)/shard_map/all_to_all | solution.py:229
  118.0 0.6 reshape_squeeze.3
  (4 shorter events, 0.1 us)
Async XLA Ops:
  8.0 29.2 %copy-start.4 = (bf16[8,2176]{1,0:T(8,128)(2,1)S(1)}, bf16[8,2176]{1,0:T(8,128)(2,1)}, u32[]{:S(2)}) copy-start(bf16[8,2176]{1,0:T(8,128)(2,1)} %shard_map.95) | copy-start | bytes 104452
  8.0 46.7 %copy-start.5 = (f32[1,3,512]{2,0,1:T(1,128)S(1)}, f32[1,3,512]{2,0,1:T(1,128)}, u32[]{:S(2)}) copy-start(f32[1,3,512]{2,0,1:T(1,128)} %param.12) | copy-start | bytes 18436
  8.0 56.2 %copy-start = (bf16[1,3,512,512]{3,2,1,0:T(8,128)(2,1)S(1)}, bf16[1,3,512,512]{3,2,1,0:T(8,128)(2,1)}, u32[]{:S(2)}) copy-start(bf16[1,3,512,512]{3,2,1,0:T(8,128)(2,1)} %param.11) | copy-start | bytes 4718596
  8.0 56.2 %copy-start.1 = (bf16[1,128,512]{2,1,0:T(8,128)(2,1)S(1)}, bf16[1,128,512]{2,1,0:T(8,128)(2,1)}, u32[]{:S(2)}) copy-start(bf16[1,128,512]{2,1,0:T(8,128)(2,1)} %param.13) | copy-start | bytes 393220
  8.0 56.2 %copy-start.2 = (s32[1,4]{1,0:T(1,128)S(1)}, s32[1,4]{1,0:T(1,128)}, u32[]{:S(2)}) copy-start(s32[1,4]{1,0:T(1,128)} %order.1) | copy-start | bytes 52
  8.0 56.1 %copy-start.3 = (f32[1,128]{1,0:T(1,128)S(1)}, f32[1,128]{1,0:T(1,128)}, u32[]{:S(2)}) copy-start(f32[1,128]{1,0:T(1,128)} %gain.1) | copy-start | bytes 1540
  8.0 29.1 %collective-permute-start.3 = (bf16[8,2176]{1,0:T(8,128)(2,1)}, bf16[8,2176]{1,0:T(8,128)(2,1)S(1)}, u32[]{:S(2)}, u32[]{:S(2)}) collective-permute-start(bf16[8,2176]{1,0:T(8,128)(2,1)} %shard_map.95), channel_id=1, source_target_pairs={{0,96},{32,0},{64,32},{96,64},{1,97},{33,1},{65,33},{97,65},{2,98}... | collective-permute-start | bytes 104456 | tf_op jit(solution)/shard_map/ppermute | solution.py:246
  14.9 22.3 %collective-permute-start.2 = (bf16[8,2176]{1,0:T(8,128)(2,1)}, bf16[8,2176]{1,0:T(8,128)(2,1)S(1)}, u32[]{:S(2)}, u32[]{:S(2)}) collective-permute-start(bf16[8,2176]{1,0:T(8,128)(2,1)} %shard_map.95), channel_id=1, source_target_pairs={{0,64},{32,96},{64,0},{96,32},{1,65},{33,97},{65,1},{97,33},{2,66}... | collective-permute-start | bytes 104456 | tf_op jit(solution)/shard_map/ppermute | solution.py:246
  18.4 18.7 %collective-permute-start.1 = (bf16[8,2176]{1,0:T(8,128)(2,1)}, bf16[8,2176]{1,0:T(8,128)(2,1)S(1)}, u32[]{:S(2)}, u32[]{:S(2)}) collective-permute-start(bf16[8,2176]{1,0:T(8,128)(2,1)} %shard_map.95), channel_id=1, source_target_pairs={{0,32},{32,64},{64,96},{96,0},{1,33},{33,65},{65,97},{97,1},{2,34}... | collective-permute-start | bytes 104456 | tf_op jit(solution)/shard_map/ppermute | solution.py:246
  25.0 39.2 %all-to-all-start = ((bf16[32,2,16,512]{3,2,1,0:T(8,128)(2,1)}), bf16[32,2,16,512]{3,2,1,0:T(8,128)(2,1)S(1)}, u32[]{:S(2)}, u32[]{:S(2)}) async-start(bf16[32,2,16,512]{3,2,1,0:T(8,128)(2,1)} %shard_map.91), calls=%async_computation | async-start | bytes 2097152 | tf_op jit(solution)/shard_map/all_to_all | solution.py:229
  37.1 70.4 %all-gather.2.cloned.1.call-start = ((), (), s32[]{:S(2)}) async-start(), calls=%async_computation.4 | async-start | bytes 2506752 | tf_op jit(solution)/shard_map/all_gather | solution.py:251
  37.2 16.7 %collective-permute-start.4 = (bf16[32,2176]{1,0:T(8,128)(2,1)S(1)}, bf16[32,2176]{1,0:T(8,128)(2,1)S(1)}, u32[]{:S(2)}, u32[]{:S(2)}) collective-permute-start(bf16[32,2176]{1,0:T(8,128)(2,1)S(1)} %pad_maximum_fusion.1), channel_id=1, source_target_pairs={{0,16},{16,0},{1,17},{17,1},{2,18},{18,2},{3,19},{19,3},{4,20},{20... | collective-permute-start | bytes 417800 | tf_op jit(solution)/shard_map/ppermute | solution.py:250
  100.1 6.1 %collective-permute-start = (bf16[16,256,128]{2,1,0:T(8,128)(2,1)S(1)}, bf16[16,256,128]{2,1,0:T(8,128)(2,1)S(1)}, u32[]{:S(2)}, u32[]{:S(2)}) collective-permute-start(bf16[16,256,128]{2,1,0:T(8,128)(2,1)S(1)} %bitcast.11), channel_id=1, source_target_pairs={{0,1},{1,0},{2,3},{3,2},{4,5},{5,4},{6,7},{7,6},{8,9},{9,8},{10,11... | collective-permute-start | bytes 3145736 | tf_op jit(solution)/shard_map/ppermute | solution.py:258
Sparse Core Ops, SparseCore 0:
  54.9 39.1 all-gather.1

commit v14 on v12

--- a/solution.py
+++ b/solution.py
@@ -259,8 +259,9 @@
 ):
     arrived = exchange(lay_out(pooled), RANK)
     rows = join(mlp_weight, mlp_bias, out_weight)
-    rows = stack(rows, lax.ppermute(rows, "yh", [(i, i ^ 1) for i in range(4)]))
-    rows = stack(rows, lax.ppermute(rows, "yh", [(i, i ^ 2) for i in range(4)]))
+    rows = stack(
+        rows, *[lax.ppermute(rows, "yh", [(i, (i + k) % 4) for i in range(4)]) for k in (1, 2, 3)]
+    )
     rows = jnp.concatenate([rows, lax.ppermute(rows, "yl", [(0, 1), (1, 0)])], axis=0)
     rows = lax.all_gather(rows, "z", axis=0, tiled=True)
     towers = tower_block(

time: 126 us -> 116 us (0.921)
  waiting for transfers between devices: 14.1 us -> 9.08 us
  blocking collectives: 40.6 us -> 38.9 us
  Pallas kernels: 15 us -> 13.6 us
  starting transfers between devices: 38.1 us -> 36.7 us
    ppermute x2 -> x3, waiting for transfers between devices: 9.92 us -> 3.96 us  [on_device(): lax.ppermute(rows, 'yh', [(i, (i + k) % 4) for i in range(4)])]
    ppermute x1, starting transfers between devices: 6.93 us -> 2.4 us  [on_device(): lax.ppermute(rows, 'yl', [(0, 1), (1, 0)])]
    ppermute x2 -> x3, starting transfers between devices: 10.7 us -> 13.9 us  [on_device(): lax.ppermute(rows, 'yh', [(i, (i + k) % 4) for i in range(4)])]
    all_to_all x3, blocking collectives: 40.6 us -> 38.9 us  [exchange(): return lax.all_to_all(x, axes, split_axis=0, concat_axis=0, tiled=True)]
    pallas_call x2 -> x1, Pallas kernels: 2.98 us -> 1.48 us  [stack(): pl.pallas_call(stack_kernel, out_shape=jax.ShapeDtypeStruct((len(parts),...]
  transfers between devices with their start and end apart: 6 -> 7, of which waited for: 4 -> 4; matrix products, arithmetic and copies ran while one was open for 1% -> 2% of each run, Pallas kernels for 8% -> 7%
where the time goes in v14:
time: 116 us
  blocking collectives  38.9 us (34%)
  starting transfers between devices  36.7 us (32%)
  Pallas kernels  13.6 us (12%)
  between operations  13.6 us (12%)
  waiting for transfers between devices  9.08 us (8%)
  local copies, waits for them, and re-layouts  2.09 us (2%)
  other arithmetic  1.64 us (1%)
    all_to_all x3, blocking collectives, exchange(): return lax.all_to_all(x, axes, split_axis=0, concat_axis=0, tiled=True)  38.9 us
    ppermute x3, starting transfers between devices, on_device(): lax.ppermute(rows, 'yh', [(i, (i + k) % 4) for i in range(4)])  13.9 us
    all_to_all x1, starting transfers between devices, exchange(): return lax.all_to_all(x, axes, split_axis=0, concat_axis=0, tiled=True)  13 us
    ppermute x1, starting transfers between devices, on_device(): other = interact_all(lax.ppermute(features, 'c', [(0, 1), (1, 0)]))  7.31 us
    ppermute x1, waiting for transfers between devices, on_device(): lax.ppermute(rows, 'yl', [(0, 1), (1, 0)])  4.09 us
    ppermute x3, waiting for transfers between devices, on_device(): lax.ppermute(rows, 'yh', [(i, (i + k) % 4) for i in range(4)])  3.96 us
    pallas_call x1, Pallas kernels, score(): pl.pallas_call(score_kernel, out_shape=jax.ShapeDtypeStruct((8, 8, 128),...  2.84 us
    pallas_call x1, Pallas kernels, tower_block(): pl.pallas_call(tower_kernel, out_shape=jax.ShapeDtypeStruct((4, 4, 2, BLO...  2.83 us
  transfers between devices with their start and end apart: 7, of which 4 were waited for; matrix products, arithmetic and copies ran while one was open for 2% of the time, Pallas kernels for 7%

profile of v14, /device:TPU:1, one launch (start us, length us, event | category | flops | bytes accessed | tf_op | source)
XLA Modules:
  0.0 115.6 jit_solution(3864837729595381958)
XLA Ops:
  6.5 0.0 copy-start.7
  6.5 0.0 copy-start.2
  6.5 0.0 copy-start
  6.5 0.0 copy-start.1
  6.5 0.0 copy-start.3
  6.5 2.4 %shard_map.91 = bf16[32,2,16,512]{3,2,1,0:T(8,128)(2,1)} custom-call(bf16[2,16,16384]{2,1,0:T(8,128)(2,1)} %pooled.1), custom_call_target="tpu_custom_call" | custom-call | bytes 4194304 | tf_op jit(solution)/shard_map/pallas_call | solution.py:192
  9.0 13.0 %all-to-all-start = ((bf16[32,2,16,512]{3,2,1,0:T(8,128)(2,1)}), bf16[32,2,16,512]{3,2,1,0:T(8,128)(2,1)S(1)}, u32[]{:S(2)}, u32[]{:S(2)}) async-start(bf16[32,2,16,512]{3,2,1,0:T(8,128)(2,1)} %shard_map.91), calls=%async_computation | async-start | bytes 2097152 | tf_op jit(solution)/shard_map/all_to_all | solution.py:246
  22.0 0.0 all-gather.2.cloned.1.call-start
  22.0 1.5 %shard_map.95.refs_0_ = bf16[8,2176]{1,0:T(8,128)(2,1)} custom-call(bf16[8,2048]{1,0:T(8,128)(2,1)} %weight.1, bf16[1,8]{1,0:T(2,128)(2,1)} %bitcast.20, bf16[1,8]{1,0:T(2,128)(2,1)} %bitcast.21), custom_call_target="tpu_custom_call" | custom-call | tf_op jit(solution)/shard_map/pallas_call | solution.py:220
  23.5 4.2 %collective-permute-start.1 = (bf16[8,2176]{1,0:T(8,128)(2,1)}, bf16[8,2176]{1,0:T(8,128)(2,1)S(1)}, u32[]{:S(2)}, u32[]{:S(2)}) collective-permute-start(bf16[8,2176]{1,0:T(8,128)(2,1)} %shard_map.95.refs_0_), channel_id=1, source_target_pairs={{0,32},{32,64},{64,96},{96,0},{1,33},{33,65},{65,97},{97,1},{2,34}... | collective-permute-start | bytes 104456 | tf_op jit(solution)/shard_map/ppermute | solution.py:263
  27.7 4.8 %collective-permute-start.2 = (bf16[8,2176]{1,0:T(8,128)(2,1)}, bf16[8,2176]{1,0:T(8,128)(2,1)S(1)}, u32[]{:S(2)}, u32[]{:S(2)}) collective-permute-start(bf16[8,2176]{1,0:T(8,128)(2,1)} %shard_map.95.refs_0_), channel_id=1, source_target_pairs={{0,64},{32,96},{64,0},{96,32},{1,65},{33,97},{65,1},{97,33},{2,66}... | collective-permute-start | bytes 104456 | tf_op jit(solution)/shard_map/ppermute | solution.py:263
  32.5 5.0 %collective-permute-start.3 = (bf16[8,2176]{1,0:T(8,128)(2,1)}, bf16[8,2176]{1,0:T(8,128)(2,1)S(1)}, u32[]{:S(2)}, u32[]{:S(2)}) collective-permute-start(bf16[8,2176]{1,0:T(8,128)(2,1)} %shard_map.95.refs_0_), channel_id=1, source_target_pairs={{0,96},{32,0},{64,32},{96,64},{1,97},{33,1},{65,33},{97,65},{2,98}... | collective-permute-start | bytes 104456 | tf_op jit(solution)/shard_map/ppermute | solution.py:263
  37.5 1.4 %collective-permute-done.1.refs_1_ = bf16[8,2176]{1,0:T(8,128)(2,1)S(1)} collective-permute-done((bf16[8,2176]{1,0:T(8,128)(2,1)}, bf16[8,2176]{1,0:T(8,128)(2,1)S(1)}, u32[]{:S(2)}, u32[]{:S(2)}) %collective-permute-start.1) | collective-permute-done | bytes 34848 | tf_op jit(solution)/shard_map/ppermute | solution.py:263
  38.9 0.0 copy-start.4
  38.9 2.6 %collective-permute-done.2.refs_2_ = bf16[8,2176]{1,0:T(8,128)(2,1)S(1)} collective-permute-done((bf16[8,2176]{1,0:T(8,128)(2,1)}, bf16[8,2176]{1,0:T(8,128)(2,1)S(1)}, u32[]{:S(2)}, u32[]{:S(2)}) %collective-permute-start.2) | collective-permute-done | bytes 34848 | tf_op jit(solution)/shard_map/ppermute | solution.py:263
  41.4 0.0 copy-start.5
  41.4 0.0 collective-permute-done.3.refs_3_
  41.4 0.0 copy-done.4
  41.4 0.6 copy-done.5
  42.0 0.0 copy-start.6
  42.0 0.6 copy-done.6
  42.6 1.5 %shard_map.96 = bf16[4,8,2176]{2,1,0:T(8,128)(2,1)} custom-call(bf16[8,2176]{1,0:T(8,128)(2,1)} %shard_map.95.refs_0_, bf16[8,2176]{1,0:T(8,128)(2,1)} %copy-done.4, bf16[8,2176]{1,0:T(8,128)(2,1)} %copy-done.5, bf16[8,2176]{1,0:T(8,128)(2,1)} %copy-done.6), custom_call_target="tpu_custom_call" | custom-call | tf_op jit(solution)/shard_map/pallas_call | solution.py:236
  44.1 2.4 %collective-permute-start.4 = (bf16[32,2176]{1,0:T(8,128)(2,1)}, bf16[32,2176]{1,0:T(8,128)(2,1)S(1)}, u32[]{:S(2)}, u32[]{:S(2)}) collective-permute-start(bf16[32,2176]{1,0:T(8,128)(2,1)} %bitcast.18), channel_id=1, source_target_pairs={{0,16},{16,0},{1,17},{17,1},{2,18},{18,2},{3,19},{19,3},{4,20},{20... | collective-permute-start | bytes 417800 | tf_op jit(solution)/shard_map/ppermute | solution.py:265
  46.5 4.1 %collective-permute-done.4 = bf16[32,2176]{1,0:T(8,128)(2,1)S(1)} collective-permute-done((bf16[32,2176]{1,0:T(8,128)(2,1)}, bf16[32,2176]{1,0:T(8,128)(2,1)S(1)}, u32[]{:S(2)}, u32[]{:S(2)}) %collective-permute-start.4) | collective-permute-done | bytes 139296 | tf_op jit(solution)/shard_map/ppermute | solution.py:265
  50.6 1.6 %pad_maximum_fusion = bf16[64,2176]{1,0:T(8,128)(2,1)} fusion(bf16[32,2176]{1,0:T(8,128)(2,1)S(1)} %collective-permute-done.4, bf16[32,2176]{1,0:T(8,128)(2,1)} %bitcast.19), kind=kLoop, calls=%fused_computation | loop fusion | flops 557056 | bytes 557056 | tf_op jit(solution)/shard_map/concatenate | solution.py:265
  52.3 0.0 all-gather.2.cloned.1.call-update
  52.3 0.0 copy-done.7
  52.3 0.0 all-to-all-done.arrived
  52.3 0.0 copy-done.2
  52.3 0.0 copy-done
  52.3 0.0 copy-done.1
  52.3 0.0 copy-done.3
  52.4 2.8 %shard_map.92 = bf16[4,4,2,32,128]{4,3,2,1,0:T(8,128)(2,1)S(1)} custom-call(s32[1,4]{1,0:T(1,128)S(1)} %copy-done.2, bf16[32,2,16,512]{3,2,1,0:T(8,128)(2,1)S(1)} %all-to-all-done.arrived, bf16[3,512,512]{2,1,0:T(8,128)(2,1)S(1)} %bitcast.15, f32[3,512]{1,0:T(4,128)S(1)} %bitcast.14, bf16[128,512]{1,0:T(8,128)(2,1)S(1)} %bitcast.16, f32[1,128]{1,0:T(1,128)S(1)} %copy-done.3), custom_call_target="tpu_custom_call" | custom-call | flops 1744830464 | bytes 4194304 | tf_op jit(solution)/shard_map/pallas_call | solution.py:60
  55.2 11.4 %all_to_all.20 = bf16[4,4,2,32,128]{4,3,2,1,0:T(8,128)(2,1)S(1)} all-to-all(bf16[4,4,2,32,128]{4,3,2,1,0:T(8,128)(2,1)S(1)} %shard_map.92), channel_id=1, replica_groups=mesh['x'=4,'yh'=4,'yl'=2,'z'=8,'c'=2] {'yh'}, dimensions={0} | all-to-all | bytes 524288 | tf_op jit(solution)/shard_map/all_to_all | solution.py:246
  66.6 0.2 broadcast_in_dim.14
  66.8 14.5 %all_to_all.21 = bf16[4,4,256,128]{3,2,1,0:T(8,128)(2,1)S(1)} all-to-all(bf16[4,4,256,128]{3,2,1,0:T(8,128)(2,1)S(1)} %broadcast_in_dim.14), channel_id=1, replica_groups=mesh['x'=4,'yh'=4,'yl'=2,'z'=8,'c'=2] {'x'}, dimensions={0} | all-to-all | bytes 2097152 | tf_op jit(solution)/shard_map/all_to_all | solution.py:246
  81.3 7.3 %collective-permute-start = (bf16[16,256,128]{2,1,0:T(8,128)(2,1)S(1)}, bf16[16,256,128]{2,1,0:T(8,128)(2,1)S(1)}, u32[]{:S(2)}, u32[]{:S(2)}) collective-permute-start(bf16[16,256,128]{2,1,0:T(8,128)(2,1)S(1)} %bitcast.12), channel_id=1, source_target_pairs={{0,1},{1,0},{2,3},{3,2},{4,5},{5,4},{6,7},{7,6},{8,9},{9,8},{10,11... | collective-permute-start | bytes 3145736 | tf_op jit(solution)/shard_map/ppermute | solution.py:273
  88.6 1.3 %shard_map.93.own = bf16[256,2048]{1,0:T(8,128)(2,1)S(1)} custom-call(bf16[16,256,128]{2,1,0:T(8,128)(2,1)S(1)} %bitcast.13), custom_call_target="tpu_custom_call" | custom-call | flops 1000000000 | bytes 2097152 | tf_op jit(solution)/shard_map/pallas_call | solution.py:102
  89.9 1.0 collective-permute-done.features
  90.9 1.3 %shard_map.94.other = bf16[256,2048]{1,0:T(8,128)(2,1)S(1)} custom-call(bf16[16,256,128]{2,1,0:T(8,128)(2,1)S(1)} %collective-permute-done.features), custom_call_target="tpu_custom_call" | custom-call | flops 1000000000 | bytes 2097152 | tf_op jit(solution)/shard_map/pallas_call | solution.py:102
  92.1 0.0 all-gather.2.cloned.1.call-done.gathered
  92.2 2.8 %shard_map.97 = f32[8,8,128]{2,1,0:T(8,128)S(1)} custom-call(s32[1]{0:T(128)} %bitcast.core, bf16[256,2048]{1,0:T(8,128)(2,1)S(1)} %shard_map.93.own, bf16[256,2048]{1,0:T(8,128)(2,1)S(1)} %shard_map.94.other, bf16[512,2176]{1,0:T(8,128)(2,1)} %all-gather.2.cloned.1.call-done.gathered), custom_call_target="tpu_custom_call" | custom-call | flops 2000000000 | bytes 6291456 | tf_op jit(solution)/shard_map/pallas_call | solution.py:142
  95.0 13.0 %all_to_all.22 = f32[8,8,128]{2,1,0:T(8,128)S(1)} all-to-all(f32[8,8,128]{2,1,0:T(8,128)S(1)} %shard_map.97), channel_id=1, replica_groups=mesh['x'=4,'yh'=4,'yl'=2,'z'=8,'c'=2] {'c','x'}, dimensions={0} | all-to-all | bytes 65536 | tf_op jit(solution)/shard_map/all_to_all | solution.py:246
  108.1 0.6 reshape_squeeze.3
  (3 shorter events, 0.0 us)
Async XLA Ops:
  6.5 45.7 %copy-start.7 = (f32[1,3,512]{2,0,1:T(1,128)S(1)}, f32[1,3,512]{2,0,1:T(1,128)}, u32[]{:S(2)}) copy-start(f32[1,3,512]{2,0,1:T(1,128)} %param.12) | copy-start | bytes 18436
  6.5 45.8 %copy-start.2 = (s32[1,4]{1,0:T(1,128)S(1)}, s32[1,4]{1,0:T(1,128)}, u32[]{:S(2)}) copy-start(s32[1,4]{1,0:T(1,128)} %order.1) | copy-start | bytes 52
  6.5 45.8 %copy-start = (bf16[1,3,512,512]{3,2,1,0:T(8,128)(2,1)S(1)}, bf16[1,3,512,512]{3,2,1,0:T(8,128)(2,1)}, u32[]{:S(2)}) copy-start(bf16[1,3,512,512]{3,2,1,0:T(8,128)(2,1)} %param.11) | copy-start | bytes 4718596
  6.5 45.8 %copy-start.1 = (bf16[1,128,512]{2,1,0:T(8,128)(2,1)S(1)}, bf16[1,128,512]{2,1,0:T(8,128)(2,1)}, u32[]{:S(2)}) copy-start(bf16[1,128,512]{2,1,0:T(8,128)(2,1)} %param.13) | copy-start | bytes 393220
  6.5 45.8 %copy-start.3 = (f32[1,128]{1,0:T(1,128)S(1)}, f32[1,128]{1,0:T(1,128)}, u32[]{:S(2)}) copy-start(f32[1,128]{1,0:T(1,128)} %gain.1) | copy-start | bytes 1540
  9.0 43.3 %all-to-all-start = ((bf16[32,2,16,512]{3,2,1,0:T(8,128)(2,1)}), bf16[32,2,16,512]{3,2,1,0:T(8,128)(2,1)S(1)}, u32[]{:S(2)}, u32[]{:S(2)}) async-start(bf16[32,2,16,512]{3,2,1,0:T(8,128)(2,1)} %shard_map.91), calls=%async_computation | async-start | bytes 2097152 | tf_op jit(solution)/shard_map/all_to_all | solution.py:246
  22.0 70.2 %all-gather.2.cloned.1.call-start = ((), (), s32[]{:S(2)}) async-start(), calls=%async_computation.4 | async-start | bytes 2506752 | tf_op jit(solution)/shard_map/all_gather | solution.py:266
  23.5 15.4 %collective-permute-start.1 = (bf16[8,2176]{1,0:T(8,128)(2,1)}, bf16[8,2176]{1,0:T(8,128)(2,1)S(1)}, u32[]{:S(2)}, u32[]{:S(2)}) collective-permute-start(bf16[8,2176]{1,0:T(8,128)(2,1)} %shard_map.95.refs_0_), channel_id=1, source_target_pairs={{0,32},{32,64},{64,96},{96,0},{1,33},{33,65},{65,97},{97,1},{2,34}... | collective-permute-start | bytes 104456 | tf_op jit(solution)/shard_map/ppermute | solution.py:263
  27.7 13.7 %collective-permute-start.2 = (bf16[8,2176]{1,0:T(8,128)(2,1)}, bf16[8,2176]{1,0:T(8,128)(2,1)S(1)}, u32[]{:S(2)}, u32[]{:S(2)}) collective-permute-start(bf16[8,2176]{1,0:T(8,128)(2,1)} %shard_map.95.refs_0_), channel_id=1, source_target_pairs={{0,64},{32,96},{64,0},{96,32},{1,65},{33,97},{65,1},{97,33},{2,66}... | collective-permute-start | bytes 104456 | tf_op jit(solution)/shard_map/ppermute | solution.py:263
  32.5 8.9 %collective-permute-start.3 = (bf16[8,2176]{1,0:T(8,128)(2,1)}, bf16[8,2176]{1,0:T(8,128)(2,1)S(1)}, u32[]{:S(2)}, u32[]{:S(2)}) collective-permute-start(bf16[8,2176]{1,0:T(8,128)(2,1)} %shard_map.95.refs_0_), channel_id=1, source_target_pairs={{0,96},{32,0},{64,32},{96,64},{1,97},{33,1},{65,33},{97,65},{2,98}... | collective-permute-start | bytes 104456 | tf_op jit(solution)/shard_map/ppermute | solution.py:263
  38.9 2.6 %copy-start.4 = (bf16[8,2176]{1,0:T(8,128)(2,1)}, bf16[8,2176]{1,0:T(8,128)(2,1)S(1)}, u32[]{:S(2)}) copy-start(bf16[8,2176]{1,0:T(8,128)(2,1)S(1)} %collective-permute-done.1.refs_1_) | copy-start | bytes 104452
  41.4 0.6 copy-start.5
  42.0 0.6 copy-start.6
  44.1 6.5 %collective-permute-start.4 = (bf16[32,2176]{1,0:T(8,128)(2,1)}, bf16[32,2176]{1,0:T(8,128)(2,1)S(1)}, u32[]{:S(2)}, u32[]{:S(2)}) collective-permute-start(bf16[32,2176]{1,0:T(8,128)(2,1)} %bitcast.18), channel_id=1, source_target_pairs={{0,16},{16,0},{1,17},{17,1},{2,18},{18,2},{3,19},{19,3},{4,20},{20... | collective-permute-start | bytes 417800 | tf_op jit(solution)/shard_map/ppermute | solution.py:265
  81.3 9.6 %collective-permute-start = (bf16[16,256,128]{2,1,0:T(8,128)(2,1)S(1)}, bf16[16,256,128]{2,1,0:T(8,128)(2,1)S(1)}, u32[]{:S(2)}, u32[]{:S(2)}) collective-permute-start(bf16[16,256,128]{2,1,0:T(8,128)(2,1)S(1)} %bitcast.12), channel_id=1, source_target_pairs={{0,1},{1,0},{2,3},{3,2},{4,5},{5,4},{6,7},{7,6},{8,9},{9,8},{10,11... | collective-permute-start | bytes 3145736 | tf_op jit(solution)/shard_map/ppermute | solution.py:273
Sparse Core Ops, SparseCore 0:
  52.4 39.1 all-gather.1

commit v15 on v13

--- a/solution.py
+++ b/solution.py
@@ -242,12 +242,8 @@
 ):
     arrived = exchange(lay_out(pooled), RANK)
     rows = join(mlp_weight, mlp_bias, out_weight)
-    rows = jnp.concatenate(
-        [rows] + [lax.ppermute(rows, "yh", [(i, (i + k) % 4) for i in range(4)]) for k in (1, 2, 3)],
-        axis=0,
-    )
-    rows = lax.optimization_barrier(rows)
-    rows = jnp.concatenate([rows, lax.ppermute(rows, "yl", [(0, 1), (1, 0)])], axis=0)
+    rows = lax.all_gather(rows, "yh", axis=0, tiled=True)
+    rows = lax.all_gather(rows, "yl", axis=0, tiled=True)
     rows = lax.all_gather(rows, "z", axis=0, tiled=True)
     towers = tower_block(
         feature_order, arrived, cross_weight[0], cross_bias[0], compress_weight[0], norm_gain

time: 126 us -> 116 us (0.921)
  blocking collectives: 40.6 us -> 67.2 us
  waiting for transfers between devices: 23.9 us -> 1.03 us
  starting transfers between devices: 33.8 us -> 20.3 us
    all_gather x0 -> x2, blocking collectives: none -> 25.8 us  [the longest x1 21.1 us: on_device(): rows = lax.all_gather(rows, 'yh', axis=0, tiled=True)]
    ppermute x4 -> x0, starting transfers between devices: 17.9 us -> none  [the longest x3 14.6 us: on_device(): lax.ppermute(rows, 'yh', [(i, (i + k) % 4) for i in range(4)])]
    ppermute x4 -> x0, waiting for transfers between devices: 13.4 us -> none  [the longest x1 13.4 us: on_device(): lax.ppermute(rows, 'yl', [(0, 1), (1, 0)])]
    all_to_all x1, waiting for transfers between devices: 9.42 us -> 0.01 us  [exchange(): return lax.all_to_all(x, axes, split_axis=0, concat_axis=0, tiled=True)]
    ppermute x1, starting transfers between devices: 3.8 us -> 7.24 us  [on_device(): other = interact_all(lax.ppermute(features, 'c', [(0, 1), (1, 0)]))]
  transfers between devices with their start and end apart: 7 -> 3, of which waited for: 3 -> 1; matrix products, arithmetic and copies ran while one was open for 1% -> 0% of each run, Pallas kernels for 6% -> 6%
where the time goes in v15:
time: 116 us; the launch traced here: 115 us
  blocking collectives  67.2 us (58%)
  starting transfers between devices  20.3 us (18%)
  between operations  13.5 us (12%)
  Pallas kernels  12.1 us (10%)
    all_to_all x3, blocking collectives, exchange(): return lax.all_to_all(x, axes, split_axis=0, concat_axis=0, tiled=True)  41.4 us
    all_gather x1, blocking collectives, on_device(): rows = lax.all_gather(rows, 'yh', axis=0, tiled=True)  21.1 us
    all_to_all x1, starting transfers between devices, exchange(): return lax.all_to_all(x, axes, split_axis=0, concat_axis=0, tiled=True)  13 us
    ppermute x1, starting transfers between devices, on_device(): other = interact_all(lax.ppermute(features, 'c', [(0, 1), (1, 0)]))  7.24 us
    all_gather x1, blocking collectives, on_device(): rows = lax.all_gather(rows, 'yl', axis=0, tiled=True)  4.68 us
    pallas_call x1, Pallas kernels, tower_block(): pl.pallas_call(tower_kernel, out_shape=jax.ShapeDtypeStruct((4, 4, 2, BLO...  2.84 us
    pallas_call x1, Pallas kernels, score(): pl.pallas_call(score_kernel, out_shape=jax.ShapeDtypeStruct((8, 8, 128),...  2.84 us
    pallas_call x2, Pallas kernels, interact_all(): pl.pallas_call(interact_kernel, out_shape=jax.ShapeDtypeStruct((features....  2.52 us
  transfers between devices with their start and end apart: 3, of which 1 were waited for; matrix products, arithmetic and copies ran while one was open for 0% of the time, Pallas kernels for 6%

profile of v15, /device:TPU:1, one launch (start us, length us, event | category | flops | bytes accessed | tf_op | source)
XLA Modules:
  0.0 115.1 jit_solution(1165486431093406086)
XLA Ops:
  6.5 0.0 copy-start.4
  6.5 0.0 copy-start
  6.5 0.0 copy-start.1
  6.5 0.0 copy-start.2
  6.5 0.0 copy-start.3
  6.5 2.4 %shard_map.91 = bf16[32,2,16,512]{3,2,1,0:T(8,128)(2,1)} custom-call(bf16[2,16,16384]{2,1,0:T(8,128)(2,1)} %pooled.1), custom_call_target="tpu_custom_call" | custom-call | bytes 4194304 | tf_op jit(solution)/shard_map/pallas_call | solution.py:192
  9.0 13.0 %all-to-all-start = ((bf16[32,2,16,512]{3,2,1,0:T(8,128)(2,1)}), bf16[32,2,16,512]{3,2,1,0:T(8,128)(2,1)S(1)}, u32[]{:S(2)}, u32[]{:S(2)}) async-start(bf16[32,2,16,512]{3,2,1,0:T(8,128)(2,1)} %shard_map.91), calls=%async_computation | async-start | bytes 2097152 | tf_op jit(solution)/shard_map/all_to_all | solution.py:229
  22.0 0.0 all-gather.2.cloned.1.call-start
  22.1 1.5 %shard_map.95 = bf16[8,2176]{1,0:T(8,128)(2,1)} custom-call(bf16[8,2048]{1,0:T(8,128)(2,1)} %weight.1, bf16[1,8]{1,0:T(2,128)(2,1)} %bitcast.17, bf16[1,8]{1,0:T(2,128)(2,1)} %bitcast.18), custom_call_target="tpu_custom_call" | custom-call | tf_op jit(solution)/shard_map/pallas_call | solution.py:220
  23.5 21.1 %all_gather.9 = bf16[32,2176]{1,0:T(8,128)(2,1)S(1)} all-gather(bf16[8,2176]{1,0:T(8,128)(2,1)} %shard_map.95), channel_id=1, replica_groups=mesh['x'=4,'yh'=4,'yl'=2,'z'=8,'c'=2] {'yh'}, dimensions={0}, use_global_device_ids=true | all-gather | bytes 174080 | tf_op jit(solution)/shard_map/all_gather | solution.py:245
  44.7 4.7 %all_gather.10 = bf16[64,2176]{1,0:T(8,128)(2,1)} all-gather(bf16[32,2176]{1,0:T(8,128)(2,1)S(1)} %all_gather.9), channel_id=1, replica_groups=mesh['x'=4,'yh'=4,'yl'=2,'z'=8,'c'=2] {'yl'}, dimensions={0}, use_global_device_ids=true | all-gather | bytes 417792 | tf_op jit(solution)/shard_map/all_gather | solution.py:246
  49.4 0.0 all-gather.2.cloned.1.call-update
  49.4 0.0 copy-done.4
  49.4 0.0 all-to-all-done.arrived
  49.4 0.0 copy-done
  49.4 0.0 copy-done.1
  49.4 0.0 copy-done.2
  49.4 0.0 copy-done.3
  49.5 2.8 %shard_map.92 = bf16[4,4,2,32,128]{4,3,2,1,0:T(8,128)(2,1)S(1)} custom-call(s32[1,4]{1,0:T(1,128)S(1)} %copy-done.2, bf16[32,2,16,512]{3,2,1,0:T(8,128)(2,1)S(1)} %all-to-all-done.arrived, bf16[3,512,512]{2,1,0:T(8,128)(2,1)S(1)} %bitcast.14, f32[3,512]{1,0:T(4,128)S(1)} %bitcast.13, bf16[128,512]{1,0:T(8,128)(2,1)S(1)} %bitcast.15, f32[1,128]{1,0:T(1,128)S(1)} %copy-done.3), custom_call_target="tpu_custom_call" | custom-call | flops 1744830464 | bytes 4194304 | tf_op jit(solution)/shard_map/pallas_call | solution.py:60
  52.3 13.9 %all_to_all.20 = bf16[4,4,2,32,128]{4,3,2,1,0:T(8,128)(2,1)S(1)} all-to-all(bf16[4,4,2,32,128]{4,3,2,1,0:T(8,128)(2,1)S(1)} %shard_map.92), channel_id=1, replica_groups=mesh['x'=4,'yh'=4,'yl'=2,'z'=8,'c'=2] {'yh'}, dimensions={0} | all-to-all | bytes 524288 | tf_op jit(solution)/shard_map/all_to_all | solution.py:229
  66.2 0.2 broadcast_in_dim.14
  66.4 14.5 %all_to_all.21 = bf16[4,4,256,128]{3,2,1,0:T(8,128)(2,1)S(1)} all-to-all(bf16[4,4,256,128]{3,2,1,0:T(8,128)(2,1)S(1)} %broadcast_in_dim.14), channel_id=1, replica_groups=mesh['x'=4,'yh'=4,'yl'=2,'z'=8,'c'=2] {'x'}, dimensions={0} | all-to-all | bytes 2097152 | tf_op jit(solution)/shard_map/all_to_all | solution.py:229
  80.9 7.2 %collective-permute-start = (bf16[16,256,128]{2,1,0:T(8,128)(2,1)S(1)}, bf16[16,256,128]{2,1,0:T(8,128)(2,1)S(1)}, u32[]{:S(2)}, u32[]{:S(2)}) collective-permute-start(bf16[16,256,128]{2,1,0:T(8,128)(2,1)S(1)} %bitcast.11), channel_id=1, source_target_pairs={{0,1},{1,0},{2,3},{3,2},{4,5},{5,4},{6,7},{7,6},{8,9},{9,8},{10,11... | collective-permute-start | bytes 3145736 | tf_op jit(solution)/shard_map/ppermute | solution.py:254
  88.2 1.3 %shard_map.93.own = bf16[256,2048]{1,0:T(8,128)(2,1)S(1)} custom-call(bf16[16,256,128]{2,1,0:T(8,128)(2,1)S(1)} %bitcast.12), custom_call_target="tpu_custom_call" | custom-call | flops 1000000000 | bytes 2097152 | tf_op jit(solution)/shard_map/pallas_call | solution.py:102
  89.5 1.0 collective-permute-done.features
  90.4 1.3 %shard_map.94.other = bf16[256,2048]{1,0:T(8,128)(2,1)S(1)} custom-call(bf16[16,256,128]{2,1,0:T(8,128)(2,1)S(1)} %collective-permute-done.features), custom_call_target="tpu_custom_call" | custom-call | flops 1000000000 | bytes 2097152 | tf_op jit(solution)/shard_map/pallas_call | solution.py:102
  91.7 0.0 all-gather.2.cloned.1.call-done.gathered
  91.7 2.8 %shard_map.96 = f32[8,8,128]{2,1,0:T(8,128)S(1)} custom-call(s32[1]{0:T(128)} %bitcast.core, bf16[256,2048]{1,0:T(8,128)(2,1)S(1)} %shard_map.93.own, bf16[256,2048]{1,0:T(8,128)(2,1)S(1)} %shard_map.94.other, bf16[512,2176]{1,0:T(8,128)(2,1)} %all-gather.2.cloned.1.call-done.gathered), custom_call_target="tpu_custom_call" | custom-call | flops 2000000000 | bytes 6291456 | tf_op jit(solution)/shard_map/pallas_call | solution.py:142
  94.6 13.0 %all_to_all.22 = f32[8,8,128]{2,1,0:T(8,128)S(1)} all-to-all(f32[8,8,128]{2,1,0:T(8,128)S(1)} %shard_map.96), channel_id=1, replica_groups=mesh['x'=4,'yh'=4,'yl'=2,'z'=8,'c'=2] {'c','x'}, dimensions={0} | all-to-all | bytes 65536 | tf_op jit(solution)/shard_map/all_to_all | solution.py:229
  107.6 0.6 reshape_squeeze.3
  (3 shorter events, 0.0 us)
Async XLA Ops:
  6.5 42.9 %copy-start.4 = (f32[1,3,512]{2,0,1:T(1,128)S(1)}, f32[1,3,512]{2,0,1:T(1,128)}, u32[]{:S(2)}) copy-start(f32[1,3,512]{2,0,1:T(1,128)} %param.12) | copy-start | bytes 18436
  6.5 42.9 %copy-start = (bf16[1,3,512,512]{3,2,1,0:T(8,128)(2,1)S(1)}, bf16[1,3,512,512]{3,2,1,0:T(8,128)(2,1)}, u32[]{:S(2)}) copy-start(bf16[1,3,512,512]{3,2,1,0:T(8,128)(2,1)} %param.11) | copy-start | bytes 4718596
  6.5 42.9 %copy-start.1 = (bf16[1,128,512]{2,1,0:T(8,128)(2,1)S(1)}, bf16[1,128,512]{2,1,0:T(8,128)(2,1)}, u32[]{:S(2)}) copy-start(bf16[1,128,512]{2,1,0:T(8,128)(2,1)} %param.13) | copy-start | bytes 393220
  6.5 42.9 %copy-start.2 = (s32[1,4]{1,0:T(1,128)S(1)}, s32[1,4]{1,0:T(1,128)}, u32[]{:S(2)}) copy-start(s32[1,4]{1,0:T(1,128)} %order.1) | copy-start | bytes 52
  6.5 42.9 %copy-start.3 = (f32[1,128]{1,0:T(1,128)S(1)}, f32[1,128]{1,0:T(1,128)}, u32[]{:S(2)}) copy-start(f32[1,128]{1,0:T(1,128)} %gain.1) | copy-start | bytes 1540
  9.0 40.4 %all-to-all-start = ((bf16[32,2,16,512]{3,2,1,0:T(8,128)(2,1)}), bf16[32,2,16,512]{3,2,1,0:T(8,128)(2,1)S(1)}, u32[]{:S(2)}, u32[]{:S(2)}) async-start(bf16[32,2,16,512]{3,2,1,0:T(8,128)(2,1)} %shard_map.91), calls=%async_computation | async-start | bytes 2097152 | tf_op jit(solution)/shard_map/all_to_all | solution.py:229
  22.0 69.7 %all-gather.2.cloned.1.call-start = ((), (), s32[]{:S(2)}) async-start(), calls=%async_computation.4 | async-start | bytes 2506752 | tf_op jit(solution)/shard_map/all_gather | solution.py:247
  80.9 9.5 %collective-permute-start = (bf16[16,256,128]{2,1,0:T(8,128)(2,1)S(1)}, bf16[16,256,128]{2,1,0:T(8,128)(2,1)S(1)}, u32[]{:S(2)}, u32[]{:S(2)}) collective-permute-start(bf16[16,256,128]{2,1,0:T(8,128)(2,1)S(1)} %bitcast.11), channel_id=1, source_target_pairs={{0,1},{1,0},{2,3},{3,2},{4,5},{5,4},{6,7},{7,6},{8,9},{9,8},{10,11... | collective-permute-start | bytes 3145736 | tf_op jit(solution)/shard_map/ppermute | solution.py:254
Sparse Core Ops, SparseCore 0:
  49.5 41.7 all-gather.1

commit v16 on v14

--- a/solution.py
+++ b/solution.py
@@ -262,7 +262,7 @@
     rows = stack(
         rows, *[lax.ppermute(rows, "yh", [(i, (i + k) % 4) for i in range(4)]) for k in (1, 2, 3)]
     )
-    rows = jnp.concatenate([rows, lax.ppermute(rows, "yl", [(0, 1), (1, 0)])], axis=0)
+    rows = lax.all_gather(rows, "yl", axis=0, tiled=True)
     rows = lax.all_gather(rows, "z", axis=0, tiled=True)
     towers = tower_block(
         feature_order, arrived, cross_weight[0], cross_bias[0], compress_weight[0], norm_gain

time: 116 us -> 114 us (0.983)
  blocking collectives: 38.9 us -> 46.5 us
  waiting for transfers between devices: 9.08 us -> 4.99 us
  starting transfers between devices: 36.7 us -> 33.1 us
  other arithmetic: 1.64 us -> 0.01 us
    all_gather x0 -> x1, blocking collectives: none -> 5.46 us  [on_device(): rows = lax.all_gather(rows, 'yl', axis=0, tiled=True)]
    ppermute x1 -> x0, waiting for transfers between devices: 4.09 us -> none  [on_device(): lax.ppermute(rows, 'yl', [(0, 1), (1, 0)])]
    ppermute x1 -> x0, starting transfers between devices: 2.4 us -> none  [on_device(): lax.ppermute(rows, 'yl', [(0, 1), (1, 0)])]
    all_to_all x3, blocking collectives: 38.9 us -> 41 us  [exchange(): return lax.all_to_all(x, axes, split_axis=0, concat_axis=0, tiled=True)]
    concatenate x1 -> x0, other arithmetic: 1.63 us -> none  [on_device(): jnp.concatenate([rows, lax.ppermute(rows, 'yl', [(0, 1), (1, 0)])], axis=0)]
    ppermute x1, starting transfers between devices: 7.31 us -> 6.09 us  [on_device(): other = interact_all(lax.ppermute(features, 'c', [(0, 1), (1, 0)]))]
  transfers between devices with their start and end apart: 7 -> 6, of which waited for: 4 -> 3; matrix products, arithmetic and copies ran while one was open for 2% -> 0% of each run, Pallas kernels for 7% -> 7%
where the time goes in v16:
time: 114 us
  blocking collectives  46.5 us (41%)
  starting transfers between devices  33.1 us (29%)
  Pallas kernels  13.6 us (12%)
  between operations  13.6 us (12%)
  waiting for transfers between devices  4.99 us (4%)
  local copies, waits for them, and re-layouts  2.1 us (2%)
    all_to_all x3, blocking collectives, exchange(): return lax.all_to_all(x, axes, split_axis=0, concat_axis=0, tiled=True)  41 us
    ppermute x3, starting transfers between devices, on_device(): lax.ppermute(rows, 'yh', [(i, (i + k) % 4) for i in range(4)])  13.9 us
    all_to_all x1, starting transfers between devices, exchange(): return lax.all_to_all(x, axes, split_axis=0, concat_axis=0, tiled=True)  13 us
    ppermute x1, starting transfers between devices, on_device(): other = interact_all(lax.ppermute(features, 'c', [(0, 1), (1, 0)]))  6.09 us
    all_gather x1, blocking collectives, on_device(): rows = lax.all_gather(rows, 'yl', axis=0, tiled=True)  5.46 us
    ppermute x3, waiting for transfers between devices, on_device(): lax.ppermute(rows, 'yh', [(i, (i + k) % 4) for i in range(4)])  3.95 us
    pallas_call x1, Pallas kernels, tower_block(): pl.pallas_call(tower_kernel, out_shape=jax.ShapeDtypeStruct((4, 4, 2, BLO...  2.84 us
    pallas_call x1, Pallas kernels, score(): pl.pallas_call(score_kernel, out_shape=jax.ShapeDtypeStruct((8, 8, 128),...  2.84 us
  transfers between devices with their start and end apart: 6, of which 3 were waited for; matrix products, arithmetic and copies ran while one was open for 0% of the time, Pallas kernels for 7%

profile of v16, /device:TPU:1, one launch (start us, length us, event | category | flops | bytes accessed | tf_op | source)
XLA Modules:
  0.0 113.8 jit_solution(13160943651003359075)
XLA Ops:
  6.5 0.0 copy-start.7
  6.5 0.0 copy-start.2
  6.5 0.0 copy-start
  6.5 0.0 copy-start.1
  6.5 0.0 copy-start.3
  6.5 2.4 %shard_map.91 = bf16[32,2,16,512]{3,2,1,0:T(8,128)(2,1)} custom-call(bf16[2,16,16384]{2,1,0:T(8,128)(2,1)} %pooled.1), custom_call_target="tpu_custom_call" | custom-call | bytes 4194304 | tf_op jit(solution)/shard_map/pallas_call | solution.py:192
  9.0 13.0 %all-to-all-start = ((bf16[32,2,16,512]{3,2,1,0:T(8,128)(2,1)}), bf16[32,2,16,512]{3,2,1,0:T(8,128)(2,1)S(1)}, u32[]{:S(2)}, u32[]{:S(2)}) async-start(bf16[32,2,16,512]{3,2,1,0:T(8,128)(2,1)} %shard_map.91), calls=%async_computation | async-start | bytes 2097152 | tf_op jit(solution)/shard_map/all_to_all | solution.py:246
  22.0 0.0 all-gather.2.cloned.1.call-start
  22.1 1.5 %shard_map.95.refs_0_ = bf16[8,2176]{1,0:T(8,128)(2,1)} custom-call(bf16[8,2048]{1,0:T(8,128)(2,1)} %weight.1, bf16[1,8]{1,0:T(2,128)(2,1)} %bitcast.19, bf16[1,8]{1,0:T(2,128)(2,1)} %bitcast.20), custom_call_target="tpu_custom_call" | custom-call | tf_op jit(solution)/shard_map/pallas_call | solution.py:220
  23.5 4.2 %collective-permute-start.1 = (bf16[8,2176]{1,0:T(8,128)(2,1)}, bf16[8,2176]{1,0:T(8,128)(2,1)S(1)}, u32[]{:S(2)}, u32[]{:S(2)}) collective-permute-start(bf16[8,2176]{1,0:T(8,128)(2,1)} %shard_map.95.refs_0_), channel_id=1, source_target_pairs={{0,32},{32,64},{64,96},{96,0},{1,33},{33,65},{65,97},{97,1},{2,34}... | collective-permute-start | bytes 104456 | tf_op jit(solution)/shard_map/ppermute | solution.py:263
  27.7 4.8 %collective-permute-start.2 = (bf16[8,2176]{1,0:T(8,128)(2,1)}, bf16[8,2176]{1,0:T(8,128)(2,1)S(1)}, u32[]{:S(2)}, u32[]{:S(2)}) collective-permute-start(bf16[8,2176]{1,0:T(8,128)(2,1)} %shard_map.95.refs_0_), channel_id=1, source_target_pairs={{0,64},{32,96},{64,0},{96,32},{1,65},{33,97},{65,1},{97,33},{2,66}... | collective-permute-start | bytes 104456 | tf_op jit(solution)/shard_map/ppermute | solution.py:263
  32.5 5.0 %collective-permute-start.3 = (bf16[8,2176]{1,0:T(8,128)(2,1)}, bf16[8,2176]{1,0:T(8,128)(2,1)S(1)}, u32[]{:S(2)}, u32[]{:S(2)}) collective-permute-start(bf16[8,2176]{1,0:T(8,128)(2,1)} %shard_map.95.refs_0_), channel_id=1, source_target_pairs={{0,96},{32,0},{64,32},{96,64},{1,97},{33,1},{65,33},{97,65},{2,98}... | collective-permute-start | bytes 104456 | tf_op jit(solution)/shard_map/ppermute | solution.py:263
  37.5 1.4 %collective-permute-done.1.refs_1_ = bf16[8,2176]{1,0:T(8,128)(2,1)S(1)} collective-permute-done((bf16[8,2176]{1,0:T(8,128)(2,1)}, bf16[8,2176]{1,0:T(8,128)(2,1)S(1)}, u32[]{:S(2)}, u32[]{:S(2)}) %collective-permute-start.1) | collective-permute-done | bytes 34848 | tf_op jit(solution)/shard_map/ppermute | solution.py:263
  38.9 0.0 copy-start.4
  38.9 2.6 %collective-permute-done.2.refs_2_ = bf16[8,2176]{1,0:T(8,128)(2,1)S(1)} collective-permute-done((bf16[8,2176]{1,0:T(8,128)(2,1)}, bf16[8,2176]{1,0:T(8,128)(2,1)S(1)}, u32[]{:S(2)}, u32[]{:S(2)}) %collective-permute-start.2) | collective-permute-done | bytes 34848 | tf_op jit(solution)/shard_map/ppermute | solution.py:263
  41.4 0.0 copy-start.5
  41.4 0.0 collective-permute-done.3.refs_3_
  41.4 0.0 copy-done.4
  41.4 0.6 copy-done.5
  42.0 0.0 copy-start.6
  42.0 0.6 copy-done.6
  42.7 1.5 %shard_map.96 = bf16[4,8,2176]{2,1,0:T(8,128)(2,1)} custom-call(bf16[8,2176]{1,0:T(8,128)(2,1)} %shard_map.95.refs_0_, bf16[8,2176]{1,0:T(8,128)(2,1)} %copy-done.4, bf16[8,2176]{1,0:T(8,128)(2,1)} %copy-done.5, bf16[8,2176]{1,0:T(8,128)(2,1)} %copy-done.6), custom_call_target="tpu_custom_call" | custom-call | tf_op jit(solution)/shard_map/pallas_call | solution.py:236
  44.1 5.5 %all_gather.6 = bf16[64,2176]{1,0:T(8,128)(2,1)} all-gather(bf16[32,2176]{1,0:T(8,128)(2,1)} %bitcast.18), channel_id=1, replica_groups=mesh['x'=4,'yh'=4,'yl'=2,'z'=8,'c'=2] {'yl'}, dimensions={0}, use_global_device_ids=true | all-gather | bytes 417792 | tf_op jit(solution)/shard_map/all_gather | solution.py:265
  49.6 0.0 all-gather.2.cloned.1.call-update
  49.6 0.0 copy-done.7
  49.6 0.0 all-to-all-done.arrived
  49.6 0.0 copy-done.2
  49.6 0.0 copy-done
  49.7 0.0 copy-done.1
  49.7 0.0 copy-done.3
  49.7 2.8 %shard_map.92 = bf16[4,4,2,32,128]{4,3,2,1,0:T(8,128)(2,1)S(1)} custom-call(s32[1,4]{1,0:T(1,128)S(1)} %copy-done.2, bf16[32,2,16,512]{3,2,1,0:T(8,128)(2,1)S(1)} %all-to-all-done.arrived, bf16[3,512,512]{2,1,0:T(8,128)(2,1)S(1)} %bitcast.15, f32[3,512]{1,0:T(4,128)S(1)} %bitcast.14, bf16[128,512]{1,0:T(8,128)(2,1)S(1)} %bitcast.16, f32[1,128]{1,0:T(1,128)S(1)} %copy-done.3), custom_call_target="tpu_custom_call" | custom-call | flops 1744830464 | bytes 4194304 | tf_op jit(solution)/shard_map/pallas_call | solution.py:60
  52.5 14.4 %all_to_all.20 = bf16[4,4,2,32,128]{4,3,2,1,0:T(8,128)(2,1)S(1)} all-to-all(bf16[4,4,2,32,128]{4,3,2,1,0:T(8,128)(2,1)S(1)} %shard_map.92), channel_id=1, replica_groups=mesh['x'=4,'yh'=4,'yl'=2,'z'=8,'c'=2] {'yh'}, dimensions={0} | all-to-all | bytes 524288 | tf_op jit(solution)/shard_map/all_to_all | solution.py:246
  66.9 0.2 broadcast_in_dim.14
  67.1 15.7 %all_to_all.21 = bf16[4,4,256,128]{3,2,1,0:T(8,128)(2,1)S(1)} all-to-all(bf16[4,4,256,128]{3,2,1,0:T(8,128)(2,1)S(1)} %broadcast_in_dim.14), channel_id=1, replica_groups=mesh['x'=4,'yh'=4,'yl'=2,'z'=8,'c'=2] {'x'}, dimensions={0} | all-to-all | bytes 2097152 | tf_op jit(solution)/shard_map/all_to_all | solution.py:246
  82.8 6.1 %collective-permute-start = (bf16[16,256,128]{2,1,0:T(8,128)(2,1)S(1)}, bf16[16,256,128]{2,1,0:T(8,128)(2,1)S(1)}, u32[]{:S(2)}, u32[]{:S(2)}) collective-permute-start(bf16[16,256,128]{2,1,0:T(8,128)(2,1)S(1)} %bitcast.12), channel_id=1, source_target_pairs={{0,1},{1,0},{2,3},{3,2},{4,5},{5,4},{6,7},{7,6},{8,9},{9,8},{10,11... | collective-permute-start | bytes 3145736 | tf_op jit(solution)/shard_map/ppermute | solution.py:273
  88.9 1.3 %shard_map.93.own = bf16[256,2048]{1,0:T(8,128)(2,1)S(1)} custom-call(bf16[16,256,128]{2,1,0:T(8,128)(2,1)S(1)} %bitcast.13), custom_call_target="tpu_custom_call" | custom-call | flops 1000000000 | bytes 2097152 | tf_op jit(solution)/shard_map/pallas_call | solution.py:102
  90.2 1.0 collective-permute-done.features
  91.2 1.3 %shard_map.94.other = bf16[256,2048]{1,0:T(8,128)(2,1)S(1)} custom-call(bf16[16,256,128]{2,1,0:T(8,128)(2,1)S(1)} %collective-permute-done.features), custom_call_target="tpu_custom_call" | custom-call | flops 1000000000 | bytes 2097152 | tf_op jit(solution)/shard_map/pallas_call | solution.py:102
  92.4 0.0 all-gather.2.cloned.1.call-done.gathered
  92.4 2.8 %shard_map.97 = f32[8,8,128]{2,1,0:T(8,128)S(1)} custom-call(s32[1]{0:T(128)} %bitcast.core, bf16[256,2048]{1,0:T(8,128)(2,1)S(1)} %shard_map.93.own, bf16[256,2048]{1,0:T(8,128)(2,1)S(1)} %shard_map.94.other, bf16[512,2176]{1,0:T(8,128)(2,1)} %all-gather.2.cloned.1.call-done.gathered), custom_call_target="tpu_custom_call" | custom-call | flops 2000000000 | bytes 6291456 | tf_op jit(solution)/shard_map/pallas_call | solution.py:142
  95.3 10.9 %all_to_all.22 = f32[8,8,128]{2,1,0:T(8,128)S(1)} all-to-all(f32[8,8,128]{2,1,0:T(8,128)S(1)} %shard_map.97), channel_id=1, replica_groups=mesh['x'=4,'yh'=4,'yl'=2,'z'=8,'c'=2] {'c','x'}, dimensions={0} | all-to-all | bytes 65536 | tf_op jit(solution)/shard_map/all_to_all | solution.py:246
  106.3 0.6 reshape_squeeze.3
  (3 shorter events, 0.0 us)
Async XLA Ops:
  6.5 43.1 %copy-start.7 = (f32[1,3,512]{2,0,1:T(1,128)S(1)}, f32[1,3,512]{2,0,1:T(1,128)}, u32[]{:S(2)}) copy-start(f32[1,3,512]{2,0,1:T(1,128)} %param.12) | copy-start | bytes 18436
  6.5 43.1 %copy-start.2 = (s32[1,4]{1,0:T(1,128)S(1)}, s32[1,4]{1,0:T(1,128)}, u32[]{:S(2)}) copy-start(s32[1,4]{1,0:T(1,128)} %order.1) | copy-start | bytes 52
  6.5 43.1 %copy-start = (bf16[1,3,512,512]{3,2,1,0:T(8,128)(2,1)S(1)}, bf16[1,3,512,512]{3,2,1,0:T(8,128)(2,1)}, u32[]{:S(2)}) copy-start(bf16[1,3,512,512]{3,2,1,0:T(8,128)(2,1)} %param.11) | copy-start | bytes 4718596
  6.5 43.1 %copy-start.1 = (bf16[1,128,512]{2,1,0:T(8,128)(2,1)S(1)}, bf16[1,128,512]{2,1,0:T(8,128)(2,1)}, u32[]{:S(2)}) copy-start(bf16[1,128,512]{2,1,0:T(8,128)(2,1)} %param.13) | copy-start | bytes 393220
  6.5 43.1 %copy-start.3 = (f32[1,128]{1,0:T(1,128)S(1)}, f32[1,128]{1,0:T(1,128)}, u32[]{:S(2)}) copy-start(f32[1,128]{1,0:T(1,128)} %gain.1) | copy-start | bytes 1540
  9.0 40.6 %all-to-all-start = ((bf16[32,2,16,512]{3,2,1,0:T(8,128)(2,1)}), bf16[32,2,16,512]{3,2,1,0:T(8,128)(2,1)S(1)}, u32[]{:S(2)}, u32[]{:S(2)}) async-start(bf16[32,2,16,512]{3,2,1,0:T(8,128)(2,1)} %shard_map.91), calls=%async_computation | async-start | bytes 2097152 | tf_op jit(solution)/shard_map/all_to_all | solution.py:246
  22.0 70.4 %all-gather.2.cloned.1.call-start = ((), (), s32[]{:S(2)}) async-start(), calls=%async_computation.4 | async-start | bytes 2506752 | tf_op jit(solution)/shard_map/all_gather | solution.py:266
  23.5 15.4 %collective-permute-start.1 = (bf16[8,2176]{1,0:T(8,128)(2,1)}, bf16[8,2176]{1,0:T(8,128)(2,1)S(1)}, u32[]{:S(2)}, u32[]{:S(2)}) collective-permute-start(bf16[8,2176]{1,0:T(8,128)(2,1)} %shard_map.95.refs_0_), channel_id=1, source_target_pairs={{0,32},{32,64},{64,96},{96,0},{1,33},{33,65},{65,97},{97,1},{2,34}... | collective-permute-start | bytes 104456 | tf_op jit(solution)/shard_map/ppermute | solution.py:263
  27.7 13.7 %collective-permute-start.2 = (bf16[8,2176]{1,0:T(8,128)(2,1)}, bf16[8,2176]{1,0:T(8,128)(2,1)S(1)}, u32[]{:S(2)}, u32[]{:S(2)}) collective-permute-start(bf16[8,2176]{1,0:T(8,128)(2,1)} %shard_map.95.refs_0_), channel_id=1, source_target_pairs={{0,64},{32,96},{64,0},{96,32},{1,65},{33,97},{65,1},{97,33},{2,66}... | collective-permute-start | bytes 104456 | tf_op jit(solution)/shard_map/ppermute | solution.py:263
  32.5 8.9 %collective-permute-start.3 = (bf16[8,2176]{1,0:T(8,128)(2,1)}, bf16[8,2176]{1,0:T(8,128)(2,1)S(1)}, u32[]{:S(2)}, u32[]{:S(2)}) collective-permute-start(bf16[8,2176]{1,0:T(8,128)(2,1)} %shard_map.95.refs_0_), channel_id=1, source_target_pairs={{0,96},{32,0},{64,32},{96,64},{1,97},{33,1},{65,33},{97,65},{2,98}... | collective-permute-start | bytes 104456 | tf_op jit(solution)/shard_map/ppermute | solution.py:263
  38.9 2.6 %copy-start.4 = (bf16[8,2176]{1,0:T(8,128)(2,1)}, bf16[8,2176]{1,0:T(8,128)(2,1)S(1)}, u32[]{:S(2)}) copy-start(bf16[8,2176]{1,0:T(8,128)(2,1)S(1)} %collective-permute-done.1.refs_1_) | copy-start | bytes 104452
  41.4 0.6 copy-start.5
  42.0 0.6 copy-start.6
  82.8 8.4 %collective-permute-start = (bf16[16,256,128]{2,1,0:T(8,128)(2,1)S(1)}, bf16[16,256,128]{2,1,0:T(8,128)(2,1)S(1)}, u32[]{:S(2)}, u32[]{:S(2)}) collective-permute-start(bf16[16,256,128]{2,1,0:T(8,128)(2,1)S(1)} %bitcast.12), channel_id=1, source_target_pairs={{0,1},{1,0},{2,3},{3,2},{4,5},{5,4},{6,7},{7,6},{8,9},{9,8},{10,11... | collective-permute-start | bytes 3145736 | tf_op jit(solution)/shard_map/ppermute | solution.py:273
Sparse Core Ops, SparseCore 0:
  49.7 40.1 all-gather.1
